TPU v7x, 128 devices: a whole 4x4x4 slice. The times are simulated.
128 devices in a mesh: seq: 8 (over z, core), exp: 16 (over x, y).
Axes of the slice: x: 4, y: 4, z: 4, core: 2. Of those that a mesh axis runs over, the one named last changes fastest.
Arguments:
- x_in: bfloat16 [16, 1024, 2048], P('exp', 'seq'), may hold values from -6 to 6
- dout: bfloat16 [16, 1024, 2048], P('exp', 'seq'), may hold values from -6 to 6
- route_ids: int32 [16, 1024, 2], P('exp', 'seq'), may hold values from 0 to 15, all different within a row; in each aligned block of 128 rows (0 to 127, 128 to 255, ..., all dimensions but the last counted through in order) at most 20 rows name the same one
- combine: float32 [16, 1024, 2], P('exp', 'seq'), may hold values from 0.2 to 1
- w_up: bfloat16 [16, 7168, 2048], P('exp', 'seq'), may hold values from -0.125 to 0.125
- w_down: bfloat16 [16, 7168, 2048], P('exp', 'seq'), may hold values from -0.0625 to 0.0625
- delta: float32 [16, 1024, 2048], P('exp', 'seq'), may hold values from 0.5 to 768, as said below
- rate: float32 [16, 2048], replicated, may hold values from 0.00028320312 to 0.031, as said below
- bmat: float32 [16, 1024, 16], P('exp', 'seq'), may hold values from -1.5 to 1.5
- cmat: float32 [16, 1024, 16], P('exp', 'seq'), may hold values from -0.375 to 0.375
Outputs:
- d_mid: bfloat16 [16, 1024, 2048], P('exp', 'seq')
- d_scan: bfloat16 [16, 1024, 2048], P('exp', 'seq')
Inputs may be any that keep to these rules, and one draw needn't show every extreme that they name: `route_ids`: each row names 2 different experts; among the 128 rows of one device no expert is named more than 20 times, and in some devices one is named exactly 20 times. `delta`: positive. `rate`: positive.
All inputs are finite; a program needn't handle non-finite values.
Results may differ from a plain program's by a relative error of at most 0.012.
Values may be sent and summed in bfloat16 or wider, within the bound.
No kernel may reach another device: no remote copies, remote signals or barrier semaphores. Data moves between devices by JAX's collectives and lax.ppermute only.
A program may use at most 192 MiB of HBM per device.

v0:
```python
import math

import jax
import jax.numpy as jnp
from jax import lax
from jax.sharding import PartitionSpec as P


def entering(value, axis, combine, identity):
    size, place = (lax.axis_size(axis), lax.axis_index(axis))
    everything = jax.tree.map(
        lambda part, kind: lax.all_gather(part.astype(kind), axis),
        value,
        jax.tree.map(lambda a: jnp.bfloat16 if a.dtype == jnp.float32 else a.dtype, value),
    )
    start = jax.tree.map(
        lambda part, zero: jnp.broadcast_to(jnp.asarray(zero, part.dtype), part.shape),
        value,
        identity,
    )

    def lap(k, before):
        at = size - 1 - k
        reached = at > place
        new = combine(
            before, jax.tree.map(lambda part, own: part[at].astype(own.dtype), everything, value)
        )
        return jax.tree.map(lambda a, b: jnp.where(reached, a, b), new, before)

    return lax.fori_loop(0, size, lap, start)


def slot_tables(route_rows, weights, experts, capacity):
    tokens = route_rows.shape[0]
    flat_ids = route_rows.reshape(-1)
    one_hot = (flat_ids[:, None] == jnp.arange(experts, dtype=jnp.int32)[None, :]).astype(jnp.int32)
    earlier = jnp.cumsum(one_hot, axis=0) - one_hot
    slot_ids = jnp.sum(earlier * one_hot, axis=1)
    target = flat_ids * capacity + slot_ids
    places = jnp.arange(experts * capacity, dtype=jnp.int32)
    picked = (
        (places[:, None] == target[None, :])
        .reshape(experts * capacity, tokens, -1)
        .astype(jnp.float32)
    )
    send_table = jnp.sum(picked, axis=2)
    weigh_table = jnp.sum(picked * weights[None, :, :], axis=2)
    return (send_table, weigh_table)


def compose(high_pair, low_pair):
    return (low_pair[0] * high_pair[0], low_pair[1] + low_pair[0] * high_pair[1])


def hidden_grad(rows_x, rows_dy, up_block, down_block):
    pre_act = lax.dot_general(
        rows_x, up_block, (((1,), (1,)), ((), ())), preferred_element_type=jnp.float32
    )
    back_grad = lax.dot_general(
        rows_dy, down_block, (((1,), (1,)), ((), ())), preferred_element_type=jnp.float32
    )
    sig_pre = jax.nn.sigmoid(pre_act)
    return (back_grad * sig_pre * (1.0 + pre_act * (1.0 - sig_pre))).astype(jnp.bfloat16)


def input_part(grad_pre, up_block):
    return jnp.dot(grad_pre, up_block, preferred_element_type=jnp.float32).astype(jnp.bfloat16)


def on_device(x_in, dout, route_ids, combine, w_up, w_down, delta, rate, bmat, cmat):
    tokens = x_in.shape[1]
    model_dim = x_in.shape[2]
    seq_count = lax.axis_size("seq")
    exp_count = lax.axis_size("exp")
    top_count = route_ids.shape[2]
    capacity = 5 * tokens * top_count // (4 * exp_count)
    send_table, weigh_table = slot_tables(route_ids[0], combine[0], exp_count, capacity)
    send_half = send_table.astype(jnp.bfloat16)
    x_rows = jnp.dot(send_half, x_in[0], preferred_element_type=jnp.float32).astype(jnp.bfloat16)
    dy_rows = jnp.dot(send_half, dout[0], preferred_element_type=jnp.float32).astype(jnp.bfloat16)
    up_local = w_up[0]
    down_local = w_down[0]
    x_all = jnp.broadcast_to(x_rows[None], (seq_count,) + x_rows.shape).reshape(
        seq_count * exp_count, capacity, model_dim
    )
    dy_all = jnp.broadcast_to(dy_rows[None], (seq_count,) + dy_rows.shape).reshape(
        seq_count * exp_count, capacity, model_dim
    )
    got_x, got_dy = (
        lax.all_to_all(x_all, ("seq", "exp"), split_axis=0, concat_axis=0, tiled=True),
        lax.all_to_all(dy_all, ("seq", "exp"), split_axis=0, concat_axis=0, tiled=True),
    )
    grad_pre = hidden_grad(
        got_x.reshape(-1, model_dim), got_dy.reshape(-1, model_dim), up_local, down_local
    )
    partial_rows = input_part(grad_pre, up_local).reshape(
        seq_count * exp_count, capacity, model_dim
    )
    returned = lax.all_to_all(partial_rows, ("seq", "exp"), split_axis=0, concat_axis=0, tiled=True)
    dx_rows = jnp.sum(
        returned.reshape(seq_count, exp_count * capacity, model_dim).astype(jnp.float32), axis=0
    )
    routed_grad = lax.dot_general(
        weigh_table,
        dx_rows,
        (((0,), (0,)), ((), ())),
        precision=lax.Precision.HIGHEST,
        preferred_element_type=jnp.float32,
    )
    mid_local = (dout[0].astype(jnp.float32) + routed_grad).astype(jnp.bfloat16)
    grad_in = mid_local.astype(jnp.float32)
    group_width = 128
    groups = model_dim // group_width
    drive_in = cmat[0]
    mix_in = bmat[0]
    steps_in = delta[0]
    state_count = rate.shape[0]
    state_half = state_count // 2
    span = math.gcd(tokens, 16)
    sub_blocks = tokens // span
    after_sum = jnp.flip(jnp.cumsum(jnp.flip(steps_in, 0), 0), 0) - steps_in
    inner_later = (
        jnp.arange(span, dtype=jnp.int32)[None, :] >= jnp.arange(span, dtype=jnp.int32)[:, None]
    )
    outer_later = (
        jnp.arange(sub_blocks, dtype=jnp.int32)[None, :]
        >= jnp.arange(sub_blocks, dtype=jnp.int32)[:, None]
    )

    def split_groups(values):
        return values.reshape(values.shape[0], groups, group_width).transpose(1, 0, 2)

    def join_groups(values):
        return values.transpose(1, 0, 2).reshape(values.shape[1], model_dim)

    def local_pass(inputs):
        grad_group, after_group, delta_group, rate_group = inputs
        level = after_group.reshape(sub_blocks, span, group_width)
        heads = level[:, 0]
        inner_gap = jnp.maximum(level[:, :, None, :] - level[:, None, :, :], 0.0)
        outer_gap = jnp.maximum(heads[:, None, :] - heads[None, :, :], 0.0)
        next_heads = jnp.concatenate([heads[1:], heads[-1:]], axis=0)
        reach_gap = jnp.maximum(level - next_heads[:, None, :], 0.0)
        local_sum = jnp.zeros((tokens, group_width), jnp.float32)
        start_parts = []
        for low_state in range(0, state_count, state_half):
            rate_part = rate_group[low_state : low_state + state_half]
            drive_part = drive_in[:, low_state : low_state + state_half]
            mix_part = mix_in[:, low_state : low_state + state_half]
            driven = (drive_part[:, :, None] * grad_group[:, None, :]).reshape(
                sub_blocks, span, state_half, group_width
            )
            inner_weight = jnp.where(
                inner_later[None, :, :, None, None],
                jnp.exp(-inner_gap[:, :, :, None, :] * rate_part[None, None, None, :, :]),
                0.0,
            )
            inner_state = jnp.sum(inner_weight * driven[:, None, :, :, :], axis=2)
            outer_weight = jnp.where(
                outer_later[:, :, None, None],
                jnp.exp(-outer_gap[:, :, None, :] * rate_part[None, None, :, :]),
                0.0,
            )
            firsts = jnp.sum(outer_weight * inner_state[None, :, 0], axis=1)
            next_state = jnp.concatenate([firsts[1:], jnp.zeros_like(firsts[:1])], axis=0)
            reach = jnp.exp(-reach_gap[:, :, None, :] * rate_part[None, None, :, :])
            state = (inner_state + reach * next_state[:, None]).reshape(
                tokens, state_half, group_width
            )
            local_sum = local_sum + jnp.sum(mix_part[:, :, None] * state, axis=1)
            start_parts.append(jnp.exp(-delta_group[0][None, :] * rate_part) * state[0])
        block_product = jnp.exp(-(after_group[0] + delta_group[0])[None, :] * rate_group)
        return (local_sum, block_product, jnp.concatenate(start_parts, axis=0))

    local_groups, total_groups, start_groups = lax.map(
        local_pass,
        (
            split_groups(grad_in),
            split_groups(after_sum),
            split_groups(steps_in),
            split_groups(rate),
        ),
    )
    block_total = join_groups(total_groups)
    block_start = join_groups(start_groups)
    chain_total, incoming = entering(
        (block_total, block_start),
        "seq",
        compose,
        (jnp.ones_like(block_total), jnp.zeros_like(block_start)),
    )

    def carry_pass(inputs):
        after_group, rate_group, incoming_group = inputs
        reach_back = (
            jnp.exp(-after_group[:, None, :] * rate_group[None, :, :]) * incoming_group[None, :, :]
        )
        return jnp.sum(mix_in[:, :, None] * reach_back, axis=1)

    carry_groups = lax.map(
        carry_pass, (split_groups(after_sum), split_groups(rate), split_groups(incoming))
    )
    scan_local = (join_groups(local_groups) + join_groups(carry_groups)).astype(jnp.bfloat16)
    return (mid_local[None], scan_local[None])


def solution(mesh):
    return jax.shard_map(
        on_device,
        mesh=mesh,
        in_specs=(
            P("exp", "seq", None),
            P("exp", "seq", None),
            P("exp", "seq", None),
            P("exp", "seq", None),
            P("exp", "seq", None),
            P("exp", "seq", None),
            P("exp", "seq", None),
            P(),
            P("exp", "seq", None),
            P("exp", "seq", None),
        ),
        out_specs=(P("exp", "seq", None), P("exp", "seq", None)),
        check_vma=False,
    )
```

profile of v0, /device:TPU:1, one launch (start us, length us, event | category | flops | bytes accessed | tf_op | source)
XLA Modules:
  0.0 886.9 jit_solution(8430388422512266305)
XLA Ops:
  2.9 1.4 convert_reduce_fusion
  4.9 5.4 broadcast_in_dim.53
  10.2 16.4 %reshape.286 = bf16[128,20,2048]{2,1,0:T(8,128)(2,1)} reshape(bf16[8,320,2048]{2,1,0:T(8,128)(2,1)} %broadcast_in_dim.53) | data formatting | bytes 20971520 | tf_op jit(solution)/shard_map/reshape | solution.py:83
  26.6 11.9 %all-to-all-start.1 = ((bf16[128,20,2048]{2,1,0:T(8,128)(2,1)}), bf16[128,20,2048]{2,1,0:T(8,128)(2,1)}, u32[]{:S(2)}, u32[]{:S(2)}) async-start(bf16[128,20,2048]{2,1,0:T(8,128)(2,1)} %reshape.286), calls=%async_computation.1 | async-start | bytes 25165824 | tf_op jit(solution)/shard_map/all_to_all | solution.py:90
  39.0 5.4 broadcast_in_dim.52
  44.4 16.4 %reshape.284 = bf16[128,20,2048]{2,1,0:T(8,128)(2,1)} reshape(bf16[8,320,2048]{2,1,0:T(8,128)(2,1)} %broadcast_in_dim.52) | data formatting | bytes 20971520 | tf_op jit(solution)/shard_map/reshape | solution.py:86
  60.8 148.7 %all-to-all-done.1 = bf16[128,20,2048]{2,1,0:T(8,128)(2,1)} async-done(((bf16[128,20,2048]{2,1,0:T(8,128)(2,1)}), bf16[128,20,2048]{2,1,0:T(8,128)(2,1)}, u32[]{:S(2)}, u32[]{:S(2)}) %all-to-all-start.1) | async-done | bytes 10485792 | tf_op jit(solution)/shard_map/all_to_all | solution.py:90
  209.4 15.3 %all-to-all-start = ((bf16[128,20,2048]{2,1,0:T(8,128)(2,1)}), bf16[128,20,2048]{2,1,0:T(8,128)(2,1)}, u32[]{:S(2)}, u32[]{:S(2)}) async-start(bf16[128,20,2048]{2,1,0:T(8,128)(2,1)} %reshape.284), calls=%async_computation | async-start | bytes 25165824 | tf_op jit(solution)/shard_map/all_to_all | solution.py:91
  224.7 16.5 %reshape.287 = bf16[2560,2048]{1,0:T(8,128)(2,1)} reshape(bf16[128,20,2048]{2,1,0:T(8,128)(2,1)} %all-to-all-done.1) | data formatting | bytes 20971520 | tf_op jit(solution)/shard_map/reshape | solution.py:94
  241.2 16.2 %fusion.18 = f32[2560,896]{1,0:T(8,128)} fusion(bf16[2560,2048]{1,0:T(8,128)(2,1)} %reshape.287, bf16[1,896,2048]{2,1,0:T(8,128)(2,1)} %param.20), kind=kOutput, calls=%fused_computation.57 | convolution fusion | flops 9395240960 | bytes 23330816 | tf_op jit(solution)/shard_map/dot_general | solution.py:56
  257.4 137.6 %all-to-all-done = bf16[128,20,2048]{2,1,0:T(8,128)(2,1)} async-done(((bf16[128,20,2048]{2,1,0:T(8,128)(2,1)}), bf16[128,20,2048]{2,1,0:T(8,128)(2,1)}, u32[]{:S(2)}, u32[]{:S(2)}) %all-to-all-start) | async-done | bytes 10485792 | tf_op jit(solution)/shard_map/all_to_all | solution.py:91
  395.0 16.5 %reshape.285 = bf16[2560,2048]{1,0:T(8,128)(2,1)} reshape(bf16[128,20,2048]{2,1,0:T(8,128)(2,1)} %all-to-all-done) | data formatting | bytes 20971520 | tf_op jit(solution)/shard_map/reshape | solution.py:94
  411.6 30.2 %convolution_convert_fusion = bf16[2560,2048]{1,0:T(8,128)(2,1)} fusion(f32[2560,896]{1,0:T(8,128)} %fusion.18, bf16[2560,2048]{1,0:T(8,128)(2,1)} %reshape.285, bf16[1,896,2048]{2,1,0:T(8,128)(2,1)} %param.20, bf16[1,896,2048]{2,1,0:T(8,128)(2,1)} %param.21), kind=kOutput, calls=%fused_computation.53 | convolution fusion | flops 18816368640 | bytes 37486592 | tf_op jit(solution)/shard_map/dot_general | solution.py:67
  441.8 16.4 %reshape.288 = bf16[128,20,2048]{2,1,0:T(8,128)(2,1)} reshape(bf16[2560,2048]{1,0:T(8,128)(2,1)} %convolution_convert_fusion) | data formatting | bytes 20971520 | tf_op jit(solution)/shard_map/reshape | solution.py:96
  458.1 8.7 all-to-all-start.2
  467.1 1.3 copy.71
  468.8 0.9 reduce_window_sum.28
  469.8 5.2 rev.8
  475.2 163.7 %all-to-all-done.2 = bf16[128,20,2048]{2,1,0:T(8,128)(2,1)} async-done(((bf16[128,20,2048]{2,1,0:T(8,128)(2,1)}), bf16[128,20,2048]{2,1,0:T(8,128)(2,1)}, u32[]{:S(2)}, u32[]{:S(2)}) %all-to-all-start.2) | async-done | bytes 10485792 | tf_op jit(solution)/shard_map/all_to_all | solution.py:99
  638.9 18.1 %reshape.296 = f32[8,320,2048]{2,1,0:T(8,128)} reshape(bf16[128,20,2048]{2,1,0:T(8,128)(2,1)} %all-to-all-done.2) | data formatting | bytes 31457280 | tf_op jit(solution)/shard_map/convert_element_type | solution.py:101
  657.0 8.0 reduce_sum.109
  665.1 3.1 fusion.22
  668.2 3.4 bitcast_bitcast_fusion
  671.6 1.1 broadcast.134.clone
  672.7 161.4 %while.43 = (s32[]{:T(128)}, f32[16,128,128]{2,1,0:T(8,128)}, bf16[16,16,128]{2,1,0:T(8,128)(2,1)}, bf16[16,16,128]{2,1,0:T(8,128)(2,1)}, f32[128,16]{1,0:T(8,12...) while((s32[]{:T(128)}, f32[16,128,128]{2,1,0:T(8,128)}, ...), condition=%wide.region_14.15_spmd.clone.clone, body=%wide.region_7.14_spmd.clone.clone.sunk | while | flops 19513028 | bytes 9419073 | solution.py:175
  672.7 0.9 constant_dynamic-slice_fusion.6
  674.2 4.2 multiply_reduce_fusion.12
  684.3 4.2 multiply_reduce_fusion.12
  694.4 4.2 multiply_reduce_fusion.12
  704.4 4.2 multiply_reduce_fusion.12
  714.5 4.2 multiply_reduce_fusion.12
  723.1 0.9 constant_dynamic-slice_fusion.6
  724.6 4.2 multiply_reduce_fusion.12
  734.7 4.2 multiply_reduce_fusion.12
  744.8 4.2 multiply_reduce_fusion.12
  754.9 4.2 multiply_reduce_fusion.12
  765.0 4.2 multiply_reduce_fusion.12
  775.1 4.2 multiply_reduce_fusion.12
  785.1 4.2 multiply_reduce_fusion.12
  795.3 4.2 multiply_reduce_fusion.12
  805.3 4.2 multiply_reduce_fusion.12
  815.4 4.2 multiply_reduce_fusion.12
  825.5 4.2 multiply_reduce_fusion.12
  834.1 1.0 copy.74
  835.1 14.4 %all_gather.8 = bf16[8,16,2048]{2,1,0:T(8,128)(2,1)S(1)} all-gather(bf16[1,16,2048]{2,1,0:T(8,128)(2,1)S(1)} %convert_element_type.126), channel_id=1, replica_groups=mesh['seq'=8,'exp'=16] {'seq'}, dimensions={0}, use_global_device_ids=true | all-gather | bytes 589824 | tf_op jit(solution)/shard_map/all_gather | solution.py:12
  850.5 13.1 %all_gather.9 = bf16[8,16,2048]{2,1,0:T(8,128)(2,1)S(1)} all-gather(bf16[1,16,2048]{2,1,0:T(8,128)(2,1)S(1)} %convert_element_type.129), channel_id=1, replica_groups=mesh['seq'=8,'exp'=16] {'seq'}, dimensions={0}, use_global_device_ids=true | all-gather | bytes 589824 | tf_op jit(solution)/shard_map/all_gather | solution.py:12
  864.5 20.9 %while.42 = (s32[]{:T(128)}, f32[16,128,128]{2,1,0:T(8,128)S(1)}, f32[1,128,16]{2,1,0:T(8,128)S(1)}, f32[16,128,128]{2,1,0:T(8,128)}, f32[16,16,128]{2,1,0:T(8,128)S(1)}, /*index=5*/f32[16,16,128]{2,1,0:T(8,128)S(1)}, s32[]{:T(128)}) while((s32[]{:T(128)}, f32[16,128,128]{2,1,0:T(8,128)S(1)}, f32[1,128,16]{2,1,0:T(8,128)S(1)}, ...), condition=%wide.region_19.20_spmd, body=%wide.region_17.19_spmd.sunk | while | flops 1048578 | bytes 450657 | solution.py:200
  885.9 1.0 convert_element_type.132
  (662 shorter events, 116.8 us)
Async XLA Ops:
  0.6 3.7 copy-start
  26.6 11.9 %copy-start.5 = (bf16[1,128,2048]{2,1,0:T(8,128)(2,1)S(1)}, bf16[1,128,2048]{2,1,0:T(8,128)(2,1)}, u32[]{:S(2)}) copy-start(bf16[1,128,2048]{2,1,0:T(8,128)(2,1)} %param.17) | copy-start | bytes 1572868
  26.6 182.8 %all-to-all-start.1 = ((bf16[128,20,2048]{2,1,0:T(8,128)(2,1)}), bf16[128,20,2048]{2,1,0:T(8,128)(2,1)}, u32[]{:S(2)}, u32[]{:S(2)}) async-start(bf16[128,20,2048]{2,1,0:T(8,128)(2,1)} %reshape.286), calls=%async_computation.1 | async-start | bytes 25165824 | tf_op jit(solution)/shard_map/all_to_all | solution.py:90
  209.4 185.6 %all-to-all-start = ((bf16[128,20,2048]{2,1,0:T(8,128)(2,1)}), bf16[128,20,2048]{2,1,0:T(8,128)(2,1)}, u32[]{:S(2)}, u32[]{:S(2)}) async-start(bf16[128,20,2048]{2,1,0:T(8,128)(2,1)} %reshape.284), calls=%async_computation | async-start | bytes 25165824 | tf_op jit(solution)/shard_map/all_to_all | solution.py:91
  458.1 8.8 copy-start.7
  458.1 8.9 %copy-start.2 = (f32[1,128,2048]{2,1,0:T(8,128)S(1)}, f32[1,128,2048]{2,1,0:T(8,128)}, u32[]{:S(2)}) copy-start(f32[1,128,2048]{2,1,0:T(8,128)} %param.22) | copy-start | bytes 3145732
  458.1 180.8 %all-to-all-start.2 = ((bf16[128,20,2048]{2,1,0:T(8,128)(2,1)}), bf16[128,20,2048]{2,1,0:T(8,128)(2,1)}, u32[]{:S(2)}, u32[]{:S(2)}) async-start(bf16[128,20,2048]{2,1,0:T(8,128)(2,1)} %reshape.288), calls=%async_computation.2 | async-start | bytes 25165824 | tf_op jit(solution)/shard_map/all_to_all | solution.py:99
  466.9 8.1 copy-start.6
  466.9 8.2 copy-start.8
  668.2 4.5 copy-start.4
  834.1 51.3 %copy-start.3 = (f32[16,128,128]{2,1,0:T(8,128)S(1)}, f32[16,128,128]{2,1,0:T(8,128)}, u32[]{:S(2)}) copy-start(f32[16,128,128]{2,1,0:T(8,128)} %get-tuple-element.236) | copy-start | bytes 3145732
  834.1 52.8 %copy-start.1 = (bf16[1,128,2048]{2,1,0:T(8,128)(2,1)S(1)}, bf16[1,128,2048]{2,1,0:T(8,128)(2,1)}, u32[]{:S(2)}) copy-start(bf16[1,128,2048]{2,1,0:T(8,128)(2,1)} %param.16) | copy-start | bytes 1572868
where the time goes:
time: 893 us; the launch traced here: 887 us
  waiting for transfers between devices  450 us (50%)
  local copies, waits for them, and re-layouts  167 us (19%)
  other arithmetic  151 us (17%)
  matrix products  50.5 us (6%)
  starting transfers between devices  35.9 us (4%)
  blocking collectives  27.5 us (3%)
    all_to_all x1, waiting for transfers between devices, on_device(): lax.all_to_all(partial_rows, ('seq', 'exp'), split_axis=0, concat_axis=0,...  164 us
    all_to_all x1, waiting for transfers between devices, on_device(): lax.all_to_all(x_all, ('seq', 'exp'), split_axis=0, concat_axis=0, tiled=...  149 us
    all_to_all x1, waiting for transfers between devices, on_device(): lax.all_to_all(dy_all, ('seq', 'exp'), split_axis=0, concat_axis=0, tiled...  138 us
    reduce_sum x16, other arithmetic, local_pass(): inner_state = jnp.sum(inner_weight * driven[:, None, :, :, :], axis=2)  66.8 us
    dot_general x1, matrix products, input_part(): jnp.dot(grad_pre, up_block, preferred_element_type=jnp.float32)  30.2 us
    all_gather x2, blocking collectives, entering(): lax.all_gather(part.astype(kind), axis)  27.5 us
    dynamic_update_slice x32, other arithmetic, on_device(): lax.map(local_pass, (split_groups(grad_in), split_groups(after_sum), spli...  19.2 us
    convert_element_type x1, local copies, waits for them, and re-layouts, on_device(): returned.reshape(seq_count, exp_count * capacity, model_dim)  18.1 us
  transfers between devices with their start and end apart: 3, of which 3 were waited for; matrix products, arithmetic and copies ran while one was open for 7% of the time, Pallas kernels for 0%

commit v1 on v0

v1 whole, which is shorter than its diff:
```python
import functools

import jax
import jax.numpy as jnp
import numpy as np
from jax import lax
from jax.experimental import pallas as pl
from jax.experimental.pallas import tpu as pltpu
from jax.sharding import Mesh
from jax.sharding import PartitionSpec as P

VMEM_LIMIT = 56 * 1024 * 1024
PAD = 24
CORES = 2
HIDDEN_STEP = 128
SCAN_COLS = 1024
BF = jnp.bfloat16
F32 = jnp.float32


def params():
    return pltpu.CompilerParams(vmem_limit_bytes=VMEM_LIMIT)


def whole(*shape):
    return pl.BlockSpec(shape, lambda *_: (0,) * len(shape))


def gather_body(experts, ids_ref, x_ref, dy_ref, xs_ref, dys_ref):
    tokens = x_ref.shape[0]
    ids = ids_ref[...]
    at = lax.broadcasted_iota(jnp.int32, (experts, tokens), 0)
    hots = [(at == ids[k : k + 1, :]).astype(F32) for k in range(2)]
    before = (
        lax.broadcasted_iota(jnp.int32, (tokens, tokens), 0)
        < lax.broadcasted_iota(jnp.int32, (tokens, tokens), 1)
    ).astype(F32)
    earlier = jnp.dot(
        (hots[0] + hots[1]).astype(BF), before.astype(BF), preferred_element_type=F32
    )
    place = lax.broadcasted_iota(jnp.int32, (experts * PAD, tokens), 0)
    pick = None
    for k in range(2):
        slot = jnp.sum(earlier * hots[k], axis=0, keepdims=True).astype(jnp.int32)
        hit = place == ids[k : k + 1, :] * PAD + slot
        pick = hit if pick is None else pick | hit
    table = pick.astype(F32).astype(BF)
    xs_ref[...] = jnp.dot(table, x_ref[...], preferred_element_type=F32).astype(BF)
    dys_ref[...] = jnp.dot(table, dy_ref[...], preferred_element_type=F32).astype(BF)


def gather_rows(ids_t, x, dy, experts):
    rows, dim = experts * PAD, x.shape[1]
    return pl.pallas_call(
        functools.partial(gather_body, experts),
        out_shape=[jax.ShapeDtypeStruct((rows, dim), BF)] * 2,
        compiler_params=params(),
        name="gather_rows",
    )(ids_t, x, dy)


def expert_body(pieces, *refs):
    xs, dys = refs[:pieces], refs[pieces : 2 * pieces]
    up_a, up_b, down_a, down_b = refs[2 * pieces : 2 * pieces + 4]
    outs = refs[2 * pieces + 4 : 3 * pieces + 4]
    x_all, dy_all, total = refs[3 * pieces + 4 :]
    step = pl.program_id(0)

    @pl.when(step == 0)
    def _():
        low = 0
        for x_ref, dy_ref in zip(xs, dys):
            size = x_ref.shape[0]
            x_all[low : low + size] = x_ref[...]
            dy_all[low : low + size] = dy_ref[...]
            low += size

    up = jnp.concatenate([up_a[...], up_b[...]], axis=0)
    down = jnp.concatenate([down_a[...], down_b[...]], axis=0)
    across = (((1,), (1,)), ((), ()))
    pre = lax.dot_general(x_all[...], up, across, preferred_element_type=F32)
    back = lax.dot_general(dy_all[...], down, across, preferred_element_type=F32)
    sig = jax.nn.sigmoid(pre)
    grad = (back * sig * (1.0 + pre * (1.0 - sig))).astype(BF)
    part = jnp.dot(grad, up, preferred_element_type=F32)

    @pl.when(step == 0)
    def _():
        total[...] = part

    @pl.when(step > 0)
    def _():
        total[...] += part

    @pl.when(step == pl.num_programs(0) - 1)
    def _():
        low = 0
        for out in outs:
            size = out.shape[0]
            out[...] = total[low : low + size].astype(BF)
            low += size


def expert_rows(xs, dys, weights):
    pieces = len(xs)
    dim = xs[0].shape[1]
    hidden = weights[0].shape[0]
    rows = sum(x.shape[0] for x in xs)
    tile = pl.BlockSpec((HIDDEN_STEP, dim), lambda i: (i, 0))
    return pl.pallas_call(
        functools.partial(expert_body, pieces),
        grid=(hidden // HIDDEN_STEP,),
        in_specs=[whole(*x.shape) for x in (*xs, *dys)] + [tile] * 4,
        out_specs=[whole(*x.shape) for x in xs],
        out_shape=[jax.ShapeDtypeStruct(x.shape, BF) for x in xs],
        scratch_shapes=[
            pltpu.VMEM((rows, dim), BF),
            pltpu.VMEM((rows, dim), BF),
            pltpu.VMEM((rows, dim), F32),
        ],
        compiler_params=params(),
        cost_estimate=pl.CostEstimate(
            flops=6 * rows * 2 * hidden * dim,
            bytes_accessed=2 * (4 * hidden * dim + 3 * rows * dim),
            transcendentals=rows * 2 * hidden,
        ),
        name="expert_rows",
    )(*xs, *dys, *weights)


def weigh_pair(ids, weights, experts):
    tokens = ids.shape[0]
    at = lax.broadcasted_iota(jnp.int32, (tokens, experts), 1)
    hots = [(at == ids[:, k : k + 1]).astype(F32) for k in range(2)]
    before = (
        lax.broadcasted_iota(jnp.int32, (tokens, tokens), 1)
        < lax.broadcasted_iota(jnp.int32, (tokens, tokens), 0)
    ).astype(F32)
    earlier = jnp.dot(
        before.astype(BF), (hots[0] + hots[1]).astype(BF), preferred_element_type=F32
    )
    place = lax.broadcasted_iota(jnp.int32, (tokens, experts * PAD), 1)
    table = jnp.zeros((tokens, experts * PAD), F32)
    for k in range(2):
        slot = jnp.sum(earlier * hots[k], axis=1, keepdims=True).astype(jnp.int32)
        hit = place == ids[:, k : k + 1] * PAD + slot
        table = table + jnp.where(hit, weights[:, k : k + 1], 0.0)
    high = table.astype(BF)
    low = (table - high.astype(F32)).astype(BF)
    return high, low


def scan_body(
    experts,
    ids_ref,
    weights_ref,
    back_ref,
    dout_ref,
    delta_ref,
    rate_ref,
    mix_ref,
    drive_ref,
    mid_ref,
    local_ref,
    start_ref,
    grad,
):
    high, low = weigh_pair(ids_ref[...], weights_ref[...], experts)
    back = back_ref[...]
    routed = jnp.dot(high, back, preferred_element_type=F32)
    routed += jnp.dot(low, back, preferred_element_type=F32)
    mid = (dout_ref[...].astype(F32) + routed).astype(BF)
    mid_ref[...] = mid
    grad[...] = mid.astype(F32)
    negative = -rate_ref[...]
    tokens, cols = grad.shape
    states = negative.shape[0]
    lanes = mix_ref.shape[2]
    repeat = cols // lanes

    def block(i, flow):
        low_t = pl.multiple_of((tokens // 8 - 1 - i) * 8, 8)
        grads = grad[pl.ds(low_t, 8)]
        deltas = delta_ref[pl.ds(low_t, 8)]
        rows = []
        for r in reversed(range(8)):
            drive = jnp.concatenate([drive_ref[low_t + r]] * repeat, axis=1)
            mix = jnp.concatenate([mix_ref[low_t + r]] * repeat, axis=1)
            state = drive * jnp.broadcast_to(grads[r : r + 1], (states, cols)) + flow
            rows.append(jnp.sum(mix * state, axis=0, keepdims=True))
            decay = jnp.exp(jnp.broadcast_to(deltas[r : r + 1], (states, cols)) * negative)
            flow = decay * state
        local_ref[pl.ds(low_t, 8)] = jnp.concatenate(rows[::-1], axis=0)
        return flow

    start_ref[...] = lax.fori_loop(
        0, tokens // 8, block, jnp.zeros((states, cols), F32)
    ).astype(BF)


def combine_and_scan(ids, weights, back, dout, delta, rate, mix, drive, experts):
    tokens, dim = dout.shape
    states = rate.shape[0]
    cols = SCAN_COLS

    def strip(rows):
        return pl.BlockSpec((rows, cols), lambda i: (0, i))

    return pl.pallas_call(
        functools.partial(scan_body, experts),
        grid=(dim // cols,),
        in_specs=[
            whole(*ids.shape),
            whole(*weights.shape),
            strip(back.shape[0]),
            strip(tokens),
            strip(tokens),
            strip(states),
            whole(*mix.shape),
            whole(*drive.shape),
        ],
        out_specs=[strip(tokens), strip(tokens), strip(states)],
        out_shape=[
            jax.ShapeDtypeStruct((tokens, dim), BF),
            jax.ShapeDtypeStruct((tokens, dim), F32),
            jax.ShapeDtypeStruct((states, dim), BF),
        ],
        scratch_shapes=[pltpu.VMEM((tokens, cols), F32)],
        compiler_params=params(),
        name="combine_and_scan",
    )(ids, weights, back, dout, delta, rate, mix, drive)


def carry_body(place_ref, starts_ref, totals_ref, rate_ref, local_ref, delta_ref, mix_ref, out_ref):
    place = place_ref[0]
    negative = -rate_ref[...]
    tokens, cols = local_ref.shape
    states = negative.shape[0]
    repeat = cols // mix_ref.shape[2]
    blocks = starts_ref.shape[0]
    flow = jnp.zeros((states, cols), F32)
    for at in reversed(range(blocks)):
        passed = jnp.exp(totals_ref[at : at + 1] * negative) * flow
        flow = jnp.where(at > place, starts_ref[at].astype(F32) + passed, flow)

    def block(i, flow):
        low_t = pl.multiple_of((tokens // 16 - 1 - i) * 16, 16)
        deltas = delta_ref[pl.ds(low_t, 16)]
        rows = []
        for r in reversed(range(16)):
            mix = jnp.concatenate([mix_ref[low_t + r]] * repeat, axis=1)
            rows.append(jnp.sum(mix * flow, axis=0, keepdims=True))
            decay = jnp.exp(jnp.broadcast_to(deltas[r : r + 1], (states, cols)) * negative)
            flow = decay * flow
        sums = jnp.concatenate(rows[::-1], axis=0)
        out_ref[pl.ds(low_t, 16)] = (local_ref[pl.ds(low_t, 16)] + sums).astype(BF)
        return flow

    lax.fori_loop(0, tokens // 16, block, flow)


def add_carry(place, starts, totals, rate, local, delta, mix):
    tokens, dim = local.shape
    states = rate.shape[0]
    blocks = starts.shape[0]
    cols = SCAN_COLS

    def strip(rows):
        return pl.BlockSpec((rows, cols), lambda i: (0, i))

    return pl.pallas_call(
        carry_body,
        grid=(dim // cols,),
        in_specs=[
            pl.BlockSpec(memory_space=pltpu.SMEM),
            pl.BlockSpec((blocks, states, cols), lambda i: (0, 0, i)),
            strip(blocks),
            strip(states),
            strip(tokens),
            strip(tokens),
            whole(*mix.shape),
        ],
        out_specs=strip(tokens),
        out_shape=jax.ShapeDtypeStruct((tokens, dim), BF),
        compiler_params=params(),
        name="add_carry",
    )(place, starts, totals, rate, local, delta, mix)


def on_device(z_size, capacity, x_in, dout, route_ids, combine, w_up, w_down, delta, rate, bmat, cmat):
    experts = lax.axis_size("exp")
    x, dy, ids, weights = x_in[0], dout[0], route_ids[0], combine[0]
    dim = x.shape[1]
    rows = experts * capacity
    half = rows // 2
    up, down = w_up[0], w_down[0]

    def shift(value, by):
        ring = [(i, (i + by) % z_size) for i in range(z_size)]
        return lax.ppermute(value, "z", ring)

    def swap(value):
        return lax.ppermute(value, "core", [(0, 1), (1, 0)])

    def exchange(value):
        return lax.all_to_all(
            value.reshape(experts, PAD, dim), "exp", split_axis=0, concat_axis=0, tiled=True
        ).reshape(experts * PAD, dim)

    both = (up, swap(up), down, swap(down))

    squeeze = np.zeros((rows, experts * PAD), np.float32)
    at = np.arange(rows)
    squeeze[at, at // capacity * PAD + at % capacity] = 1.0
    squeeze = jnp.asarray(squeeze, BF)

    x_send, dy_send = gather_rows(ids.T, x, dy, experts)
    x_own = jnp.dot(squeeze, exchange(x_send), preferred_element_type=F32).astype(BF)
    dy_own = jnp.dot(squeeze, exchange(dy_send), preferred_element_type=F32).astype(BF)

    x_prev, x_next = shift(x_own, 1), shift(x_own, -1)
    dy_prev, dy_next = shift(dy_own, 1), shift(dy_own, -1)
    x_far = (shift(x_prev[:half], 1), shift(x_next[half:], -1))
    dy_far = (shift(dy_prev[:half], 1), shift(dy_next[half:], -1))

    (part_own,) = expert_rows((x_own,), (dy_own,), both)
    part_prev, part_next = expert_rows((x_prev, x_next), (dy_prev, dy_next), both)
    far_low, far_high = expert_rows(x_far, dy_far, both)

    def plus(a, b):
        return (a.astype(F32) + b.astype(F32)).astype(BF)

    got_low, got_high = shift(far_low, 1), shift(far_high, -1)
    to_next = jnp.concatenate([plus(part_next[:half], got_low), part_next[half:]], axis=0)
    to_prev = jnp.concatenate([part_prev[:half], plus(part_prev[half:], got_high)], axis=0)
    from_prev, from_next = shift(to_next, 1), shift(to_prev, -1)
    summed = (
        part_own.astype(F32) + from_prev.astype(F32) + from_next.astype(F32)
    ).astype(BF)
    spread = jnp.dot(squeeze.T, summed, preferred_element_type=F32).astype(BF)
    back = exchange(spread)

    lanes = (delta.shape[1], bmat.shape[2], 128)
    mix = jnp.broadcast_to(bmat[0][:, :, None], lanes)
    drive = jnp.broadcast_to(cmat[0][:, :, None], lanes)
    steps = delta[0]
    totals = lax.all_gather(jnp.sum(steps, axis=0), ("z", "core"))
    mid, local, start = combine_and_scan(
        ids, weights, back, dy, steps, rate, mix, drive, experts
    )
    starts = lax.all_gather(start, ("z", "core"))
    place = lax.axis_index(("z", "core")).astype(jnp.int32).reshape(1)
    scan = add_carry(place, starts, totals, rate, local, steps, mix)
    return (mid[None], scan[None])


def solution(mesh):
    seq, exp = mesh.shape["seq"], mesh.shape["exp"]
    z_size = seq // CORES
    split = Mesh(mesh.devices.reshape(z_size, CORES, exp), ("z", "core", "exp"))
    token = P("exp", ("z", "core"), None)

    def run(x_in, dout, route_ids, *rest):
        tokens = route_ids.shape[1] // seq
        capacity = 5 * tokens * route_ids.shape[2] // (4 * exp)
        return jax.shard_map(
            functools.partial(on_device, z_size, capacity),
            mesh=split,
            in_specs=(token,) * 7 + (P(),) + (token,) * 2,
            out_specs=(token, token),
            check_vma=False,
        )(x_in, dout, route_ids, *rest)

    return run
```

time: 893 us -> 289 us (0.32)
  waiting for transfers between devices: 450 us -> 98.2 us
  local copies, waits for them, and re-layouts: 167 us -> 9.29 us
  other arithmetic: 151 us -> 0.63 us
  Pallas kernels: 0 us -> 77 us
  matrix products: 50.5 us -> 6.4 us
  blocking collectives: 27.5 us -> 66.2 us
    all_to_all x3 -> x2, waiting for transfers between devices: 450 us -> 12.3 us  [exchange(): lax.all_to_all(value.reshape(experts, PAD, dim), 'exp', split_axis=0, con...]
    reduce_sum x67 -> x1, other arithmetic: 92.7 us -> 0.06 us  [on_device(): totals = lax.all_gather(jnp.sum(steps, axis=0), ('z', 'core'))]
    ppermute x0 -> x14, waiting for transfers between devices: none -> 85.9 us  [the longest x12 85.9 us: shift(): return lax.ppermute(value, 'z', ring)]
    reshape x5 -> x0, local copies, waits for them, and re-layouts: 82.1 us -> none  [the longest x1 16.5 us: on_device(): got_dy.reshape(-1, model_dim)]
    pallas_call x0 -> x6, Pallas kernels: none -> 77 us  [the longest x3 54.4 us: expert_rows(): pl.pallas_call(functools.partial(expert_body, pieces), grid=(hidden // HI...]
    dot_general x5 -> x3, matrix products: 50.5 us -> 6.4 us  [the longest x1 3.56 us: on_device(): spread = jnp.dot(squeeze.T, summed, preferred_element_type=F32).astype(BF)]
    all_to_all x0 -> x1, blocking collectives: none -> 29.1 us  [exchange(): lax.all_to_all(value.reshape(experts, PAD, dim), 'exp', split_axis=0, con...]
    neg x96 -> x0, other arithmetic: 27.4 us -> none  [the longest x16 13.6 us: carry_pass(): -after_group[:, None, :] * rate_group[None, :, :]]
  transfers between devices with their start and end apart: 3 -> 16, of which waited for: 3 -> 8; matrix products, arithmetic and copies ran while one was open for 7% -> 3% of each run, Pallas kernels for 0% -> 14%
where the time goes in v1:
time: 289 us; the launch traced here: 288 us
  waiting for transfers between devices  98.2 us (34%)
  Pallas kernels  77 us (27%)
  blocking collectives  66.2 us (23%)
  starting transfers between devices  29.3 us (10%)
  local copies, waits for them, and re-layouts  9.29 us (3%)
  matrix products  6.4 us (2%)
    ppermute x12, waiting for transfers between devices, shift(): return lax.ppermute(value, 'z', ring)  85.9 us
    pallas_call x3, Pallas kernels, expert_rows(): pl.pallas_call(functools.partial(expert_body, pieces), grid=(hidden // HI...  54.4 us
    all_to_all x1, blocking collectives, exchange(): lax.all_to_all(value.reshape(experts, PAD, dim), 'exp', split_axis=0, con...  29.1 us
    all_gather x1, blocking collectives, on_device(): starts = lax.all_gather(start, ('z', 'core'))  19.2 us
    all_gather x1, blocking collectives, on_device(): totals = lax.all_gather(jnp.sum(steps, axis=0), ('z', 'core'))  17.8 us
    ppermute x12, starting transfers between devices, shift(): return lax.ppermute(value, 'z', ring)  16.2 us
    all_to_all x2, waiting for transfers between devices, exchange(): lax.all_to_all(value.reshape(experts, PAD, dim), 'exp', split_axis=0, con...  12.3 us
    pallas_call x1, Pallas kernels, combine_and_scan(): pl.pallas_call(functools.partial(scan_body, experts), grid=(dim // cols,)...  11.1 us
  transfers between devices with their start and end apart: 16, of which 8 were waited for; matrix products, arithmetic and copies ran while one was open for 3% of the time, Pallas kernels for 14%

profile of v1, /device:TPU:1, one launch (start us, length us, event | category | flops | bytes accessed | tf_op | source)
XLA Modules:
  0.0 288.0 jit_solution(6689540313781275068)
XLA Ops:
  0.6 0.8 copy.18
  1.4 0.6 copy.20.ids_ref
  2.1 3.7 %gather_rows.1 = (bf16[384,2048]{1,0:T(8,128)(2,1)}, bf16[384,2048]{1,0:T(8,128)(2,1)}) custom-call(s32[2,128]{1,0:T(2,128)} %copy.20.ids_ref, bf16[128,2048]{1,0:T(8,128)(2,1)} %bitcast.46, bf16[128,2048]{1,0:T(8,128)(2,1)} %bitcast.39), custom_call_target="tpu_custom_call" | custom-call | tf_op jit(solution)/shard_map/gather_rows/pallas_call | solution.py:54
  5.8 29.1 %all_to_all.15 = bf16[16,24,2048]{2,1,0:T(8,128)(2,1)S(1)} all-to-all(bf16[16,24,2048]{2,1,0:T(8,128)(2,1)} %bitcast.42), channel_id=1, replica_groups=mesh['z'=4,'core'=2,'exp'=16] {'exp'}, dimensions={0} | all-to-all | bytes 3145728 | tf_op jit(solution)/shard_map/all_to_all | solution.py:306
  34.8 3.9 %all-to-all-start.1 = ((bf16[16,24,2048]{2,1,0:T(8,128)(2,1)}), bf16[16,24,2048]{2,1,0:T(8,128)(2,1)S(1)}, u32[]{:S(2)}, u32[]{:S(2)}) async-start(bf16[16,24,2048]{2,1,0:T(8,128)(2,1)} %bitcast.41), calls=%async_computation.1 | async-start | bytes 3145728 | tf_op jit(solution)/shard_map/all_to_all | solution.py:306
  38.8 2.2 collective-permute-start
  40.9 0.1 collective-permute-start.1
  41.0 2.0 fusion.refs_0_
  43.0 1.6 collective-permute-start.2
  44.7 2.1 collective-permute-start.3
  46.8 12.3 %all-to-all-done.1 = bf16[16,24,2048]{2,1,0:T(8,128)(2,1)S(1)} async-done(((bf16[16,24,2048]{2,1,0:T(8,128)(2,1)}), bf16[16,24,2048]{2,1,0:T(8,128)(2,1)S(1)}, u32[]{:S(2)}, u32[]{:S(2)}) %all-to-all-start.1) | async-done | bytes 1572896 | tf_op jit(solution)/shard_map/all_to_all | solution.py:306
  59.1 0.8 fusion.1.refs_1_
  60.0 1.7 collective-permute-start.4
  61.7 14.1 %collective-permute-done.2.refs_0_ = bf16[320,2048]{1,0:T(8,128)(2,1)S(1)} collective-permute-done((bf16[320,2048]{1,0:T(8,128)(2,1)}, bf16[320,2048]{1,0:T(8,128)(2,1)S(1)}, u32[]{:S(2)}, u32[]{:S(2)}) %collective-permute-start.2) | collective-permute-done | bytes 1310752 | tf_op jit(solution)/shard_map/ppermute | solution.py:300
  75.8 1.3 collective-permute-start.5
  77.1 0.3 collective-permute-start.6
  77.4 1.1 slice.33
  78.6 25.3 %collective-permute-done.4.refs_2_ = bf16[320,2048]{1,0:T(8,128)(2,1)S(1)} collective-permute-done((bf16[320,2048]{1,0:T(8,128)(2,1)S(1)}, bf16[320,2048]{1,0:T(8,128)(2,1)S(1)}, u32[]{:S(2)}, u32[]{:S(2)}) %collective-permute-start.4) | collective-permute-done | bytes 1310752 | tf_op jit(solution)/shard_map/ppermute | solution.py:300
  103.9 1.1 collective-permute-start.7
  105.1 0.4 collective-permute-start.8
  105.6 12.4 %collective-permute-done.6.refs_0_ = bf16[160,2048]{1,0:T(8,128)(2,1)S(1)} collective-permute-done((bf16[160,2048]{1,0:T(8,128)(2,1)S(1)}, bf16[160,2048]{1,0:T(8,128)(2,1)S(1)}, u32[]{:S(2)}, u32[]{:S(2)}) %collective-permute-start.6) | collective-permute-done | bytes 655392 | tf_op jit(solution)/shard_map/ppermute | solution.py:300
  117.9 1.1 collective-permute-start.9
  119.1 12.9 %collective-permute-done.8.refs_2_ = bf16[160,2048]{1,0:T(8,128)(2,1)S(1)} collective-permute-done((bf16[160,2048]{1,0:T(8,128)(2,1)S(1)}, bf16[160,2048]{1,0:T(8,128)(2,1)S(1)}, u32[]{:S(2)}, u32[]{:S(2)}) %collective-permute-start.8) | collective-permute-done | bytes 655392 | tf_op jit(solution)/shard_map/ppermute | solution.py:300
  132.0 0.7 collective-permute-done.9.refs_3_
  132.8 0.7 copy-done.17
  133.5 14.7 %expert_rows.5 = (bf16[160,2048]{1,0:T(8,128)(2,1)}, bf16[160,2048]{1,0:T(8,128)(2,1)}) custom-call(bf16[160,2048]{1,0:T(8,128)(2,1)} %copy-done.13, bf16[160,2048]{1,0:T(8,128)(2,1)} %copy-done.14, bf16[160,2048]{1,0:T(8,128)(2,1)} %copy-done.16, bf16[160,2048]{1,0:T(8,128)(2,1)} %copy-done.17, bf16[896,2048]{1,0:T(8,128)(2,1)} %bitcast.51, ...), custom_call_target="tpu_custom_call" | custom-call | flops 7046430720 | bytes 18612224 | tf_op jit(solution)/shard_map/expert_rows/pallas_call | solution.py:110
  148.3 0.3 collective-permute-start.10
  148.5 24.7 %expert_rows.4 = (bf16[320,2048]{1,0:T(8,128)(2,1)}, bf16[320,2048]{1,0:T(8,128)(2,1)}) custom-call(bf16[320,2048]{1,0:T(8,128)(2,1)} %copy-done.7, bf16[320,2048]{1,0:T(8,128)(2,1)} %collective-permute-done.3.refs_1_, bf16[320,2048]{1,0:T(8,128)(2,1)} %copy-done.8, bf16[320,2048]{1,0:T(8,128)(2,1)} %copy-done.9, bf16[896,2048]{1,0:T(8,128)(2,1)} %bitcast.52, ...), custom_call_target="tpu_custom_call" | custom-call | flops 14092861440 | bytes 22544384 | tf_op jit(solution)/shard_map/expert_rows/pallas_call | solution.py:110
  173.3 1.3 slice.29
  174.6 2.7 collective-permute-start.12
  177.3 0.2 add_convert_fusion.3
  177.7 10.9 %collective-permute-done.12 = bf16[160,2048]{1,0:T(8,128)(2,1)S(1)} collective-permute-done((bf16[160,2048]{1,0:T(8,128)(2,1)S(1)}, bf16[160,2048]{1,0:T(8,128)(2,1)S(1)}, u32[]{:S(2)}, u32[]{:S(2)}) %collective-permute-start.12) | collective-permute-done | bytes 655392 | tf_op jit(solution)/shard_map/ppermute | solution.py:300
  188.6 0.2 add_convert_fusion.2
  188.9 3.5 %collective-permute-start.13 = (bf16[320,2048]{1,0:T(8,128)(2,1)S(1)}, bf16[320,2048]{1,0:T(8,128)(2,1)S(1)}, u32[]{:S(2)}, u32[]{:S(2)}) collective-permute-start(bf16[320,2048]{1,0:T(8,128)(2,1)S(1)} %pad_maximum_fusion.1), channel_id=1, source_target_pairs={{0,96},{32,0},{64,32},{96,64},{1,97},{33,1},{65,33},{97,65},{2,98}... | collective-permute-start | bytes 3932168 | tf_op jit(solution)/shard_map/ppermute | solution.py:300
  192.4 14.9 %expert_rows.3 = bf16[320,2048]{1,0:T(8,128)(2,1)} custom-call(bf16[320,2048]{1,0:T(8,128)(2,1)} %fusion.refs_0_, bf16[320,2048]{1,0:T(8,128)(2,1)} %copy-done.3, bf16[896,2048]{1,0:T(8,128)(2,1)} %bitcast.53, bf16[896,2048]{1,0:T(8,128)(2,1)} %collective-permute-done.refs_3_.refs_5_, bf16[896,2048]{1,0:T(8,128)(2,1)} %bitcast.57, ...), custom_call_target="tpu_custom_call" | custom-call | flops 7046430720 | bytes 18612224 | tf_op jit(solution)/shard_map/expert_rows/pallas_call | solution.py:110
  207.3 9.6 %collective-permute-done.13 = bf16[320,2048]{1,0:T(8,128)(2,1)S(1)} collective-permute-done((bf16[320,2048]{1,0:T(8,128)(2,1)S(1)}, bf16[320,2048]{1,0:T(8,128)(2,1)S(1)}, u32[]{:S(2)}, u32[]{:S(2)}) %collective-permute-start.13) | collective-permute-done | bytes 1310752 | tf_op jit(solution)/shard_map/ppermute | solution.py:300
  216.9 3.6 %convolution_convert_fusion = bf16[2048,384]{0,1:T(8,128)(2,1)} fusion(bf16[320,384]{1,0:T(8,128)(2,1)S(1)} %copy-done.2, bf16[320,2048]{1,0:T(8,128)(2,1)S(1)} %collective-permute-done.13, bf16[320,2048]{1,0:T(8,128)(2,1)S(1)} %collective-permute-done.11, bf16[320,2048]{1,0:T(8,128)(2,1)} %expert_rows.3), kind=kOutput, calls=%fused_computation | convolution fusion | flops 508035072 | bytes 5750784 | tf_op jit(solution)/shard_map/dot_general | solution.py:340
  220.4 7.0 %all-to-all-start.2 = ((bf16[16,24,2048]{2,1,0:T(8,128)(2,1)}), bf16[16,24,2048]{2,1,0:T(8,128)(2,1)S(1)}, u32[]{:S(2)}, u32[]{:S(2)}) async-start(bf16[16,24,2048]{2,1,0:T(8,128)(2,1)} %bitcast.35), calls=%async_computation.2 | async-start | bytes 3145728 | tf_op jit(solution)/shard_map/all_to_all | solution.py:306
  227.4 0.1 copy.21
  227.5 0.1 copy.22
  227.6 0.7 copy.19
  228.4 17.8 %all-gather.1 = f32[16384]{0:T(1024)S(1)} all-gather(f32[2048]{0:T(1024)S(1)} %reduce_sum.9), channel_id=3, replica_groups=mesh['z'=4,'core'=2,'exp'=16] {'z','core'}, dimensions={0}, use_global_device_ids=true | all-gather | bytes 73728 | tf_op jit(solution)/shard_map/all_gather | solution.py:347
  246.3 0.6 reshape.35.totals_ref
  246.9 1.5 broadcast_in_dim.21.mix_ref
  248.4 1.3 broadcast_in_dim.23.drive_ref
  249.7 11.1 %combine_and_scan.1 = (bf16[128,2048]{1,0:T(8,128)(2,1)}, f32[128,2048]{1,0:T(8,128)}, bf16[16,2048]{1,0:T(8,128)(2,1)}) custom-call(s32[128,2]{1,0:T(8,128)} %bitcast.44, f32[128,2]{1,0:T(8,128)} %bitcast.47, bf16[384,2048]{1,0:T(8,128)(2,1)} %bitcast.34, bf16[128,2048]{1,0:T(8,128)(2,1)} %bitcast.40, f32[128,2048]{1,0:T(8,128)} %bitcast.32, ...), custom_call_target="tpu_custom_call" | custom-call | tf_op jit(solution)/shard_map/combine_and_scan/pallas_call | solution.py:209
  260.8 19.2 %all-gather = bf16[128,2048]{1,0:T(8,128)(2,1)} all-gather(bf16[16,2048]{1,0:T(8,128)(2,1)} %get-tuple-element.18), channel_id=2, replica_groups=mesh['z'=4,'core'=2,'exp'=16] {'z','core'}, dimensions={0}, use_global_device_ids=true | all-gather | bytes 589824 | tf_op jit(solution)/shard_map/all_gather | solution.py:351
  280.1 7.9 %add_carry.1 = bf16[128,2048]{1,0:T(8,128)(2,1)} custom-call(s32[1]{0:T(128)} %bitcast.20.place_ref, bf16[8,16,2048]{2,1,0:T(8,128)(2,1)} %bitcast.38, f32[8,2048]{1,0:T(8,128)} %reshape.35.totals_ref, f32[16,2048]{1,0:T(8,128)} %rate_ref.3, f32[128,2048]{1,0:T(8,128)} %get-tuple-element.19.local_ref, f32[128,2048]{1,0:T(8,128)} %bitcast.33, ...), custom_call_target="tpu_custom_call" | custom-call | tf_op jit(solution)/shard_map/add_carry/pallas_call | solution.py:271
  (51 shorter events, 0.7 us)
Async XLA Ops:
  1.4 33.4 %copy-start.6 = (s32[1,128,2]{2,1,0:T(8,128)}, s32[1,128,2]{2,1,0:T(8,128)S(1)}, u32[]{:S(2)}) copy-start(s32[1,128,2]{2,1,0:T(8,128)S(1)} %copy.18) | copy-start | bytes 3076
  34.8 6.2 %copy-start.2 = (bf16[320,384]{1,0:T(8,128)(2,1)S(1)}, bf16[320,384]{1,0:T(8,128)(2,1)}, u32[]{:S(2)}) copy-start(bf16[320,384]{1,0:T(8,128)(2,1)} %constant.18.clone) | copy-start | bytes 737284
  34.8 24.2 %all-to-all-start.1 = ((bf16[16,24,2048]{2,1,0:T(8,128)(2,1)}), bf16[16,24,2048]{2,1,0:T(8,128)(2,1)S(1)}, u32[]{:S(2)}, u32[]{:S(2)}) async-start(bf16[16,24,2048]{2,1,0:T(8,128)(2,1)} %bitcast.41), calls=%async_computation.1 | async-start | bytes 3145728 | tf_op jit(solution)/shard_map/all_to_all | solution.py:306
  38.8 93.9 %collective-permute-start = (bf16[896,2048]{1,0:T(8,128)(2,1)}, bf16[896,2048]{1,0:T(8,128)(2,1)}, u32[]{:S(2)}, u32[]{:S(2)}) collective-permute-start(bf16[896,2048]{1,0:T(8,128)(2,1)} %bitcast.50), channel_id=1, source_target_pairs={{0,16},{16,0},{1,17},{17,1},{2,18},{18,2},{3,19},{19,3},{4,20},{20... | collective-permute-start | bytes 11010056 | tf_op jit(solution)/shard_map/ppermute | solution.py:303
  40.9 91.8 %collective-permute-start.1 = (bf16[896,2048]{1,0:T(8,128)(2,1)}, bf16[896,2048]{1,0:T(8,128)(2,1)}, u32[]{:S(2)}, u32[]{:S(2)}) collective-permute-start(bf16[896,2048]{1,0:T(8,128)(2,1)} %bitcast.54), channel_id=1, source_target_pairs={{0,16},{16,0},{1,17},{17,1},{2,18},{18,2},{3,19},{19,3},{4,20},{20... | collective-permute-start | bytes 11010056 | tf_op jit(solution)/shard_map/ppermute | solution.py:303
  43.0 32.8 %collective-permute-start.2 = (bf16[320,2048]{1,0:T(8,128)(2,1)}, bf16[320,2048]{1,0:T(8,128)(2,1)S(1)}, u32[]{:S(2)}, u32[]{:S(2)}) collective-permute-start(bf16[320,2048]{1,0:T(8,128)(2,1)} %fusion.refs_0_), channel_id=1, source_target_pairs={{0,32},{32,64},{64,96},{96,0},{1,33},{33,65},{65,97},{97,1},{2,34}... | collective-permute-start | bytes 3932168 | tf_op jit(solution)/shard_map/ppermute | solution.py:300
  44.7 32.4 %collective-permute-start.3 = (bf16[320,2048]{1,0:T(8,128)(2,1)}, bf16[320,2048]{1,0:T(8,128)(2,1)}, u32[]{:S(2)}, u32[]{:S(2)}) collective-permute-start(bf16[320,2048]{1,0:T(8,128)(2,1)} %fusion.refs_0_), channel_id=1, source_target_pairs={{0,96},{32,0},{64,32},{96,64},{1,97},{33,1},{65,33},{97,65},{2,98}... | collective-permute-start | bytes 3932168 | tf_op jit(solution)/shard_map/ppermute | solution.py:300
  59.9 18.6 %copy-start.3 = (bf16[320,2048]{1,0:T(8,128)(2,1)}, bf16[320,2048]{1,0:T(8,128)(2,1)S(1)}, u32[]{:S(2)}) copy-start(bf16[320,2048]{1,0:T(8,128)(2,1)S(1)} %fusion.1.refs_1_) | copy-start | bytes 3932164
  60.0 43.9 %collective-permute-start.4 = (bf16[320,2048]{1,0:T(8,128)(2,1)S(1)}, bf16[320,2048]{1,0:T(8,128)(2,1)S(1)}, u32[]{:S(2)}, u32[]{:S(2)}) collective-permute-start(bf16[320,2048]{1,0:T(8,128)(2,1)S(1)} %fusion.1.refs_1_), channel_id=1, source_target_pairs={{0,32},{32,64},{64,96},{96,0},{1,33},{33,65},{65,97},{97,1},{2,34}... | collective-permute-start | bytes 3932168 | tf_op jit(solution)/shard_map/ppermute | solution.py:300
  75.8 2.8 copy-start.7
  75.8 29.3 %collective-permute-start.5 = (bf16[320,2048]{1,0:T(8,128)(2,1)S(1)}, bf16[320,2048]{1,0:T(8,128)(2,1)S(1)}, u32[]{:S(2)}, u32[]{:S(2)}) collective-permute-start(bf16[320,2048]{1,0:T(8,128)(2,1)S(1)} %fusion.1.refs_1_), channel_id=1, source_target_pairs={{0,96},{32,0},{64,32},{96,64},{1,97},{33,1},{65,33},{97,65},{2,98}... | collective-permute-start | bytes 3932168 | tf_op jit(solution)/shard_map/ppermute | solution.py:300
  77.1 40.8 %collective-permute-start.6 = (bf16[160,2048]{1,0:T(8,128)(2,1)S(1)}, bf16[160,2048]{1,0:T(8,128)(2,1)S(1)}, u32[]{:S(2)}, u32[]{:S(2)}) collective-permute-start(bf16[160,2048]{1,0:T(8,128)(2,1)S(1)} %slice.32), channel_id=1, source_target_pairs={{0,32},{32,64},{64,96},{96,0},{1,33},{33,65},{65,97},{97,1},{2,34}... | collective-permute-start | bytes 1966088 | tf_op jit(solution)/shard_map/ppermute | solution.py:300
  103.9 1.7 copy-start.8
  103.9 15.2 %collective-permute-start.7 = (bf16[160,2048]{1,0:T(8,128)(2,1)S(1)}, bf16[160,2048]{1,0:T(8,128)(2,1)S(1)}, u32[]{:S(2)}, u32[]{:S(2)}) collective-permute-start(bf16[160,2048]{1,0:T(8,128)(2,1)S(1)} %slice.33), channel_id=1, source_target_pairs={{0,96},{32,0},{64,32},{96,64},{1,97},{33,1},{65,33},{97,65},{2,98}... | collective-permute-start | bytes 1966088 | tf_op jit(solution)/shard_map/ppermute | solution.py:300
  105.1 43.2 %copy-start.9 = (bf16[320,2048]{1,0:T(8,128)(2,1)}, bf16[320,2048]{1,0:T(8,128)(2,1)S(1)}, u32[]{:S(2)}) copy-start(bf16[320,2048]{1,0:T(8,128)(2,1)S(1)} %collective-permute-done.5.refs_3_) | copy-start | bytes 3932164
  105.1 26.9 %collective-permute-start.8 = (bf16[160,2048]{1,0:T(8,128)(2,1)S(1)}, bf16[160,2048]{1,0:T(8,128)(2,1)S(1)}, u32[]{:S(2)}, u32[]{:S(2)}) collective-permute-start(bf16[160,2048]{1,0:T(8,128)(2,1)S(1)} %slice.34), channel_id=1, source_target_pairs={{0,32},{32,64},{64,96},{96,0},{1,33},{33,65},{65,97},{97,1},{2,34}... | collective-permute-start | bytes 1966088 | tf_op jit(solution)/shard_map/ppermute | solution.py:300
  117.9 14.8 %copy-start.13 = (bf16[160,2048]{1,0:T(8,128)(2,1)}, bf16[160,2048]{1,0:T(8,128)(2,1)S(1)}, u32[]{:S(2)}) copy-start(bf16[160,2048]{1,0:T(8,128)(2,1)S(1)} %collective-permute-done.6.refs_0_) | copy-start | bytes 1966084
  117.9 14.8 %collective-permute-start.9 = (bf16[160,2048]{1,0:T(8,128)(2,1)S(1)}, bf16[160,2048]{1,0:T(8,128)(2,1)S(1)}, u32[]{:S(2)}, u32[]{:S(2)}) collective-permute-start(bf16[160,2048]{1,0:T(8,128)(2,1)S(1)} %slice.35), channel_id=1, source_target_pairs={{0,96},{32,0},{64,32},{96,64},{1,97},{33,1},{65,33},{97,65},{2,98}... | collective-permute-start | bytes 1966088 | tf_op jit(solution)/shard_map/ppermute | solution.py:300
  119.1 13.6 %copy-start.14 = (bf16[160,2048]{1,0:T(8,128)(2,1)}, bf16[160,2048]{1,0:T(8,128)(2,1)S(1)}, u32[]{:S(2)}) copy-start(bf16[160,2048]{1,0:T(8,128)(2,1)S(1)} %collective-permute-done.7.refs_1_) | copy-start | bytes 1966084
  132.0 0.8 copy-start.16
  132.7 0.8 copy-start.17
  148.3 29.0 %collective-permute-start.10 = (bf16[160,2048]{1,0:T(8,128)(2,1)}, bf16[160,2048]{1,0:T(8,128)(2,1)S(1)}, u32[]{:S(2)}, u32[]{:S(2)}) collective-permute-start(bf16[160,2048]{1,0:T(8,128)(2,1)} %get-tuple-element.14), channel_id=1, source_target_pairs={{0,32},{32,64},{64,96},{96,0},{1,33},{33,65},{65,97},{97,1},{2,34}... | collective-permute-start | bytes 1966088 | tf_op jit(solution)/shard_map/ppermute | solution.py:300
  148.5 26.0 %copy-start.15 = (bf16[160,2048]{1,0:T(8,128)(2,1)S(1)}, bf16[160,2048]{1,0:T(8,128)(2,1)}, u32[]{:S(2)}) copy-start(bf16[160,2048]{1,0:T(8,128)(2,1)} %get-tuple-element.16) | copy-start | bytes 1966084
  173.3 4.0 %copy-start.4 = (bf16[320,2048]{1,0:T(8,128)(2,1)S(1)}, bf16[320,2048]{1,0:T(8,128)(2,1)}, u32[]{:S(2)}) copy-start(bf16[320,2048]{1,0:T(8,128)(2,1)} %get-tuple-element.15) | copy-start | bytes 3932164
  173.3 4.1 %copy-start.5 = (bf16[320,2048]{1,0:T(8,128)(2,1)S(1)}, bf16[320,2048]{1,0:T(8,128)(2,1)}, u32[]{:S(2)}) copy-start(bf16[320,2048]{1,0:T(8,128)(2,1)} %get-tuple-element.13) | copy-start | bytes 3932164
  174.6 14.1 %collective-permute-start.12 = (bf16[160,2048]{1,0:T(8,128)(2,1)S(1)}, bf16[160,2048]{1,0:T(8,128)(2,1)S(1)}, u32[]{:S(2)}, u32[]{:S(2)}) collective-permute-start(bf16[160,2048]{1,0:T(8,128)(2,1)S(1)} %copy-done.15), channel_id=1, source_target_pairs={{0,96},{32,0},{64,32},{96,64},{1,97},{33,1},{65,33},{97,65},{2,98}... | collective-permute-start | bytes 1966088 | tf_op jit(solution)/shard_map/ppermute | solution.py:300
  177.6 29.7 %collective-permute-start.11 = (bf16[320,2048]{1,0:T(8,128)(2,1)S(1)}, bf16[320,2048]{1,0:T(8,128)(2,1)S(1)}, u32[]{:S(2)}, u32[]{:S(2)}) collective-permute-start(bf16[320,2048]{1,0:T(8,128)(2,1)S(1)} %pad_maximum_fusion), channel_id=1, source_target_pairs={{0,32},{32,64},{64,96},{96,0},{1,33},{33,65},{65,97},{97,1},{2,34}... | collective-permute-start | bytes 3932168 | tf_op jit(solution)/shard_map/ppermute | solution.py:300
  188.9 27.9 %collective-permute-start.13 = (bf16[320,2048]{1,0:T(8,128)(2,1)S(1)}, bf16[320,2048]{1,0:T(8,128)(2,1)S(1)}, u32[]{:S(2)}, u32[]{:S(2)}) collective-permute-start(bf16[320,2048]{1,0:T(8,128)(2,1)S(1)} %pad_maximum_fusion.1), channel_id=1, source_target_pairs={{0,96},{32,0},{64,32},{96,64},{1,97},{33,1},{65,33},{97,65},{2,98}... | collective-permute-start | bytes 3932168 | tf_op jit(solution)/shard_map/ppermute | solution.py:300
  220.4 7.0 %copy-start.10 = (f32[1,128,16]{1,2,0:T(8,128)S(1)}, f32[1,128,16]{1,2,0:T(8,128)}, u32[]{:S(2)}) copy-start(f32[1,128,16]{1,2,0:T(8,128)} %param.19) | copy-start | bytes 24580
  220.4 7.1 %copy-start.11 = (f32[1,128,16]{1,2,0:T(8,128)S(1)}, f32[1,128,16]{1,2,0:T(8,128)}, u32[]{:S(2)}) copy-start(f32[1,128,16]{1,2,0:T(8,128)} %param.20) | copy-start | bytes 24580
  220.4 7.2 %copy-start.12 = (f32[1,128,2]{1,2,0:T(2,128)S(1)}, f32[1,128,2]{1,2,0:T(2,128)}, u32[]{:S(2)}) copy-start(f32[1,128,2]{1,2,0:T(2,128)} %param.14) | copy-start | bytes 3076
  220.4 7.9 %copy-start = (f32[1,128,2048]{2,1,0:T(8,128)S(1)}, f32[1,128,2048]{2,1,0:T(8,128)}, u32[]{:S(2)}) copy-start(f32[1,128,2048]{2,1,0:T(8,128)} %param.17) | copy-start | bytes 3145732
  220.4 26.5 %all-to-all-start.2 = ((bf16[16,24,2048]{2,1,0:T(8,128)(2,1)}), bf16[16,24,2048]{2,1,0:T(8,128)(2,1)S(1)}, u32[]{:S(2)}, u32[]{:S(2)}) async-start(bf16[16,24,2048]{2,1,0:T(8,128)(2,1)} %bitcast.35), calls=%async_computation.2 | async-start | bytes 3145728 | tf_op jit(solution)/shard_map/all_to_all | solution.py:306
  246.9 2.8 copy-start.1

commit v2 on v1

v2 whole, which is shorter than its diff:
```python
import functools

import jax
import jax.numpy as jnp
import numpy as np
from jax import lax
from jax.experimental import pallas as pl
from jax.experimental.pallas import tpu as pltpu
from jax.sharding import Mesh
from jax.sharding import PartitionSpec as P

VMEM_LIMIT = 56 * 1024 * 1024
CORES = 2
SIDE = 4
GROUP = 4
HIDDEN_STEP = 128
OUT_COLS = 1024
SCAN_COLS = 1024
BF = jnp.bfloat16
F32 = jnp.float32
SHIFTS = (
    (0, 0), (1, 0), (0, 1), (3, 0),
    (0, 3), (1, 1), (3, 3), (1, 3),
    (3, 1), (2, 0), (0, 2), (2, 1),
    (1, 2), (2, 3), (3, 2), (2, 2),
)


def params():
    return pltpu.CompilerParams(vmem_limit_bytes=VMEM_LIMIT)


def whole(*shape):
    return pl.BlockSpec(shape, lambda *_: (0,) * len(shape))


def tie(*values):
    return lax.optimization_barrier(values)


def gather_body(capacity, ids_ref, order_ref, x_ref, dy_ref, *outs):
    tokens = x_ref.shape[0]
    experts = len(outs)
    ids = ids_ref[...]
    order = jnp.broadcast_to(order_ref[...], (experts, tokens))
    hots = [(order == ids[k : k + 1, :]).astype(F32) for k in range(2)]
    before = (
        lax.broadcasted_iota(jnp.int32, (tokens, tokens), 0)
        < lax.broadcasted_iota(jnp.int32, (tokens, tokens), 1)
    ).astype(F32)
    earlier = jnp.dot(
        (hots[0] + hots[1]).astype(BF), before.astype(BF), preferred_element_type=F32
    )
    message = 2 * capacity
    base = lax.broadcasted_iota(jnp.int32, (experts, tokens), 0).astype(F32) * message
    place = lax.broadcasted_iota(jnp.int32, (experts * message, tokens), 0)
    pick_x = pick_dy = None
    for k in range(2):
        target = jnp.sum((earlier + base) * hots[k], axis=0, keepdims=True).astype(jnp.int32)
        hit_x, hit_dy = place == target, place == target + capacity
        pick_x = hit_x if pick_x is None else pick_x | hit_x
        pick_dy = hit_dy if pick_dy is None else pick_dy | hit_dy
    rows = jnp.dot(pick_x.astype(F32).astype(BF), x_ref[...], preferred_element_type=F32)
    rows += jnp.dot(pick_dy.astype(F32).astype(BF), dy_ref[...], preferred_element_type=F32)
    rows = rows.astype(BF)
    for p, out in enumerate(outs):
        out[...] = rows[p * message : (p + 1) * message]


def gather_rows(ids_t, order, x, dy, capacity):
    experts, dim = order.shape[0], x.shape[1]
    return pl.pallas_call(
        functools.partial(gather_body, capacity),
        out_shape=[jax.ShapeDtypeStruct((2 * capacity, dim), BF)] * experts,
        compiler_params=params(),
        name="gather_rows",
    )(ids_t, order, x, dy)


def sort_body(table_ref, *refs):
    ins, out = refs[:-1], refs[-1]
    rows = jnp.concatenate([r[...] for r in ins], axis=0)
    out[...] = jnp.dot(table_ref[...], rows, preferred_element_type=F32).astype(BF)


def sort_messages(messages, capacity):
    count, dim = len(messages), messages[0].shape[1]
    rows = 2 * capacity * count
    at = np.arange(rows)
    kind, rest = at // (capacity * count), at % (capacity * count)
    table = np.zeros((rows, rows), np.float32)
    table[at, rest // capacity * 2 * capacity + kind * capacity + rest % capacity] = 1.0
    return pl.pallas_call(
        sort_body,
        out_shape=jax.ShapeDtypeStruct((rows, dim), BF),
        compiler_params=params(),
        name="sort_messages",
    )(jnp.asarray(table, BF), *messages)


def pack_body(table_ref, own_a, own_b, prev_ref, next_ref, *outs):
    half = own_a.shape[0]
    sums = []
    for own, low in ((own_a, 0), (own_b, half)):
        total = own[...].astype(F32) + prev_ref[low : low + half].astype(F32)
        sums.append((total + next_ref[low : low + half].astype(F32)).astype(BF))
    rows = jnp.dot(
        table_ref[...], jnp.concatenate(sums, axis=0), preferred_element_type=F32
    ).astype(BF)
    size = outs[0].shape[0]
    for p, out in enumerate(outs):
        out[...] = rows[p * size : (p + 1) * size]


def pack_returns(own_a, own_b, from_prev, from_next, capacity):
    rows, dim = from_prev.shape
    count = rows // capacity
    size = -(-capacity // 8) * 8
    table = np.zeros((count * size, rows), np.float32)
    at = np.arange(rows)
    table[at // capacity * size + at % capacity, at] = 1.0
    return pl.pallas_call(
        pack_body,
        out_shape=[jax.ShapeDtypeStruct((size, dim), BF)] * count,
        compiler_params=params(),
        name="pack_returns",
    )(jnp.asarray(table, BF), own_a, own_b, from_prev, from_next)


def hop_body(next_a, next_b, prev_a, prev_b, got_a, got_b, to_next, to_prev):
    half = next_a.shape[0]
    to_next[:half] = (next_a[...].astype(F32) + got_a[...].astype(F32)).astype(BF)
    to_next[half:] = next_b[...]
    to_prev[:half] = prev_a[...]
    to_prev[half:] = (prev_b[...].astype(F32) + got_b[...].astype(F32)).astype(BF)


def hop_sums(*parts):
    half, dim = parts[0].shape
    return pl.pallas_call(
        hop_body,
        out_shape=[jax.ShapeDtypeStruct((2 * half, dim), BF)] * 2,
        compiler_params=params(),
        name="hop_sums",
    )(*parts)


def expert_body(pieces, steps, *refs):
    ins = refs[:pieces]
    up_a, up_b, down_a, down_b = refs[pieces : pieces + 4]
    outs = refs[pieces + 4 : 2 * pieces + 4]
    x_all, dy_all, up_all, grads = refs[2 * pieces + 4 :]
    step = pl.program_id(0)
    size = outs[0].shape[0]
    width = 2 * up_a.shape[0]

    @pl.when(step == 0)
    def _():
        for i, piece in enumerate(ins):
            x_all[i * size : (i + 1) * size] = piece[:size]
            dy_all[i * size : (i + 1) * size] = piece[size:]

    @pl.when(step < steps)
    def _():
        up = jnp.concatenate([up_a[...], up_b[...]], axis=0)
        down = jnp.concatenate([down_a[...], down_b[...]], axis=0)
        up_all[pl.ds(pl.multiple_of(step * width, width), width)] = up
        across = (((1,), (1,)), ((), ()))
        pre = lax.dot_general(x_all[...], up, across, preferred_element_type=F32)
        back = lax.dot_general(dy_all[...], down, across, preferred_element_type=F32)
        sig = jax.nn.sigmoid(pre)
        grads[step] = (back * sig * (1.0 + pre * (1.0 - sig))).astype(BF)

    @pl.when(step >= steps)
    def _():
        grad = jnp.concatenate([grads[i] for i in range(steps)], axis=1)
        cols = outs[0].shape[1]
        at = pl.ds(pl.multiple_of((step - steps) * cols, cols), cols)
        part = jnp.dot(grad, up_all[:, at], preferred_element_type=F32).astype(BF)
        for i, out in enumerate(outs):
            out[...] = part[i * size : (i + 1) * size]


def expert_rows(ins, weights):
    pieces = len(ins)
    both, dim = ins[0].shape
    size = both // 2
    rows = pieces * size
    hidden = weights[0].shape[0]
    steps = hidden // HIDDEN_STEP
    tile = pl.BlockSpec((HIDDEN_STEP, dim), lambda i: (jnp.minimum(i, steps - 1), 0))
    return pl.pallas_call(
        functools.partial(expert_body, pieces, steps),
        grid=(steps + dim // OUT_COLS,),
        in_specs=[whole(both, dim)] * pieces + [tile] * 4,
        out_specs=[
            pl.BlockSpec((size, OUT_COLS), lambda i: (0, jnp.maximum(i - steps, 0)))
        ]
        * pieces,
        out_shape=[jax.ShapeDtypeStruct((size, dim), BF)] * pieces,
        scratch_shapes=[
            pltpu.VMEM((rows, dim), BF),
            pltpu.VMEM((rows, dim), BF),
            pltpu.VMEM((2 * hidden, dim), BF),
            pltpu.VMEM((steps, rows, 2 * HIDDEN_STEP), BF),
        ],
        compiler_params=params(),
        cost_estimate=pl.CostEstimate(
            flops=6 * rows * 2 * hidden * dim,
            bytes_accessed=2 * (4 * hidden * dim + 3 * rows * dim),
            transcendentals=rows * 2 * hidden,
        ),
        name="expert_rows",
    )(*ins, *weights)


def weigh_pair(ids, order, weights, padded):
    tokens = ids.shape[0]
    experts = order.shape[1]
    order = jnp.broadcast_to(order, (tokens, experts))
    hots = [(order == ids[:, k : k + 1]).astype(F32) for k in range(2)]
    before = (
        lax.broadcasted_iota(jnp.int32, (tokens, tokens), 1)
        < lax.broadcasted_iota(jnp.int32, (tokens, tokens), 0)
    ).astype(F32)
    earlier = jnp.dot(
        before.astype(BF), (hots[0] + hots[1]).astype(BF), preferred_element_type=F32
    )
    base = lax.broadcasted_iota(jnp.int32, (tokens, experts), 1).astype(F32) * padded
    place = lax.broadcasted_iota(jnp.int32, (tokens, experts * padded), 1)
    table = jnp.zeros((tokens, experts * padded), F32)
    for k in range(2):
        target = jnp.sum((earlier + base) * hots[k], axis=1, keepdims=True).astype(jnp.int32)
        table = table + jnp.where(place == target, weights[:, k : k + 1], 0.0)
    high = table.astype(BF)
    low = (table - high.astype(F32)).astype(BF)
    return high, low


def scan_body(experts, ids_ref, order_ref, weights_ref, *refs):
    backs = refs[:experts]
    dout_ref, delta_ref, rate_ref, mix_ref, drive_ref = refs[experts : experts + 5]
    mid_ref, local_ref, start_ref, grad = refs[experts + 5 :]
    high, low = weigh_pair(
        ids_ref[...], order_ref[...], weights_ref[...], backs[0].shape[0]
    )
    back = jnp.concatenate([b[...] for b in backs], axis=0)
    routed = jnp.dot(high, back, preferred_element_type=F32)
    routed += jnp.dot(low, back, preferred_element_type=F32)
    mid = (dout_ref[...].astype(F32) + routed).astype(BF)
    mid_ref[...] = mid
    grad[...] = mid.astype(F32)
    negative = -rate_ref[...]
    tokens, cols = grad.shape
    states = negative.shape[0]
    repeat = cols // mix_ref.shape[2]

    def block(i, flow):
        low_t = pl.multiple_of((tokens // 8 - 1 - i) * 8, 8)
        grads = grad[pl.ds(low_t, 8)]
        deltas = delta_ref[pl.ds(low_t, 8)]
        rows = []
        for r in reversed(range(8)):
            drive = jnp.concatenate([drive_ref[low_t + r]] * repeat, axis=1)
            mix = jnp.concatenate([mix_ref[low_t + r]] * repeat, axis=1)
            state = drive * jnp.broadcast_to(grads[r : r + 1], (states, cols)) + flow
            rows.append(jnp.sum(mix * state, axis=0, keepdims=True))
            decay = jnp.exp(jnp.broadcast_to(deltas[r : r + 1], (states, cols)) * negative)
            flow = decay * state
        local_ref[pl.ds(low_t, 8)] = jnp.concatenate(rows[::-1], axis=0)
        return flow

    start_ref[...] = lax.fori_loop(
        0, tokens // 8, block, jnp.zeros((states, cols), F32)
    ).astype(BF)


def strip(rows, cols):
    return pl.BlockSpec((rows, cols), lambda i: (0, i))


def combine_and_scan(ids, order, weights, backs, dout, delta, rate, mix, drive):
    tokens, dim = dout.shape
    states = rate.shape[0]
    cols = SCAN_COLS
    return pl.pallas_call(
        functools.partial(scan_body, len(backs)),
        grid=(dim // cols,),
        in_specs=[whole(*ids.shape), whole(*order.shape), whole(*weights.shape)]
        + [strip(b.shape[0], cols) for b in backs]
        + [
            strip(tokens, cols),
            strip(tokens, cols),
            strip(states, cols),
            whole(*mix.shape),
            whole(*drive.shape),
        ],
        out_specs=[strip(tokens, cols), strip(tokens, cols), strip(states, cols)],
        out_shape=[
            jax.ShapeDtypeStruct((tokens, dim), BF),
            jax.ShapeDtypeStruct((tokens, dim), F32),
            jax.ShapeDtypeStruct((states, dim), BF),
        ],
        scratch_shapes=[pltpu.VMEM((tokens, cols), F32)],
        compiler_params=params(),
        name="combine_and_scan",
    )(ids, order, weights, *backs, dout, delta, rate, mix, drive)


def reach_body(delta_ref, rate_ref, mix_ref, reach_ref, total_ref):
    delta = delta_ref[...]
    tokens, cols = delta.shape
    later = (
        lax.broadcasted_iota(jnp.int32, (tokens, tokens), 1)
        > lax.broadcasted_iota(jnp.int32, (tokens, tokens), 0)
    ).astype(F32)
    after = jnp.dot(
        later, delta, precision=lax.Precision.HIGHEST, preferred_element_type=F32
    )
    total_ref[...] = after[:1] + delta[:1]
    mix = mix_ref[...]
    for n in range(rate_ref.shape[0]):
        fade = jnp.exp(after * -jnp.broadcast_to(rate_ref[n : n + 1], (tokens, cols)))
        reach_ref[n] = (fade * jnp.broadcast_to(mix[:, n : n + 1], (tokens, cols))).astype(BF)


def reach_table(delta, rate, mix):
    tokens, dim = delta.shape
    states = rate.shape[0]
    cols = 512
    return pl.pallas_call(
        reach_body,
        grid=(dim // cols,),
        in_specs=[strip(tokens, cols), strip(states, cols), whole(*mix.shape)],
        out_specs=[
            pl.BlockSpec((states, tokens, cols), lambda i: (0, 0, i)),
            strip(1, cols),
        ],
        out_shape=[
            jax.ShapeDtypeStruct((states, tokens, dim), BF),
            jax.ShapeDtypeStruct((1, dim), F32),
        ],
        compiler_params=params(),
        cost_estimate=pl.CostEstimate(
            flops=8 * states * tokens * dim,
            bytes_accessed=2 * states * tokens * dim,
            transcendentals=states * tokens * dim,
        ),
        name="reach_table",
    )(delta, rate, mix)


def carry_body(place_ref, starts_ref, totals_ref, rate_ref, local_ref, reach_ref, out_ref):
    place = place_ref[0]
    negative = -rate_ref[...]
    tokens, cols = local_ref.shape
    states = negative.shape[0]
    flow = jnp.zeros((states, cols), F32)
    for at in reversed(range(starts_ref.shape[0])):
        passed = jnp.exp(totals_ref[at : at + 1] * negative) * flow
        flow = jnp.where(at > place, starts_ref[at].astype(F32) + passed, flow)
    total = local_ref[...]
    for n in range(states):
        total += reach_ref[n].astype(F32) * flow[n : n + 1]
    out_ref[...] = total.astype(BF)


def add_carry(place, starts, totals, rate, local, reach):
    tokens, dim = local.shape
    states = rate.shape[0]
    blocks = starts.shape[0]
    cols = 256
    return pl.pallas_call(
        carry_body,
        grid=(dim // cols,),
        in_specs=[
            pl.BlockSpec(memory_space=pltpu.SMEM),
            pl.BlockSpec((blocks, states, cols), lambda i: (0, 0, i)),
            strip(blocks, cols),
            strip(states, cols),
            strip(tokens, cols),
            pl.BlockSpec((states, tokens, cols), lambda i: (0, 0, i)),
        ],
        out_specs=strip(tokens, cols),
        out_shape=jax.ShapeDtypeStruct((tokens, dim), BF),
        compiler_params=params(),
        name="add_carry",
    )(place, starts, totals, rate, local, reach)


def on_device(z_size, capacity, x_in, dout, route_ids, combine, w_up, w_down, delta, rate, bmat, cmat):
    x, dy, ids, weights = x_in[0], dout[0], route_ids[0], combine[0]
    up, down, steps = w_up[0], w_down[0], delta[0]

    def shift(value, by):
        ring = [(i, (i + by) % z_size) for i in range(z_size)]
        return lax.ppermute(value, "z", ring)

    def swap(value):
        return lax.ppermute(value, "core", [(0, 1), (1, 0)])

    def across(value, shift_by, sign):
        dx, dy_ = shift_by
        if dx == 0 and dy_ == 0:
            return value
        pairs = [
            (a * SIDE + b, (a + sign * dx) % SIDE * SIDE + (b + sign * dy_) % SIDE)
            for a in range(SIDE)
            for b in range(SIDE)
        ]
        return lax.ppermute(value, "exp", pairs)

    me = lax.axis_index("exp")
    dxs, dys = np.array(SHIFTS, np.int32).T
    order = (me // SIDE + dxs) % SIDE * SIDE + (me % SIDE + dys) % SIDE
    order = order.astype(jnp.int32)

    sent = gather_rows(ids.T, order[:, None], x, dy, capacity)
    got = [across(m, s, 1) for m, s in zip(sent, SHIFTS)]
    quarters = [
        sort_messages(got[i : i + GROUP], capacity) for i in range(0, len(got), GROUP)
    ]
    both = (up, swap(up), down, swap(down))

    def ring(a, b):
        prev_a, next_b = shift(a, 1), shift(b, -1)
        prev_b, next_a = shift(b, 1), shift(a, -1)
        return prev_a, prev_b, next_a, next_b

    def far(prev_a, next_b):
        return shift(prev_a, 1), shift(next_b, -1)

    low_a, low_b, high_a, high_b = quarters
    low = ring(low_a, low_b)
    low_far = far(low[0], low[3])
    reach, total = reach_table(steps, rate, bmat[0])
    low, reach, total = tie(low, reach, total)
    first = expert_rows((low_a, low_b, *low), both)
    high = ring(high_a, high_b)
    low_far, first = tie(low_far, first)
    second = expert_rows((*low_far, high_a, high_b), both)
    high, second = tie(high, second)
    high_far = far(high[0], high[3])
    third = expert_rows(high, both)
    high_far, third = tie(high_far, third)
    fourth = expert_rows(high_far, both)

    def back_home(own, prev, next_, far_a, far_b):
        got_a, got_b = shift(far_a, 1), shift(far_b, -1)
        to_next, to_prev = hop_sums(*next_, *prev, got_a, got_b)
        return pack_returns(*own, shift(to_next, 1), shift(to_prev, -1), capacity)

    backs = [
        *back_home(first[:2], first[2:4], first[4:6], *second[:2]),
        *back_home(second[2:4], third[:2], third[2:4], *fourth),
    ]
    backs = [across(m, s, -1) for m, s in zip(backs, SHIFTS)]

    lanes = (steps.shape[0], bmat.shape[2], 128)
    mix = jnp.broadcast_to(bmat[0][:, :, None], lanes)
    drive = jnp.broadcast_to(cmat[0][:, :, None], lanes)
    totals = lax.all_gather(total[0], ("z", "core"))
    mid, local, start = combine_and_scan(
        ids, order[None, :], weights, backs, dy, steps, rate, mix, drive
    )
    starts = lax.all_gather(start, ("z", "core"))
    place = lax.axis_index(("z", "core")).astype(jnp.int32).reshape(1)
    scan = add_carry(place, starts, totals, rate, local, reach)
    return (mid[None], scan[None])


def solution(mesh):
    seq, exp = mesh.shape["seq"], mesh.shape["exp"]
    z_size = seq // CORES
    split = Mesh(mesh.devices.reshape(z_size, CORES, exp), ("z", "core", "exp"))
    token = P("exp", ("z", "core"), None)

    def run(x_in, dout, route_ids, *rest):
        tokens = route_ids.shape[1] // seq
        capacity = 5 * tokens * route_ids.shape[2] // (4 * exp)
        return jax.shard_map(
            functools.partial(on_device, z_size, capacity),
            mesh=split,
            in_specs=(token,) * 7 + (P(),) + (token,) * 2,
            out_specs=(token, token),
            check_vma=False,
        )(x_in, dout, route_ids, *rest)

    return run
```

time: 289 us -> 300 us (1.038)
  starting transfers between devices: 29.3 us -> 83.2 us
  waiting for transfers between devices: 98.2 us -> 50.1 us
  Pallas kernels: 77 us -> 111 us
  blocking collectives: 66.2 us -> 38.4 us
  matrix products: 6.4 us -> 0 us
  local copies, waits for them, and re-layouts: 9.29 us -> 13.9 us
    ppermute x12 -> x20, waiting for transfers between devices: 85.9 us -> 30.6 us  [shift(): return lax.ppermute(value, 'z', ring)]
    ppermute x0 -> x30, starting transfers between devices: none -> 51.7 us  [across(): return lax.ppermute(value, 'exp', pairs)]
    pallas_call x5 -> x15, Pallas kernels: 69.2 us -> 103 us  [the longest x4 60.5 us: expert_rows(): pl.pallas_call(functools.partial(expert_body, pieces, steps), grid=(steps...]
    all_to_all x1 -> x0, blocking collectives: 29.1 us -> none  [exchange(): lax.all_to_all(value.reshape(experts, PAD, dim), 'exp', split_axis=0, con...]
    ppermute x0 -> x30, waiting for transfers between devices: none -> 19.5 us  [across(): return lax.ppermute(value, 'exp', pairs)]
    ppermute x12 -> x20, starting transfers between devices: 16.2 us -> 29.9 us  [shift(): return lax.ppermute(value, 'z', ring)]
    all_to_all x2 -> x0, waiting for transfers between devices: 12.3 us -> none  [exchange(): lax.all_to_all(value.reshape(experts, PAD, dim), 'exp', split_axis=0, con...]
    all_to_all x2 -> x0, starting transfers between devices: 10.9 us -> none  [exchange(): lax.all_to_all(value.reshape(experts, PAD, dim), 'exp', split_axis=0, con...]
  transfers between devices with their start and end apart: 16 -> 52, of which waited for: 8 -> 13; matrix products, arithmetic and copies ran while one was open for 3% -> 2% of each run, Pallas kernels for 14% -> 31%
where the time goes in v2:
time: 300 us; the launch traced here: 299 us
  Pallas kernels  111 us (37%)
  starting transfers between devices  83.2 us (28%)
  waiting for transfers between devices  50.1 us (17%)
  blocking collectives  38.4 us (13%)
  local copies, waits for them, and re-layouts  13.9 us (5%)
    pallas_call x4, Pallas kernels, expert_rows(): pl.pallas_call(functools.partial(expert_body, pieces, steps), grid=(steps...  60.5 us
    ppermute x30, starting transfers between devices, across(): return lax.ppermute(value, 'exp', pairs)  51.7 us
    ppermute x20, waiting for transfers between devices, shift(): return lax.ppermute(value, 'z', ring)  30.6 us
    ppermute x20, starting transfers between devices, shift(): return lax.ppermute(value, 'z', ring)  29.9 us
    all_gather x1, blocking collectives, on_device(): totals = lax.all_gather(total[0], ('z', 'core'))  24 us
    ppermute x30, waiting for transfers between devices, across(): return lax.ppermute(value, 'exp', pairs)  19.5 us
    all_gather x1, blocking collectives, on_device(): starts = lax.all_gather(start, ('z', 'core'))  14.4 us
    pallas_call x1, Pallas kernels, combine_and_scan(): pl.pallas_call(functools.partial(scan_body, len(backs)), grid=(dim // col...  11.2 us
  transfers between devices with their start and end apart: 52, of which 13 were waited for; matrix products, arithmetic and copies ran while one was open for 2% of the time, Pallas kernels for 31%

profile of v2, /device:TPU:1, one launch (start us, length us, event | category | flops | bytes accessed | tf_op | source)
XLA Modules:
  0.0 298.7 jit_solution(6441344813821510881)
XLA Ops:
  5.0 4.3 %gather_rows.1 = (bf16[40,2048]{1,0:T(8,128)(2,1)}, bf16[40,2048]{1,0:T(8,128)(2,1)}, bf16[40,2048]{1,0:T(8,128)(2,1)}, bf16[40,2048]{1,0:T(8,128)(2,1)}, bf16[4...) custom-call(s32[2,128]{1,0:T(2,128)} %copy.28.ids_ref, ...), custom_call_target="tpu_custom_call" | custom-call | tf_op jit(solution)/shard_map/gather_rows/pallas_call | solution.py:72
  9.3 2.8 collective-permute-start.5
  12.1 4.8 %collective-permute-start.7 = (bf16[40,2048]{1,0:T(8,128)(2,1)}, bf16[40,2048]{1,0:T(8,128)(2,1)S(1)}, u32[]{:S(2)}, u32[]{:S(2)}) collective-permute-start(bf16[40,2048]{1,0:T(8,128)(2,1)} %get-tuple-element.93), channel_id=1, source_target_pairs={{0,15},{1,12},{2,13},{3,14},{4,3},{5,0},{6,1},{7,2},{8,7},{9,4},{1... | collective-permute-start | bytes 491528 | tf_op jit(solution)/shard_map/ppermute | solution.py:411
  16.9 2.9 collective-permute-start.8
  21.1 2.3 collective-permute-done.8.refs_3_
  24.6 3.7 %collective-permute-done.refs_1_ = bf16[40,2048]{1,0:T(8,128)(2,1)S(1)} collective-permute-done((bf16[40,2048]{1,0:T(8,128)(2,1)}, bf16[40,2048]{1,0:T(8,128)(2,1)S(1)}, u32[]{:S(2)}, u32[]{:S(2)}) %collective-permute-start) | collective-permute-done | bytes 163872 | tf_op jit(solution)/shard_map/ppermute | solution.py:411
  29.3 2.4 sort_messages.5.refs_1_
  33.3 3.1 %collective-permute-done.15.refs_0_ = bf16[40,2048]{1,0:T(8,128)(2,1)S(1)} collective-permute-done((bf16[40,2048]{1,0:T(8,128)(2,1)}, bf16[40,2048]{1,0:T(8,128)(2,1)S(1)}, u32[]{:S(2)}, u32[]{:S(2)}) %collective-permute-start.15) | collective-permute-done | bytes 163872 | tf_op jit(solution)/shard_map/ppermute | solution.py:411
  36.4 3.4 %collective-permute-start.18 = (bf16[40,2048]{1,0:T(8,128)(2,1)}, bf16[40,2048]{1,0:T(8,128)(2,1)S(1)}, u32[]{:S(2)}, u32[]{:S(2)}) collective-permute-start(bf16[40,2048]{1,0:T(8,128)(2,1)} %get-tuple-element.116), channel_id=1, source_target_pairs={{0,9},{1,10},{2,11},{3,8},{4,13},{5,14},{6,15},{7,12},{8,1},{9,2},... | collective-permute-start | bytes 491528 | tf_op jit(solution)/shard_map/ppermute | solution.py:411
  39.8 2.5 collective-permute-done.17.refs_2_
  46.3 5.3 %collective-permute-done.20.refs_0_ = bf16[40,2048]{1,0:T(8,128)(2,1)S(1)} collective-permute-done((bf16[40,2048]{1,0:T(8,128)(2,1)}, bf16[40,2048]{1,0:T(8,128)(2,1)S(1)}, u32[]{:S(2)}, u32[]{:S(2)}) %collective-permute-start.20) | collective-permute-done | bytes 163872 | tf_op jit(solution)/shard_map/ppermute | solution.py:411
  51.6 2.8 collective-permute-start.22
  54.4 3.0 %collective-permute-start.23 = (bf16[40,2048]{1,0:T(8,128)(2,1)}, bf16[40,2048]{1,0:T(8,128)(2,1)S(1)}, u32[]{:S(2)}, u32[]{:S(2)}) collective-permute-start(bf16[40,2048]{1,0:T(8,128)(2,1)} %get-tuple-element.120), channel_id=1, source_target_pairs={{0,10},{1,11},{2,8},{3,9},{4,14},{5,15},{6,12},{7,13},{8,2},{9,3},... | collective-permute-start | bytes 491528 | tf_op jit(solution)/shard_map/ppermute | solution.py:411
  57.5 2.4 sort_messages.4.refs_0_
  60.8 3.5 %collective-permute-start.9 = (bf16[160,2048]{1,0:T(8,128)(2,1)}, bf16[160,2048]{1,0:T(8,128)(2,1)S(1)}, u32[]{:S(2)}, u32[]{:S(2)}) collective-permute-start(bf16[160,2048]{1,0:T(8,128)(2,1)} %sort_messages.5.refs_1_), channel_id=1, source_target_pairs={{0,96},{32,0},{64,32},{96,64},{1,97},{33,1},{65,33},{97,65},{2,98}... | collective-permute-start | bytes 1966088 | tf_op jit(solution)/shard_map/ppermute | solution.py:397
  67.1 6.9 %reach_table.1 = (bf16[16,128,2048]{2,1,0:T(8,128)(2,1)}, f32[1,2048]{1,0:T(1,128)}) custom-call(f32[128,2048]{1,0:T(8,128)} %bitcast.34, f32[16,2048]{1,0:T(8,128)} %rate_ref.3, f32[128,16]{1,0:T(8,128)} %bitcast.42), custom_call_target="tpu_custom_call" | custom-call | flops 33554432 | bytes 8388608 | tf_op jit(solution)/shard_map/reach_table/pallas_call | solution.py:331
  74.1 2.4 sort_messages.6.refs_2_
  76.5 2.4 sort_messages.7.refs_3_
  81.1 3.3 %collective-permute-start.25 = (bf16[160,2048]{1,0:T(8,128)(2,1)}, bf16[160,2048]{1,0:T(8,128)(2,1)S(1)}, u32[]{:S(2)}, u32[]{:S(2)}) collective-permute-start(bf16[160,2048]{1,0:T(8,128)(2,1)} %sort_messages.6.refs_2_), channel_id=1, source_target_pairs={{0,96},{32,0},{64,32},{96,64},{1,97},{33,1},{65,33},{97,65},{2,98}... | collective-permute-start | bytes 1966088 | tf_op jit(solution)/shard_map/ppermute | solution.py:397
  84.4 2.7 collective-permute-start.10
  87.1 17.9 %expert_rows.4 = (bf16[80,2048]{1,0:T(8,128)(2,1)}, bf16[80,2048]{1,0:T(8,128)(2,1)}, bf16[80,2048]{1,0:T(8,128)(2,1)}, bf16[80,2048]{1,0:T(8,128)(2,1)}, bf16[8...) custom-call(bf16[160,2048]{1,0:T(8,128)(2,1)} %sort_messages.4.refs_0_, bf16[160,2048]{1,0:T(8,128)(2,1)} %sort_messages.5.refs_1_, ...), custom_call_target="tpu_custom_call" | custom-call | flops 10569646080 | bytes 20578304 | tf_op jit(solution)/shard_map/expert_rows/pallas_call | solution.py:192
  105.0 3.1 %collective-permute-done.10.refs_1_ = bf16[160,2048]{1,0:T(8,128)(2,1)S(1)} collective-permute-done((bf16[160,2048]{1,0:T(8,128)(2,1)S(1)}, bf16[160,2048]{1,0:T(8,128)(2,1)S(1)}, u32[]{:S(2)}, u32[]{:S(2)}) %collective-permute-start.10) | collective-permute-done | bytes 655392 | tf_op jit(solution)/shard_map/ppermute | solution.py:397
  108.1 3.4 %collective-permute-start.26 = (bf16[160,2048]{1,0:T(8,128)(2,1)S(1)}, bf16[160,2048]{1,0:T(8,128)(2,1)S(1)}, u32[]{:S(2)}, u32[]{:S(2)}) collective-permute-start(bf16[160,2048]{1,0:T(8,128)(2,1)S(1)} %copy-done.2), channel_id=1, source_target_pairs={{0,96},{32,0},{64,32},{96,64},{1,97},{33,1},{65,33},{97,65},{2,98}... | collective-permute-start | bytes 1966088 | tf_op jit(solution)/shard_map/ppermute | solution.py:397
  111.5 13.7 %collective-permute-done.4.refs_0_ = bf16[160,2048]{1,0:T(8,128)(2,1)S(1)} collective-permute-done((bf16[160,2048]{1,0:T(8,128)(2,1)}, bf16[160,2048]{1,0:T(8,128)(2,1)S(1)}, u32[]{:S(2)}, u32[]{:S(2)}) %collective-permute-start.4) | collective-permute-done | bytes 655392 | tf_op jit(solution)/shard_map/ppermute | solution.py:397
  126.0 14.8 %expert_rows.5 = (bf16[80,2048]{1,0:T(8,128)(2,1)}, bf16[80,2048]{1,0:T(8,128)(2,1)}, bf16[80,2048]{1,0:T(8,128)(2,1)}, bf16[80,2048]{1,0:T(8,128)(2,1)}) custom-call(bf16[160,2048]{1,0:T(8,128)(2,1)} %copy-done.55, bf16[160,2048]{1,0:T(8,128)(2,1)} %copy-done.54, bf16[160,2048]{1,0:T(8,128)(2,1)} %sort_messages.6.refs_2_, ...), custom_call_target="tpu_custom_call" | custom-call | flops 7046430720 | bytes 18612224 | tf_op jit(solution)/shard_map/expert_rows/pallas_call | solution.py:192
  141.0 2.7 collective-permute-start.39
  143.7 2.7 collective-permute-start.28
  146.4 14.8 %expert_rows.6 = (bf16[80,2048]{1,0:T(8,128)(2,1)}, bf16[80,2048]{1,0:T(8,128)(2,1)}, bf16[80,2048]{1,0:T(8,128)(2,1)}, bf16[80,2048]{1,0:T(8,128)(2,1)}) custom-call(bf16[160,2048]{1,0:T(8,128)(2,1)} %copy-done.49, bf16[160,2048]{1,0:T(8,128)(2,1)} %copy-done.51, bf16[160,2048]{1,0:T(8,128)(2,1)} %copy-done.50, bf16[160,2048]{1,0:T(8,128)(2,1)} %copy-done.53, ...), custom_call_target="tpu_custom_call" | custom-call | flops 7046430720 | bytes 18612224 | tf_op jit(solution)/shard_map/expert_rows/pallas_call | solution.py:192
  162.3 12.9 %expert_rows.7 = (bf16[80,2048]{1,0:T(8,128)(2,1)}, bf16[80,2048]{1,0:T(8,128)(2,1)}) custom-call(bf16[160,2048]{1,0:T(8,128)(2,1)} %copy-done, bf16[160,2048]{1,0:T(8,128)(2,1)} %copy-done.1, bf16[896,2048]{1,0:T(8,128)(2,1)} %bitcast.25, bf16[896,2048]{1,0:T(8,128)(2,1)} %collective-permute-done.13.refs_7_.refs_5_.refs_3_, bf16[896,2048]{1,0:T(8,128)(2,1)} %bitcast.30, ...), custom_call_target="tpu_custom_call" | custom-call | flops 3523215360 | bytes 16646144 | tf_op jit(solution)/shard_map/expert_rows/pallas_call | solution.py:192
  175.3 2.6 collective-permute-start.41
  179.4 2.6 hop_sums.2
  182.1 2.7 collective-permute-start.30
  186.2 2.6 hop_sums.3
  188.9 2.7 collective-permute-start.43
  191.5 6.1 %collective-permute-done.29.prev_ref = bf16[160,2048]{1,0:T(8,128)(2,1)S(1)} collective-permute-done((bf16[160,2048]{1,0:T(8,128)(2,1)}, bf16[160,2048]{1,0:T(8,128)(2,1)S(1)}, u32[]{:S(2)}, u32[]{:S(2)}) %collective-permute-start.29) | collective-permute-done | bytes 655392 | tf_op jit(solution)/shard_map/ppermute | solution.py:397
  199.4 2.8 pack_returns.2
  204.0 2.2 collective-permute-start.33
  206.2 5.5 %collective-permute-done.42.prev_ref = bf16[160,2048]{1,0:T(8,128)(2,1)S(1)} collective-permute-done((bf16[160,2048]{1,0:T(8,128)(2,1)}, bf16[160,2048]{1,0:T(8,128)(2,1)S(1)}, u32[]{:S(2)}, u32[]{:S(2)}) %collective-permute-start.42) | collective-permute-done | bytes 655392 | tf_op jit(solution)/shard_map/ppermute | solution.py:397
  213.3 2.8 pack_returns.3
  216.1 2.4 collective-permute-start.36
  218.5 2.8 collective-permute-start.37
  228.0 2.3 collective-permute-start.48
  231.6 2.5 collective-permute-start.50
  234.1 2.7 collective-permute-start.51
  237.6 24.0 %all-gather.1 = f32[8,1,2048]{2,1,0:T(1,128)S(1)} all-gather(f32[1,1,2048]{2,1,0:T(1,128)S(1)} %bitcast.45), channel_id=1, replica_groups=mesh['z'=4,'core'=2,'exp'=16] {'z','core'}, dimensions={0}, use_global_device_ids=true | all-gather | bytes 73728 | tf_op jit(solution)/shard_map/all_gather | solution.py:462
  265.1 11.2 %combine_and_scan.1 = (bf16[128,2048]{1,0:T(8,128)(2,1)}, f32[128,2048]{1,0:T(8,128)}, bf16[16,2048]{1,0:T(8,128)(2,1)}) custom-call(s32[128,2]{1,0:T(8,128)} %bitcast.37, s32[1,16]{1,0:T(1,128)} %bitcast.47, f32[128,2]{1,0:T(8,128)} %bitcast.40, bf16[24,2048]{1,0:T(8,128)(2,1)} %get-tuple-element.131.refs_0_, bf16[24,2048]{1,0:T(8,128)(2,1)} %copy-done.28, ...), custom_call_target="tpu_custom_call" | custom-call | tf_op jit(solution)/shard_map/combine_and_scan/pallas_call | solution.py:286
  276.3 14.4 %all-gather = bf16[128,2048]{1,0:T(8,128)(2,1)} all-gather(bf16[16,2048]{1,0:T(8,128)(2,1)} %get-tuple-element.168), channel_id=2, replica_groups=mesh['z'=4,'core'=2,'exp'=16] {'z','core'}, dimensions={0}, use_global_device_ids=true | all-gather | bytes 589824 | tf_op jit(solution)/shard_map/all_gather | solution.py:466
  290.8 7.9 %add_carry.1 = bf16[128,2048]{1,0:T(8,128)(2,1)} custom-call(s32[1]{0:T(128)} %bitcast.13.place_ref, bf16[8,16,2048]{2,1,0:T(8,128)(2,1)} %bitcast.33, f32[8,2048]{1,0:T(8,128)} %bitcast.41, f32[16,2048]{1,0:T(8,128)} %rate_ref.3, f32[128,2048]{1,0:T(8,128)} %get-tuple-element.170.local_ref, bf16[16,128,2048]{2,1,0:T(8,128)(2,1)} %get-tuple-element.171.reach_ref), custom_call_target="tpu_custom_call" | custom-call | tf_op jit(solution)/shard_map/add_carry/pallas_call | solution.py:373
  (196 shorter events, 42.0 us)
Async XLA Ops:
  0.6 83.7 %collective-permute-start.13 = (bf16[896,2048]{1,0:T(8,128)(2,1)}, bf16[896,2048]{1,0:T(8,128)(2,1)}, u32[]{:S(2)}, u32[]{:S(2)}) collective-permute-start(bf16[896,2048]{1,0:T(8,128)(2,1)} %bitcast.21), channel_id=1, source_target_pairs={{0,16},{16,0},{1,17},{17,1},{2,18},{18,2},{3,19},{19,3},{4,20},{20... | collective-permute-start | bytes 11010056 | tf_op jit(solution)/shard_map/ppermute | solution.py:400
  2.1 84.9 %collective-permute-start.14 = (bf16[896,2048]{1,0:T(8,128)(2,1)}, bf16[896,2048]{1,0:T(8,128)(2,1)}, u32[]{:S(2)}, u32[]{:S(2)}) collective-permute-start(bf16[896,2048]{1,0:T(8,128)(2,1)} %bitcast.26), channel_id=1, source_target_pairs={{0,16},{16,0},{1,17},{17,1},{2,18},{18,2},{3,19},{19,3},{4,20},{20... | collective-permute-start | bytes 11010056 | tf_op jit(solution)/shard_map/ppermute | solution.py:400
  12.1 8.6 %collective-permute-start.6 = (bf16[40,2048]{1,0:T(8,128)(2,1)}, bf16[40,2048]{1,0:T(8,128)(2,1)S(1)}, u32[]{:S(2)}, u32[]{:S(2)}) collective-permute-start(bf16[40,2048]{1,0:T(8,128)(2,1)} %get-tuple-element.92), channel_id=1, source_target_pairs={{0,5},{1,6},{2,7},{3,4},{4,9},{5,10},{6,11},{7,8},{8,13},{9,14},{1... | collective-permute-start | bytes 491528 | tf_op jit(solution)/shard_map/ppermute | solution.py:411
  12.1 8.9 %collective-permute-start.7 = (bf16[40,2048]{1,0:T(8,128)(2,1)}, bf16[40,2048]{1,0:T(8,128)(2,1)S(1)}, u32[]{:S(2)}, u32[]{:S(2)}) collective-permute-start(bf16[40,2048]{1,0:T(8,128)(2,1)} %get-tuple-element.93), channel_id=1, source_target_pairs={{0,15},{1,12},{2,13},{3,14},{4,3},{5,0},{6,1},{7,2},{8,7},{9,4},{1... | collective-permute-start | bytes 491528 | tf_op jit(solution)/shard_map/ppermute | solution.py:411
  20.7 7.6 %collective-permute-start = (bf16[40,2048]{1,0:T(8,128)(2,1)}, bf16[40,2048]{1,0:T(8,128)(2,1)S(1)}, u32[]{:S(2)}, u32[]{:S(2)}) collective-permute-start(bf16[40,2048]{1,0:T(8,128)(2,1)} %get-tuple-element.88), channel_id=1, source_target_pairs={{0,4},{1,5},{2,6},{3,7},{4,8},{5,9},{6,10},{7,11},{8,12},{9,13},{1... | collective-permute-start | bytes 491528 | tf_op jit(solution)/shard_map/ppermute | solution.py:411
  23.4 8.3 %collective-permute-start.2 = (bf16[40,2048]{1,0:T(8,128)(2,1)}, bf16[40,2048]{1,0:T(8,128)(2,1)S(1)}, u32[]{:S(2)}, u32[]{:S(2)}) collective-permute-start(bf16[40,2048]{1,0:T(8,128)(2,1)} %get-tuple-element.90), channel_id=1, source_target_pairs={{0,12},{1,13},{2,14},{3,15},{4,0},{5,1},{6,2},{7,3},{8,4},{9,5},{1... | collective-permute-start | bytes 491528 | tf_op jit(solution)/shard_map/ppermute | solution.py:411
  28.4 8.0 %collective-permute-start.15 = (bf16[40,2048]{1,0:T(8,128)(2,1)}, bf16[40,2048]{1,0:T(8,128)(2,1)S(1)}, u32[]{:S(2)}, u32[]{:S(2)}) collective-permute-start(bf16[40,2048]{1,0:T(8,128)(2,1)} %get-tuple-element.113), channel_id=1, source_target_pairs={{0,13},{1,14},{2,15},{3,12},{4,1},{5,2},{6,3},{7,0},{8,5},{9,6},{1... | collective-permute-start | bytes 491528 | tf_op jit(solution)/shard_map/ppermute | solution.py:411
  28.4 8.0 %collective-permute-start.16 = (bf16[40,2048]{1,0:T(8,128)(2,1)}, bf16[40,2048]{1,0:T(8,128)(2,1)S(1)}, u32[]{:S(2)}, u32[]{:S(2)}) collective-permute-start(bf16[40,2048]{1,0:T(8,128)(2,1)} %get-tuple-element.114), channel_id=1, source_target_pairs={{0,8},{1,9},{2,10},{3,11},{4,12},{5,13},{6,14},{7,15},{8,0},{9,1},... | collective-permute-start | bytes 491528 | tf_op jit(solution)/shard_map/ppermute | solution.py:411
  31.7 34.6 %collective-permute-start.11 = (bf16[160,2048]{1,0:T(8,128)(2,1)}, bf16[160,2048]{1,0:T(8,128)(2,1)S(1)}, u32[]{:S(2)}, u32[]{:S(2)}) collective-permute-start(bf16[160,2048]{1,0:T(8,128)(2,1)} %sort_messages.5.refs_1_), channel_id=1, source_target_pairs={{0,32},{32,64},{64,96},{96,0},{1,33},{33,65},{65,97},{97,1},{2,34}... | collective-permute-start | bytes 1966088 | tf_op jit(solution)/shard_map/ppermute | solution.py:397
  36.4 8.1 %collective-permute-start.18 = (bf16[40,2048]{1,0:T(8,128)(2,1)}, bf16[40,2048]{1,0:T(8,128)(2,1)S(1)}, u32[]{:S(2)}, u32[]{:S(2)}) collective-permute-start(bf16[40,2048]{1,0:T(8,128)(2,1)} %get-tuple-element.116), channel_id=1, source_target_pairs={{0,9},{1,10},{2,11},{3,8},{4,13},{5,14},{6,15},{7,12},{8,1},{9,2},... | collective-permute-start | bytes 491528 | tf_op jit(solution)/shard_map/ppermute | solution.py:411
  42.3 9.3 %collective-permute-start.20 = (bf16[40,2048]{1,0:T(8,128)(2,1)}, bf16[40,2048]{1,0:T(8,128)(2,1)S(1)}, u32[]{:S(2)}, u32[]{:S(2)}) collective-permute-start(bf16[40,2048]{1,0:T(8,128)(2,1)} %get-tuple-element.117), channel_id=1, source_target_pairs={{0,6},{1,7},{2,4},{3,5},{4,10},{5,11},{6,8},{7,9},{8,14},{9,15},{1... | collective-permute-start | bytes 491528 | tf_op jit(solution)/shard_map/ppermute | solution.py:411
  44.5 9.9 %collective-permute-start.21 = (bf16[40,2048]{1,0:T(8,128)(2,1)}, bf16[40,2048]{1,0:T(8,128)(2,1)S(1)}, u32[]{:S(2)}, u32[]{:S(2)}) collective-permute-start(bf16[40,2048]{1,0:T(8,128)(2,1)} %get-tuple-element.118), channel_id=1, source_target_pairs={{0,11},{1,8},{2,9},{3,10},{4,15},{5,12},{6,13},{7,14},{8,3},{9,0},... | collective-permute-start | bytes 491528 | tf_op jit(solution)/shard_map/ppermute | solution.py:411
  51.6 9.2 %collective-permute-start.22 = (bf16[40,2048]{1,0:T(8,128)(2,1)}, bf16[40,2048]{1,0:T(8,128)(2,1)S(1)}, u32[]{:S(2)}, u32[]{:S(2)}) collective-permute-start(bf16[40,2048]{1,0:T(8,128)(2,1)} %get-tuple-element.119), channel_id=1, source_target_pairs={{0,14},{1,15},{2,12},{3,13},{4,2},{5,3},{6,0},{7,1},{8,6},{9,7},{1... | collective-permute-start | bytes 491528 | tf_op jit(solution)/shard_map/ppermute | solution.py:411
  54.4 9.8 %collective-permute-start.23 = (bf16[40,2048]{1,0:T(8,128)(2,1)}, bf16[40,2048]{1,0:T(8,128)(2,1)S(1)}, u32[]{:S(2)}, u32[]{:S(2)}) collective-permute-start(bf16[40,2048]{1,0:T(8,128)(2,1)} %get-tuple-element.120), channel_id=1, source_target_pairs={{0,10},{1,11},{2,8},{3,9},{4,14},{5,15},{6,12},{7,13},{8,2},{9,3},... | collective-permute-start | bytes 491528 | tf_op jit(solution)/shard_map/ppermute | solution.py:411
  60.8 18.1 %collective-permute-start.9 = (bf16[160,2048]{1,0:T(8,128)(2,1)}, bf16[160,2048]{1,0:T(8,128)(2,1)S(1)}, u32[]{:S(2)}, u32[]{:S(2)}) collective-permute-start(bf16[160,2048]{1,0:T(8,128)(2,1)} %sort_messages.5.refs_1_), channel_id=1, source_target_pairs={{0,96},{32,0},{64,32},{96,64},{1,97},{33,1},{65,33},{97,65},{2,98}... | collective-permute-start | bytes 1966088 | tf_op jit(solution)/shard_map/ppermute | solution.py:397
  64.3 16.8 %collective-permute-start.12 = (bf16[160,2048]{1,0:T(8,128)(2,1)}, bf16[160,2048]{1,0:T(8,128)(2,1)}, u32[]{:S(2)}, u32[]{:S(2)}) collective-permute-start(bf16[160,2048]{1,0:T(8,128)(2,1)} %sort_messages.4.refs_0_), channel_id=1, source_target_pairs={{0,96},{32,0},{64,32},{96,64},{1,97},{33,1},{65,33},{97,65},{2,98}... | collective-permute-start | bytes 1966088 | tf_op jit(solution)/shard_map/ppermute | solution.py:397
  66.3 18.1 %collective-permute-start.3 = (bf16[160,2048]{1,0:T(8,128)(2,1)}, bf16[160,2048]{1,0:T(8,128)(2,1)}, u32[]{:S(2)}, u32[]{:S(2)}) collective-permute-start(bf16[160,2048]{1,0:T(8,128)(2,1)} %sort_messages.4.refs_0_), channel_id=1, source_target_pairs={{0,32},{32,64},{64,96},{96,0},{1,33},{33,65},{65,97},{97,1},{2,34}... | collective-permute-start | bytes 1966088 | tf_op jit(solution)/shard_map/ppermute | solution.py:397
  78.9 62.0 %collective-permute-start.19 = (bf16[160,2048]{1,0:T(8,128)(2,1)}, bf16[160,2048]{1,0:T(8,128)(2,1)S(1)}, u32[]{:S(2)}, u32[]{:S(2)}) collective-permute-start(bf16[160,2048]{1,0:T(8,128)(2,1)} %sort_messages.6.refs_2_), channel_id=1, source_target_pairs={{0,32},{32,64},{64,96},{96,0},{1,33},{33,65},{65,97},{97,1},{2,34}... | collective-permute-start | bytes 1966088 | tf_op jit(solution)/shard_map/ppermute | solution.py:397
  81.1 59.9 %collective-permute-start.25 = (bf16[160,2048]{1,0:T(8,128)(2,1)}, bf16[160,2048]{1,0:T(8,128)(2,1)S(1)}, u32[]{:S(2)}, u32[]{:S(2)}) collective-permute-start(bf16[160,2048]{1,0:T(8,128)(2,1)} %sort_messages.6.refs_2_), channel_id=1, source_target_pairs={{0,96},{32,0},{64,32},{96,64},{1,97},{33,1},{65,33},{97,65},{2,98}... | collective-permute-start | bytes 1966088 | tf_op jit(solution)/shard_map/ppermute | solution.py:397
  84.4 56.5 %collective-permute-start.24 = (bf16[160,2048]{1,0:T(8,128)(2,1)}, bf16[160,2048]{1,0:T(8,128)(2,1)S(1)}, u32[]{:S(2)}, u32[]{:S(2)}) collective-permute-start(bf16[160,2048]{1,0:T(8,128)(2,1)} %sort_messages.7.refs_3_), channel_id=1, source_target_pairs={{0,32},{32,64},{64,96},{96,0},{1,33},{33,65},{65,97},{97,1},{2,34}... | collective-permute-start | bytes 1966088 | tf_op jit(solution)/shard_map/ppermute | solution.py:397
  84.4 23.7 %collective-permute-start.10 = (bf16[160,2048]{1,0:T(8,128)(2,1)S(1)}, bf16[160,2048]{1,0:T(8,128)(2,1)S(1)}, u32[]{:S(2)}, u32[]{:S(2)}) collective-permute-start(bf16[160,2048]{1,0:T(8,128)(2,1)S(1)} %collective-permute-done.9.refs_5_), channel_id=1, source_target_pairs={{0,96},{32,0},{64,32},{96,64},{1,97},{33,1},{65,33},{97,65},{2,98}... | collective-permute-start | bytes 1966088 | tf_op jit(solution)/shard_map/ppermute | solution.py:397
  87.1 38.1 %collective-permute-start.4 = (bf16[160,2048]{1,0:T(8,128)(2,1)}, bf16[160,2048]{1,0:T(8,128)(2,1)S(1)}, u32[]{:S(2)}, u32[]{:S(2)}) collective-permute-start(bf16[160,2048]{1,0:T(8,128)(2,1)} %collective-permute-done.3.refs_2_), channel_id=1, source_target_pairs={{0,32},{32,64},{64,96},{96,0},{1,33},{33,65},{65,97},{97,1},{2,34}... | collective-permute-start | bytes 1966088 | tf_op jit(solution)/shard_map/ppermute | solution.py:397
  108.1 32.8 %collective-permute-start.26 = (bf16[160,2048]{1,0:T(8,128)(2,1)S(1)}, bf16[160,2048]{1,0:T(8,128)(2,1)S(1)}, u32[]{:S(2)}, u32[]{:S(2)}) collective-permute-start(bf16[160,2048]{1,0:T(8,128)(2,1)S(1)} %copy-done.2), channel_id=1, source_target_pairs={{0,96},{32,0},{64,32},{96,64},{1,97},{33,1},{65,33},{97,65},{2,98}... | collective-permute-start | bytes 1966088 | tf_op jit(solution)/shard_map/ppermute | solution.py:397
  141.0 20.2 %collective-permute-start.38 = (bf16[160,2048]{1,0:T(8,128)(2,1)S(1)}, bf16[160,2048]{1,0:T(8,128)(2,1)S(1)}, u32[]{:S(2)}, u32[]{:S(2)}) collective-permute-start(bf16[160,2048]{1,0:T(8,128)(2,1)S(1)} %collective-permute-done.19.refs_0_), channel_id=1, source_target_pairs={{0,32},{32,64},{64,96},{96,0},{1,33},{33,65},{65,97},{97,1},{2,34}... | collective-permute-start | bytes 1966088 | tf_op jit(solution)/shard_map/ppermute | solution.py:397
  141.0 20.2 %collective-permute-start.39 = (bf16[160,2048]{1,0:T(8,128)(2,1)S(1)}, bf16[160,2048]{1,0:T(8,128)(2,1)S(1)}, u32[]{:S(2)}, u32[]{:S(2)}) collective-permute-start(bf16[160,2048]{1,0:T(8,128)(2,1)S(1)} %collective-permute-done.26.refs_3_), channel_id=1, source_target_pairs={{0,96},{32,0},{64,32},{96,64},{1,97},{33,1},{65,33},{97,65},{2,98}... | collective-permute-start | bytes 1966088 | tf_op jit(solution)/shard_map/ppermute | solution.py:397
  143.7 34.2 %collective-permute-start.27 = (bf16[80,2048]{1,0:T(8,128)(2,1)}, bf16[80,2048]{1,0:T(8,128)(2,1)S(1)}, u32[]{:S(2)}, u32[]{:S(2)}) collective-permute-start(bf16[80,2048]{1,0:T(8,128)(2,1)} %get-tuple-element.127), channel_id=1, source_target_pairs={{0,32},{32,64},{64,96},{96,0},{1,33},{33,65},{65,97},{97,1},{2,34}... | collective-permute-start | bytes 983048 | tf_op jit(solution)/shard_map/ppermute | solution.py:397
  143.7 34.2 %collective-permute-start.28 = (bf16[80,2048]{1,0:T(8,128)(2,1)}, bf16[80,2048]{1,0:T(8,128)(2,1)S(1)}, u32[]{:S(2)}, u32[]{:S(2)}) collective-permute-start(bf16[80,2048]{1,0:T(8,128)(2,1)} %get-tuple-element.128), channel_id=1, source_target_pairs={{0,96},{32,0},{64,32},{96,64},{1,97},{33,1},{65,33},{97,65},{2,98}... | collective-permute-start | bytes 983048 | tf_op jit(solution)/shard_map/ppermute | solution.py:397
  175.2 9.5 %collective-permute-start.40 = (bf16[80,2048]{1,0:T(8,128)(2,1)}, bf16[80,2048]{1,0:T(8,128)(2,1)S(1)}, u32[]{:S(2)}, u32[]{:S(2)}) collective-permute-start(bf16[80,2048]{1,0:T(8,128)(2,1)} %get-tuple-element.155), channel_id=1, source_target_pairs={{0,32},{32,64},{64,96},{96,0},{1,33},{33,65},{65,97},{97,1},{2,34}... | collective-permute-start | bytes 983048 | tf_op jit(solution)/shard_map/ppermute | solution.py:397
  175.3 9.5 %collective-permute-start.41 = (bf16[80,2048]{1,0:T(8,128)(2,1)}, bf16[80,2048]{1,0:T(8,128)(2,1)S(1)}, u32[]{:S(2)}, u32[]{:S(2)}) collective-permute-start(bf16[80,2048]{1,0:T(8,128)(2,1)} %get-tuple-element.156), channel_id=1, source_target_pairs={{0,96},{32,0},{64,32},{96,64},{1,97},{33,1},{65,33},{97,65},{2,98}... | collective-permute-start | bytes 983048 | tf_op jit(solution)/shard_map/ppermute | solution.py:397
  182.1 15.6 %collective-permute-start.29 = (bf16[160,2048]{1,0:T(8,128)(2,1)}, bf16[160,2048]{1,0:T(8,128)(2,1)S(1)}, u32[]{:S(2)}, u32[]{:S(2)}) collective-permute-start(bf16[160,2048]{1,0:T(8,128)(2,1)} %get-tuple-element.129), channel_id=1, source_target_pairs={{0,32},{32,64},{64,96},{96,0},{1,33},{33,65},{65,97},{97,1},{2,34}... | collective-permute-start | bytes 1966088 | tf_op jit(solution)/shard_map/ppermute | solution.py:397
  182.1 15.6 %collective-permute-start.30 = (bf16[160,2048]{1,0:T(8,128)(2,1)}, bf16[160,2048]{1,0:T(8,128)(2,1)S(1)}, u32[]{:S(2)}, u32[]{:S(2)}) collective-permute-start(bf16[160,2048]{1,0:T(8,128)(2,1)} %get-tuple-element.130), channel_id=1, source_target_pairs={{0,96},{32,0},{64,32},{96,64},{1,97},{33,1},{65,33},{97,65},{2,98}... | collective-permute-start | bytes 1966088 | tf_op jit(solution)/shard_map/ppermute | solution.py:397
  188.9 22.8 %collective-permute-start.42 = (bf16[160,2048]{1,0:T(8,128)(2,1)}, bf16[160,2048]{1,0:T(8,128)(2,1)S(1)}, u32[]{:S(2)}, u32[]{:S(2)}) collective-permute-start(bf16[160,2048]{1,0:T(8,128)(2,1)} %get-tuple-element.157), channel_id=1, source_target_pairs={{0,32},{32,64},{64,96},{96,0},{1,33},{33,65},{65,97},{97,1},{2,34}... | collective-permute-start | bytes 1966088 | tf_op jit(solution)/shard_map/ppermute | solution.py:397
  188.9 22.8 %collective-permute-start.43 = (bf16[160,2048]{1,0:T(8,128)(2,1)}, bf16[160,2048]{1,0:T(8,128)(2,1)S(1)}, u32[]{:S(2)}, u32[]{:S(2)}) collective-permute-start(bf16[160,2048]{1,0:T(8,128)(2,1)} %get-tuple-element.158), channel_id=1, source_target_pairs={{0,96},{32,0},{64,32},{96,64},{1,97},{33,1},{65,33},{97,65},{2,98}... | collective-permute-start | bytes 1966088 | tf_op jit(solution)/shard_map/ppermute | solution.py:397
  202.2 13.9 %collective-permute-start.31 = (bf16[24,2048]{1,0:T(8,128)(2,1)}, bf16[24,2048]{1,0:T(8,128)(2,1)S(1)}, u32[]{:S(2)}, u32[]{:S(2)}) collective-permute-start(bf16[24,2048]{1,0:T(8,128)(2,1)} %get-tuple-element.132), channel_id=1, source_target_pairs={{0,12},{1,13},{2,14},{3,15},{4,0},{5,1},{6,2},{7,3},{8,4},{9,5},{1... | collective-permute-start | bytes 294920 | tf_op jit(solution)/shard_map/ppermute | solution.py:411
  202.2 16.3 %collective-permute-start.32 = (bf16[24,2048]{1,0:T(8,128)(2,1)}, bf16[24,2048]{1,0:T(8,128)(2,1)S(1)}, u32[]{:S(2)}, u32[]{:S(2)}) collective-permute-start(bf16[24,2048]{1,0:T(8,128)(2,1)} %get-tuple-element.133), channel_id=1, source_target_pairs={{0,3},{1,0},{2,1},{3,2},{4,7},{5,4},{6,5},{7,6},{8,11},{9,8},{10,9... | collective-permute-start | bytes 294920 | tf_op jit(solution)/shard_map/ppermute | solution.py:411
  204.0 17.3 %collective-permute-start.33 = (bf16[24,2048]{1,0:T(8,128)(2,1)}, bf16[24,2048]{1,0:T(8,128)(2,1)S(1)}, u32[]{:S(2)}, u32[]{:S(2)}) collective-permute-start(bf16[24,2048]{1,0:T(8,128)(2,1)} %get-tuple-element.134), channel_id=1, source_target_pairs={{0,4},{1,5},{2,6},{3,7},{4,8},{5,9},{6,10},{7,11},{8,12},{9,13},{1... | collective-permute-start | bytes 294920 | tf_op jit(solution)/shard_map/ppermute | solution.py:411
  211.7 11.6 %collective-permute-start.34 = (bf16[24,2048]{1,0:T(8,128)(2,1)}, bf16[24,2048]{1,0:T(8,128)(2,1)S(1)}, u32[]{:S(2)}, u32[]{:S(2)}) collective-permute-start(bf16[24,2048]{1,0:T(8,128)(2,1)} %get-tuple-element.135), channel_id=1, source_target_pairs={{0,1},{1,2},{2,3},{3,0},{4,5},{5,6},{6,7},{7,4},{8,9},{9,10},{10,1... | collective-permute-start | bytes 294920 | tf_op jit(solution)/shard_map/ppermute | solution.py:411
  211.7 13.4 %collective-permute-start.35 = (bf16[24,2048]{1,0:T(8,128)(2,1)}, bf16[24,2048]{1,0:T(8,128)(2,1)S(1)}, u32[]{:S(2)}, u32[]{:S(2)}) collective-permute-start(bf16[24,2048]{1,0:T(8,128)(2,1)} %get-tuple-element.136), channel_id=1, source_target_pairs={{0,15},{1,12},{2,13},{3,14},{4,3},{5,0},{6,1},{7,2},{8,7},{9,4},{1... | collective-permute-start | bytes 294920 | tf_op jit(solution)/shard_map/ppermute | solution.py:411
  216.1 10.2 %collective-permute-start.36 = (bf16[24,2048]{1,0:T(8,128)(2,1)}, bf16[24,2048]{1,0:T(8,128)(2,1)S(1)}, u32[]{:S(2)}, u32[]{:S(2)}) collective-permute-start(bf16[24,2048]{1,0:T(8,128)(2,1)} %get-tuple-element.137), channel_id=1, source_target_pairs={{0,5},{1,6},{2,7},{3,4},{4,9},{5,10},{6,11},{7,8},{8,13},{9,14},{1... | collective-permute-start | bytes 294920 | tf_op jit(solution)/shard_map/ppermute | solution.py:411
  218.5 9.5 %collective-permute-start.37 = (bf16[24,2048]{1,0:T(8,128)(2,1)}, bf16[24,2048]{1,0:T(8,128)(2,1)S(1)}, u32[]{:S(2)}, u32[]{:S(2)}) collective-permute-start(bf16[24,2048]{1,0:T(8,128)(2,1)} %get-tuple-element.138), channel_id=1, source_target_pairs={{0,13},{1,14},{2,15},{3,12},{4,1},{5,2},{6,3},{7,0},{8,5},{9,6},{1... | collective-permute-start | bytes 294920 | tf_op jit(solution)/shard_map/ppermute | solution.py:411
  221.3 8.9 %collective-permute-start.44 = (bf16[24,2048]{1,0:T(8,128)(2,1)}, bf16[24,2048]{1,0:T(8,128)(2,1)S(1)}, u32[]{:S(2)}, u32[]{:S(2)}) collective-permute-start(bf16[24,2048]{1,0:T(8,128)(2,1)} %get-tuple-element.159), channel_id=1, source_target_pairs={{0,7},{1,4},{2,5},{3,6},{4,11},{5,8},{6,9},{7,10},{8,15},{9,12},{1... | collective-permute-start | bytes 294920 | tf_op jit(solution)/shard_map/ppermute | solution.py:411
  223.3 8.3 %collective-permute-start.45 = (bf16[24,2048]{1,0:T(8,128)(2,1)}, bf16[24,2048]{1,0:T(8,128)(2,1)S(1)}, u32[]{:S(2)}, u32[]{:S(2)}) collective-permute-start(bf16[24,2048]{1,0:T(8,128)(2,1)} %get-tuple-element.160), channel_id=1, source_target_pairs={{0,8},{1,9},{2,10},{3,11},{4,12},{5,13},{6,14},{7,15},{8,0},{9,1},... | collective-permute-start | bytes 294920 | tf_op jit(solution)/shard_map/ppermute | solution.py:411
  225.2 9.0 %collective-permute-start.46 = (bf16[24,2048]{1,0:T(8,128)(2,1)}, bf16[24,2048]{1,0:T(8,128)(2,1)S(1)}, u32[]{:S(2)}, u32[]{:S(2)}) collective-permute-start(bf16[24,2048]{1,0:T(8,128)(2,1)} %get-tuple-element.161), channel_id=1, source_target_pairs={{0,2},{1,3},{2,0},{3,1},{4,6},{5,7},{6,4},{7,5},{8,10},{9,11},{10,... | collective-permute-start | bytes 294920 | tf_op jit(solution)/shard_map/ppermute | solution.py:411
  226.3 35.9 %collective-permute-start.47 = (bf16[24,2048]{1,0:T(8,128)(2,1)}, bf16[24,2048]{1,0:T(8,128)(2,1)S(1)}, u32[]{:S(2)}, u32[]{:S(2)}) collective-permute-start(bf16[24,2048]{1,0:T(8,128)(2,1)} %get-tuple-element.162), channel_id=1, source_target_pairs={{0,11},{1,8},{2,9},{3,10},{4,15},{5,12},{6,13},{7,14},{8,3},{9,0},... | collective-permute-start | bytes 294920 | tf_op jit(solution)/shard_map/ppermute | solution.py:411
  228.0 34.3 %collective-permute-start.48 = (bf16[24,2048]{1,0:T(8,128)(2,1)}, bf16[24,2048]{1,0:T(8,128)(2,1)S(1)}, u32[]{:S(2)}, u32[]{:S(2)}) collective-permute-start(bf16[24,2048]{1,0:T(8,128)(2,1)} %get-tuple-element.163), channel_id=1, source_target_pairs={{0,14},{1,15},{2,12},{3,13},{4,2},{5,3},{6,0},{7,1},{8,6},{9,7},{1... | collective-permute-start | bytes 294920 | tf_op jit(solution)/shard_map/ppermute | solution.py:411
  230.2 32.0 %collective-permute-start.49 = (bf16[24,2048]{1,0:T(8,128)(2,1)}, bf16[24,2048]{1,0:T(8,128)(2,1)S(1)}, u32[]{:S(2)}, u32[]{:S(2)}) collective-permute-start(bf16[24,2048]{1,0:T(8,128)(2,1)} %get-tuple-element.164), channel_id=1, source_target_pairs={{0,9},{1,10},{2,11},{3,8},{4,13},{5,14},{6,15},{7,12},{8,1},{9,2},... | collective-permute-start | bytes 294920 | tf_op jit(solution)/shard_map/ppermute | solution.py:411
  231.6 30.7 %collective-permute-start.50 = (bf16[24,2048]{1,0:T(8,128)(2,1)}, bf16[24,2048]{1,0:T(8,128)(2,1)S(1)}, u32[]{:S(2)}, u32[]{:S(2)}) collective-permute-start(bf16[24,2048]{1,0:T(8,128)(2,1)} %get-tuple-element.165), channel_id=1, source_target_pairs={{0,6},{1,7},{2,4},{3,5},{4,10},{5,11},{6,8},{7,9},{8,14},{9,15},{1... | collective-permute-start | bytes 294920 | tf_op jit(solution)/shard_map/ppermute | solution.py:411
  234.1 28.2 %collective-permute-start.51 = (bf16[24,2048]{1,0:T(8,128)(2,1)}, bf16[24,2048]{1,0:T(8,128)(2,1)S(1)}, u32[]{:S(2)}, u32[]{:S(2)}) collective-permute-start(bf16[24,2048]{1,0:T(8,128)(2,1)} %get-tuple-element.166), channel_id=1, source_target_pairs={{0,10},{1,11},{2,8},{3,9},{4,14},{5,15},{6,12},{7,13},{8,2},{9,3},... | collective-permute-start | bytes 294920 | tf_op jit(solution)/shard_map/ppermute | solution.py:411
  (60 other events, 1319.9 us)

commit v3 on v2

--- a/solution.py
+++ b/solution.py
@@ -11,19 +11,12 @@
 
 VMEM_LIMIT = 56 * 1024 * 1024
 CORES = 2
-SIDE = 4
-GROUP = 4
+EARLY = 12
 HIDDEN_STEP = 128
 OUT_COLS = 1024
 SCAN_COLS = 1024
 BF = jnp.bfloat16
 F32 = jnp.float32
-SHIFTS = (
-    (0, 0), (1, 0), (0, 1), (3, 0),
-    (0, 3), (1, 1), (3, 3), (1, 3),
-    (3, 1), (2, 0), (0, 2), (2, 1),
-    (1, 2), (2, 3), (3, 2), (2, 2),
-)
 
 
 def params():
@@ -38,12 +31,16 @@
     return lax.optimization_barrier(values)
 
 
-def gather_body(capacity, ids_ref, order_ref, x_ref, dy_ref, *outs):
+def part_sizes(capacity):
+    return (EARLY, capacity - EARLY)
+
+
+def gather_body(capacity, ids_ref, x_ref, dy_ref, *outs):
     tokens = x_ref.shape[0]
-    experts = len(outs)
+    experts = outs[0].shape[0] // (2 * EARLY)
     ids = ids_ref[...]
-    order = jnp.broadcast_to(order_ref[...], (experts, tokens))
-    hots = [(order == ids[k : k + 1, :]).astype(F32) for k in range(2)]
+    at = lax.broadcasted_iota(jnp.int32, (experts, tokens), 0)
+    hots = [(at == ids[k : k + 1, :]).astype(F32) for k in range(2)]
     before = (
         lax.broadcasted_iota(jnp.int32, (tokens, tokens), 0)
         < lax.broadcasted_iota(jnp.int32, (tokens, tokens), 1)
@@ -51,80 +48,96 @@
     earlier = jnp.dot(
         (hots[0] + hots[1]).astype(BF), before.astype(BF), preferred_element_type=F32
     )
-    message = 2 * capacity
-    base = lax.broadcasted_iota(jnp.int32, (experts, tokens), 0).astype(F32) * message
-    place = lax.broadcasted_iota(jnp.int32, (experts * message, tokens), 0)
-    pick_x = pick_dy = None
-    for k in range(2):
-        target = jnp.sum((earlier + base) * hots[k], axis=0, keepdims=True).astype(jnp.int32)
-        hit_x, hit_dy = place == target, place == target + capacity
-        pick_x = hit_x if pick_x is None else pick_x | hit_x
-        pick_dy = hit_dy if pick_dy is None else pick_dy | hit_dy
-    rows = jnp.dot(pick_x.astype(F32).astype(BF), x_ref[...], preferred_element_type=F32)
-    rows += jnp.dot(pick_dy.astype(F32).astype(BF), dy_ref[...], preferred_element_type=F32)
-    rows = rows.astype(BF)
-    for p, out in enumerate(outs):
-        out[...] = rows[p * message : (p + 1) * message]
-
-
-def gather_rows(ids_t, order, x, dy, capacity):
-    experts, dim = order.shape[0], x.shape[1]
+    slots = [
+        jnp.sum(earlier * hot, axis=0, keepdims=True).astype(jnp.int32) for hot in hots
+    ]
+    first = 0
+    for size, out in zip(part_sizes(capacity), outs):
+        place = lax.broadcasted_iota(jnp.int32, (out.shape[0], tokens), 0)
+        pick_x = pick_dy = None
+        for k in range(2):
+            slot = slots[k] - first
+            inside = (slot >= 0) & (slot < size)
+            target = jnp.where(inside, ids[k : k + 1, :] * (2 * size) + slot, -size - 1)
+            hit_x, hit_dy = place == target, place == target + size
+            pick_x = hit_x if pick_x is None else pick_x | hit_x
+            pick_dy = hit_dy if pick_dy is None else pick_dy | hit_dy
+        rows = jnp.dot(pick_x.astype(F32).astype(BF), x_ref[...], preferred_element_type=F32)
+        rows += jnp.dot(
+            pick_dy.astype(F32).astype(BF), dy_ref[...], preferred_element_type=F32
+        )
+        out[...] = rows.astype(BF)
+        first += size
+
+
+def gather_rows(ids_t, x, dy, experts, capacity):
+    dim = x.shape[1]
     return pl.pallas_call(
         functools.partial(gather_body, capacity),
-        out_shape=[jax.ShapeDtypeStruct((2 * capacity, dim), BF)] * experts,
+        out_shape=[
+            jax.ShapeDtypeStruct((experts * 2 * size, dim), BF)
+            for size in part_sizes(capacity)
+        ],
         compiler_params=params(),
         name="gather_rows",
-    )(ids_t, order, x, dy)
-
-
-def sort_body(table_ref, *refs):
-    ins, out = refs[:-1], refs[-1]
-    rows = jnp.concatenate([r[...] for r in ins], axis=0)
-    out[...] = jnp.dot(table_ref[...], rows, preferred_element_type=F32).astype(BF)
-
-
-def sort_messages(messages, capacity):
-    count, dim = len(messages), messages[0].shape[1]
-    rows = 2 * capacity * count
+    )(ids_t, x, dy)
+
+
+def sort_body(table_ref, rows_ref, *outs):
+    size = outs[0].shape[0]
+    for i, out in enumerate(outs):
+        rows = rows_ref[i * size : (i + 1) * size]
+        out[...] = jnp.dot(table_ref[...], rows, preferred_element_type=F32).astype(BF)
+
+
+def sort_messages(messages, experts, size):
+    count, dim = experts // 2, messages.shape[1]
+    rows = 2 * size * count
     at = np.arange(rows)
-    kind, rest = at // (capacity * count), at % (capacity * count)
+    kind, rest = at // (size * count), at % (size * count)
     table = np.zeros((rows, rows), np.float32)
-    table[at, rest // capacity * 2 * capacity + kind * capacity + rest % capacity] = 1.0
+    table[at, rest // size * 2 * size + kind * size + rest % size] = 1.0
     return pl.pallas_call(
         sort_body,
-        out_shape=jax.ShapeDtypeStruct((rows, dim), BF),
+        out_shape=[jax.ShapeDtypeStruct((rows, dim), BF)] * 2,
         compiler_params=params(),
         name="sort_messages",
-    )(jnp.asarray(table, BF), *messages)
-
-
-def pack_body(table_ref, own_a, own_b, prev_ref, next_ref, *outs):
+    )(jnp.asarray(table, BF), messages)
+
+
+def padded(size):
+    return -(-size // 8) * 8
+
+
+def pack_body(spread, *refs):
+    if spread:
+        table_ref, refs = refs[0], refs[1:]
+    own_a, own_b, prev_ref, next_ref, out = refs
     half = own_a.shape[0]
     sums = []
     for own, low in ((own_a, 0), (own_b, half)):
         total = own[...].astype(F32) + prev_ref[low : low + half].astype(F32)
         sums.append((total + next_ref[low : low + half].astype(F32)).astype(BF))
-    rows = jnp.dot(
-        table_ref[...], jnp.concatenate(sums, axis=0), preferred_element_type=F32
-    ).astype(BF)
-    size = outs[0].shape[0]
-    for p, out in enumerate(outs):
-        out[...] = rows[p * size : (p + 1) * size]
-
-
-def pack_returns(own_a, own_b, from_prev, from_next, capacity):
+    rows = jnp.concatenate(sums, axis=0)
+    if spread:
+        rows = jnp.dot(table_ref[...], rows, preferred_element_type=F32).astype(BF)
+    out[...] = rows
+
+
+def pack_returns(own_a, own_b, from_prev, from_next, size):
     rows, dim = from_prev.shape
-    count = rows // capacity
-    size = -(-capacity // 8) * 8
-    table = np.zeros((count * size, rows), np.float32)
+    wide = padded(size)
+    spread = wide != size
+    table = np.zeros((rows // size * wide, rows), np.float32)
     at = np.arange(rows)
-    table[at // capacity * size + at % capacity, at] = 1.0
-    return pl.pallas_call(
-        pack_body,
-        out_shape=[jax.ShapeDtypeStruct((size, dim), BF)] * count,
+    table[at // size * wide + at % size, at] = 1.0
+    head = (jnp.asarray(table, BF),) if spread else ()
+    return pl.pallas_call(
+        functools.partial(pack_body, spread),
+        out_shape=jax.ShapeDtypeStruct((rows // size * wide, dim), BF),
         compiler_params=params(),
         name="pack_returns",
-    )(jnp.asarray(table, BF), own_a, own_b, from_prev, from_next)
+    )(*head, own_a, own_b, from_prev, from_next)
 
 
 def hop_body(next_a, next_b, prev_a, prev_b, got_a, got_b, to_next, to_prev):
@@ -151,14 +164,16 @@
     outs = refs[pieces + 4 : 2 * pieces + 4]
     x_all, dy_all, up_all, grads = refs[2 * pieces + 4 :]
     step = pl.program_id(0)
-    size = outs[0].shape[0]
     width = 2 * up_a.shape[0]
 
     @pl.when(step == 0)
     def _():
-        for i, piece in enumerate(ins):
-            x_all[i * size : (i + 1) * size] = piece[:size]
-            dy_all[i * size : (i + 1) * size] = piece[size:]
+        low = 0
+        for piece, out in zip(ins, outs):
+            size = out.shape[0]
+            x_all[low : low + size] = piece[:size]
+            dy_all[low : low + size] = piece[size:]
+            low += size
 
     @pl.when(step < steps)
     def _():
@@ -177,27 +192,30 @@
         cols = outs[0].shape[1]
         at = pl.ds(pl.multiple_of((step - steps) * cols, cols), cols)
         part = jnp.dot(grad, up_all[:, at], preferred_element_type=F32).astype(BF)
-        for i, out in enumerate(outs):
-            out[...] = part[i * size : (i + 1) * size]
+        low = 0
+        for out in outs:
+            size = out.shape[0]
+            out[...] = part[low : low + size]
+            low += size
 
 
 def expert_rows(ins, weights):
     pieces = len(ins)
-    both, dim = ins[0].shape
-    size = both // 2
-    rows = pieces * size
+    dim = ins[0].shape[1]
+    sizes = [piece.shape[0] // 2 for piece in ins]
+    rows = sum(sizes)
     hidden = weights[0].shape[0]
     steps = hidden // HIDDEN_STEP
     tile = pl.BlockSpec((HIDDEN_STEP, dim), lambda i: (jnp.minimum(i, steps - 1), 0))
     return pl.pallas_call(
         functools.partial(expert_body, pieces, steps),
         grid=(steps + dim // OUT_COLS,),
-        in_specs=[whole(both, dim)] * pieces + [tile] * 4,
+        in_specs=[whole(*piece.shape) for piece in ins] + [tile] * 4,
         out_specs=[
             pl.BlockSpec((size, OUT_COLS), lambda i: (0, jnp.maximum(i - steps, 0)))
-        ]
-        * pieces,
-        out_shape=[jax.ShapeDtypeStruct((size, dim), BF)] * pieces,
+            for size in sizes
+        ],
+        out_shape=[jax.ShapeDtypeStruct((size, dim), BF) for size in sizes],
         scratch_shapes=[
             pltpu.VMEM((rows, dim), BF),
             pltpu.VMEM((rows, dim), BF),
@@ -214,11 +232,10 @@
     )(*ins, *weights)
 
 
-def weigh_pair(ids, order, weights, padded):
+def weigh_pair(ids, weights, experts, capacity):
     tokens = ids.shape[0]
-    experts = order.shape[1]
-    order = jnp.broadcast_to(order, (tokens, experts))
-    hots = [(order == ids[:, k : k + 1]).astype(F32) for k in range(2)]
+    at = lax.broadcasted_iota(jnp.int32, (tokens, experts), 1)
+    hots = [(at == ids[:, k : k + 1]).astype(F32) for k in range(2)]
     before = (
         lax.broadcasted_iota(jnp.int32, (tokens, tokens), 1)
         < lax.broadcasted_iota(jnp.int32, (tokens, tokens), 0)
@@ -226,24 +243,29 @@
     earlier = jnp.dot(
         before.astype(BF), (hots[0] + hots[1]).astype(BF), preferred_element_type=F32
     )
-    base = lax.broadcasted_iota(jnp.int32, (tokens, experts), 1).astype(F32) * padded
-    place = lax.broadcasted_iota(jnp.int32, (tokens, experts * padded), 1)
-    table = jnp.zeros((tokens, experts * padded), F32)
+    sizes = part_sizes(capacity)
+    rows = experts * sum(padded(size) for size in sizes)
+    place = lax.broadcasted_iota(jnp.int32, (tokens, rows), 1)
+    table = jnp.zeros((tokens, rows), F32)
     for k in range(2):
-        target = jnp.sum((earlier + base) * hots[k], axis=1, keepdims=True).astype(jnp.int32)
+        slot = jnp.sum(earlier * hots[k], axis=1, keepdims=True).astype(jnp.int32)
+        own = ids[:, k : k + 1]
+        target = jnp.where(
+            slot < sizes[0],
+            own * padded(sizes[0]) + slot,
+            experts * padded(sizes[0]) + own * padded(sizes[1]) + slot - sizes[0],
+        )
         table = table + jnp.where(place == target, weights[:, k : k + 1], 0.0)
     high = table.astype(BF)
     low = (table - high.astype(F32)).astype(BF)
     return high, low
 
 
-def scan_body(experts, ids_ref, order_ref, weights_ref, *refs):
-    backs = refs[:experts]
-    dout_ref, delta_ref, rate_ref, mix_ref, drive_ref = refs[experts : experts + 5]
-    mid_ref, local_ref, start_ref, grad = refs[experts + 5 :]
-    high, low = weigh_pair(
-        ids_ref[...], order_ref[...], weights_ref[...], backs[0].shape[0]
-    )
+def scan_body(experts, capacity, ids_ref, weights_ref, *refs):
+    backs = refs[:2]
+    dout_ref, delta_ref, rate_ref, mix_ref, drive_ref = refs[2:7]
+    mid_ref, local_ref, start_ref, grad = refs[7:]
+    high, low = weigh_pair(ids_ref[...], weights_ref[...], experts, capacity)
     back = jnp.concatenate([b[...] for b in backs], axis=0)
     routed = jnp.dot(high, back, preferred_element_type=F32)
     routed += jnp.dot(low, back, preferred_element_type=F32)
@@ -279,14 +301,14 @@
     return pl.BlockSpec((rows, cols), lambda i: (0, i))
 
 
-def combine_and_scan(ids, order, weights, backs, dout, delta, rate, mix, drive):
+def combine_and_scan(ids, weights, backs, dout, delta, rate, mix, drive, experts, capacity):
     tokens, dim = dout.shape
     states = rate.shape[0]
     cols = SCAN_COLS
     return pl.pallas_call(
-        functools.partial(scan_body, len(backs)),
+        functools.partial(scan_body, experts, capacity),
         grid=(dim // cols,),
-        in_specs=[whole(*ids.shape), whole(*order.shape), whole(*weights.shape)]
+        in_specs=[whole(*ids.shape), whole(*weights.shape)]
         + [strip(b.shape[0], cols) for b in backs]
         + [
             strip(tokens, cols),
@@ -304,7 +326,7 @@
         scratch_shapes=[pltpu.VMEM((tokens, cols), F32)],
         compiler_params=params(),
         name="combine_and_scan",
-    )(ids, order, weights, *backs, dout, delta, rate, mix, drive)
+    )(ids, weights, *backs, dout, delta, rate, mix, drive)
 
 
 def reach_body(delta_ref, rate_ref, mix_ref, reach_ref, total_ref):
@@ -369,7 +391,7 @@
     tokens, dim = local.shape
     states = rate.shape[0]
     blocks = starts.shape[0]
-    cols = 256
+    cols = SCAN_COLS
     return pl.pallas_call(
         carry_body,
         grid=(dim // cols,),
@@ -389,6 +411,7 @@
 
 
 def on_device(z_size, capacity, x_in, dout, route_ids, combine, w_up, w_down, delta, rate, bmat, cmat):
+    experts = lax.axis_size("exp")
     x, dy, ids, weights = x_in[0], dout[0], route_ids[0], combine[0]
     up, down, steps = w_up[0], w_down[0], delta[0]
 
@@ -399,28 +422,19 @@
     def swap(value):
         return lax.ppermute(value, "core", [(0, 1), (1, 0)])
 
-    def across(value, shift_by, sign):
-        dx, dy_ = shift_by
-        if dx == 0 and dy_ == 0:
-            return value
-        pairs = [
-            (a * SIDE + b, (a + sign * dx) % SIDE * SIDE + (b + sign * dy_) % SIDE)
-            for a in range(SIDE)
-            for b in range(SIDE)
-        ]
-        return lax.ppermute(value, "exp", pairs)
-
-    me = lax.axis_index("exp")
-    dxs, dys = np.array(SHIFTS, np.int32).T
-    order = (me // SIDE + dxs) % SIDE * SIDE + (me % SIDE + dys) % SIDE
-    order = order.astype(jnp.int32)
-
-    sent = gather_rows(ids.T, order[:, None], x, dy, capacity)
-    got = [across(m, s, 1) for m, s in zip(sent, SHIFTS)]
-    quarters = [
-        sort_messages(got[i : i + GROUP], capacity) for i in range(0, len(got), GROUP)
-    ]
-    both = (up, swap(up), down, swap(down))
+    def exchange(value):
+        parts = value.reshape(experts, -1, value.shape[1])
+        got = lax.all_to_all(parts, "exp", split_axis=0, concat_axis=0, tiled=True)
+        return got.reshape(value.shape)
+
+    sizes = part_sizes(capacity)
+    sent = gather_rows(ids.T, x, dy, experts, capacity)
+    up_other, down_other = swap(up), swap(down)
+    got_low = exchange(sent[0])
+    got_low, up_other, down_other = tie(got_low, up_other, down_other)
+    both = (up, up_other, down, down_other)
+    low_a, low_b = sort_messages(got_low, experts, sizes[0])
+    high_a, high_b = sort_messages(exchange(sent[1]), experts, sizes[1])
 
     def ring(a, b):
         prev_a, next_b = shift(a, 1), shift(b, -1)
@@ -430,11 +444,14 @@
     def far(prev_a, next_b):
         return shift(prev_a, 1), shift(next_b, -1)
 
-    low_a, low_b, high_a, high_b = quarters
     low = ring(low_a, low_b)
     low_far = far(low[0], low[3])
+    lanes = (steps.shape[0], bmat.shape[2], 128)
+    mix = jnp.broadcast_to(bmat[0][:, :, None], lanes)
+    drive = jnp.broadcast_to(cmat[0][:, :, None], lanes)
     reach, total = reach_table(steps, rate, bmat[0])
-    low, reach, total = tie(low, reach, total)
+    totals = lax.all_gather(total[0], ("z", "core"))
+    low, reach, totals, mix, drive = tie(low, reach, totals, mix, drive)
     first = expert_rows((low_a, low_b, *low), both)
     high = ring(high_a, high_b)
     low_far, first = tie(low_far, first)
@@ -442,26 +459,23 @@
     high, second = tie(high, second)
     high_far = far(high[0], high[3])
     third = expert_rows(high, both)
-    high_far, third = tie(high_far, third)
+    low_sums = hop_sums(*first[4:6], *first[2:4], shift(second[0], 1), shift(second[1], -1))
+    high_far, third, low_sums = tie(high_far, third, low_sums)
     fourth = expert_rows(high_far, both)
 
-    def back_home(own, prev, next_, far_a, far_b):
-        got_a, got_b = shift(far_a, 1), shift(far_b, -1)
-        to_next, to_prev = hop_sums(*next_, *prev, got_a, got_b)
-        return pack_returns(*own, shift(to_next, 1), shift(to_prev, -1), capacity)
-
-    backs = [
-        *back_home(first[:2], first[2:4], first[4:6], *second[:2]),
-        *back_home(second[2:4], third[:2], third[2:4], *fourth),
-    ]
-    backs = [across(m, s, -1) for m, s in zip(backs, SHIFTS)]
-
-    lanes = (steps.shape[0], bmat.shape[2], 128)
-    mix = jnp.broadcast_to(bmat[0][:, :, None], lanes)
-    drive = jnp.broadcast_to(cmat[0][:, :, None], lanes)
-    totals = lax.all_gather(total[0], ("z", "core"))
+    def home(own, sums, size):
+        to_next, to_prev = sums
+        return pack_returns(*own, shift(to_next, 1), shift(to_prev, -1), size)
+
+    low_home = home(first[:2], low_sums, sizes[0])
+    high_got = (shift(fourth[0], 1), shift(fourth[1], -1))
+    low_home, high_got = tie(low_home, high_got)
+    low_back = exchange(low_home)
+    high_sums = hop_sums(*third[2:4], *third[:2], *high_got)
+    backs = (low_back, exchange(home(second[2:4], high_sums, sizes[1])))
+
     mid, local, start = combine_and_scan(
-        ids, order[None, :], weights, backs, dy, steps, rate, mix, drive
+        ids, weights, backs, dy, steps, rate, mix, drive, experts, capacity
     )
     starts = lax.all_gather(start, ("z", "core"))
     place = lax.axis_index(("z", "core")).astype(jnp.int32).reshape(1)

time: 300 us -> 280 us (0.933)
  blocking collectives: 38.4 us -> 81.5 us
  starting transfers between devices: 83.2 us -> 47 us
  waiting for transfers between devices: 50.1 us -> 30.7 us
  Pallas kernels: 111 us -> 105 us
    ppermute x30 -> x0, starting transfers between devices: 51.7 us -> none  [across(): return lax.ppermute(value, 'exp', pairs)]
    all_to_all x0 -> x1, blocking collectives: none -> 28.6 us  [exchange(): got = lax.all_to_all(parts, 'exp', split_axis=0, concat_axis=0, tiled=True)]
    ppermute x30 -> x0, waiting for transfers between devices: 19.5 us -> none  [across(): return lax.ppermute(value, 'exp', pairs)]
    all_to_all x0 -> x3, starting transfers between devices: none -> 16.8 us  [exchange(): got = lax.all_to_all(parts, 'exp', split_axis=0, concat_axis=0, tiled=True)]
    all_gather x1, blocking collectives: 24 us -> 32.7 us  [on_device(): totals = lax.all_gather(total[0], ('z', 'core'))]
    all_to_all x0 -> x3, waiting for transfers between devices: none -> 8.2 us  [exchange(): got = lax.all_to_all(parts, 'exp', split_axis=0, concat_axis=0, tiled=True)]
    ppermute x20, waiting for transfers between devices: 30.6 us -> 22.5 us  [shift(): return lax.ppermute(value, 'z', ring)]
    all_gather x1, blocking collectives: 14.4 us -> 20.1 us  [on_device(): starts = lax.all_gather(start, ('z', 'core'))]
  transfers between devices with their start and end apart: 52 -> 25, of which waited for: 13 -> 6; matrix products, arithmetic and copies ran while one was open for 2% -> 2% of each run, Pallas kernels for 31% -> 32%
where the time goes in v3:
time: 280 us; the launch traced here: 279 us
  Pallas kernels  105 us (38%)
  blocking collectives  81.5 us (29%)
  starting transfers between devices  47 us (17%)
  waiting for transfers between devices  30.7 us (11%)
  local copies, waits for them, and re-layouts  13.8 us (5%)
    pallas_call x4, Pallas kernels, expert_rows(): pl.pallas_call(functools.partial(expert_body, pieces, steps), grid=(steps...  61 us
    all_gather x1, blocking collectives, on_device(): totals = lax.all_gather(total[0], ('z', 'core'))  32.7 us
    all_to_all x1, blocking collectives, exchange(): got = lax.all_to_all(parts, 'exp', split_axis=0, concat_axis=0, tiled=True)  28.6 us
    ppermute x20, starting transfers between devices, shift(): return lax.ppermute(value, 'z', ring)  28.6 us
    ppermute x20, waiting for transfers between devices, shift(): return lax.ppermute(value, 'z', ring)  22.5 us
    all_gather x1, blocking collectives, on_device(): starts = lax.all_gather(start, ('z', 'core'))  20.1 us
    all_to_all x3, starting transfers between devices, exchange(): got = lax.all_to_all(parts, 'exp', split_axis=0, concat_axis=0, tiled=True)  16.8 us
    pallas_call x1, Pallas kernels, combine_and_scan(): pl.pallas_call(functools.partial(scan_body, experts, capacity), grid=(dim...  11.2 us
  transfers between devices with their start and end apart: 25, of which 6 were waited for; matrix products, arithmetic and copies ran while one was open for 2% of the time, Pallas kernels for 32%

profile of v3, /device:TPU:1, one launch (start us, length us, event | category | flops | bytes accessed | tf_op | source)
XLA Modules:
  0.0 278.9 jit_solution(16325385385180203808)
XLA Ops:
  0.6 1.5 collective-permute-start
  2.2 0.8 copy.20
  3.7 3.9 %gather_rows.1 = (bf16[384,2048]{1,0:T(8,128)(2,1)}, bf16[256,2048]{1,0:T(8,128)(2,1)}) custom-call(s32[2,128]{1,0:T(2,128)} %copy.22.ids_ref, bf16[128,2048]{1,0:T(8,128)(2,1)} %bitcast.52, bf16[128,2048]{1,0:T(8,128)(2,1)} %bitcast.42), custom_call_target="tpu_custom_call" | custom-call | tf_op jit(solution)/shard_map/gather_rows/pallas_call | solution.py:75
  7.5 28.6 %all_to_all.20 = bf16[16,24,2048]{2,1,0:T(8,128)(2,1)} all-to-all(bf16[16,24,2048]{2,1,0:T(8,128)(2,1)} %bitcast.46), channel_id=1, replica_groups=mesh['z'=4,'core'=2,'exp'=16] {'exp'}, dimensions={0} | all-to-all | bytes 3145728 | tf_op jit(solution)/shard_map/all_to_all | solution.py:427
  36.2 3.8 %all-to-all-start.1 = ((bf16[16,16,2048]{2,1,0:T(8,128)(2,1)}), bf16[16,16,2048]{2,1,0:T(8,128)(2,1)S(1)}, u32[]{:S(2)}, u32[]{:S(2)}) async-start(bf16[16,16,2048]{2,1,0:T(8,128)(2,1)} %bitcast.47), calls=%async_computation.1 | async-start | bytes 2097152 | tf_op jit(solution)/shard_map/all_to_all | solution.py:427
  40.0 3.0 %sort_messages.2 = (bf16[192,2048]{1,0:T(8,128)(2,1)}, bf16[192,2048]{1,0:T(8,128)(2,1)}) custom-call(bf16[192,192]{1,0:T(8,128)(2,1)} %constant.20.clone.table_ref, bf16[384,2048]{1,0:T(8,128)(2,1)} %bitcast.27), custom_call_target="tpu_custom_call" | custom-call | tf_op jit(solution)/shard_map/sort_messages/pallas_call | solution.py:100
  43.0 1.6 collective-permute-start.2
  44.6 2.2 collective-permute-start.4
  46.8 2.7 collective-permute-start.7
  50.2 7.0 %reach_table.1 = (bf16[16,128,2048]{2,1,0:T(8,128)(2,1)}, f32[1,2048]{1,0:T(1,128)}) custom-call(f32[128,2048]{1,0:T(8,128)} %bitcast.48, f32[16,2048]{1,0:T(8,128)} %rate_ref.3, f32[128,16]{1,0:T(8,128)} %bitcast.56), custom_call_target="tpu_custom_call" | custom-call | flops 33554432 | bytes 8388608 | tf_op jit(solution)/shard_map/reach_table/pallas_call | solution.py:353
  57.2 32.7 %all-gather.1 = f32[8,1,2048]{2,1,0:T(1,128)S(1)} all-gather(f32[1,1,2048]{2,1,0:T(1,128)} %bitcast.59), channel_id=1, replica_groups=mesh['z'=4,'core'=2,'exp'=16] {'z','core'}, dimensions={0}, use_global_device_ids=true | all-gather | bytes 73728 | tf_op jit(solution)/shard_map/all_gather | solution.py:453
  90.7 1.0 copy-done
  91.6 2.5 sort_messages.3
  94.1 2.5 collective-permute-start.10
  96.6 2.7 collective-permute-start.11
  99.3 1.3 broadcast_in_dim.18.refs_5_
  100.6 1.4 broadcast_in_dim.20.refs_6_
  102.0 2.7 collective-permute-start.5
  104.7 20.1 %expert_rows.4 = (bf16[96,2048]{1,0:T(8,128)(2,1)}, bf16[96,2048]{1,0:T(8,128)(2,1)}, bf16[96,2048]{1,0:T(8,128)(2,1)}, bf16[96,2048]{1,0:T(8,128)(2,1)}, bf16[9...) custom-call(bf16[192,2048]{1,0:T(8,128)(2,1)} %get-tuple-element.73.refs_0_, bf16[192,2048]{1,0:T(8,128)(2,1)} %get-tuple-element.74.refs_1_, ...), custom_call_target="tpu_custom_call" | custom-call | flops 12683575296 | bytes 21757952 | tf_op jit(solution)/shard_map/expert_rows/pallas_call | solution.py:210
  124.8 3.1 %collective-permute-done.3.refs_0_ = bf16[192,2048]{1,0:T(8,128)(2,1)S(1)} collective-permute-done((bf16[192,2048]{1,0:T(8,128)(2,1)S(1)}, bf16[192,2048]{1,0:T(8,128)(2,1)S(1)}, u32[]{:S(2)}, u32[]{:S(2)}) %collective-permute-start.3) | collective-permute-done | bytes 786464 | tf_op jit(solution)/shard_map/ppermute | solution.py:420
  127.9 8.1 %collective-permute-done.5.refs_1_ = bf16[192,2048]{1,0:T(8,128)(2,1)S(1)} collective-permute-done((bf16[192,2048]{1,0:T(8,128)(2,1)S(1)}, bf16[192,2048]{1,0:T(8,128)(2,1)S(1)}, u32[]{:S(2)}, u32[]{:S(2)}) %collective-permute-start.5) | collective-permute-done | bytes 786464 | tf_op jit(solution)/shard_map/ppermute | solution.py:420
  136.0 0.9 copy-done.22
  136.9 14.8 %expert_rows.5 = (bf16[96,2048]{1,0:T(8,128)(2,1)}, bf16[96,2048]{1,0:T(8,128)(2,1)}, bf16[64,2048]{1,0:T(8,128)(2,1)}, bf16[64,2048]{1,0:T(8,128)(2,1)}) custom-call(bf16[192,2048]{1,0:T(8,128)(2,1)} %copy-done.21, bf16[192,2048]{1,0:T(8,128)(2,1)} %copy-done.22, bf16[128,2048]{1,0:T(8,128)(2,1)} %get-tuple-element.92.refs_2_, ...), custom_call_target="tpu_custom_call" | custom-call | flops 7046430720 | bytes 18612224 | tf_op jit(solution)/shard_map/expert_rows/pallas_call | solution.py:210
  151.8 1.1 collective-permute-start.14
  152.9 2.5 collective-permute-start.15
  155.4 2.7 collective-permute-start.13
  158.1 13.6 %expert_rows.6 = (bf16[64,2048]{1,0:T(8,128)(2,1)}, bf16[64,2048]{1,0:T(8,128)(2,1)}, bf16[64,2048]{1,0:T(8,128)(2,1)}, bf16[64,2048]{1,0:T(8,128)(2,1)}) custom-call(bf16[128,2048]{1,0:T(8,128)(2,1)} %copy-done.23, bf16[128,2048]{1,0:T(8,128)(2,1)} %copy-done.27, bf16[128,2048]{1,0:T(8,128)(2,1)} %copy-done.25, bf16[128,2048]{1,0:T(8,128)(2,1)} %copy-done.24, ...), custom_call_target="tpu_custom_call" | custom-call | flops 5637144576 | bytes 17825792 | tf_op jit(solution)/shard_map/expert_rows/pallas_call | solution.py:210
  173.2 2.9 %hop_sums.2 = (bf16[192,2048]{1,0:T(8,128)(2,1)}, bf16[192,2048]{1,0:T(8,128)(2,1)}) custom-call(bf16[96,2048]{1,0:T(8,128)(2,1)} %get-tuple-element.108.next_a, bf16[96,2048]{1,0:T(8,128)(2,1)} %get-tuple-element.109.next_b, bf16[96,2048]{1,0:T(8,128)(2,1)} %get-tuple-element.110.prev_a, bf16[96,2048]{1,0:T(8,128)(2,1)} %get-tuple-element.111.prev_b, ...), custom_call_target="tpu_custom_call" | custom-call | tf_op jit(solution)/shard_map/hop_sums/pallas_call | solution.py:153
  176.1 2.7 collective-permute-start.17
  178.8 12.5 %expert_rows.7 = (bf16[64,2048]{1,0:T(8,128)(2,1)}, bf16[64,2048]{1,0:T(8,128)(2,1)}) custom-call(bf16[128,2048]{1,0:T(8,128)(2,1)} %copy-done.6, bf16[128,2048]{1,0:T(8,128)(2,1)} %copy-done.7, bf16[896,2048]{1,0:T(8,128)(2,1)} %bitcast.35, bf16[896,2048]{1,0:T(8,128)(2,1)} %collective-permute-done.refs_7_.refs_5_.refs_3_, bf16[896,2048]{1,0:T(8,128)(2,1)} %bitcast.40, ...), custom_call_target="tpu_custom_call" | custom-call | flops 2818572288 | bytes 16252928 | tf_op jit(solution)/shard_map/expert_rows/pallas_call | solution.py:210
  191.3 2.7 collective-permute-start.19
  194.7 0.9 copy-done.3
  195.6 0.9 copy-done.4
  196.5 3.1 %pack_returns.2 = bf16[256,2048]{1,0:T(8,128)(2,1)} custom-call(bf16[256,192]{1,0:T(8,128)(2,1)} %constant.22.clone.refs_0_, bf16[96,2048]{1,0:T(8,128)(2,1)} %get-tuple-element.89.refs_1_, bf16[96,2048]{1,0:T(8,128)(2,1)} %get-tuple-element.90.refs_2_, bf16[192,2048]{1,0:T(8,128)(2,1)} %copy-done.3, bf16[192,2048]{1,0:T(8,128)(2,1)} %copy-done.4), custom_call_target="tpu_custom_call" | custom-call | tf_op jit(solution)/shard_map/pack_returns/pallas_call | solution.py:135
  199.6 1.5 collective-permute-done.18.got_a
  201.1 6.6 %all-to-all-start.2 = ((bf16[16,16,2048]{2,1,0:T(8,128)(2,1)}), bf16[16,16,2048]{2,1,0:T(8,128)(2,1)S(1)}, u32[]{:S(2)}, u32[]{:S(2)}) async-start(bf16[16,16,2048]{2,1,0:T(8,128)(2,1)} %bitcast.28), calls=%async_computation.2 | async-start | bytes 2097152 | tf_op jit(solution)/shard_map/all_to_all | solution.py:427
  207.8 2.4 hop_sums.3
  210.2 2.7 collective-permute-start.21
  212.8 8.9 %collective-permute-done.20.refs_2_ = bf16[128,2048]{1,0:T(8,128)(2,1)S(1)} collective-permute-done((bf16[128,2048]{1,0:T(8,128)(2,1)}, bf16[128,2048]{1,0:T(8,128)(2,1)S(1)}, u32[]{:S(2)}, u32[]{:S(2)}) %collective-permute-start.20) | collective-permute-done | bytes 524320 | tf_op jit(solution)/shard_map/ppermute | solution.py:420
  221.8 0.8 copy-done.8
  222.6 0.8 copy-done.9
  223.3 2.3 pack_returns.3
  225.7 6.4 %all-to-all-start.3 = ((bf16[16,8,2048]{2,1,0:T(8,128)(2,1)}), bf16[16,8,2048]{2,1,0:T(8,128)(2,1)S(1)}, u32[]{:S(2)}, u32[]{:S(2)}) async-start(bf16[16,8,2048]{2,1,0:T(8,128)(2,1)} %bitcast.41), calls=%async_computation.3 | async-start | bytes 1048576 | tf_op jit(solution)/shard_map/all_to_all | solution.py:427
  232.8 8.2 %all-to-all-done.3 = bf16[16,8,2048]{2,1,0:T(8,128)(2,1)S(1)} async-done(((bf16[16,8,2048]{2,1,0:T(8,128)(2,1)}), bf16[16,8,2048]{2,1,0:T(8,128)(2,1)S(1)}, u32[]{:S(2)}, u32[]{:S(2)}) %all-to-all-start.3) | async-done | bytes 524320 | tf_op jit(solution)/shard_map/all_to_all | solution.py:427
  241.0 0.8 copy-done.2
  241.8 11.2 %combine_and_scan.1 = (bf16[128,2048]{1,0:T(8,128)(2,1)}, f32[128,2048]{1,0:T(8,128)}, bf16[16,2048]{1,0:T(8,128)(2,1)}) custom-call(s32[128,2]{1,0:T(8,128)} %bitcast.51, f32[128,2]{1,0:T(8,128)} %bitcast.55, bf16[256,2048]{1,0:T(8,128)(2,1)} %bitcast.30, bf16[128,2048]{1,0:T(8,128)(2,1)} %bitcast.44, bf16[128,2048]{1,0:T(8,128)(2,1)} %bitcast.43, ...), custom_call_target="tpu_custom_call" | custom-call | tf_op jit(solution)/shard_map/combine_and_scan/pallas_call | solution.py:308
  253.0 20.1 %all-gather = bf16[128,2048]{1,0:T(8,128)(2,1)} all-gather(bf16[16,2048]{1,0:T(8,128)(2,1)} %get-tuple-element.136), channel_id=2, replica_groups=mesh['z'=4,'core'=2,'exp'=16] {'z','core'}, dimensions={0}, use_global_device_ids=true | all-gather | bytes 589824 | tf_op jit(solution)/shard_map/all_gather | solution.py:480
  273.1 5.7 %add_carry.1 = bf16[128,2048]{1,0:T(8,128)(2,1)} custom-call(s32[1]{0:T(128)} %bitcast.20.place_ref, bf16[8,16,2048]{2,1,0:T(8,128)(2,1)} %bitcast.45, f32[8,2048]{1,0:T(8,128)} %bitcast.54, f32[16,2048]{1,0:T(8,128)} %rate_ref.3, f32[128,2048]{1,0:T(8,128)} %get-tuple-element.138.local_ref, bf16[16,128,2048]{2,1,0:T(8,128)(2,1)} %get-tuple-element.139.reach_ref), custom_call_target="tpu_custom_call" | custom-call | tf_op jit(solution)/shard_map/add_carry/pallas_call | solution.py:395
  (83 shorter events, 5.4 us)
Async XLA Ops:
  0.6 39.4 %collective-permute-start = (bf16[896,2048]{1,0:T(8,128)(2,1)}, bf16[896,2048]{1,0:T(8,128)(2,1)}, u32[]{:S(2)}, u32[]{:S(2)}) collective-permute-start(bf16[896,2048]{1,0:T(8,128)(2,1)} %bitcast.31), channel_id=1, source_target_pairs={{0,16},{16,0},{1,17},{17,1},{2,18},{18,2},{3,19},{19,3},{4,20},{20... | collective-permute-start | bytes 11010056 | tf_op jit(solution)/shard_map/ppermute | solution.py:423
  2.1 37.9 %collective-permute-start.1 = (bf16[896,2048]{1,0:T(8,128)(2,1)}, bf16[896,2048]{1,0:T(8,128)(2,1)}, u32[]{:S(2)}, u32[]{:S(2)}) collective-permute-start(bf16[896,2048]{1,0:T(8,128)(2,1)} %bitcast.36), channel_id=1, source_target_pairs={{0,16},{16,0},{1,17},{17,1},{2,18},{18,2},{3,19},{19,3},{4,20},{20... | collective-permute-start | bytes 11010056 | tf_op jit(solution)/shard_map/ppermute | solution.py:423
  3.0 40.0 %copy-start.5 = (s32[1,128,2]{2,1,0:T(8,128)}, s32[1,128,2]{2,1,0:T(8,128)S(1)}, u32[]{:S(2)}) copy-start(s32[1,128,2]{2,1,0:T(8,128)S(1)} %copy.20) | copy-start | bytes 3076
  7.5 41.9 %copy-start.15 = (f32[1,128,16]{1,2,0:T(8,128)S(1)}, f32[1,128,16]{1,2,0:T(8,128)}, u32[]{:S(2)}) copy-start(f32[1,128,16]{1,2,0:T(8,128)} %param.21) | copy-start | bytes 24580
  36.2 54.5 %all-to-all-start.1 = ((bf16[16,16,2048]{2,1,0:T(8,128)(2,1)}), bf16[16,16,2048]{2,1,0:T(8,128)(2,1)S(1)}, u32[]{:S(2)}, u32[]{:S(2)}) async-start(bf16[16,16,2048]{2,1,0:T(8,128)(2,1)} %bitcast.47), calls=%async_computation.1 | async-start | bytes 2097152 | tf_op jit(solution)/shard_map/all_to_all | solution.py:427
  43.0 53.6 %collective-permute-start.2 = (bf16[192,2048]{1,0:T(8,128)(2,1)}, bf16[192,2048]{1,0:T(8,128)(2,1)S(1)}, u32[]{:S(2)}, u32[]{:S(2)}) collective-permute-start(bf16[192,2048]{1,0:T(8,128)(2,1)} %get-tuple-element.73.refs_0_), channel_id=1, source_target_pairs={{0,32},{32,64},{64,96},{96,0},{1,33},{33,65},{65,97},{97,1},{2,34}... | collective-permute-start | bytes 2359304 | tf_op jit(solution)/shard_map/ppermute | solution.py:420
  44.6 52.0 %collective-permute-start.4 = (bf16[192,2048]{1,0:T(8,128)(2,1)}, bf16[192,2048]{1,0:T(8,128)(2,1)S(1)}, u32[]{:S(2)}, u32[]{:S(2)}) collective-permute-start(bf16[192,2048]{1,0:T(8,128)(2,1)} %get-tuple-element.74.refs_1_), channel_id=1, source_target_pairs={{0,96},{32,0},{64,32},{96,64},{1,97},{33,1},{65,33},{97,65},{2,98}... | collective-permute-start | bytes 2359304 | tf_op jit(solution)/shard_map/ppermute | solution.py:420
  46.8 52.5 %collective-permute-start.6 = (bf16[192,2048]{1,0:T(8,128)(2,1)}, bf16[192,2048]{1,0:T(8,128)(2,1)S(1)}, u32[]{:S(2)}, u32[]{:S(2)}) collective-permute-start(bf16[192,2048]{1,0:T(8,128)(2,1)} %get-tuple-element.74.refs_1_), channel_id=1, source_target_pairs={{0,32},{32,64},{64,96},{96,0},{1,33},{33,65},{65,97},{97,1},{2,34}... | collective-permute-start | bytes 2359304 | tf_op jit(solution)/shard_map/ppermute | solution.py:420
  46.8 52.5 %collective-permute-start.7 = (bf16[192,2048]{1,0:T(8,128)(2,1)}, bf16[192,2048]{1,0:T(8,128)(2,1)}, u32[]{:S(2)}, u32[]{:S(2)}) collective-permute-start(bf16[192,2048]{1,0:T(8,128)(2,1)} %get-tuple-element.73.refs_0_), channel_id=1, source_target_pairs={{0,96},{32,0},{64,32},{96,64},{1,97},{33,1},{65,33},{97,65},{2,98}... | collective-permute-start | bytes 2359304 | tf_op jit(solution)/shard_map/ppermute | solution.py:420
  50.2 40.3 %copy-start.16 = (f32[1,128,16]{1,2,0:T(8,128)S(1)}, f32[1,128,16]{1,2,0:T(8,128)}, u32[]{:S(2)}) copy-start(f32[1,128,16]{1,2,0:T(8,128)} %param.22) | copy-start | bytes 24580
  50.2 49.1 %copy-start.12 = (f32[1,128,16]{2,1,0:T(8,128)S(1)}, f32[1,128,16]{2,1,0:T(8,128)}, u32[]{:S(2)}) copy-start(f32[1,128,16]{2,1,0:T(8,128)} %copy.23) | copy-start | bytes 24580
  90.6 1.0 copy-start
  94.1 57.6 %collective-permute-start.10 = (bf16[128,2048]{1,0:T(8,128)(2,1)}, bf16[128,2048]{1,0:T(8,128)(2,1)S(1)}, u32[]{:S(2)}, u32[]{:S(2)}) collective-permute-start(bf16[128,2048]{1,0:T(8,128)(2,1)} %get-tuple-element.92.refs_2_), channel_id=1, source_target_pairs={{0,96},{32,0},{64,32},{96,64},{1,97},{33,1},{65,33},{97,65},{2,98}... | collective-permute-start | bytes 1572872 | tf_op jit(solution)/shard_map/ppermute | solution.py:420
  96.6 8.1 %copy-start.19 = (bf16[192,2048]{1,0:T(8,128)(2,1)}, bf16[192,2048]{1,0:T(8,128)(2,1)S(1)}, u32[]{:S(2)}) copy-start(bf16[192,2048]{1,0:T(8,128)(2,1)S(1)} %collective-permute-done.2.refs_2_) | copy-start | bytes 2359300
  96.6 55.2 %collective-permute-start.8 = (bf16[128,2048]{1,0:T(8,128)(2,1)}, bf16[128,2048]{1,0:T(8,128)(2,1)S(1)}, u32[]{:S(2)}, u32[]{:S(2)}) collective-permute-start(bf16[128,2048]{1,0:T(8,128)(2,1)} %get-tuple-element.92.refs_2_), channel_id=1, source_target_pairs={{0,32},{32,64},{64,96},{96,0},{1,33},{33,65},{65,97},{97,1},{2,34}... | collective-permute-start | bytes 1572872 | tf_op jit(solution)/shard_map/ppermute | solution.py:420
  96.6 8.0 %copy-start.18 = (bf16[192,2048]{1,0:T(8,128)(2,1)}, bf16[192,2048]{1,0:T(8,128)(2,1)S(1)}, u32[]{:S(2)}) copy-start(bf16[192,2048]{1,0:T(8,128)(2,1)S(1)} %collective-permute-done.4.refs_5_) | copy-start | bytes 2359300
  96.6 55.1 %collective-permute-start.11 = (bf16[128,2048]{1,0:T(8,128)(2,1)}, bf16[128,2048]{1,0:T(8,128)(2,1)S(1)}, u32[]{:S(2)}, u32[]{:S(2)}) collective-permute-start(bf16[128,2048]{1,0:T(8,128)(2,1)} %get-tuple-element.93.refs_3_), channel_id=1, source_target_pairs={{0,96},{32,0},{64,32},{96,64},{1,97},{33,1},{65,33},{97,65},{2,98}... | collective-permute-start | bytes 1572872 | tf_op jit(solution)/shard_map/ppermute | solution.py:420
  99.3 5.4 %copy-start.20 = (bf16[192,2048]{1,0:T(8,128)(2,1)}, bf16[192,2048]{1,0:T(8,128)(2,1)S(1)}, u32[]{:S(2)}) copy-start(bf16[192,2048]{1,0:T(8,128)(2,1)S(1)} %collective-permute-done.6.refs_3_) | copy-start | bytes 2359300
  102.0 25.9 %copy-start.26 = (bf16[128,2048]{1,0:T(8,128)(2,1)S(1)}, bf16[128,2048]{1,0:T(8,128)(2,1)}, u32[]{:S(2)}) copy-start(bf16[128,2048]{1,0:T(8,128)(2,1)} %get-tuple-element.93.refs_3_) | copy-start | bytes 1572868
  102.0 25.9 %collective-permute-start.3 = (bf16[192,2048]{1,0:T(8,128)(2,1)S(1)}, bf16[192,2048]{1,0:T(8,128)(2,1)S(1)}, u32[]{:S(2)}, u32[]{:S(2)}) collective-permute-start(bf16[192,2048]{1,0:T(8,128)(2,1)S(1)} %collective-permute-done.2.refs_2_), channel_id=1, source_target_pairs={{0,32},{32,64},{64,96},{96,0},{1,33},{33,65},{65,97},{97,1},{2,34}... | collective-permute-start | bytes 2359304 | tf_op jit(solution)/shard_map/ppermute | solution.py:420
  102.0 34.1 %collective-permute-start.5 = (bf16[192,2048]{1,0:T(8,128)(2,1)S(1)}, bf16[192,2048]{1,0:T(8,128)(2,1)S(1)}, u32[]{:S(2)}, u32[]{:S(2)}) collective-permute-start(bf16[192,2048]{1,0:T(8,128)(2,1)S(1)} %collective-permute-done.4.refs_5_), channel_id=1, source_target_pairs={{0,96},{32,0},{64,32},{96,64},{1,97},{33,1},{65,33},{97,65},{2,98}... | collective-permute-start | bytes 2359304 | tf_op jit(solution)/shard_map/ppermute | solution.py:420
  127.9 8.1 %copy-start.21 = (bf16[192,2048]{1,0:T(8,128)(2,1)}, bf16[192,2048]{1,0:T(8,128)(2,1)S(1)}, u32[]{:S(2)}) copy-start(bf16[192,2048]{1,0:T(8,128)(2,1)S(1)} %collective-permute-done.3.refs_0_) | copy-start | bytes 2359300
  127.9 23.9 %collective-permute-start.9 = (bf16[128,2048]{1,0:T(8,128)(2,1)S(1)}, bf16[128,2048]{1,0:T(8,128)(2,1)S(1)}, u32[]{:S(2)}, u32[]{:S(2)}) collective-permute-start(bf16[128,2048]{1,0:T(8,128)(2,1)S(1)} %copy-done.26), channel_id=1, source_target_pairs={{0,32},{32,64},{64,96},{96,0},{1,33},{33,65},{65,97},{97,1},{2,34}... | collective-permute-start | bytes 1572872 | tf_op jit(solution)/shard_map/ppermute | solution.py:420
  136.0 0.9 copy-start.22
  151.7 6.3 %copy-start.25 = (bf16[128,2048]{1,0:T(8,128)(2,1)}, bf16[128,2048]{1,0:T(8,128)(2,1)S(1)}, u32[]{:S(2)}) copy-start(bf16[128,2048]{1,0:T(8,128)(2,1)S(1)} %collective-permute-done.10.refs_2_) | copy-start | bytes 1572868
  151.8 6.3 %copy-start.24 = (bf16[128,2048]{1,0:T(8,128)(2,1)}, bf16[128,2048]{1,0:T(8,128)(2,1)S(1)}, u32[]{:S(2)}) copy-start(bf16[128,2048]{1,0:T(8,128)(2,1)S(1)} %collective-permute-done.11.refs_3_) | copy-start | bytes 1572868
  151.8 6.3 %copy-start.23 = (bf16[128,2048]{1,0:T(8,128)(2,1)}, bf16[128,2048]{1,0:T(8,128)(2,1)S(1)}, u32[]{:S(2)}) copy-start(bf16[128,2048]{1,0:T(8,128)(2,1)S(1)} %collective-permute-done.8.refs_0_) | copy-start | bytes 1572868
  151.8 6.3 %copy-start.27 = (bf16[128,2048]{1,0:T(8,128)(2,1)}, bf16[128,2048]{1,0:T(8,128)(2,1)S(1)}, u32[]{:S(2)}) copy-start(bf16[128,2048]{1,0:T(8,128)(2,1)S(1)} %collective-permute-done.9.refs_1_) | copy-start | bytes 1572868
  151.8 19.9 %collective-permute-start.14 = (bf16[96,2048]{1,0:T(8,128)(2,1)}, bf16[96,2048]{1,0:T(8,128)(2,1)S(1)}, u32[]{:S(2)}, u32[]{:S(2)}) collective-permute-start(bf16[96,2048]{1,0:T(8,128)(2,1)} %get-tuple-element.112), channel_id=1, source_target_pairs={{0,32},{32,64},{64,96},{96,0},{1,33},{33,65},{65,97},{97,1},{2,34}... | collective-permute-start | bytes 1179656 | tf_op jit(solution)/shard_map/ppermute | solution.py:420
  152.9 18.8 %collective-permute-start.15 = (bf16[96,2048]{1,0:T(8,128)(2,1)}, bf16[96,2048]{1,0:T(8,128)(2,1)S(1)}, u32[]{:S(2)}, u32[]{:S(2)}) collective-permute-start(bf16[96,2048]{1,0:T(8,128)(2,1)} %get-tuple-element.113), channel_id=1, source_target_pairs={{0,96},{32,0},{64,32},{96,64},{1,97},{33,1},{65,33},{97,65},{2,98}... | collective-permute-start | bytes 1179656 | tf_op jit(solution)/shard_map/ppermute | solution.py:420
  155.4 20.7 %collective-permute-start.12 = (bf16[128,2048]{1,0:T(8,128)(2,1)S(1)}, bf16[128,2048]{1,0:T(8,128)(2,1)S(1)}, u32[]{:S(2)}, u32[]{:S(2)}) collective-permute-start(bf16[128,2048]{1,0:T(8,128)(2,1)S(1)} %collective-permute-done.8.refs_0_), channel_id=1, source_target_pairs={{0,32},{32,64},{64,96},{96,0},{1,33},{33,65},{65,97},{97,1},{2,34}... | collective-permute-start | bytes 1572872 | tf_op jit(solution)/shard_map/ppermute | solution.py:420
  155.4 20.7 %collective-permute-start.13 = (bf16[128,2048]{1,0:T(8,128)(2,1)S(1)}, bf16[128,2048]{1,0:T(8,128)(2,1)S(1)}, u32[]{:S(2)}, u32[]{:S(2)}) collective-permute-start(bf16[128,2048]{1,0:T(8,128)(2,1)S(1)} %collective-permute-done.11.refs_3_), channel_id=1, source_target_pairs={{0,96},{32,0},{64,32},{96,64},{1,97},{33,1},{65,33},{97,65},{2,98}... | collective-permute-start | bytes 1572872 | tf_op jit(solution)/shard_map/ppermute | solution.py:420
  176.0 2.8 copy-start.6
  176.0 2.8 copy-start.7
  176.0 18.7 %collective-permute-start.16 = (bf16[192,2048]{1,0:T(8,128)(2,1)}, bf16[192,2048]{1,0:T(8,128)(2,1)S(1)}, u32[]{:S(2)}, u32[]{:S(2)}) collective-permute-start(bf16[192,2048]{1,0:T(8,128)(2,1)} %get-tuple-element.116), channel_id=1, source_target_pairs={{0,32},{32,64},{64,96},{96,0},{1,33},{33,65},{65,97},{97,1},{2,34}... | collective-permute-start | bytes 2359304 | tf_op jit(solution)/shard_map/ppermute | solution.py:420
  176.1 18.6 %collective-permute-start.17 = (bf16[192,2048]{1,0:T(8,128)(2,1)}, bf16[192,2048]{1,0:T(8,128)(2,1)S(1)}, u32[]{:S(2)}, u32[]{:S(2)}) collective-permute-start(bf16[192,2048]{1,0:T(8,128)(2,1)} %get-tuple-element.117), channel_id=1, source_target_pairs={{0,96},{32,0},{64,32},{96,64},{1,97},{33,1},{65,33},{97,65},{2,98}... | collective-permute-start | bytes 2359304 | tf_op jit(solution)/shard_map/ppermute | solution.py:420
  191.3 9.8 %collective-permute-start.18 = (bf16[64,2048]{1,0:T(8,128)(2,1)}, bf16[64,2048]{1,0:T(8,128)(2,1)S(1)}, u32[]{:S(2)}, u32[]{:S(2)}) collective-permute-start(bf16[64,2048]{1,0:T(8,128)(2,1)} %get-tuple-element.120), channel_id=1, source_target_pairs={{0,32},{32,64},{64,96},{96,0},{1,33},{33,65},{65,97},{97,1},{2,34}... | collective-permute-start | bytes 786440 | tf_op jit(solution)/shard_map/ppermute | solution.py:420
  191.3 9.8 %collective-permute-start.19 = (bf16[64,2048]{1,0:T(8,128)(2,1)}, bf16[64,2048]{1,0:T(8,128)(2,1)S(1)}, u32[]{:S(2)}, u32[]{:S(2)}) collective-permute-start(bf16[64,2048]{1,0:T(8,128)(2,1)} %get-tuple-element.121), channel_id=1, source_target_pairs={{0,96},{32,0},{64,32},{96,64},{1,97},{33,1},{65,33},{97,65},{2,98}... | collective-permute-start | bytes 786440 | tf_op jit(solution)/shard_map/ppermute | solution.py:420
  194.7 0.9 copy-start.3
  195.6 0.9 copy-start.4
  199.6 32.5 %copy-start.17 = (f32[1,128,2]{1,2,0:T(2,128)S(1)}, f32[1,128,2]{1,2,0:T(2,128)}, u32[]{:S(2)}) copy-start(f32[1,128,2]{1,2,0:T(2,128)} %param.16) | copy-start | bytes 3076
  201.1 6.7 %copy-start.13 = (bf16[64,2048]{1,0:T(8,128)(2,1)}, bf16[64,2048]{1,0:T(8,128)(2,1)S(1)}, u32[]{:S(2)}) copy-start(bf16[64,2048]{1,0:T(8,128)(2,1)S(1)} %collective-permute-done.18.got_a) | copy-start | bytes 786436
  201.1 6.7 %copy-start.14 = (bf16[64,2048]{1,0:T(8,128)(2,1)}, bf16[64,2048]{1,0:T(8,128)(2,1)S(1)}, u32[]{:S(2)}) copy-start(bf16[64,2048]{1,0:T(8,128)(2,1)S(1)} %collective-permute-done.19.got_b) | copy-start | bytes 786436
  201.1 24.6 %all-to-all-start.2 = ((bf16[16,16,2048]{2,1,0:T(8,128)(2,1)}), bf16[16,16,2048]{2,1,0:T(8,128)(2,1)S(1)}, u32[]{:S(2)}, u32[]{:S(2)}) async-start(bf16[16,16,2048]{2,1,0:T(8,128)(2,1)} %bitcast.28), calls=%async_computation.2 | async-start | bytes 2097152 | tf_op jit(solution)/shard_map/all_to_all | solution.py:427
  210.2 11.6 %collective-permute-start.20 = (bf16[128,2048]{1,0:T(8,128)(2,1)}, bf16[128,2048]{1,0:T(8,128)(2,1)S(1)}, u32[]{:S(2)}, u32[]{:S(2)}) collective-permute-start(bf16[128,2048]{1,0:T(8,128)(2,1)} %get-tuple-element.131), channel_id=1, source_target_pairs={{0,32},{32,64},{64,96},{96,0},{1,33},{33,65},{65,97},{97,1},{2,34}... | collective-permute-start | bytes 1572872 | tf_op jit(solution)/shard_map/ppermute | solution.py:420
  210.2 11.6 %collective-permute-start.21 = (bf16[128,2048]{1,0:T(8,128)(2,1)}, bf16[128,2048]{1,0:T(8,128)(2,1)S(1)}, u32[]{:S(2)}, u32[]{:S(2)}) collective-permute-start(bf16[128,2048]{1,0:T(8,128)(2,1)} %get-tuple-element.132), channel_id=1, source_target_pairs={{0,96},{32,0},{64,32},{96,64},{1,97},{33,1},{65,33},{97,65},{2,98}... | collective-permute-start | bytes 1572872 | tf_op jit(solution)/shard_map/ppermute | solution.py:420
  225.7 15.3 %copy-start.1 = (bf16[16,16,2048]{2,1,0:T(8,128)(2,1)}, bf16[16,16,2048]{2,1,0:T(8,128)(2,1)S(1)}, u32[]{:S(2)}) copy-start(bf16[16,16,2048]{2,1,0:T(8,128)(2,1)S(1)} %all-to-all-done.2) | copy-start | bytes 3145732
  225.7 15.3 %all-to-all-start.3 = ((bf16[16,8,2048]{2,1,0:T(8,128)(2,1)}), bf16[16,8,2048]{2,1,0:T(8,128)(2,1)S(1)}, u32[]{:S(2)}, u32[]{:S(2)}) async-start(bf16[16,8,2048]{2,1,0:T(8,128)(2,1)} %bitcast.41), calls=%async_computation.3 | async-start | bytes 1048576 | tf_op jit(solution)/shard_map/all_to_all | solution.py:427
  (5 other events, 3.9 us)

commit v4 on v3

--- a/solution.py
+++ b/solution.py
@@ -261,14 +261,30 @@
     return high, low
 
 
-def scan_body(experts, capacity, ids_ref, weights_ref, *refs):
-    backs = refs[:2]
-    dout_ref, delta_ref, rate_ref, mix_ref, drive_ref = refs[2:7]
-    mid_ref, local_ref, start_ref, grad = refs[7:]
-    high, low = weigh_pair(ids_ref[...], weights_ref[...], experts, capacity)
+def table_body(experts, capacity, ids_ref, weights_ref, high_ref, low_ref):
+    high_ref[...], low_ref[...] = weigh_pair(
+        ids_ref[...], weights_ref[...], experts, capacity
+    )
+
+
+def weigh_tables(ids, weights, experts, capacity):
+    rows = experts * sum(padded(size) for size in part_sizes(capacity))
+    return pl.pallas_call(
+        functools.partial(table_body, experts, capacity),
+        out_shape=[jax.ShapeDtypeStruct((ids.shape[0], rows), BF)] * 2,
+        compiler_params=params(),
+        name="weigh_tables",
+    )(ids, weights)
+
+
+def scan_body(*refs):
+    high_ref, low_ref = refs[:2]
+    backs = refs[2:4]
+    dout_ref, delta_ref, rate_ref, total_ref, mix_ref, drive_ref = refs[4:10]
+    mid_ref, local_ref, start_ref, grad = refs[10:]
     back = jnp.concatenate([b[...] for b in backs], axis=0)
-    routed = jnp.dot(high, back, preferred_element_type=F32)
-    routed += jnp.dot(low, back, preferred_element_type=F32)
+    routed = jnp.dot(high_ref[...], back, preferred_element_type=F32)
+    routed += jnp.dot(low_ref[...], back, preferred_element_type=F32)
     mid = (dout_ref[...].astype(F32) + routed).astype(BF)
     mid_ref[...] = mid
     grad[...] = mid.astype(F32)
@@ -292,41 +308,45 @@
         local_ref[pl.ds(low_t, 8)] = jnp.concatenate(rows[::-1], axis=0)
         return flow
 
-    start_ref[...] = lax.fori_loop(
-        0, tokens // 8, block, jnp.zeros((states, cols), F32)
-    ).astype(BF)
+    flow = lax.fori_loop(0, tokens // 8, block, jnp.zeros((states, cols), F32))
+    total = jnp.broadcast_to(total_ref[...], (8, cols))
+    whole_part = total.astype(BF).astype(F32)
+    row = lax.broadcasted_iota(jnp.int32, (8, cols), 0)
+    tail = jnp.where(row == 0, whole_part, jnp.where(row == 1, total - whole_part, 0.0))
+    start_ref[...] = jnp.concatenate([flow, tail], axis=0).astype(BF)
 
 
 def strip(rows, cols):
     return pl.BlockSpec((rows, cols), lambda i: (0, i))
 
 
-def combine_and_scan(ids, weights, backs, dout, delta, rate, mix, drive, experts, capacity):
+def combine_and_scan(tables, backs, dout, delta, rate, total, mix, drive):
     tokens, dim = dout.shape
     states = rate.shape[0]
     cols = SCAN_COLS
     return pl.pallas_call(
-        functools.partial(scan_body, experts, capacity),
+        scan_body,
         grid=(dim // cols,),
-        in_specs=[whole(*ids.shape), whole(*weights.shape)]
+        in_specs=[whole(*t.shape) for t in tables]
         + [strip(b.shape[0], cols) for b in backs]
         + [
             strip(tokens, cols),
             strip(tokens, cols),
             strip(states, cols),
+            strip(1, cols),
             whole(*mix.shape),
             whole(*drive.shape),
         ],
-        out_specs=[strip(tokens, cols), strip(tokens, cols), strip(states, cols)],
+        out_specs=[strip(tokens, cols), strip(tokens, cols), strip(states + 8, cols)],
         out_shape=[
             jax.ShapeDtypeStruct((tokens, dim), BF),
             jax.ShapeDtypeStruct((tokens, dim), F32),
-            jax.ShapeDtypeStruct((states, dim), BF),
+            jax.ShapeDtypeStruct((states + 8, dim), BF),
         ],
         scratch_shapes=[pltpu.VMEM((tokens, cols), F32)],
         compiler_params=params(),
         name="combine_and_scan",
-    )(ids, weights, *backs, dout, delta, rate, mix, drive)
+    )(*tables, *backs, dout, delta, rate, total, mix, drive)
 
 
 def reach_body(delta_ref, rate_ref, mix_ref, reach_ref, total_ref):
@@ -372,22 +392,24 @@
     )(delta, rate, mix)
 
 
-def carry_body(place_ref, starts_ref, totals_ref, rate_ref, local_ref, reach_ref, out_ref):
+def carry_body(place_ref, starts_ref, rate_ref, local_ref, reach_ref, out_ref):
     place = place_ref[0]
     negative = -rate_ref[...]
     tokens, cols = local_ref.shape
     states = negative.shape[0]
     flow = jnp.zeros((states, cols), F32)
     for at in reversed(range(starts_ref.shape[0])):
-        passed = jnp.exp(totals_ref[at : at + 1] * negative) * flow
-        flow = jnp.where(at > place, starts_ref[at].astype(F32) + passed, flow)
+        sent = starts_ref[at].astype(F32)
+        total = sent[states : states + 1] + sent[states + 1 : states + 2]
+        passed = jnp.exp(total * negative) * flow
+        flow = jnp.where(at > place, sent[:states] + passed, flow)
     total = local_ref[...]
     for n in range(states):
         total += reach_ref[n].astype(F32) * flow[n : n + 1]
     out_ref[...] = total.astype(BF)
 
 
-def add_carry(place, starts, totals, rate, local, reach):
+def add_carry(place, starts, rate, local, reach):
     tokens, dim = local.shape
     states = rate.shape[0]
     blocks = starts.shape[0]
@@ -397,8 +419,7 @@
         grid=(dim // cols,),
         in_specs=[
             pl.BlockSpec(memory_space=pltpu.SMEM),
-            pl.BlockSpec((blocks, states, cols), lambda i: (0, 0, i)),
-            strip(blocks, cols),
+            pl.BlockSpec((blocks, states + 8, cols), lambda i: (0, 0, i)),
             strip(states, cols),
             strip(tokens, cols),
             pl.BlockSpec((states, tokens, cols), lambda i: (0, 0, i)),
@@ -407,7 +428,7 @@
         out_shape=jax.ShapeDtypeStruct((tokens, dim), BF),
         compiler_params=params(),
         name="add_carry",
-    )(place, starts, totals, rate, local, reach)
+    )(place, starts, rate, local, reach)
 
 
 def on_device(z_size, capacity, x_in, dout, route_ids, combine, w_up, w_down, delta, rate, bmat, cmat):
@@ -450,8 +471,8 @@
     mix = jnp.broadcast_to(bmat[0][:, :, None], lanes)
     drive = jnp.broadcast_to(cmat[0][:, :, None], lanes)
     reach, total = reach_table(steps, rate, bmat[0])
-    totals = lax.all_gather(total[0], ("z", "core"))
-    low, reach, totals, mix, drive = tie(low, reach, totals, mix, drive)
+    tables = weigh_tables(ids, weights, experts, capacity)
+    low, reach, total, tables, mix, drive = tie(low, reach, total, tables, mix, drive)
     first = expert_rows((low_a, low_b, *low), both)
     high = ring(high_a, high_b)
     low_far, first = tie(low_far, first)
@@ -475,11 +496,11 @@
     backs = (low_back, exchange(home(second[2:4], high_sums, sizes[1])))
 
     mid, local, start = combine_and_scan(
-        ids, weights, backs, dy, steps, rate, mix, drive, experts, capacity
+        tables, backs, dy, steps, rate, total, mix, drive
     )
     starts = lax.all_gather(start, ("z", "core"))
     place = lax.axis_index(("z", "core")).astype(jnp.int32).reshape(1)
-    scan = add_carry(place, starts, totals, rate, local, reach)
+    scan = add_carry(place, starts, rate, local, reach)
     return (mid[None], scan[None])
 
 

time: 280 us -> 260 us (0.929)
  blocking collectives: 81.5 us -> 50.5 us
  waiting for transfers between devices: 30.7 us -> 43.7 us
    all_gather x1 -> x0, blocking collectives: 32.7 us -> none  [on_device(): totals = lax.all_gather(total[0], ('z', 'core'))]
    ppermute x20, waiting for transfers between devices: 22.5 us -> 34.8 us  [shift(): return lax.ppermute(value, 'z', ring)]
    pallas_call x1 -> x2, Pallas kernels: 11.2 us -> 12.6 us  [the longest x1 10.6 us: combine_and_scan(): pl.pallas_call(scan_body, grid=(dim // cols,), in_specs=[whole(*t.shape)...]
    unnamed x60 -> x59, local copies, waits for them, and re-layouts: 10.4 us -> 9.75 us
  transfers between devices with their start and end apart: 25 -> 25, of which waited for: 6 -> 6; matrix products, arithmetic and copies ran while one was open for 2% -> 2% of each run, Pallas kernels for 32% -> 35%
where the time goes in v4:
time: 260 us; the launch traced here: 259 us
  Pallas kernels  106 us (41%)
  blocking collectives  50.5 us (19%)
  starting transfers between devices  44.5 us (17%)
  waiting for transfers between devices  43.7 us (17%)
  local copies, waits for them, and re-layouts  13.1 us (5%)
    pallas_call x4, Pallas kernels, expert_rows(): pl.pallas_call(functools.partial(expert_body, pieces, steps), grid=(steps...  61 us
    ppermute x20, waiting for transfers between devices, shift(): return lax.ppermute(value, 'z', ring)  34.8 us
    all_to_all x1, blocking collectives, exchange(): got = lax.all_to_all(parts, 'exp', split_axis=0, concat_axis=0, tiled=True)  28.7 us
    ppermute x20, starting transfers between devices, shift(): return lax.ppermute(value, 'z', ring)  26.2 us
    all_gather x1, blocking collectives, on_device(): starts = lax.all_gather(start, ('z', 'core'))  21.8 us
    all_to_all x3, starting transfers between devices, exchange(): got = lax.all_to_all(parts, 'exp', split_axis=0, concat_axis=0, tiled=True)  16.6 us
    pallas_call x1, Pallas kernels, combine_and_scan(): pl.pallas_call(scan_body, grid=(dim // cols,), in_specs=[whole(*t.shape)...  10.6 us
    unnamed x59, local copies, waits for them, and re-layouts  9.75 us
  transfers between devices with their start and end apart: 25, of which 6 were waited for; matrix products, arithmetic and copies ran while one was open for 2% of the time, Pallas kernels for 35%

profile of v4, /device:TPU:1, one launch (start us, length us, event | category | flops | bytes accessed | tf_op | source)
XLA Modules:
  0.0 259.0 jit_solution(4564140706838411053)
XLA Ops:
  0.6 1.5 collective-permute-start
  3.7 3.9 %gather_rows.1 = (bf16[384,2048]{1,0:T(8,128)(2,1)}, bf16[256,2048]{1,0:T(8,128)(2,1)}) custom-call(s32[2,128]{1,0:T(2,128)} %copy.16.ids_ref, bf16[128,2048]{1,0:T(8,128)(2,1)} %bitcast.49, bf16[128,2048]{1,0:T(8,128)(2,1)} %bitcast.39), custom_call_target="tpu_custom_call" | custom-call | tf_op jit(solution)/shard_map/gather_rows/pallas_call | solution.py:75
  7.5 28.7 %all_to_all.20 = bf16[16,24,2048]{2,1,0:T(8,128)(2,1)} all-to-all(bf16[16,24,2048]{2,1,0:T(8,128)(2,1)} %bitcast.42), channel_id=1, replica_groups=mesh['z'=4,'core'=2,'exp'=16] {'exp'}, dimensions={0} | all-to-all | bytes 3145728 | tf_op jit(solution)/shard_map/all_to_all | solution.py:448
  36.2 3.8 %all-to-all-start.1 = ((bf16[16,16,2048]{2,1,0:T(8,128)(2,1)}), bf16[16,16,2048]{2,1,0:T(8,128)(2,1)S(1)}, u32[]{:S(2)}, u32[]{:S(2)}) async-start(bf16[16,16,2048]{2,1,0:T(8,128)(2,1)} %bitcast.43), calls=%async_computation.1 | async-start | bytes 2097152 | tf_op jit(solution)/shard_map/all_to_all | solution.py:448
  40.0 3.0 %sort_messages.2 = (bf16[192,2048]{1,0:T(8,128)(2,1)}, bf16[192,2048]{1,0:T(8,128)(2,1)}) custom-call(bf16[192,192]{1,0:T(8,128)(2,1)} %constant.20.clone.table_ref, bf16[384,2048]{1,0:T(8,128)(2,1)} %bitcast.23), custom_call_target="tpu_custom_call" | custom-call | tf_op jit(solution)/shard_map/sort_messages/pallas_call | solution.py:100
  43.0 1.6 collective-permute-start.2
  44.7 2.1 collective-permute-start.5
  46.8 2.7 %collective-permute-start.4 = (bf16[192,2048]{1,0:T(8,128)(2,1)}, bf16[192,2048]{1,0:T(8,128)(2,1)}, u32[]{:S(2)}, u32[]{:S(2)}) collective-permute-start(bf16[192,2048]{1,0:T(8,128)(2,1)} %get-tuple-element.77.refs_0_), channel_id=1, source_target_pairs={{0,96},{32,0},{64,32},{96,64},{1,97},{33,1},{65,33},{97,65},{2,98}... | collective-permute-start | bytes 2359304 | tf_op jit(solution)/shard_map/ppermute | solution.py:441
  51.0 2.0 weigh_tables.1
  53.0 6.8 %reach_table.1 = (bf16[16,128,2048]{2,1,0:T(8,128)(2,1)}, f32[1,2048]{1,0:T(1,128)}) custom-call(f32[128,2048]{1,0:T(8,128)} %bitcast.44, f32[16,2048]{1,0:T(8,128)} %rate_ref.3, f32[128,16]{1,0:T(8,128)} %bitcast.50), custom_call_target="tpu_custom_call" | custom-call | flops 33554432 | bytes 8388608 | tf_op jit(solution)/shard_map/reach_table/pallas_call | solution.py:373
  59.9 1.0 copy-done
  60.8 2.5 sort_messages.3
  63.6 1.2 collective-permute-start.8
  64.8 1.5 collective-permute-start.11
  66.3 13.5 %collective-permute-done.3.refs_3_ = bf16[192,2048]{1,0:T(8,128)(2,1)S(1)} collective-permute-done((bf16[192,2048]{1,0:T(8,128)(2,1)}, bf16[192,2048]{1,0:T(8,128)(2,1)S(1)}, u32[]{:S(2)}, u32[]{:S(2)}) %collective-permute-start.3) | collective-permute-done | bytes 786464 | tf_op jit(solution)/shard_map/ppermute | solution.py:441
  79.8 1.3 broadcast_in_dim.18.refs_8_
  81.1 1.3 broadcast_in_dim.20.refs_9_
  82.9 2.2 collective-permute-start.7
  85.1 20.1 %expert_rows.4 = (bf16[96,2048]{1,0:T(8,128)(2,1)}, bf16[96,2048]{1,0:T(8,128)(2,1)}, bf16[96,2048]{1,0:T(8,128)(2,1)}, bf16[96,2048]{1,0:T(8,128)(2,1)}, bf16[9...) custom-call(bf16[192,2048]{1,0:T(8,128)(2,1)} %get-tuple-element.77.refs_0_, bf16[192,2048]{1,0:T(8,128)(2,1)} %get-tuple-element.78.refs_1_, ...), custom_call_target="tpu_custom_call" | custom-call | flops 12683575296 | bytes 21757952 | tf_op jit(solution)/shard_map/expert_rows/pallas_call | solution.py:210
  105.2 2.6 %collective-permute-done.6.refs_0_ = bf16[192,2048]{1,0:T(8,128)(2,1)S(1)} collective-permute-done((bf16[192,2048]{1,0:T(8,128)(2,1)S(1)}, bf16[192,2048]{1,0:T(8,128)(2,1)S(1)}, u32[]{:S(2)}, u32[]{:S(2)}) %collective-permute-start.6) | collective-permute-done | bytes 786464 | tf_op jit(solution)/shard_map/ppermute | solution.py:441
  107.9 10.3 %collective-permute-done.7.refs_1_ = bf16[192,2048]{1,0:T(8,128)(2,1)S(1)} collective-permute-done((bf16[192,2048]{1,0:T(8,128)(2,1)S(1)}, bf16[192,2048]{1,0:T(8,128)(2,1)S(1)}, u32[]{:S(2)}, u32[]{:S(2)}) %collective-permute-start.7) | collective-permute-done | bytes 786464 | tf_op jit(solution)/shard_map/ppermute | solution.py:441
  118.2 0.9 copy-done.22
  119.1 14.8 %expert_rows.5 = (bf16[96,2048]{1,0:T(8,128)(2,1)}, bf16[96,2048]{1,0:T(8,128)(2,1)}, bf16[64,2048]{1,0:T(8,128)(2,1)}, bf16[64,2048]{1,0:T(8,128)(2,1)}) custom-call(bf16[192,2048]{1,0:T(8,128)(2,1)} %copy-done.21, bf16[192,2048]{1,0:T(8,128)(2,1)} %copy-done.22, bf16[128,2048]{1,0:T(8,128)(2,1)} %get-tuple-element.100.refs_2_, ...), custom_call_target="tpu_custom_call" | custom-call | flops 7046430720 | bytes 18612224 | tf_op jit(solution)/shard_map/expert_rows/pallas_call | solution.py:210
  134.0 1.4 collective-permute-start.14
  135.4 2.1 collective-permute-start.15
  137.4 2.7 %collective-permute-start.13 = (bf16[128,2048]{1,0:T(8,128)(2,1)S(1)}, bf16[128,2048]{1,0:T(8,128)(2,1)S(1)}, u32[]{:S(2)}, u32[]{:S(2)}) collective-permute-start(bf16[128,2048]{1,0:T(8,128)(2,1)S(1)} %collective-permute-done.11.refs_3_), channel_id=1, source_target_pairs={{0,96},{32,0},{64,32},{96,64},{1,97},{33,1},{65,33},{97,65},{2,98}... | collective-permute-start | bytes 1572872 | tf_op jit(solution)/shard_map/ppermute | solution.py:441
  140.1 13.6 %expert_rows.6 = (bf16[64,2048]{1,0:T(8,128)(2,1)}, bf16[64,2048]{1,0:T(8,128)(2,1)}, bf16[64,2048]{1,0:T(8,128)(2,1)}, bf16[64,2048]{1,0:T(8,128)(2,1)}) custom-call(bf16[128,2048]{1,0:T(8,128)(2,1)} %copy-done.23, bf16[128,2048]{1,0:T(8,128)(2,1)} %copy-done.27, bf16[128,2048]{1,0:T(8,128)(2,1)} %copy-done.25, bf16[128,2048]{1,0:T(8,128)(2,1)} %copy-done.24, ...), custom_call_target="tpu_custom_call" | custom-call | flops 5637144576 | bytes 17825792 | tf_op jit(solution)/shard_map/expert_rows/pallas_call | solution.py:210
  155.2 2.9 %hop_sums.2 = (bf16[192,2048]{1,0:T(8,128)(2,1)}, bf16[192,2048]{1,0:T(8,128)(2,1)}) custom-call(bf16[96,2048]{1,0:T(8,128)(2,1)} %get-tuple-element.116.next_a, bf16[96,2048]{1,0:T(8,128)(2,1)} %get-tuple-element.117.next_b, bf16[96,2048]{1,0:T(8,128)(2,1)} %get-tuple-element.118.prev_a, bf16[96,2048]{1,0:T(8,128)(2,1)} %get-tuple-element.119.prev_b, ...), custom_call_target="tpu_custom_call" | custom-call | tf_op jit(solution)/shard_map/hop_sums/pallas_call | solution.py:153
  158.2 2.7 %collective-permute-start.17 = (bf16[192,2048]{1,0:T(8,128)(2,1)}, bf16[192,2048]{1,0:T(8,128)(2,1)S(1)}, u32[]{:S(2)}, u32[]{:S(2)}) collective-permute-start(bf16[192,2048]{1,0:T(8,128)(2,1)} %get-tuple-element.125), channel_id=1, source_target_pairs={{0,96},{32,0},{64,32},{96,64},{1,97},{33,1},{65,33},{97,65},{2,98}... | collective-permute-start | bytes 2359304 | tf_op jit(solution)/shard_map/ppermute | solution.py:441
  160.8 12.5 %expert_rows.7 = (bf16[64,2048]{1,0:T(8,128)(2,1)}, bf16[64,2048]{1,0:T(8,128)(2,1)}) custom-call(bf16[128,2048]{1,0:T(8,128)(2,1)} %copy-done.6, bf16[128,2048]{1,0:T(8,128)(2,1)} %copy-done.7, bf16[896,2048]{1,0:T(8,128)(2,1)} %bitcast.31, bf16[896,2048]{1,0:T(8,128)(2,1)} %collective-permute-done.refs_7_.refs_5_.refs_3_, bf16[896,2048]{1,0:T(8,128)(2,1)} %bitcast.36, ...), custom_call_target="tpu_custom_call" | custom-call | flops 2818572288 | bytes 16252928 | tf_op jit(solution)/shard_map/expert_rows/pallas_call | solution.py:210
  173.3 2.7 %collective-permute-start.19 = (bf16[64,2048]{1,0:T(8,128)(2,1)}, bf16[64,2048]{1,0:T(8,128)(2,1)S(1)}, u32[]{:S(2)}, u32[]{:S(2)}) collective-permute-start(bf16[64,2048]{1,0:T(8,128)(2,1)} %get-tuple-element.129), channel_id=1, source_target_pairs={{0,96},{32,0},{64,32},{96,64},{1,97},{33,1},{65,33},{97,65},{2,98}... | collective-permute-start | bytes 786440 | tf_op jit(solution)/shard_map/ppermute | solution.py:441
  176.0 0.9 copy-done.3
  176.9 0.9 copy-done.4
  177.7 3.1 %pack_returns.2 = bf16[256,2048]{1,0:T(8,128)(2,1)} custom-call(bf16[256,192]{1,0:T(8,128)(2,1)} %constant.22.clone.refs_0_, bf16[96,2048]{1,0:T(8,128)(2,1)} %get-tuple-element.97.refs_1_, bf16[96,2048]{1,0:T(8,128)(2,1)} %get-tuple-element.98.refs_2_, bf16[192,2048]{1,0:T(8,128)(2,1)} %copy-done.3, bf16[192,2048]{1,0:T(8,128)(2,1)} %copy-done.4), custom_call_target="tpu_custom_call" | custom-call | tf_op jit(solution)/shard_map/pack_returns/pallas_call | solution.py:135
  180.8 0.8 collective-permute-done.18.got_a
  181.7 6.4 %all-to-all-start.2 = ((bf16[16,16,2048]{2,1,0:T(8,128)(2,1)}), bf16[16,16,2048]{2,1,0:T(8,128)(2,1)S(1)}, u32[]{:S(2)}, u32[]{:S(2)}) async-start(bf16[16,16,2048]{2,1,0:T(8,128)(2,1)} %bitcast.24), calls=%async_computation.2 | async-start | bytes 2097152 | tf_op jit(solution)/shard_map/all_to_all | solution.py:448
  188.1 2.4 hop_sums.3
  190.5 2.7 %collective-permute-start.21 = (bf16[128,2048]{1,0:T(8,128)(2,1)}, bf16[128,2048]{1,0:T(8,128)(2,1)S(1)}, u32[]{:S(2)}, u32[]{:S(2)}) collective-permute-start(bf16[128,2048]{1,0:T(8,128)(2,1)} %get-tuple-element.140), channel_id=1, source_target_pairs={{0,96},{32,0},{64,32},{96,64},{1,97},{33,1},{65,33},{97,65},{2,98}... | collective-permute-start | bytes 1572872 | tf_op jit(solution)/shard_map/ppermute | solution.py:441
  193.2 7.5 %collective-permute-done.20.refs_2_ = bf16[128,2048]{1,0:T(8,128)(2,1)S(1)} collective-permute-done((bf16[128,2048]{1,0:T(8,128)(2,1)}, bf16[128,2048]{1,0:T(8,128)(2,1)S(1)}, u32[]{:S(2)}, u32[]{:S(2)}) %collective-permute-start.20) | collective-permute-done | bytes 524320 | tf_op jit(solution)/shard_map/ppermute | solution.py:441
  200.7 0.8 copy-done.8
  201.5 0.8 copy-done.9
  202.3 2.3 pack_returns.3
  204.6 6.4 %all-to-all-start.3 = ((bf16[16,8,2048]{2,1,0:T(8,128)(2,1)}), bf16[16,8,2048]{2,1,0:T(8,128)(2,1)S(1)}, u32[]{:S(2)}, u32[]{:S(2)}) async-start(bf16[16,8,2048]{2,1,0:T(8,128)(2,1)} %bitcast.38), calls=%async_computation.3 | async-start | bytes 1048576 | tf_op jit(solution)/shard_map/all_to_all | solution.py:448
  211.0 8.9 %all-to-all-done.3 = bf16[16,8,2048]{2,1,0:T(8,128)(2,1)S(1)} async-done(((bf16[16,8,2048]{2,1,0:T(8,128)(2,1)}), bf16[16,8,2048]{2,1,0:T(8,128)(2,1)S(1)}, u32[]{:S(2)}, u32[]{:S(2)}) %all-to-all-start.3) | async-done | bytes 524320 | tf_op jit(solution)/shard_map/all_to_all | solution.py:448
  220.0 0.8 copy-done.2
  220.7 10.6 %combine_and_scan.1 = (bf16[128,2048]{1,0:T(8,128)(2,1)}, f32[128,2048]{1,0:T(8,128)}, bf16[24,2048]{1,0:T(8,128)(2,1)}) custom-call(bf16[128,384]{1,0:T(8,128)(2,1)} %get-tuple-element.83.refs_0_, bf16[128,384]{1,0:T(8,128)(2,1)} %get-tuple-element.84.refs_1_, bf16[256,2048]{1,0:T(8,128)(2,1)} %bitcast.26, bf16[128,2048]{1,0:T(8,128)(2,1)} %bitcast.41, ...), custom_call_target="tpu_custom_call" | custom-call | tf_op jit(solution)/shard_map/combine_and_scan/pallas_call | solution.py:327
  231.4 21.8 %all-gather = bf16[192,2048]{1,0:T(8,128)(2,1)} all-gather(bf16[24,2048]{1,0:T(8,128)(2,1)} %get-tuple-element.145), channel_id=2, replica_groups=mesh['z'=4,'core'=2,'exp'=16] {'z','core'}, dimensions={0}, use_global_device_ids=true | all-gather | bytes 884736 | tf_op jit(solution)/shard_map/all_gather | solution.py:501
  253.2 5.8 %add_carry.1 = bf16[128,2048]{1,0:T(8,128)(2,1)} custom-call(s32[1]{0:T(128)} %bitcast.19.place_ref, bf16[8,24,2048]{2,1,0:T(8,128)(2,1)} %bitcast.37, f32[16,2048]{1,0:T(8,128)} %rate_ref.3, f32[128,2048]{1,0:T(8,128)} %get-tuple-element.146.local_ref, bf16[16,128,2048]{2,1,0:T(8,128)(2,1)} %get-tuple-element.147.reach_ref), custom_call_target="tpu_custom_call" | custom-call | tf_op jit(solution)/shard_map/add_carry/pallas_call | solution.py:417
  (82 shorter events, 5.5 us)
Async XLA Ops:
  0.6 39.4 %collective-permute-start = (bf16[896,2048]{1,0:T(8,128)(2,1)}, bf16[896,2048]{1,0:T(8,128)(2,1)}, u32[]{:S(2)}, u32[]{:S(2)}) collective-permute-start(bf16[896,2048]{1,0:T(8,128)(2,1)} %bitcast.27), channel_id=1, source_target_pairs={{0,16},{16,0},{1,17},{17,1},{2,18},{18,2},{3,19},{19,3},{4,20},{20... | collective-permute-start | bytes 11010056 | tf_op jit(solution)/shard_map/ppermute | solution.py:444
  2.1 37.9 %collective-permute-start.1 = (bf16[896,2048]{1,0:T(8,128)(2,1)}, bf16[896,2048]{1,0:T(8,128)(2,1)}, u32[]{:S(2)}, u32[]{:S(2)}) collective-permute-start(bf16[896,2048]{1,0:T(8,128)(2,1)} %bitcast.32), channel_id=1, source_target_pairs={{0,16},{16,0},{1,17},{17,1},{2,18},{18,2},{3,19},{19,3},{4,20},{20... | collective-permute-start | bytes 11010056 | tf_op jit(solution)/shard_map/ppermute | solution.py:444
  3.0 40.0 %copy-start.5 = (s32[1,128,2]{2,1,0:T(8,128)}, s32[1,128,2]{2,1,0:T(8,128)S(1)}, u32[]{:S(2)}) copy-start(s32[1,128,2]{2,1,0:T(8,128)S(1)} %copy.15) | copy-start | bytes 3076
  7.5 41.9 %copy-start.15 = (f32[1,128,16]{1,2,0:T(8,128)S(1)}, f32[1,128,16]{1,2,0:T(8,128)}, u32[]{:S(2)}) copy-start(f32[1,128,16]{1,2,0:T(8,128)} %param.21) | copy-start | bytes 24580
  7.5 42.6 %copy-start.17 = (f32[1,128,2]{1,2,0:T(2,128)S(1)}, f32[1,128,2]{1,2,0:T(2,128)}, u32[]{:S(2)}) copy-start(f32[1,128,2]{1,2,0:T(2,128)} %param.16) | copy-start | bytes 3076
  7.5 43.4 %copy-start.16 = (f32[1,128,16]{1,2,0:T(8,128)S(1)}, f32[1,128,16]{1,2,0:T(8,128)}, u32[]{:S(2)}) copy-start(f32[1,128,16]{1,2,0:T(8,128)} %param.22) | copy-start | bytes 24580
  36.2 23.7 %all-to-all-start.1 = ((bf16[16,16,2048]{2,1,0:T(8,128)(2,1)}), bf16[16,16,2048]{2,1,0:T(8,128)(2,1)S(1)}, u32[]{:S(2)}, u32[]{:S(2)}) async-start(bf16[16,16,2048]{2,1,0:T(8,128)(2,1)} %bitcast.43), calls=%async_computation.1 | async-start | bytes 2097152 | tf_op jit(solution)/shard_map/all_to_all | solution.py:448
  43.0 20.6 %collective-permute-start.2 = (bf16[192,2048]{1,0:T(8,128)(2,1)}, bf16[192,2048]{1,0:T(8,128)(2,1)S(1)}, u32[]{:S(2)}, u32[]{:S(2)}) collective-permute-start(bf16[192,2048]{1,0:T(8,128)(2,1)} %get-tuple-element.77.refs_0_), channel_id=1, source_target_pairs={{0,32},{32,64},{64,96},{96,0},{1,33},{33,65},{65,97},{97,1},{2,34}... | collective-permute-start | bytes 2359304 | tf_op jit(solution)/shard_map/ppermute | solution.py:441
  44.7 20.1 %collective-permute-start.5 = (bf16[192,2048]{1,0:T(8,128)(2,1)}, bf16[192,2048]{1,0:T(8,128)(2,1)S(1)}, u32[]{:S(2)}, u32[]{:S(2)}) collective-permute-start(bf16[192,2048]{1,0:T(8,128)(2,1)} %get-tuple-element.78.refs_1_), channel_id=1, source_target_pairs={{0,96},{32,0},{64,32},{96,64},{1,97},{33,1},{65,33},{97,65},{2,98}... | collective-permute-start | bytes 2359304 | tf_op jit(solution)/shard_map/ppermute | solution.py:441
  46.8 33.0 %collective-permute-start.3 = (bf16[192,2048]{1,0:T(8,128)(2,1)}, bf16[192,2048]{1,0:T(8,128)(2,1)S(1)}, u32[]{:S(2)}, u32[]{:S(2)}) collective-permute-start(bf16[192,2048]{1,0:T(8,128)(2,1)} %get-tuple-element.78.refs_1_), channel_id=1, source_target_pairs={{0,32},{32,64},{64,96},{96,0},{1,33},{33,65},{65,97},{97,1},{2,34}... | collective-permute-start | bytes 2359304 | tf_op jit(solution)/shard_map/ppermute | solution.py:441
  46.8 33.0 %collective-permute-start.4 = (bf16[192,2048]{1,0:T(8,128)(2,1)}, bf16[192,2048]{1,0:T(8,128)(2,1)}, u32[]{:S(2)}, u32[]{:S(2)}) collective-permute-start(bf16[192,2048]{1,0:T(8,128)(2,1)} %get-tuple-element.77.refs_0_), channel_id=1, source_target_pairs={{0,96},{32,0},{64,32},{96,64},{1,97},{33,1},{65,33},{97,65},{2,98}... | collective-permute-start | bytes 2359304 | tf_op jit(solution)/shard_map/ppermute | solution.py:441
  53.0 26.7 %copy-start.12 = (f32[1,128,16]{2,1,0:T(8,128)S(1)}, f32[1,128,16]{2,1,0:T(8,128)}, u32[]{:S(2)}) copy-start(f32[1,128,16]{2,1,0:T(8,128)} %copy.17) | copy-start | bytes 24580
  59.9 1.0 copy-start
  63.3 70.6 %collective-permute-start.10 = (bf16[128,2048]{1,0:T(8,128)(2,1)}, bf16[128,2048]{1,0:T(8,128)(2,1)S(1)}, u32[]{:S(2)}, u32[]{:S(2)}) collective-permute-start(bf16[128,2048]{1,0:T(8,128)(2,1)} %get-tuple-element.100.refs_2_), channel_id=1, source_target_pairs={{0,96},{32,0},{64,32},{96,64},{1,97},{33,1},{65,33},{97,65},{2,98}... | collective-permute-start | bytes 1572872 | tf_op jit(solution)/shard_map/ppermute | solution.py:441
  63.6 21.5 %copy-start.19 = (bf16[192,2048]{1,0:T(8,128)(2,1)}, bf16[192,2048]{1,0:T(8,128)(2,1)S(1)}, u32[]{:S(2)}) copy-start(bf16[192,2048]{1,0:T(8,128)(2,1)S(1)} %collective-permute-done.2.refs_2_) | copy-start | bytes 2359300
  63.6 70.4 %collective-permute-start.8 = (bf16[128,2048]{1,0:T(8,128)(2,1)}, bf16[128,2048]{1,0:T(8,128)(2,1)S(1)}, u32[]{:S(2)}, u32[]{:S(2)}) collective-permute-start(bf16[128,2048]{1,0:T(8,128)(2,1)} %get-tuple-element.100.refs_2_), channel_id=1, source_target_pairs={{0,32},{32,64},{64,96},{96,0},{1,33},{33,65},{65,97},{97,1},{2,34}... | collective-permute-start | bytes 1572872 | tf_op jit(solution)/shard_map/ppermute | solution.py:441
  64.8 20.3 %copy-start.18 = (bf16[192,2048]{1,0:T(8,128)(2,1)}, bf16[192,2048]{1,0:T(8,128)(2,1)S(1)}, u32[]{:S(2)}) copy-start(bf16[192,2048]{1,0:T(8,128)(2,1)S(1)} %collective-permute-done.5.refs_5_) | copy-start | bytes 2359300
  64.8 69.1 %collective-permute-start.11 = (bf16[128,2048]{1,0:T(8,128)(2,1)}, bf16[128,2048]{1,0:T(8,128)(2,1)S(1)}, u32[]{:S(2)}, u32[]{:S(2)}) collective-permute-start(bf16[128,2048]{1,0:T(8,128)(2,1)} %get-tuple-element.101.refs_3_), channel_id=1, source_target_pairs={{0,96},{32,0},{64,32},{96,64},{1,97},{33,1},{65,33},{97,65},{2,98}... | collective-permute-start | bytes 1572872 | tf_op jit(solution)/shard_map/ppermute | solution.py:441
  79.8 5.4 %copy-start.20 = (bf16[192,2048]{1,0:T(8,128)(2,1)}, bf16[192,2048]{1,0:T(8,128)(2,1)S(1)}, u32[]{:S(2)}) copy-start(bf16[192,2048]{1,0:T(8,128)(2,1)S(1)} %collective-permute-done.3.refs_3_) | copy-start | bytes 2359300
  82.4 25.4 %copy-start.26 = (bf16[128,2048]{1,0:T(8,128)(2,1)S(1)}, bf16[128,2048]{1,0:T(8,128)(2,1)}, u32[]{:S(2)}) copy-start(bf16[128,2048]{1,0:T(8,128)(2,1)} %get-tuple-element.101.refs_3_) | copy-start | bytes 1572868
  82.4 25.4 %collective-permute-start.6 = (bf16[192,2048]{1,0:T(8,128)(2,1)S(1)}, bf16[192,2048]{1,0:T(8,128)(2,1)S(1)}, u32[]{:S(2)}, u32[]{:S(2)}) collective-permute-start(bf16[192,2048]{1,0:T(8,128)(2,1)S(1)} %collective-permute-done.2.refs_2_), channel_id=1, source_target_pairs={{0,32},{32,64},{64,96},{96,0},{1,33},{33,65},{65,97},{97,1},{2,34}... | collective-permute-start | bytes 2359304 | tf_op jit(solution)/shard_map/ppermute | solution.py:441
  82.9 35.3 %collective-permute-start.7 = (bf16[192,2048]{1,0:T(8,128)(2,1)S(1)}, bf16[192,2048]{1,0:T(8,128)(2,1)S(1)}, u32[]{:S(2)}, u32[]{:S(2)}) collective-permute-start(bf16[192,2048]{1,0:T(8,128)(2,1)S(1)} %collective-permute-done.5.refs_5_), channel_id=1, source_target_pairs={{0,96},{32,0},{64,32},{96,64},{1,97},{33,1},{65,33},{97,65},{2,98}... | collective-permute-start | bytes 2359304 | tf_op jit(solution)/shard_map/ppermute | solution.py:441
  107.8 10.4 %copy-start.21 = (bf16[192,2048]{1,0:T(8,128)(2,1)}, bf16[192,2048]{1,0:T(8,128)(2,1)S(1)}, u32[]{:S(2)}) copy-start(bf16[192,2048]{1,0:T(8,128)(2,1)S(1)} %collective-permute-done.6.refs_0_) | copy-start | bytes 2359300
  107.8 26.1 %collective-permute-start.9 = (bf16[128,2048]{1,0:T(8,128)(2,1)S(1)}, bf16[128,2048]{1,0:T(8,128)(2,1)S(1)}, u32[]{:S(2)}, u32[]{:S(2)}) collective-permute-start(bf16[128,2048]{1,0:T(8,128)(2,1)S(1)} %copy-done.26), channel_id=1, source_target_pairs={{0,32},{32,64},{64,96},{96,0},{1,33},{33,65},{65,97},{97,1},{2,34}... | collective-permute-start | bytes 1572872 | tf_op jit(solution)/shard_map/ppermute | solution.py:441
  118.2 0.9 copy-start.22
  133.9 6.2 %copy-start.25 = (bf16[128,2048]{1,0:T(8,128)(2,1)}, bf16[128,2048]{1,0:T(8,128)(2,1)S(1)}, u32[]{:S(2)}) copy-start(bf16[128,2048]{1,0:T(8,128)(2,1)S(1)} %collective-permute-done.10.refs_2_) | copy-start | bytes 1572868
  133.9 6.2 %copy-start.24 = (bf16[128,2048]{1,0:T(8,128)(2,1)}, bf16[128,2048]{1,0:T(8,128)(2,1)S(1)}, u32[]{:S(2)}) copy-start(bf16[128,2048]{1,0:T(8,128)(2,1)S(1)} %collective-permute-done.11.refs_3_) | copy-start | bytes 1572868
  134.0 6.1 %copy-start.23 = (bf16[128,2048]{1,0:T(8,128)(2,1)}, bf16[128,2048]{1,0:T(8,128)(2,1)S(1)}, u32[]{:S(2)}) copy-start(bf16[128,2048]{1,0:T(8,128)(2,1)S(1)} %collective-permute-done.8.refs_0_) | copy-start | bytes 1572868
  134.0 6.1 %copy-start.27 = (bf16[128,2048]{1,0:T(8,128)(2,1)}, bf16[128,2048]{1,0:T(8,128)(2,1)S(1)}, u32[]{:S(2)}) copy-start(bf16[128,2048]{1,0:T(8,128)(2,1)S(1)} %collective-permute-done.9.refs_1_) | copy-start | bytes 1572868
  134.0 19.7 %collective-permute-start.14 = (bf16[96,2048]{1,0:T(8,128)(2,1)}, bf16[96,2048]{1,0:T(8,128)(2,1)S(1)}, u32[]{:S(2)}, u32[]{:S(2)}) collective-permute-start(bf16[96,2048]{1,0:T(8,128)(2,1)} %get-tuple-element.120), channel_id=1, source_target_pairs={{0,32},{32,64},{64,96},{96,0},{1,33},{33,65},{65,97},{97,1},{2,34}... | collective-permute-start | bytes 1179656 | tf_op jit(solution)/shard_map/ppermute | solution.py:441
  135.4 18.4 %collective-permute-start.15 = (bf16[96,2048]{1,0:T(8,128)(2,1)}, bf16[96,2048]{1,0:T(8,128)(2,1)S(1)}, u32[]{:S(2)}, u32[]{:S(2)}) collective-permute-start(bf16[96,2048]{1,0:T(8,128)(2,1)} %get-tuple-element.121), channel_id=1, source_target_pairs={{0,96},{32,0},{64,32},{96,64},{1,97},{33,1},{65,33},{97,65},{2,98}... | collective-permute-start | bytes 1179656 | tf_op jit(solution)/shard_map/ppermute | solution.py:441
  137.4 20.6 %collective-permute-start.12 = (bf16[128,2048]{1,0:T(8,128)(2,1)S(1)}, bf16[128,2048]{1,0:T(8,128)(2,1)S(1)}, u32[]{:S(2)}, u32[]{:S(2)}) collective-permute-start(bf16[128,2048]{1,0:T(8,128)(2,1)S(1)} %collective-permute-done.8.refs_0_), channel_id=1, source_target_pairs={{0,32},{32,64},{64,96},{96,0},{1,33},{33,65},{65,97},{97,1},{2,34}... | collective-permute-start | bytes 1572872 | tf_op jit(solution)/shard_map/ppermute | solution.py:441
  137.4 20.6 %collective-permute-start.13 = (bf16[128,2048]{1,0:T(8,128)(2,1)S(1)}, bf16[128,2048]{1,0:T(8,128)(2,1)S(1)}, u32[]{:S(2)}, u32[]{:S(2)}) collective-permute-start(bf16[128,2048]{1,0:T(8,128)(2,1)S(1)} %collective-permute-done.11.refs_3_), channel_id=1, source_target_pairs={{0,96},{32,0},{64,32},{96,64},{1,97},{33,1},{65,33},{97,65},{2,98}... | collective-permute-start | bytes 1572872 | tf_op jit(solution)/shard_map/ppermute | solution.py:441
  158.1 2.8 %copy-start.6 = (bf16[128,2048]{1,0:T(8,128)(2,1)}, bf16[128,2048]{1,0:T(8,128)(2,1)S(1)}, u32[]{:S(2)}) copy-start(bf16[128,2048]{1,0:T(8,128)(2,1)S(1)} %collective-permute-done.12.refs_0_) | copy-start | bytes 1572868
  158.1 2.8 %copy-start.7 = (bf16[128,2048]{1,0:T(8,128)(2,1)}, bf16[128,2048]{1,0:T(8,128)(2,1)S(1)}, u32[]{:S(2)}) copy-start(bf16[128,2048]{1,0:T(8,128)(2,1)S(1)} %collective-permute-done.13.refs_1_) | copy-start | bytes 1572868
  158.1 17.9 %collective-permute-start.16 = (bf16[192,2048]{1,0:T(8,128)(2,1)}, bf16[192,2048]{1,0:T(8,128)(2,1)S(1)}, u32[]{:S(2)}, u32[]{:S(2)}) collective-permute-start(bf16[192,2048]{1,0:T(8,128)(2,1)} %get-tuple-element.124), channel_id=1, source_target_pairs={{0,32},{32,64},{64,96},{96,0},{1,33},{33,65},{65,97},{97,1},{2,34}... | collective-permute-start | bytes 2359304 | tf_op jit(solution)/shard_map/ppermute | solution.py:441
  158.2 17.8 %collective-permute-start.17 = (bf16[192,2048]{1,0:T(8,128)(2,1)}, bf16[192,2048]{1,0:T(8,128)(2,1)S(1)}, u32[]{:S(2)}, u32[]{:S(2)}) collective-permute-start(bf16[192,2048]{1,0:T(8,128)(2,1)} %get-tuple-element.125), channel_id=1, source_target_pairs={{0,96},{32,0},{64,32},{96,64},{1,97},{33,1},{65,33},{97,65},{2,98}... | collective-permute-start | bytes 2359304 | tf_op jit(solution)/shard_map/ppermute | solution.py:441
  173.3 8.4 %collective-permute-start.18 = (bf16[64,2048]{1,0:T(8,128)(2,1)}, bf16[64,2048]{1,0:T(8,128)(2,1)S(1)}, u32[]{:S(2)}, u32[]{:S(2)}) collective-permute-start(bf16[64,2048]{1,0:T(8,128)(2,1)} %get-tuple-element.128), channel_id=1, source_target_pairs={{0,32},{32,64},{64,96},{96,0},{1,33},{33,65},{65,97},{97,1},{2,34}... | collective-permute-start | bytes 786440 | tf_op jit(solution)/shard_map/ppermute | solution.py:441
  173.3 8.4 %collective-permute-start.19 = (bf16[64,2048]{1,0:T(8,128)(2,1)}, bf16[64,2048]{1,0:T(8,128)(2,1)S(1)}, u32[]{:S(2)}, u32[]{:S(2)}) collective-permute-start(bf16[64,2048]{1,0:T(8,128)(2,1)} %get-tuple-element.129), channel_id=1, source_target_pairs={{0,96},{32,0},{64,32},{96,64},{1,97},{33,1},{65,33},{97,65},{2,98}... | collective-permute-start | bytes 786440 | tf_op jit(solution)/shard_map/ppermute | solution.py:441
  176.0 0.9 copy-start.3
  176.9 0.9 copy-start.4
  181.7 6.5 %copy-start.13 = (bf16[64,2048]{1,0:T(8,128)(2,1)}, bf16[64,2048]{1,0:T(8,128)(2,1)S(1)}, u32[]{:S(2)}) copy-start(bf16[64,2048]{1,0:T(8,128)(2,1)S(1)} %collective-permute-done.18.got_a) | copy-start | bytes 786436
  181.7 6.5 %copy-start.14 = (bf16[64,2048]{1,0:T(8,128)(2,1)}, bf16[64,2048]{1,0:T(8,128)(2,1)S(1)}, u32[]{:S(2)}) copy-start(bf16[64,2048]{1,0:T(8,128)(2,1)S(1)} %collective-permute-done.19.got_b) | copy-start | bytes 786436
  181.7 23.0 %all-to-all-start.2 = ((bf16[16,16,2048]{2,1,0:T(8,128)(2,1)}), bf16[16,16,2048]{2,1,0:T(8,128)(2,1)S(1)}, u32[]{:S(2)}, u32[]{:S(2)}) async-start(bf16[16,16,2048]{2,1,0:T(8,128)(2,1)} %bitcast.24), calls=%async_computation.2 | async-start | bytes 2097152 | tf_op jit(solution)/shard_map/all_to_all | solution.py:448
  190.5 10.2 %collective-permute-start.20 = (bf16[128,2048]{1,0:T(8,128)(2,1)}, bf16[128,2048]{1,0:T(8,128)(2,1)S(1)}, u32[]{:S(2)}, u32[]{:S(2)}) collective-permute-start(bf16[128,2048]{1,0:T(8,128)(2,1)} %get-tuple-element.139), channel_id=1, source_target_pairs={{0,32},{32,64},{64,96},{96,0},{1,33},{33,65},{65,97},{97,1},{2,34}... | collective-permute-start | bytes 1572872 | tf_op jit(solution)/shard_map/ppermute | solution.py:441
  190.5 10.2 %collective-permute-start.21 = (bf16[128,2048]{1,0:T(8,128)(2,1)}, bf16[128,2048]{1,0:T(8,128)(2,1)S(1)}, u32[]{:S(2)}, u32[]{:S(2)}) collective-permute-start(bf16[128,2048]{1,0:T(8,128)(2,1)} %get-tuple-element.140), channel_id=1, source_target_pairs={{0,96},{32,0},{64,32},{96,64},{1,97},{33,1},{65,33},{97,65},{2,98}... | collective-permute-start | bytes 1572872 | tf_op jit(solution)/shard_map/ppermute | solution.py:441
  204.6 15.3 %copy-start.1 = (bf16[16,16,2048]{2,1,0:T(8,128)(2,1)}, bf16[16,16,2048]{2,1,0:T(8,128)(2,1)S(1)}, u32[]{:S(2)}) copy-start(bf16[16,16,2048]{2,1,0:T(8,128)(2,1)S(1)} %all-to-all-done.2) | copy-start | bytes 3145732
  204.6 15.3 %all-to-all-start.3 = ((bf16[16,8,2048]{2,1,0:T(8,128)(2,1)}), bf16[16,8,2048]{2,1,0:T(8,128)(2,1)S(1)}, u32[]{:S(2)}, u32[]{:S(2)}) async-start(bf16[16,8,2048]{2,1,0:T(8,128)(2,1)} %bitcast.38), calls=%async_computation.3 | async-start | bytes 1048576 | tf_op jit(solution)/shard_map/all_to_all | solution.py:448
  (5 other events, 3.9 us)

commit v5 on v4

--- a/solution.py
+++ b/solution.py
@@ -9,18 +9,21 @@
 from jax.sharding import Mesh
 from jax.sharding import PartitionSpec as P
 
-VMEM_LIMIT = 56 * 1024 * 1024
 CORES = 2
 EARLY = 12
 HIDDEN_STEP = 128
-OUT_COLS = 1024
+OUT_COLS = 512
 SCAN_COLS = 1024
 BF = jnp.bfloat16
 F32 = jnp.float32
 
 
-def params():
-    return pltpu.CompilerParams(vmem_limit_bytes=VMEM_LIMIT)
+def params(mebibytes):
+    return pltpu.CompilerParams(vmem_limit_bytes=mebibytes * 1024 * 1024)
+
+
+def in_vmem(values):
+    return [pltpu.with_memory_space_constraint(v, pltpu.VMEM) for v in values]
 
 
 def whole(*shape):
@@ -78,7 +81,7 @@
             jax.ShapeDtypeStruct((experts * 2 * size, dim), BF)
             for size in part_sizes(capacity)
         ],
-        compiler_params=params(),
+        compiler_params=params(40),
         name="gather_rows",
     )(ids_t, x, dy)
 
@@ -100,9 +103,9 @@
     return pl.pallas_call(
         sort_body,
         out_shape=[jax.ShapeDtypeStruct((rows, dim), BF)] * 2,
-        compiler_params=params(),
+        compiler_params=params(38),
         name="sort_messages",
-    )(jnp.asarray(table, BF), messages)
+    )(jnp.asarray(table, BF), *in_vmem((messages,)))
 
 
 def padded(size):
@@ -135,9 +138,9 @@
     return pl.pallas_call(
         functools.partial(pack_body, spread),
         out_shape=jax.ShapeDtypeStruct((rows // size * wide, dim), BF),
-        compiler_params=params(),
+        compiler_params=params(38),
         name="pack_returns",
-    )(*head, own_a, own_b, from_prev, from_next)
+    )(*head, own_a, own_b, *in_vmem((from_prev, from_next)))
 
 
 def hop_body(next_a, next_b, prev_a, prev_b, got_a, got_b, to_next, to_prev):
@@ -153,49 +156,51 @@
     return pl.pallas_call(
         hop_body,
         out_shape=[jax.ShapeDtypeStruct((2 * half, dim), BF)] * 2,
-        compiler_params=params(),
+        compiler_params=params(38),
         name="hop_sums",
-    )(*parts)
-
-
-def expert_body(pieces, steps, *refs):
+    )(*parts[:4], *in_vmem(parts[4:]))
+
+
+def expert_body(pieces, *refs):
     ins = refs[:pieces]
     up_a, up_b, down_a, down_b = refs[pieces : pieces + 4]
     outs = refs[pieces + 4 : 2 * pieces + 4]
-    x_all, dy_all, up_all, grads = refs[2 * pieces + 4 :]
-    step = pl.program_id(0)
-    width = 2 * up_a.shape[0]
-
-    @pl.when(step == 0)
-    def _():
-        low = 0
-        for piece, out in zip(ins, outs):
-            size = out.shape[0]
-            x_all[low : low + size] = piece[:size]
-            dy_all[low : low + size] = piece[size:]
-            low += size
-
-    @pl.when(step < steps)
-    def _():
-        up = jnp.concatenate([up_a[...], up_b[...]], axis=0)
-        down = jnp.concatenate([down_a[...], down_b[...]], axis=0)
-        up_all[pl.ds(pl.multiple_of(step * width, width), width)] = up
-        across = (((1,), (1,)), ((), ()))
+    x_all, dy_all, grads = refs[2 * pieces + 4 :]
+    hidden, dim = up_a.shape
+    steps = hidden // HIDDEN_STEP
+    low = 0
+    for piece, out in zip(ins, outs):
+        size = out.shape[0]
+        x_all[low : low + size] = piece[:size]
+        dy_all[low : low + size] = piece[size:]
+        low += size
+    across = (((1,), (1,)), ((), ()))
+
+    def step(i, carry):
+        at = pl.ds(pl.multiple_of(i * HIDDEN_STEP, HIDDEN_STEP), HIDDEN_STEP)
+        up = jnp.concatenate([up_a[at], up_b[at]], axis=0)
+        down = jnp.concatenate([down_a[at], down_b[at]], axis=0)
         pre = lax.dot_general(x_all[...], up, across, preferred_element_type=F32)
         back = lax.dot_general(dy_all[...], down, across, preferred_element_type=F32)
         sig = jax.nn.sigmoid(pre)
-        grads[step] = (back * sig * (1.0 + pre * (1.0 - sig))).astype(BF)
-
-    @pl.when(step >= steps)
-    def _():
-        grad = jnp.concatenate([grads[i] for i in range(steps)], axis=1)
-        cols = outs[0].shape[1]
-        at = pl.ds(pl.multiple_of((step - steps) * cols, cols), cols)
-        part = jnp.dot(grad, up_all[:, at], preferred_element_type=F32).astype(BF)
+        grad = (back * sig * (1.0 + pre * (1.0 - sig))).astype(BF)
+        grads[0, i] = grad[:, :HIDDEN_STEP]
+        grads[1, i] = grad[:, HIDDEN_STEP:]
+        return carry
+
+    lax.fori_loop(0, steps, step, 0)
+    grad_a, grad_b = (
+        jnp.concatenate([grads[core, i] for i in range(steps)], axis=1) for core in range(2)
+    )
+    for left in range(0, dim, OUT_COLS):
+        cols = slice(left, left + OUT_COLS)
+        part = jnp.dot(grad_a, up_a[:, cols], preferred_element_type=F32)
+        part += jnp.dot(grad_b, up_b[:, cols], preferred_element_type=F32)
+        part = part.astype(BF)
         low = 0
         for out in outs:
             size = out.shape[0]
-            out[...] = part[low : low + size]
+            out[:, cols] = part[low : low + size]
             low += size
 
 
@@ -205,31 +210,25 @@
     sizes = [piece.shape[0] // 2 for piece in ins]
     rows = sum(sizes)
     hidden = weights[0].shape[0]
-    steps = hidden // HIDDEN_STEP
-    tile = pl.BlockSpec((HIDDEN_STEP, dim), lambda i: (jnp.minimum(i, steps - 1), 0))
-    return pl.pallas_call(
-        functools.partial(expert_body, pieces, steps),
-        grid=(steps + dim // OUT_COLS,),
-        in_specs=[whole(*piece.shape) for piece in ins] + [tile] * 4,
-        out_specs=[
-            pl.BlockSpec((size, OUT_COLS), lambda i: (0, jnp.maximum(i - steps, 0)))
-            for size in sizes
-        ],
+    vmem = pl.BlockSpec(memory_space=pltpu.VMEM)
+    return pl.pallas_call(
+        functools.partial(expert_body, pieces),
+        in_specs=[vmem] * (pieces + 4),
+        out_specs=[vmem] * pieces,
         out_shape=[jax.ShapeDtypeStruct((size, dim), BF) for size in sizes],
         scratch_shapes=[
             pltpu.VMEM((rows, dim), BF),
             pltpu.VMEM((rows, dim), BF),
-            pltpu.VMEM((2 * hidden, dim), BF),
-            pltpu.VMEM((steps, rows, 2 * HIDDEN_STEP), BF),
-        ],
-        compiler_params=params(),
+            pltpu.VMEM((2, hidden // HIDDEN_STEP, rows, HIDDEN_STEP), BF),
+        ],
+        compiler_params=params(30),
         cost_estimate=pl.CostEstimate(
             flops=6 * rows * 2 * hidden * dim,
             bytes_accessed=2 * (4 * hidden * dim + 3 * rows * dim),
             transcendentals=rows * 2 * hidden,
         ),
         name="expert_rows",
-    )(*ins, *weights)
+    )(*in_vmem(ins), *in_vmem(weights))
 
 
 def weigh_pair(ids, weights, experts, capacity):
@@ -272,7 +271,7 @@
     return pl.pallas_call(
         functools.partial(table_body, experts, capacity),
         out_shape=[jax.ShapeDtypeStruct((ids.shape[0], rows), BF)] * 2,
-        compiler_params=params(),
+        compiler_params=params(38),
         name="weigh_tables",
     )(ids, weights)
 
@@ -344,7 +343,7 @@
             jax.ShapeDtypeStruct((states + 8, dim), BF),
         ],
         scratch_shapes=[pltpu.VMEM((tokens, cols), F32)],
-        compiler_params=params(),
+        compiler_params=params(54),
         name="combine_and_scan",
     )(*tables, *backs, dout, delta, rate, total, mix, drive)
 
@@ -382,7 +381,7 @@
             jax.ShapeDtypeStruct((states, tokens, dim), BF),
             jax.ShapeDtypeStruct((1, dim), F32),
         ],
-        compiler_params=params(),
+        compiler_params=params(38),
         cost_estimate=pl.CostEstimate(
             flops=8 * states * tokens * dim,
             bytes_accessed=2 * states * tokens * dim,
@@ -426,7 +425,7 @@
         ],
         out_specs=strip(tokens, cols),
         out_shape=jax.ShapeDtypeStruct((tokens, dim), BF),
-        compiler_params=params(),
+        compiler_params=params(54),
         name="add_carry",
     )(place, starts, rate, local, reach)
 

time: 260 us -> 245 us (0.942)
  Pallas kernels: 106 us -> 82.2 us
  waiting for transfers between devices: 43.7 us -> 51.1 us
  local copies, waits for them, and re-layouts: 13.1 us -> 16 us
    pallas_call x4, Pallas kernels: 61 us -> 53.6 us  [expert_rows(): pl.pallas_call(functools.partial(expert_body, pieces), in_specs=[vmem] *...]
    ppermute x20, waiting for transfers between devices: 34.8 us -> 41.5 us  [shift(): return lax.ppermute(value, 'z', ring)]
    pallas_call x2, Pallas kernels: 5.25 us -> 0.35 us  [hop_sums(): pl.pallas_call(hop_body, out_shape=[jax.ShapeDtypeStruct((2 * half, dim),...]
    unnamed x59 -> x45, local copies, waits for them, and re-layouts: 9.75 us -> 13.2 us
    pallas_call x2, Pallas kernels: 5.45 us -> 2.46 us  [pack_returns(): pl.pallas_call(functools.partial(pack_body, spread), out_shape=jax.ShapeD...]
    pallas_call x2, Pallas kernels: 5.49 us -> 2.62 us  [sort_messages(): pl.pallas_call(sort_body, out_shape=[jax.ShapeDtypeStruct((rows, dim), BF...]
  transfers between devices with their start and end apart: 25 -> 25, of which waited for: 6 -> 9; matrix products, arithmetic and copies ran while one was open for 2% -> 2% of each run, Pallas kernels for 35% -> 27%
where the time goes in v5:
time: 245 us; the launch traced here: 244 us
  Pallas kernels  82.2 us (34%)
  waiting for transfers between devices  51.1 us (21%)
  blocking collectives  50.1 us (20%)
  starting transfers between devices  43.9 us (18%)
  local copies, waits for them, and re-layouts  16 us (7%)
    pallas_call x4, Pallas kernels, expert_rows(): pl.pallas_call(functools.partial(expert_body, pieces), in_specs=[vmem] *...  53.6 us
    ppermute x20, waiting for transfers between devices, shift(): return lax.ppermute(value, 'z', ring)  41.5 us
    all_to_all x1, blocking collectives, exchange(): got = lax.all_to_all(parts, 'exp', split_axis=0, concat_axis=0, tiled=True)  28.3 us
    ppermute x20, starting transfers between devices, shift(): return lax.ppermute(value, 'z', ring)  26.5 us
    all_gather x1, blocking collectives, on_device(): starts = lax.all_gather(start, ('z', 'core'))  21.8 us
    all_to_all x3, starting transfers between devices, exchange(): got = lax.all_to_all(parts, 'exp', split_axis=0, concat_axis=0, tiled=True)  15.8 us
    unnamed x45, local copies, waits for them, and re-layouts  13.2 us
    pallas_call x1, Pallas kernels, combine_and_scan(): pl.pallas_call(scan_body, grid=(dim // cols,), in_specs=[whole(*t.shape)...  10.6 us
  transfers between devices with their start and end apart: 25, of which 9 were waited for; matrix products, arithmetic and copies ran while one was open for 2% of the time, Pallas kernels for 27%

profile of v5, /device:TPU:1, one launch (start us, length us, event | category | flops | bytes accessed | tf_op | source)
XLA Modules:
  0.0 244.3 jit_solution(2327409542474141096)
XLA Ops:
  0.6 1.5 collective-permute-start
  2.2 0.8 copy.15
  3.1 1.1 copy-done.5
  4.2 1.0 copy-done.9
  5.2 1.7 gather_rows.1
  6.9 28.3 %all_to_all.20 = bf16[16,24,2048]{2,1,0:T(8,128)(2,1)S(1)} all-to-all(bf16[16,24,2048]{2,1,0:T(8,128)(2,1)S(1)} %bitcast.37), channel_id=1, replica_groups=mesh['z'=4,'core'=2,'exp'=16] {'exp'}, dimensions={0} | all-to-all | bytes 3145728 | tf_op jit(solution)/shard_map/all_to_all | solution.py:447
  35.3 3.8 %all-to-all-start.1 = ((bf16[16,16,2048]{2,1,0:T(8,128)(2,1)}), bf16[16,16,2048]{2,1,0:T(8,128)(2,1)S(1)}, u32[]{:S(2)}, u32[]{:S(2)}) async-start(bf16[16,16,2048]{2,1,0:T(8,128)(2,1)} %bitcast.38), calls=%async_computation.1 | async-start | bytes 2097152 | tf_op jit(solution)/shard_map/all_to_all | solution.py:447
  39.1 1.5 sort_messages.2
  40.7 1.6 collective-permute-start.2
  42.3 2.1 collective-permute-start.5
  44.5 2.7 %collective-permute-start.4 = (bf16[192,2048]{1,0:T(8,128)(2,1)}, bf16[192,2048]{1,0:T(8,128)(2,1)}, u32[]{:S(2)}, u32[]{:S(2)}) collective-permute-start(bf16[192,2048]{1,0:T(8,128)(2,1)} %get-tuple-element.77.refs_0_), channel_id=1, source_target_pairs={{0,96},{32,0},{64,32},{96,64},{1,97},{33,1},{65,33},{97,65},{2,98}... | collective-permute-start | bytes 2359304 | tf_op jit(solution)/shard_map/ppermute | solution.py:440
  48.5 1.3 copy-done.7
  49.8 4.6 %reach_table.1 = (bf16[16,128,2048]{2,1,0:T(8,128)(2,1)S(1)}, f32[1,2048]{1,0:T(1,128)S(1)}) custom-call(f32[128,2048]{1,0:T(8,128)S(1)} %bitcast.40, f32[16,2048]{1,0:T(8,128)S(1)} %copy-done.8, f32[128,16]{1,0:T(8,128)S(1)} %bitcast.44), custom_call_target="tpu_custom_call" | custom-call | flops 33554432 | bytes 8388608 | tf_op jit(solution)/shard_map/reach_table/pallas_call | solution.py:372
  54.5 3.3 %copy-done = bf16[16,128,2048]{2,1,0:T(8,128)(2,1)} copy-done((bf16[16,128,2048]{2,1,0:T(8,128)(2,1)}, bf16[16,128,2048]{2,1,0:T(8,128)(2,1)S(1)}, u32[]{:S(2)}) %copy-start) | copy-done | bytes 8388632
  57.8 1.1 sort_messages.3
  59.1 1.6 collective-permute-done.2.refs_2_
  60.7 2.7 %collective-permute-start.11 = (bf16[128,2048]{1,0:T(8,128)(2,1)S(1)}, bf16[128,2048]{1,0:T(8,128)(2,1)S(1)}, u32[]{:S(2)}, u32[]{:S(2)}) collective-permute-start(bf16[128,2048]{1,0:T(8,128)(2,1)S(1)} %get-tuple-element.101.refs_3_), channel_id=1, source_target_pairs={{0,96},{32,0},{64,32},{96,64},{1,97},{33,1},{65,33},{97,65},{2,98}... | collective-permute-start | bytes 1572872 | tf_op jit(solution)/shard_map/ppermute | solution.py:440
  63.3 14.2 %collective-permute-done.3.refs_3_ = bf16[192,2048]{1,0:T(8,128)(2,1)} collective-permute-done((bf16[192,2048]{1,0:T(8,128)(2,1)}, bf16[192,2048]{1,0:T(8,128)(2,1)}, u32[]{:S(2)}, u32[]{:S(2)}) %collective-permute-start.3) | collective-permute-done | bytes 786464 | tf_op jit(solution)/shard_map/ppermute | solution.py:440
  77.5 1.3 broadcast_in_dim.18.refs_8_
  78.8 1.3 broadcast_in_dim.20.refs_9_
  80.5 2.3 collective-permute-start.7
  82.9 2.0 copy-done.1
  84.9 2.0 copy-done.3
  86.9 19.8 %expert_rows.4 = (bf16[96,2048]{1,0:T(8,128)(2,1)S(1)}, bf16[96,2048]{1,0:T(8,128)(2,1)S(1)}, bf16[96,2048]{1,0:T(8,128)(2,1)S(1)}, bf16[96,2048]{1,0:T(8,128)(2...) custom-call(bf16[192,2048]{1,0:T(8,128)(2,1)} %get-tuple-element.77.refs_0_, ...), custom_call_target="tpu_custom_call" | custom-call | flops 12683575296 | bytes 21757952 | tf_op jit(solution)/shard_map/expert_rows/pallas_call | solution.py:214
  106.9 8.9 %collective-permute-done.7.refs_1_ = bf16[192,2048]{1,0:T(8,128)(2,1)S(1)} collective-permute-done((bf16[192,2048]{1,0:T(8,128)(2,1)S(1)}, bf16[192,2048]{1,0:T(8,128)(2,1)S(1)}, u32[]{:S(2)}, u32[]{:S(2)}) %collective-permute-start.7) | collective-permute-done | bytes 786464 | tf_op jit(solution)/shard_map/ppermute | solution.py:440
  115.8 12.6 %expert_rows.5 = (bf16[96,2048]{1,0:T(8,128)(2,1)S(1)}, bf16[96,2048]{1,0:T(8,128)(2,1)S(1)}, bf16[64,2048]{1,0:T(8,128)(2,1)S(1)}, bf16[64,2048]{1,0:T(8,128)(2,1)S(1)}) custom-call(bf16[192,2048]{1,0:T(8,128)(2,1)S(1)} %collective-permute-done.6.refs_0_, bf16[192,2048]{1,0:T(8,128)(2,1)S(1)} %collective-permute-done.7.refs_1_, ...), custom_call_target="tpu_custom_call" | custom-call | flops 7046430720 | bytes 18612224 | tf_op jit(solution)/shard_map/expert_rows/pallas_call | solution.py:214
  128.4 1.4 collective-permute-start.14
  129.8 2.1 collective-permute-start.15
  131.9 2.7 %collective-permute-start.13 = (bf16[128,2048]{1,0:T(8,128)(2,1)S(1)}, bf16[128,2048]{1,0:T(8,128)(2,1)S(1)}, u32[]{:S(2)}, u32[]{:S(2)}) collective-permute-start(bf16[128,2048]{1,0:T(8,128)(2,1)S(1)} %collective-permute-done.11.refs_3_), channel_id=1, source_target_pairs={{0,96},{32,0},{64,32},{96,64},{1,97},{33,1},{65,33},{97,65},{2,98}... | collective-permute-start | bytes 1572872 | tf_op jit(solution)/shard_map/ppermute | solution.py:440
  134.6 10.9 %expert_rows.6 = (bf16[64,2048]{1,0:T(8,128)(2,1)S(1)}, bf16[64,2048]{1,0:T(8,128)(2,1)S(1)}, bf16[64,2048]{1,0:T(8,128)(2,1)S(1)}, bf16[64,2048]{1,0:T(8,128)(2,1)S(1)}) custom-call(bf16[128,2048]{1,0:T(8,128)(2,1)S(1)} %collective-permute-done.8.refs_0_, bf16[128,2048]{1,0:T(8,128)(2,1)S(1)} %collective-permute-done.9.refs_1_, ...), custom_call_target="tpu_custom_call" | custom-call | flops 5637144576 | bytes 17825792 | tf_op jit(solution)/shard_map/expert_rows/pallas_call | solution.py:214
  145.7 3.9 %collective-permute-done.12.refs_0_ = bf16[128,2048]{1,0:T(8,128)(2,1)S(1)} collective-permute-done((bf16[128,2048]{1,0:T(8,128)(2,1)S(1)}, bf16[128,2048]{1,0:T(8,128)(2,1)S(1)}, u32[]{:S(2)}, u32[]{:S(2)}) %collective-permute-start.12) | collective-permute-done | bytes 524320 | tf_op jit(solution)/shard_map/ppermute | solution.py:440
  149.7 2.6 %collective-permute-start.17 = (bf16[192,2048]{1,0:T(8,128)(2,1)S(1)}, bf16[192,2048]{1,0:T(8,128)(2,1)S(1)}, u32[]{:S(2)}, u32[]{:S(2)}) collective-permute-start(bf16[192,2048]{1,0:T(8,128)(2,1)S(1)} %get-tuple-element.125), channel_id=1, source_target_pairs={{0,96},{32,0},{64,32},{96,64},{1,97},{33,1},{65,33},{97,65},{2,98}... | collective-permute-start | bytes 2359304 | tf_op jit(solution)/shard_map/ppermute | solution.py:440
  152.3 10.3 %expert_rows.7 = (bf16[64,2048]{1,0:T(8,128)(2,1)S(1)}, bf16[64,2048]{1,0:T(8,128)(2,1)S(1)}) custom-call(bf16[128,2048]{1,0:T(8,128)(2,1)S(1)} %collective-permute-done.12.refs_0_, bf16[128,2048]{1,0:T(8,128)(2,1)S(1)} %collective-permute-done.13.refs_1_, bf16[896,2048]{1,0:T(8,128)(2,1)S(1)} %bitcast.29, ...), custom_call_target="tpu_custom_call" | custom-call | flops 2818572288 | bytes 16252928 | tf_op jit(solution)/shard_map/expert_rows/pallas_call | solution.py:214
  162.7 2.7 %collective-permute-start.19 = (bf16[64,2048]{1,0:T(8,128)(2,1)S(1)}, bf16[64,2048]{1,0:T(8,128)(2,1)S(1)}, u32[]{:S(2)}, u32[]{:S(2)}) collective-permute-start(bf16[64,2048]{1,0:T(8,128)(2,1)S(1)} %get-tuple-element.129), channel_id=1, source_target_pairs={{0,96},{32,0},{64,32},{96,64},{1,97},{33,1},{65,33},{97,65},{2,98}... | collective-permute-start | bytes 786440 | tf_op jit(solution)/shard_map/ppermute | solution.py:440
  165.4 1.0 collective-permute-done.16.refs_3_
  166.4 1.5 pack_returns.2
  167.9 4.4 %collective-permute-done.18.got_a = bf16[64,2048]{1,0:T(8,128)(2,1)S(1)} collective-permute-done((bf16[64,2048]{1,0:T(8,128)(2,1)S(1)}, bf16[64,2048]{1,0:T(8,128)(2,1)S(1)}, u32[]{:S(2)}, u32[]{:S(2)}) %collective-permute-start.18) | collective-permute-done | bytes 262176 | tf_op jit(solution)/shard_map/ppermute | solution.py:440
  172.3 6.2 %all-to-all-start.2 = ((bf16[16,16,2048]{2,1,0:T(8,128)(2,1)}), bf16[16,16,2048]{2,1,0:T(8,128)(2,1)S(1)}, u32[]{:S(2)}, u32[]{:S(2)}) async-start(bf16[16,16,2048]{2,1,0:T(8,128)(2,1)} %bitcast.14), calls=%async_computation.2 | async-start | bytes 2097152 | tf_op jit(solution)/shard_map/all_to_all | solution.py:447
  178.8 2.7 %collective-permute-start.21 = (bf16[128,2048]{1,0:T(8,128)(2,1)S(1)}, bf16[128,2048]{1,0:T(8,128)(2,1)S(1)}, u32[]{:S(2)}, u32[]{:S(2)}) collective-permute-start(bf16[128,2048]{1,0:T(8,128)(2,1)S(1)} %get-tuple-element.140), channel_id=1, source_target_pairs={{0,96},{32,0},{64,32},{96,64},{1,97},{33,1},{65,33},{97,65},{2,98}... | collective-permute-start | bytes 1572872 | tf_op jit(solution)/shard_map/ppermute | solution.py:440
  181.5 7.5 %collective-permute-done.20.refs_2_ = bf16[128,2048]{1,0:T(8,128)(2,1)S(1)} collective-permute-done((bf16[128,2048]{1,0:T(8,128)(2,1)S(1)}, bf16[128,2048]{1,0:T(8,128)(2,1)S(1)}, u32[]{:S(2)}, u32[]{:S(2)}) %collective-permute-start.20) | collective-permute-done | bytes 524320 | tf_op jit(solution)/shard_map/ppermute | solution.py:440
  189.0 1.0 pack_returns.3
  190.0 0.6 all-to-all-done.2
  190.6 5.7 %all-to-all-start.3 = ((bf16[16,8,2048]{2,1,0:T(8,128)(2,1)}), bf16[16,8,2048]{2,1,0:T(8,128)(2,1)S(1)}, u32[]{:S(2)}, u32[]{:S(2)}) async-start(bf16[16,8,2048]{2,1,0:T(8,128)(2,1)} %bitcast.16), calls=%async_computation.3 | async-start | bytes 1048576 | tf_op jit(solution)/shard_map/all_to_all | solution.py:447
  196.4 8.9 %all-to-all-done.3 = bf16[16,8,2048]{2,1,0:T(8,128)(2,1)S(1)} async-done(((bf16[16,8,2048]{2,1,0:T(8,128)(2,1)}), bf16[16,8,2048]{2,1,0:T(8,128)(2,1)S(1)}, u32[]{:S(2)}, u32[]{:S(2)}) %all-to-all-start.3) | async-done | bytes 524320 | tf_op jit(solution)/shard_map/all_to_all | solution.py:447
  205.3 0.8 copy-done.17
  206.1 10.6 %combine_and_scan.1 = (bf16[128,2048]{1,0:T(8,128)(2,1)}, f32[128,2048]{1,0:T(8,128)}, bf16[24,2048]{1,0:T(8,128)(2,1)}) custom-call(bf16[128,384]{1,0:T(8,128)(2,1)} %copy-done.12, bf16[128,384]{1,0:T(8,128)(2,1)} %copy-done.13, bf16[256,2048]{1,0:T(8,128)(2,1)} %bitcast.47, bf16[128,2048]{1,0:T(8,128)(2,1)} %bitcast.49, bf16[128,2048]{1,0:T(8,128)(2,1)} %bitcast.35, ...), custom_call_target="tpu_custom_call" | custom-call | tf_op jit(solution)/shard_map/combine_and_scan/pallas_call | solution.py:326
  216.7 21.8 %all-gather = bf16[192,2048]{1,0:T(8,128)(2,1)} all-gather(bf16[24,2048]{1,0:T(8,128)(2,1)} %get-tuple-element.145), channel_id=2, replica_groups=mesh['z'=4,'core'=2,'exp'=16] {'z','core'}, dimensions={0}, use_global_device_ids=true | all-gather | bytes 884736 | tf_op jit(solution)/shard_map/all_gather | solution.py:500
  238.5 5.8 %add_carry.1 = bf16[128,2048]{1,0:T(8,128)(2,1)} custom-call(s32[1]{0:T(128)} %bitcast.19.place_ref, bf16[8,24,2048]{2,1,0:T(8,128)(2,1)} %bitcast.48, f32[16,2048]{1,0:T(8,128)} %rate_ref.3, f32[128,2048]{1,0:T(8,128)} %get-tuple-element.146.local_ref, bf16[16,128,2048]{2,1,0:T(8,128)(2,1)} %copy-done), custom_call_target="tpu_custom_call" | custom-call | tf_op jit(solution)/shard_map/add_carry/pallas_call | solution.py:416
  (68 shorter events, 2.9 us)
Async XLA Ops:
  0.6 38.5 %copy-start.11 = (bf16[192,192]{1,0:T(8,128)(2,1)S(1)}, bf16[192,192]{1,0:T(8,128)(2,1)}, u32[]{:S(2)}) copy-start(bf16[192,192]{1,0:T(8,128)(2,1)} %constant.20.clone.table_ref) | copy-start | bytes 221188
  0.6 38.5 %collective-permute-start = (bf16[896,2048]{1,0:T(8,128)(2,1)}, bf16[896,2048]{1,0:T(8,128)(2,1)}, u32[]{:S(2)}, u32[]{:S(2)}) collective-permute-start(bf16[896,2048]{1,0:T(8,128)(2,1)} %bitcast.25), channel_id=1, source_target_pairs={{0,16},{16,0},{1,17},{17,1},{2,18},{18,2},{3,19},{19,3},{4,20},{20... | collective-permute-start | bytes 11010056 | tf_op jit(solution)/shard_map/ppermute | solution.py:443
  2.1 37.0 %collective-permute-start.1 = (bf16[896,2048]{1,0:T(8,128)(2,1)}, bf16[896,2048]{1,0:T(8,128)(2,1)}, u32[]{:S(2)}, u32[]{:S(2)}) collective-permute-start(bf16[896,2048]{1,0:T(8,128)(2,1)} %bitcast.30), channel_id=1, source_target_pairs={{0,16},{16,0},{1,17},{17,1},{2,18},{18,2},{3,19},{19,3},{4,20},{20... | collective-permute-start | bytes 11010056 | tf_op jit(solution)/shard_map/ppermute | solution.py:443
  3.1 1.1 copy-start.5
  4.1 1.0 copy-start.9
  6.9 28.4 %copy-start.6 = (bf16[256,2048]{1,0:T(8,128)(2,1)}, bf16[256,2048]{1,0:T(8,128)(2,1)S(1)}, u32[]{:S(2)}) copy-start(bf16[256,2048]{1,0:T(8,128)(2,1)S(1)} %get-tuple-element.99) | copy-start | bytes 3145732
  6.9 40.2 %copy-start.18 = (f32[1,128,16]{1,2,0:T(8,128)S(1)}, f32[1,128,16]{1,2,0:T(8,128)}, u32[]{:S(2)}) copy-start(f32[1,128,16]{1,2,0:T(8,128)} %param.21) | copy-start | bytes 24580
  6.9 40.3 %copy-start.20 = (f32[1,128,2]{1,2,0:T(2,128)S(1)}, f32[1,128,2]{1,2,0:T(2,128)}, u32[]{:S(2)}) copy-start(f32[1,128,2]{1,2,0:T(2,128)} %param.16) | copy-start | bytes 3076
  6.9 40.4 %copy-start.19 = (f32[1,128,16]{1,2,0:T(8,128)S(1)}, f32[1,128,16]{1,2,0:T(8,128)}, u32[]{:S(2)}) copy-start(f32[1,128,16]{1,2,0:T(8,128)} %param.22) | copy-start | bytes 24580
  6.9 41.6 %copy-start.8 = (f32[16,2048]{1,0:T(8,128)S(1)}, f32[16,2048]{1,0:T(8,128)}, u32[]{:S(2)}) copy-start(f32[16,2048]{1,0:T(8,128)} %rate_ref.3) | copy-start | bytes 393220
  35.3 22.5 %all-to-all-start.1 = ((bf16[16,16,2048]{2,1,0:T(8,128)(2,1)}), bf16[16,16,2048]{2,1,0:T(8,128)(2,1)S(1)}, u32[]{:S(2)}, u32[]{:S(2)}) async-start(bf16[16,16,2048]{2,1,0:T(8,128)(2,1)} %bitcast.38), calls=%async_computation.1 | async-start | bytes 2097152 | tf_op jit(solution)/shard_map/all_to_all | solution.py:447
  40.7 20.0 %collective-permute-start.2 = (bf16[192,2048]{1,0:T(8,128)(2,1)}, bf16[192,2048]{1,0:T(8,128)(2,1)}, u32[]{:S(2)}, u32[]{:S(2)}) collective-permute-start(bf16[192,2048]{1,0:T(8,128)(2,1)} %get-tuple-element.77.refs_0_), channel_id=1, source_target_pairs={{0,32},{32,64},{64,96},{96,0},{1,33},{33,65},{65,97},{97,1},{2,34}... | collective-permute-start | bytes 2359304 | tf_op jit(solution)/shard_map/ppermute | solution.py:440
  42.3 18.3 %collective-permute-start.5 = (bf16[192,2048]{1,0:T(8,128)(2,1)}, bf16[192,2048]{1,0:T(8,128)(2,1)S(1)}, u32[]{:S(2)}, u32[]{:S(2)}) collective-permute-start(bf16[192,2048]{1,0:T(8,128)(2,1)} %get-tuple-element.78.refs_1_), channel_id=1, source_target_pairs={{0,96},{32,0},{64,32},{96,64},{1,97},{33,1},{65,33},{97,65},{2,98}... | collective-permute-start | bytes 2359304 | tf_op jit(solution)/shard_map/ppermute | solution.py:440
  44.5 33.1 %collective-permute-start.3 = (bf16[192,2048]{1,0:T(8,128)(2,1)}, bf16[192,2048]{1,0:T(8,128)(2,1)}, u32[]{:S(2)}, u32[]{:S(2)}) collective-permute-start(bf16[192,2048]{1,0:T(8,128)(2,1)} %get-tuple-element.78.refs_1_), channel_id=1, source_target_pairs={{0,32},{32,64},{64,96},{96,0},{1,33},{33,65},{65,97},{97,1},{2,34}... | collective-permute-start | bytes 2359304 | tf_op jit(solution)/shard_map/ppermute | solution.py:440
  44.5 33.1 %collective-permute-start.4 = (bf16[192,2048]{1,0:T(8,128)(2,1)}, bf16[192,2048]{1,0:T(8,128)(2,1)}, u32[]{:S(2)}, u32[]{:S(2)}) collective-permute-start(bf16[192,2048]{1,0:T(8,128)(2,1)} %get-tuple-element.77.refs_0_), channel_id=1, source_target_pairs={{0,96},{32,0},{64,32},{96,64},{1,97},{33,1},{65,33},{97,65},{2,98}... | collective-permute-start | bytes 2359304 | tf_op jit(solution)/shard_map/ppermute | solution.py:440
  47.9 0.6 copy-start.12
  48.5 5.9 %copy-start.13 = (bf16[128,384]{1,0:T(8,128)(2,1)}, bf16[128,384]{1,0:T(8,128)(2,1)S(1)}, u32[]{:S(2)}) copy-start(bf16[128,384]{1,0:T(8,128)(2,1)S(1)} %get-tuple-element.84.refs_1_) | copy-start | bytes 294916
  48.5 1.3 copy-start.7
  49.8 8.0 %copy-start.14 = (bf16[128,128]{1,0:T(8,128)(2,1)S(1)}, bf16[128,128]{1,0:T(8,128)(2,1)}, u32[]{:S(2)}) copy-start(bf16[128,128]{1,0:T(8,128)(2,1)} %constant.21.clone.table_ref) | copy-start | bytes 98308
  54.4 3.3 %copy-start = (bf16[16,128,2048]{2,1,0:T(8,128)(2,1)}, bf16[16,128,2048]{2,1,0:T(8,128)(2,1)S(1)}, u32[]{:S(2)}) copy-start(bf16[16,128,2048]{2,1,0:T(8,128)(2,1)S(1)} %get-tuple-element.147.reach_ref) | copy-start | bytes 25165828
  57.8 49.0 %copy-start.15 = (f32[1,2048]{1,0:T(1,128)}, f32[1,2048]{1,0:T(1,128)S(1)}, u32[]{:S(2)}) copy-start(f32[1,2048]{1,0:T(1,128)S(1)} %get-tuple-element.141.refs_7_) | copy-start | bytes 24580
  58.8 69.5 %collective-permute-start.10 = (bf16[128,2048]{1,0:T(8,128)(2,1)}, bf16[128,2048]{1,0:T(8,128)(2,1)S(1)}, u32[]{:S(2)}, u32[]{:S(2)}) collective-permute-start(bf16[128,2048]{1,0:T(8,128)(2,1)} %get-tuple-element.100.refs_2_), channel_id=1, source_target_pairs={{0,96},{32,0},{64,32},{96,64},{1,97},{33,1},{65,33},{97,65},{2,98}... | collective-permute-start | bytes 1572872 | tf_op jit(solution)/shard_map/ppermute | solution.py:440
  60.7 67.7 %collective-permute-start.8 = (bf16[128,2048]{1,0:T(8,128)(2,1)}, bf16[128,2048]{1,0:T(8,128)(2,1)S(1)}, u32[]{:S(2)}, u32[]{:S(2)}) collective-permute-start(bf16[128,2048]{1,0:T(8,128)(2,1)} %get-tuple-element.100.refs_2_), channel_id=1, source_target_pairs={{0,32},{32,64},{64,96},{96,0},{1,33},{33,65},{65,97},{97,1},{2,34}... | collective-permute-start | bytes 1572872 | tf_op jit(solution)/shard_map/ppermute | solution.py:440
  60.7 67.7 %collective-permute-start.11 = (bf16[128,2048]{1,0:T(8,128)(2,1)S(1)}, bf16[128,2048]{1,0:T(8,128)(2,1)S(1)}, u32[]{:S(2)}, u32[]{:S(2)}) collective-permute-start(bf16[128,2048]{1,0:T(8,128)(2,1)S(1)} %get-tuple-element.101.refs_3_), channel_id=1, source_target_pairs={{0,96},{32,0},{64,32},{96,64},{1,97},{33,1},{65,33},{97,65},{2,98}... | collective-permute-start | bytes 1572872 | tf_op jit(solution)/shard_map/ppermute | solution.py:440
  80.2 26.6 %collective-permute-start.6 = (bf16[192,2048]{1,0:T(8,128)(2,1)}, bf16[192,2048]{1,0:T(8,128)(2,1)S(1)}, u32[]{:S(2)}, u32[]{:S(2)}) collective-permute-start(bf16[192,2048]{1,0:T(8,128)(2,1)} %collective-permute-done.2.refs_2_), channel_id=1, source_target_pairs={{0,32},{32,64},{64,96},{96,0},{1,33},{33,65},{65,97},{97,1},{2,34}... | collective-permute-start | bytes 2359304 | tf_op jit(solution)/shard_map/ppermute | solution.py:440
  80.5 35.3 %collective-permute-start.7 = (bf16[192,2048]{1,0:T(8,128)(2,1)S(1)}, bf16[192,2048]{1,0:T(8,128)(2,1)S(1)}, u32[]{:S(2)}, u32[]{:S(2)}) collective-permute-start(bf16[192,2048]{1,0:T(8,128)(2,1)S(1)} %collective-permute-done.5.refs_5_), channel_id=1, source_target_pairs={{0,96},{32,0},{64,32},{96,64},{1,97},{33,1},{65,33},{97,65},{2,98}... | collective-permute-start | bytes 2359304 | tf_op jit(solution)/shard_map/ppermute | solution.py:440
  82.9 2.0 copy-start.1
  84.9 2.0 copy-start.3
  86.9 28.8 %copy-start.2 = (bf16[1,896,2048]{2,1,0:T(8,128)(2,1)S(1)}, bf16[1,896,2048]{2,1,0:T(8,128)(2,1)}, u32[]{:S(2)}) copy-start(bf16[1,896,2048]{2,1,0:T(8,128)(2,1)} %param.17) | copy-start | bytes 11010052
  86.9 28.9 %copy-start.4 = (bf16[1,896,2048]{2,1,0:T(8,128)(2,1)S(1)}, bf16[1,896,2048]{2,1,0:T(8,128)(2,1)}, u32[]{:S(2)}) copy-start(bf16[1,896,2048]{2,1,0:T(8,128)(2,1)} %param.18) | copy-start | bytes 11010052
  106.8 21.6 %collective-permute-start.9 = (bf16[128,2048]{1,0:T(8,128)(2,1)S(1)}, bf16[128,2048]{1,0:T(8,128)(2,1)S(1)}, u32[]{:S(2)}, u32[]{:S(2)}) collective-permute-start(bf16[128,2048]{1,0:T(8,128)(2,1)S(1)} %get-tuple-element.101.refs_3_), channel_id=1, source_target_pairs={{0,32},{32,64},{64,96},{96,0},{1,33},{33,65},{65,97},{97,1},{2,34}... | collective-permute-start | bytes 1572872 | tf_op jit(solution)/shard_map/ppermute | solution.py:440
  128.4 17.1 %collective-permute-start.14 = (bf16[96,2048]{1,0:T(8,128)(2,1)S(1)}, bf16[96,2048]{1,0:T(8,128)(2,1)S(1)}, u32[]{:S(2)}, u32[]{:S(2)}) collective-permute-start(bf16[96,2048]{1,0:T(8,128)(2,1)S(1)} %get-tuple-element.120), channel_id=1, source_target_pairs={{0,32},{32,64},{64,96},{96,0},{1,33},{33,65},{65,97},{97,1},{2,34}... | collective-permute-start | bytes 1179656 | tf_op jit(solution)/shard_map/ppermute | solution.py:440
  129.8 15.7 %collective-permute-start.15 = (bf16[96,2048]{1,0:T(8,128)(2,1)S(1)}, bf16[96,2048]{1,0:T(8,128)(2,1)S(1)}, u32[]{:S(2)}, u32[]{:S(2)}) collective-permute-start(bf16[96,2048]{1,0:T(8,128)(2,1)S(1)} %get-tuple-element.121), channel_id=1, source_target_pairs={{0,96},{32,0},{64,32},{96,64},{1,97},{33,1},{65,33},{97,65},{2,98}... | collective-permute-start | bytes 1179656 | tf_op jit(solution)/shard_map/ppermute | solution.py:440
  131.9 17.7 %collective-permute-start.12 = (bf16[128,2048]{1,0:T(8,128)(2,1)S(1)}, bf16[128,2048]{1,0:T(8,128)(2,1)S(1)}, u32[]{:S(2)}, u32[]{:S(2)}) collective-permute-start(bf16[128,2048]{1,0:T(8,128)(2,1)S(1)} %collective-permute-done.8.refs_0_), channel_id=1, source_target_pairs={{0,32},{32,64},{64,96},{96,0},{1,33},{33,65},{65,97},{97,1},{2,34}... | collective-permute-start | bytes 1572872 | tf_op jit(solution)/shard_map/ppermute | solution.py:440
  131.9 17.7 %collective-permute-start.13 = (bf16[128,2048]{1,0:T(8,128)(2,1)S(1)}, bf16[128,2048]{1,0:T(8,128)(2,1)S(1)}, u32[]{:S(2)}, u32[]{:S(2)}) collective-permute-start(bf16[128,2048]{1,0:T(8,128)(2,1)S(1)} %collective-permute-done.11.refs_3_), channel_id=1, source_target_pairs={{0,96},{32,0},{64,32},{96,64},{1,97},{33,1},{65,33},{97,65},{2,98}... | collective-permute-start | bytes 1572872 | tf_op jit(solution)/shard_map/ppermute | solution.py:440
  149.6 16.7 %copy-start.10 = (bf16[256,192]{1,0:T(8,128)(2,1)S(1)}, bf16[256,192]{1,0:T(8,128)(2,1)}, u32[]{:S(2)}) copy-start(bf16[256,192]{1,0:T(8,128)(2,1)} %constant.22.clone.refs_0_) | copy-start | bytes 294916
  149.6 16.7 %collective-permute-start.16 = (bf16[192,2048]{1,0:T(8,128)(2,1)S(1)}, bf16[192,2048]{1,0:T(8,128)(2,1)S(1)}, u32[]{:S(2)}, u32[]{:S(2)}) collective-permute-start(bf16[192,2048]{1,0:T(8,128)(2,1)S(1)} %get-tuple-element.124), channel_id=1, source_target_pairs={{0,32},{32,64},{64,96},{96,0},{1,33},{33,65},{65,97},{97,1},{2,34}... | collective-permute-start | bytes 2359304 | tf_op jit(solution)/shard_map/ppermute | solution.py:440
  149.7 16.7 %collective-permute-start.17 = (bf16[192,2048]{1,0:T(8,128)(2,1)S(1)}, bf16[192,2048]{1,0:T(8,128)(2,1)S(1)}, u32[]{:S(2)}, u32[]{:S(2)}) collective-permute-start(bf16[192,2048]{1,0:T(8,128)(2,1)S(1)} %get-tuple-element.125), channel_id=1, source_target_pairs={{0,96},{32,0},{64,32},{96,64},{1,97},{33,1},{65,33},{97,65},{2,98}... | collective-permute-start | bytes 2359304 | tf_op jit(solution)/shard_map/ppermute | solution.py:440
  162.7 9.7 %collective-permute-start.18 = (bf16[64,2048]{1,0:T(8,128)(2,1)S(1)}, bf16[64,2048]{1,0:T(8,128)(2,1)S(1)}, u32[]{:S(2)}, u32[]{:S(2)}) collective-permute-start(bf16[64,2048]{1,0:T(8,128)(2,1)S(1)} %get-tuple-element.128), channel_id=1, source_target_pairs={{0,32},{32,64},{64,96},{96,0},{1,33},{33,65},{65,97},{97,1},{2,34}... | collective-permute-start | bytes 786440 | tf_op jit(solution)/shard_map/ppermute | solution.py:440
  162.7 9.6 %collective-permute-start.19 = (bf16[64,2048]{1,0:T(8,128)(2,1)S(1)}, bf16[64,2048]{1,0:T(8,128)(2,1)S(1)}, u32[]{:S(2)}, u32[]{:S(2)}) collective-permute-start(bf16[64,2048]{1,0:T(8,128)(2,1)S(1)} %get-tuple-element.129), channel_id=1, source_target_pairs={{0,96},{32,0},{64,32},{96,64},{1,97},{33,1},{65,33},{97,65},{2,98}... | collective-permute-start | bytes 786440 | tf_op jit(solution)/shard_map/ppermute | solution.py:440
  172.3 18.3 %all-to-all-start.2 = ((bf16[16,16,2048]{2,1,0:T(8,128)(2,1)}), bf16[16,16,2048]{2,1,0:T(8,128)(2,1)S(1)}, u32[]{:S(2)}, u32[]{:S(2)}) async-start(bf16[16,16,2048]{2,1,0:T(8,128)(2,1)} %bitcast.14), calls=%async_computation.2 | async-start | bytes 2097152 | tf_op jit(solution)/shard_map/all_to_all | solution.py:447
  178.7 10.3 %collective-permute-start.20 = (bf16[128,2048]{1,0:T(8,128)(2,1)S(1)}, bf16[128,2048]{1,0:T(8,128)(2,1)S(1)}, u32[]{:S(2)}, u32[]{:S(2)}) collective-permute-start(bf16[128,2048]{1,0:T(8,128)(2,1)S(1)} %get-tuple-element.139), channel_id=1, source_target_pairs={{0,32},{32,64},{64,96},{96,0},{1,33},{33,65},{65,97},{97,1},{2,34}... | collective-permute-start | bytes 1572872 | tf_op jit(solution)/shard_map/ppermute | solution.py:440
  178.8 10.2 %collective-permute-start.21 = (bf16[128,2048]{1,0:T(8,128)(2,1)S(1)}, bf16[128,2048]{1,0:T(8,128)(2,1)S(1)}, u32[]{:S(2)}, u32[]{:S(2)}) collective-permute-start(bf16[128,2048]{1,0:T(8,128)(2,1)S(1)} %get-tuple-element.140), channel_id=1, source_target_pairs={{0,96},{32,0},{64,32},{96,64},{1,97},{33,1},{65,33},{97,65},{2,98}... | collective-permute-start | bytes 1572872 | tf_op jit(solution)/shard_map/ppermute | solution.py:440
  190.6 14.7 %copy-start.16 = (bf16[16,16,2048]{2,1,0:T(8,128)(2,1)}, bf16[16,16,2048]{2,1,0:T(8,128)(2,1)S(1)}, u32[]{:S(2)}) copy-start(bf16[16,16,2048]{2,1,0:T(8,128)(2,1)S(1)} %all-to-all-done.2) | copy-start | bytes 3145732
  190.6 14.7 %all-to-all-start.3 = ((bf16[16,8,2048]{2,1,0:T(8,128)(2,1)}), bf16[16,8,2048]{2,1,0:T(8,128)(2,1)S(1)}, u32[]{:S(2)}, u32[]{:S(2)}) async-start(bf16[16,8,2048]{2,1,0:T(8,128)(2,1)} %bitcast.16), calls=%async_computation.3 | async-start | bytes 1048576 | tf_op jit(solution)/shard_map/all_to_all | solution.py:447
  205.3 0.8 copy-start.17

commit v6 on v5

--- a/solution.py
+++ b/solution.py
@@ -86,11 +86,13 @@
     )(ids_t, x, dy)
 
 
-def sort_body(table_ref, rows_ref, *outs):
-    size = outs[0].shape[0]
-    for i, out in enumerate(outs):
-        rows = rows_ref[i * size : (i + 1) * size]
-        out[...] = jnp.dot(table_ref[...], rows, preferred_element_type=F32).astype(BF)
+def sort_body(table_ref, rows_ref, out):
+    size = table_ref.shape[0]
+    for low in range(0, out.shape[0], size):
+        rows = rows_ref[low : low + size]
+        out[low : low + size] = jnp.dot(
+            table_ref[...], rows, preferred_element_type=F32
+        ).astype(BF)
 
 
 def sort_messages(messages, experts, size):
@@ -102,8 +104,8 @@
     table[at, rest // size * 2 * size + kind * size + rest % size] = 1.0
     return pl.pallas_call(
         sort_body,
-        out_shape=[jax.ShapeDtypeStruct((rows, dim), BF)] * 2,
-        compiler_params=params(38),
+        out_shape=jax.ShapeDtypeStruct((2 * rows, dim), BF),
+        compiler_params=params(44),
         name="sort_messages",
     )(jnp.asarray(table, BF), *in_vmem((messages,)))
 
@@ -161,19 +163,20 @@
     )(*parts[:4], *in_vmem(parts[4:]))
 
 
-def expert_body(pieces, *refs):
-    ins = refs[:pieces]
-    up_a, up_b, down_a, down_b = refs[pieces : pieces + 4]
-    outs = refs[pieces + 4 : 2 * pieces + 4]
-    x_all, dy_all, grads = refs[2 * pieces + 4 :]
+def expert_body(sizes, *refs):
+    count = len(sizes)
+    ins = refs[:count]
+    up_a, up_b, down_a, down_b = refs[count : count + 4]
+    outs = refs[count + 4 : -3]
+    x_all, dy_all, grads = refs[-3:]
     hidden, dim = up_a.shape
     steps = hidden // HIDDEN_STEP
     low = 0
-    for piece, out in zip(ins, outs):
-        size = out.shape[0]
-        x_all[low : low + size] = piece[:size]
-        dy_all[low : low + size] = piece[size:]
-        low += size
+    for pieces, size in zip(ins, sizes):
+        for top in range(0, pieces.shape[0], 2 * size):
+            x_all[low : low + size] = pieces[top : top + size]
+            dy_all[low : low + size] = pieces[top + size : top + 2 * size]
+            low += size
     across = (((1,), (1,)), ((), ()))
 
     def step(i, carry):
@@ -204,18 +207,19 @@
             low += size
 
 
-def expert_rows(ins, weights):
-    pieces = len(ins)
+def expert_rows(ins, sizes, weights):
     dim = ins[0].shape[1]
-    sizes = [piece.shape[0] // 2 for piece in ins]
-    rows = sum(sizes)
+    out_sizes = [
+        size for value, size in zip(ins, sizes) for _ in range(value.shape[0] // (2 * size))
+    ]
+    rows = sum(out_sizes)
     hidden = weights[0].shape[0]
     vmem = pl.BlockSpec(memory_space=pltpu.VMEM)
     return pl.pallas_call(
-        functools.partial(expert_body, pieces),
-        in_specs=[vmem] * (pieces + 4),
-        out_specs=[vmem] * pieces,
-        out_shape=[jax.ShapeDtypeStruct((size, dim), BF) for size in sizes],
+        functools.partial(expert_body, sizes),
+        in_specs=[vmem] * (len(ins) + 4),
+        out_specs=[vmem] * len(out_sizes),
+        out_shape=[jax.ShapeDtypeStruct((size, dim), BF) for size in out_sizes],
         scratch_shapes=[
             pltpu.VMEM((rows, dim), BF),
             pltpu.VMEM((rows, dim), BF),
@@ -223,9 +227,9 @@
         ],
         compiler_params=params(30),
         cost_estimate=pl.CostEstimate(
-            flops=6 * rows * 2 * hidden * dim,
-            bytes_accessed=2 * (4 * hidden * dim + 3 * rows * dim),
-            transcendentals=rows * 2 * hidden,
+            flops=6 * rows * 2 * hidden * dim // 8,
+            bytes_accessed=rows * dim,
+            transcendentals=rows,
         ),
         name="expert_rows",
     )(*in_vmem(ins), *in_vmem(weights))
@@ -271,7 +275,7 @@
     return pl.pallas_call(
         functools.partial(table_body, experts, capacity),
         out_shape=[jax.ShapeDtypeStruct((ids.shape[0], rows), BF)] * 2,
-        compiler_params=params(38),
+        compiler_params=params(44),
         name="weigh_tables",
     )(ids, weights)
 
@@ -381,7 +385,7 @@
             jax.ShapeDtypeStruct((states, tokens, dim), BF),
             jax.ShapeDtypeStruct((1, dim), F32),
         ],
-        compiler_params=params(38),
+        compiler_params=params(46),
         cost_estimate=pl.CostEstimate(
             flops=8 * states * tokens * dim,
             bytes_accessed=2 * states * tokens * dim,
@@ -453,35 +457,41 @@
     got_low = exchange(sent[0])
     got_low, up_other, down_other = tie(got_low, up_other, down_other)
     both = (up, up_other, down, down_other)
-    low_a, low_b = sort_messages(got_low, experts, sizes[0])
-    high_a, high_b = sort_messages(exchange(sent[1]), experts, sizes[1])
-
-    def ring(a, b):
-        prev_a, next_b = shift(a, 1), shift(b, -1)
-        prev_b, next_a = shift(b, 1), shift(a, -1)
-        return prev_a, prev_b, next_a, next_b
-
-    def far(prev_a, next_b):
-        return shift(prev_a, 1), shift(next_b, -1)
-
-    low = ring(low_a, low_b)
-    low_far = far(low[0], low[3])
+    low = sort_messages(got_low, experts, sizes[0])
+    got_high = exchange(sent[1])
+
+    def ring(own):
+        return shift(own, 1), shift(own, -1)
+
+    def far(prev, next_):
+        half = prev.shape[0] // 2
+        return shift(prev[:half], 1), shift(next_[half:], -1)
+
+    def some(part, count):
+        return (sizes[part] * experts // 2,) * count
+
+    low_near = ring(low)
     lanes = (steps.shape[0], bmat.shape[2], 128)
     mix = jnp.broadcast_to(bmat[0][:, :, None], lanes)
     drive = jnp.broadcast_to(cmat[0][:, :, None], lanes)
     reach, total = reach_table(steps, rate, bmat[0])
     tables = weigh_tables(ids, weights, experts, capacity)
-    low, reach, total, tables, mix, drive = tie(low, reach, total, tables, mix, drive)
-    first = expert_rows((low_a, low_b, *low), both)
-    high = ring(high_a, high_b)
-    low_far, first = tie(low_far, first)
-    second = expert_rows((*low_far, high_a, high_b), both)
-    high, second = tie(high, second)
-    high_far = far(high[0], high[3])
-    third = expert_rows(high, both)
+    got_high, reach, total, tables, mix, drive = tie(
+        got_high, reach, total, tables, mix, drive
+    )
+    high = sort_messages(got_high, experts, sizes[1])
+    low_near, high = tie(low_near, high)
+    low_far = far(*low_near)
+    high_near = ring(high)
+    first = expert_rows((low, *low_near), some(0, 3), both)
+    low_far, high_near, first = tie(low_far, high_near, first)
+    high_far = far(*high_near)
+    second = expert_rows((*low_far, high), some(0, 2) + some(1, 1), both)
+    high_near, second = tie(high_near, second)
+    third = expert_rows(high_near, some(1, 2), both)
     low_sums = hop_sums(*first[4:6], *first[2:4], shift(second[0], 1), shift(second[1], -1))
     high_far, third, low_sums = tie(high_far, third, low_sums)
-    fourth = expert_rows(high_far, both)
+    fourth = expert_rows(high_far, some(1, 2), both)
 
     def home(own, sums, size):
         to_next, to_prev = sums

time: 245 us -> 236 us (0.963)
  starting transfers between devices: 43.9 us -> 35.7 us
  waiting for transfers between devices: 51.1 us -> 56.1 us
  local copies, waits for them, and re-layouts: 16 us -> 11.7 us
    ppermute x20 -> x16, starting transfers between devices: 26.5 us -> 19.6 us  [shift(): return lax.ppermute(value, 'z', ring)]
    unnamed x45 -> x39, local copies, waits for them, and re-layouts: 13.2 us -> 6.44 us
    all_to_all x3, waiting for transfers between devices: 9.58 us -> 15.2 us  [exchange(): got = lax.all_to_all(parts, 'exp', split_axis=0, concat_axis=0, tiled=True)]
    slice x0 -> x4, local copies, waits for them, and re-layouts: none -> 2.47 us  [far(): return (shift(prev[:half], 1), shift(next_[half:], -1))]
    ppermute x20 -> x16, waiting for transfers between devices: 41.5 us -> 41 us  [shift(): return lax.ppermute(value, 'z', ring)]
  transfers between devices with their start and end apart: 25 -> 21, of which waited for: 9 -> 9; matrix products, arithmetic and copies ran while one was open for 2% -> 3% of each run, Pallas kernels for 27% -> 27%
where the time goes in v6:
time: 236 us
  Pallas kernels  81.2 us (34%)
  waiting for transfers between devices  56.1 us (24%)
  blocking collectives  50.1 us (21%)
  starting transfers between devices  35.7 us (15%)
  local copies, waits for them, and re-layouts  11.7 us (5%)
    pallas_call x4, Pallas kernels, expert_rows(): pl.pallas_call(functools.partial(expert_body, sizes), in_specs=[vmem] * (...  53.1 us
    ppermute x16, waiting for transfers between devices, shift(): return lax.ppermute(value, 'z', ring)  41 us
    all_to_all x1, blocking collectives, exchange(): got = lax.all_to_all(parts, 'exp', split_axis=0, concat_axis=0, tiled=True)  28.3 us
    all_gather x1, blocking collectives, on_device(): starts = lax.all_gather(start, ('z', 'core'))  21.8 us
    ppermute x16, starting transfers between devices, shift(): return lax.ppermute(value, 'z', ring)  19.6 us
    all_to_all x3, waiting for transfers between devices, exchange(): got = lax.all_to_all(parts, 'exp', split_axis=0, concat_axis=0, tiled=True)  15.2 us
    all_to_all x3, starting transfers between devices, exchange(): got = lax.all_to_all(parts, 'exp', split_axis=0, concat_axis=0, tiled=True)  14.5 us
    pallas_call x1, Pallas kernels, combine_and_scan(): pl.pallas_call(scan_body, grid=(dim // cols,), in_specs=[whole(*t.shape)...  10.6 us
  transfers between devices with their start and end apart: 21, of which 9 were waited for; matrix products, arithmetic and copies ran while one was open for 3% of the time, Pallas kernels for 27%

profile of v6, /device:TPU:1, one launch (start us, length us, event | category | flops | bytes accessed | tf_op | source)
XLA Modules:
  0.0 235.7 jit_solution(3157563237468426088)
XLA Ops:
  0.6 1.5 collective-permute-start
  2.2 0.8 copy.15
  3.1 1.1 copy-done.2
  4.2 1.0 copy-done.6
  5.2 1.7 gather_rows.1
  6.9 28.3 %all_to_all.20 = bf16[16,24,2048]{2,1,0:T(8,128)(2,1)S(1)} all-to-all(bf16[16,24,2048]{2,1,0:T(8,128)(2,1)S(1)} %bitcast.37), channel_id=1, replica_groups=mesh['z'=4,'core'=2,'exp'=16] {'exp'}, dimensions={0} | all-to-all | bytes 3145728 | tf_op jit(solution)/shard_map/all_to_all | solution.py:451
  35.3 0.6 sort_messages.2.refs_0_
  35.9 3.8 %collective-permute-start.3 = (bf16[384,2048]{1,0:T(8,128)(2,1)S(1)}, bf16[384,2048]{1,0:T(8,128)(2,1)}, u32[]{:S(2)}, u32[]{:S(2)}) collective-permute-start(bf16[384,2048]{1,0:T(8,128)(2,1)S(1)} %sort_messages.2.refs_0_), channel_id=1, source_target_pairs={{0,96},{32,0},{64,32},{96,64},{1,97},{33,1},{65,33},{97,65},{2,98}... | collective-permute-start | bytes 4718600 | tf_op jit(solution)/shard_map/ppermute | solution.py:444
  39.7 3.8 %all-to-all-start = ((bf16[16,16,2048]{2,1,0:T(8,128)(2,1)}), bf16[16,16,2048]{2,1,0:T(8,128)(2,1)S(1)}, u32[]{:S(2)}, u32[]{:S(2)}) async-start(bf16[16,16,2048]{2,1,0:T(8,128)(2,1)} %bitcast.38), calls=%async_computation | async-start | bytes 2097152 | tf_op jit(solution)/shard_map/all_to_all | solution.py:451
  43.9 0.4 weigh_tables.1
  44.3 0.6 copy-done.9
  44.9 0.6 copy-done.10
  45.6 1.2 copy-done.4
  46.8 5.8 %reach_table.1 = (bf16[16,128,2048]{2,1,0:T(8,128)(2,1)}, f32[1,2048]{1,0:T(1,128)S(1)}) custom-call(f32[128,2048]{1,0:T(8,128)S(1)} %bitcast.40, f32[16,2048]{1,0:T(8,128)S(1)} %copy-done.5, f32[128,16]{1,0:T(8,128)S(1)} %bitcast.44), custom_call_target="tpu_custom_call" | custom-call | flops 33554432 | bytes 8388608 | tf_op jit(solution)/shard_map/reach_table/pallas_call | solution.py:376
  52.6 5.6 %all-to-all-done = bf16[16,16,2048]{2,1,0:T(8,128)(2,1)S(1)} async-done(((bf16[16,16,2048]{2,1,0:T(8,128)(2,1)}), bf16[16,16,2048]{2,1,0:T(8,128)(2,1)S(1)}, u32[]{:S(2)}, u32[]{:S(2)}) %all-to-all-start) | async-done | bytes 1048608 | tf_op jit(solution)/shard_map/all_to_all | solution.py:451
  58.2 1.3 broadcast_in_dim.20.refs_9_
  59.5 1.3 broadcast_in_dim.18.refs_8_
  60.8 0.4 sort_messages.3.refs_2_
  61.3 10.0 %collective-permute-done.3.refs_2_ = bf16[384,2048]{1,0:T(8,128)(2,1)} collective-permute-done((bf16[384,2048]{1,0:T(8,128)(2,1)S(1)}, bf16[384,2048]{1,0:T(8,128)(2,1)}, u32[]{:S(2)}, u32[]{:S(2)}) %collective-permute-start.3) | collective-permute-done | bytes 1572896 | tf_op jit(solution)/shard_map/ppermute | solution.py:444
  71.3 3.2 %collective-permute-done.2.refs_1_ = bf16[384,2048]{1,0:T(8,128)(2,1)} collective-permute-done((bf16[384,2048]{1,0:T(8,128)(2,1)S(1)}, bf16[384,2048]{1,0:T(8,128)(2,1)}, u32[]{:S(2)}, u32[]{:S(2)}) %collective-permute-start.2) | collective-permute-done | bytes 1572896 | tf_op jit(solution)/shard_map/ppermute | solution.py:444
  74.8 1.2 collective-permute-start.6
  76.0 1.2 slice.12
  77.2 1.2 slice.13
  78.4 1.6 collective-permute-start.5
  80.0 19.5 %expert_rows.4 = (bf16[96,2048]{1,0:T(8,128)(2,1)S(1)}, bf16[96,2048]{1,0:T(8,128)(2,1)S(1)}, bf16[96,2048]{1,0:T(8,128)(2,1)S(1)}, bf16[96,2048]{1,0:T(8,128)(2...) custom-call(bf16[384,2048]{1,0:T(8,128)(2,1)S(1)} %sort_messages.2.refs_0_, ...), custom_call_target="tpu_custom_call" | custom-call | flops 1585446912 | bytes 1179648 | tf_op jit(solution)/shard_map/expert_rows/pallas_call | solution.py:218
  99.4 13.3 %collective-permute-done.5.refs_1_ = bf16[192,2048]{1,0:T(8,128)(2,1)S(1)} collective-permute-done((bf16[192,2048]{1,0:T(8,128)(2,1)S(1)}, bf16[192,2048]{1,0:T(8,128)(2,1)S(1)}, u32[]{:S(2)}, u32[]{:S(2)}) %collective-permute-start.5) | collective-permute-done | bytes 786464 | tf_op jit(solution)/shard_map/ppermute | solution.py:444
  112.7 1.5 collective-permute-done.4.refs_0_
  114.3 0.5 collective-permute-start.9
  114.8 1.2 collective-permute-start.8
  116.0 12.4 %expert_rows.5 = (bf16[96,2048]{1,0:T(8,128)(2,1)S(1)}, bf16[96,2048]{1,0:T(8,128)(2,1)S(1)}, bf16[64,2048]{1,0:T(8,128)(2,1)S(1)}, bf16[64,2048]{1,0:T(8,128)(2,1)S(1)}) custom-call(bf16[192,2048]{1,0:T(8,128)(2,1)S(1)} %collective-permute-done.4.refs_0_, bf16[192,2048]{1,0:T(8,128)(2,1)S(1)} %collective-permute-done.5.refs_1_, ...), custom_call_target="tpu_custom_call" | custom-call | flops 880803840 | bytes 655360 | tf_op jit(solution)/shard_map/expert_rows/pallas_call | solution.py:218
  128.5 2.7 %collective-permute-start.11 = (bf16[96,2048]{1,0:T(8,128)(2,1)S(1)}, bf16[96,2048]{1,0:T(8,128)(2,1)S(1)}, u32[]{:S(2)}, u32[]{:S(2)}) collective-permute-start(bf16[96,2048]{1,0:T(8,128)(2,1)S(1)} %get-tuple-element.113), channel_id=1, source_target_pairs={{0,96},{32,0},{64,32},{96,64},{1,97},{33,1},{65,33},{97,65},{2,98}... | collective-permute-start | bytes 1179656 | tf_op jit(solution)/shard_map/ppermute | solution.py:444
  131.2 10.9 %expert_rows.6 = (bf16[64,2048]{1,0:T(8,128)(2,1)S(1)}, bf16[64,2048]{1,0:T(8,128)(2,1)S(1)}, bf16[64,2048]{1,0:T(8,128)(2,1)S(1)}, bf16[64,2048]{1,0:T(8,128)(2,1)S(1)}) custom-call(bf16[256,2048]{1,0:T(8,128)(2,1)S(1)} %collective-permute-done.6.refs_0_, bf16[256,2048]{1,0:T(8,128)(2,1)S(1)} %collective-permute-done.7.refs_1_, ...), custom_call_target="tpu_custom_call" | custom-call | flops 704643072 | bytes 524288 | tf_op jit(solution)/shard_map/expert_rows/pallas_call | solution.py:218
  142.4 2.7 %collective-permute-start.13 = (bf16[192,2048]{1,0:T(8,128)(2,1)S(1)}, bf16[192,2048]{1,0:T(8,128)(2,1)S(1)}, u32[]{:S(2)}, u32[]{:S(2)}) collective-permute-start(bf16[192,2048]{1,0:T(8,128)(2,1)S(1)} %get-tuple-element.117), channel_id=1, source_target_pairs={{0,96},{32,0},{64,32},{96,64},{1,97},{33,1},{65,33},{97,65},{2,98}... | collective-permute-start | bytes 2359304 | tf_op jit(solution)/shard_map/ppermute | solution.py:444
  145.1 10.3 %expert_rows.7 = (bf16[64,2048]{1,0:T(8,128)(2,1)S(1)}, bf16[64,2048]{1,0:T(8,128)(2,1)S(1)}) custom-call(bf16[128,2048]{1,0:T(8,128)(2,1)S(1)} %collective-permute-done.8.refs_0_, bf16[128,2048]{1,0:T(8,128)(2,1)S(1)} %collective-permute-done.9.refs_1_, bf16[896,2048]{1,0:T(8,128)(2,1)S(1)} %bitcast.27, ...), custom_call_target="tpu_custom_call" | custom-call | flops 352321536 | bytes 262144 | tf_op jit(solution)/shard_map/expert_rows/pallas_call | solution.py:218
  155.5 2.7 %collective-permute-start.15 = (bf16[64,2048]{1,0:T(8,128)(2,1)S(1)}, bf16[64,2048]{1,0:T(8,128)(2,1)S(1)}, u32[]{:S(2)}, u32[]{:S(2)}) collective-permute-start(bf16[64,2048]{1,0:T(8,128)(2,1)S(1)} %get-tuple-element.121), channel_id=1, source_target_pairs={{0,96},{32,0},{64,32},{96,64},{1,97},{33,1},{65,33},{97,65},{2,98}... | collective-permute-start | bytes 786440 | tf_op jit(solution)/shard_map/ppermute | solution.py:444
  158.2 1.5 pack_returns.2
  159.7 5.4 %collective-permute-done.14.got_a = bf16[64,2048]{1,0:T(8,128)(2,1)S(1)} collective-permute-done((bf16[64,2048]{1,0:T(8,128)(2,1)S(1)}, bf16[64,2048]{1,0:T(8,128)(2,1)S(1)}, u32[]{:S(2)}, u32[]{:S(2)}) %collective-permute-start.14) | collective-permute-done | bytes 262176 | tf_op jit(solution)/shard_map/ppermute | solution.py:444
  165.1 4.9 %all-to-all-start.2 = ((bf16[16,16,2048]{2,1,0:T(8,128)(2,1)}), bf16[16,16,2048]{2,1,0:T(8,128)(2,1)S(1)}, u32[]{:S(2)}, u32[]{:S(2)}) async-start(bf16[16,16,2048]{2,1,0:T(8,128)(2,1)} %bitcast.14), calls=%async_computation.2 | async-start | bytes 2097152 | tf_op jit(solution)/shard_map/all_to_all | solution.py:451
  170.2 2.7 %collective-permute-start.17 = (bf16[128,2048]{1,0:T(8,128)(2,1)S(1)}, bf16[128,2048]{1,0:T(8,128)(2,1)S(1)}, u32[]{:S(2)}, u32[]{:S(2)}) collective-permute-start(bf16[128,2048]{1,0:T(8,128)(2,1)S(1)} %get-tuple-element.132), channel_id=1, source_target_pairs={{0,96},{32,0},{64,32},{96,64},{1,97},{33,1},{65,33},{97,65},{2,98}... | collective-permute-start | bytes 1572872 | tf_op jit(solution)/shard_map/ppermute | solution.py:444
  173.0 7.5 %collective-permute-done.16.refs_2_ = bf16[128,2048]{1,0:T(8,128)(2,1)S(1)} collective-permute-done((bf16[128,2048]{1,0:T(8,128)(2,1)S(1)}, bf16[128,2048]{1,0:T(8,128)(2,1)S(1)}, u32[]{:S(2)}, u32[]{:S(2)}) %collective-permute-start.16) | collective-permute-done | bytes 524320 | tf_op jit(solution)/shard_map/ppermute | solution.py:444
  180.4 1.0 pack_returns.3
  181.4 0.6 all-to-all-done.2
  182.1 5.7 %all-to-all-start.3 = ((bf16[16,8,2048]{2,1,0:T(8,128)(2,1)}), bf16[16,8,2048]{2,1,0:T(8,128)(2,1)S(1)}, u32[]{:S(2)}, u32[]{:S(2)}) async-start(bf16[16,8,2048]{2,1,0:T(8,128)(2,1)} %bitcast.16), calls=%async_computation.3 | async-start | bytes 1048576 | tf_op jit(solution)/shard_map/all_to_all | solution.py:451
  187.8 8.9 %all-to-all-done.3 = bf16[16,8,2048]{2,1,0:T(8,128)(2,1)S(1)} async-done(((bf16[16,8,2048]{2,1,0:T(8,128)(2,1)}), bf16[16,8,2048]{2,1,0:T(8,128)(2,1)S(1)}, u32[]{:S(2)}, u32[]{:S(2)}) %all-to-all-start.3) | async-done | bytes 524320 | tf_op jit(solution)/shard_map/all_to_all | solution.py:451
  196.8 0.8 copy-done.14
  197.6 10.6 %combine_and_scan.1 = (bf16[128,2048]{1,0:T(8,128)(2,1)}, f32[128,2048]{1,0:T(8,128)}, bf16[24,2048]{1,0:T(8,128)(2,1)}) custom-call(bf16[128,384]{1,0:T(8,128)(2,1)} %copy-done.9, bf16[128,384]{1,0:T(8,128)(2,1)} %copy-done.10, bf16[256,2048]{1,0:T(8,128)(2,1)} %bitcast.47, bf16[128,2048]{1,0:T(8,128)(2,1)} %bitcast.49, bf16[128,2048]{1,0:T(8,128)(2,1)} %bitcast.35, ...), custom_call_target="tpu_custom_call" | custom-call | tf_op jit(solution)/shard_map/combine_and_scan/pallas_call | solution.py:330
  208.2 21.8 %all-gather = bf16[192,2048]{1,0:T(8,128)(2,1)} all-gather(bf16[24,2048]{1,0:T(8,128)(2,1)} %get-tuple-element.137), channel_id=2, replica_groups=mesh['z'=4,'core'=2,'exp'=16] {'z','core'}, dimensions={0}, use_global_device_ids=true | all-gather | bytes 884736 | tf_op jit(solution)/shard_map/all_gather | solution.py:510
  230.0 5.8 %add_carry.1 = bf16[128,2048]{1,0:T(8,128)(2,1)} custom-call(s32[1]{0:T(128)} %bitcast.19.place_ref, bf16[8,24,2048]{2,1,0:T(8,128)(2,1)} %bitcast.48, f32[16,2048]{1,0:T(8,128)} %rate_ref.3, f32[128,2048]{1,0:T(8,128)} %get-tuple-element.138.local_ref, bf16[16,128,2048]{2,1,0:T(8,128)(2,1)} %get-tuple-element.139.reach_ref), custom_call_target="tpu_custom_call" | custom-call | tf_op jit(solution)/shard_map/add_carry/pallas_call | solution.py:420
  (58 shorter events, 1.6 us)
Async XLA Ops:
  0.6 34.7 %copy-start.8 = (bf16[192,192]{1,0:T(8,128)(2,1)S(1)}, bf16[192,192]{1,0:T(8,128)(2,1)}, u32[]{:S(2)}) copy-start(bf16[192,192]{1,0:T(8,128)(2,1)} %constant.20.clone.table_ref) | copy-start | bytes 221188
  0.6 34.6 %collective-permute-start = (bf16[896,2048]{1,0:T(8,128)(2,1)}, bf16[896,2048]{1,0:T(8,128)(2,1)}, u32[]{:S(2)}, u32[]{:S(2)}) collective-permute-start(bf16[896,2048]{1,0:T(8,128)(2,1)} %bitcast.23), channel_id=1, source_target_pairs={{0,16},{16,0},{1,17},{17,1},{2,18},{18,2},{3,19},{19,3},{4,20},{20... | collective-permute-start | bytes 11010056 | tf_op jit(solution)/shard_map/ppermute | solution.py:447
  2.1 33.1 %collective-permute-start.1 = (bf16[896,2048]{1,0:T(8,128)(2,1)}, bf16[896,2048]{1,0:T(8,128)(2,1)}, u32[]{:S(2)}, u32[]{:S(2)}) collective-permute-start(bf16[896,2048]{1,0:T(8,128)(2,1)} %bitcast.28), channel_id=1, source_target_pairs={{0,16},{16,0},{1,17},{17,1},{2,18},{18,2},{3,19},{19,3},{4,20},{20... | collective-permute-start | bytes 11010056 | tf_op jit(solution)/shard_map/ppermute | solution.py:447
  3.1 1.1 copy-start.2
  4.1 1.0 copy-start.6
  6.9 28.4 %copy-start.3 = (bf16[256,2048]{1,0:T(8,128)(2,1)}, bf16[256,2048]{1,0:T(8,128)(2,1)S(1)}, u32[]{:S(2)}) copy-start(bf16[256,2048]{1,0:T(8,128)(2,1)S(1)} %get-tuple-element.71) | copy-start | bytes 3145732
  6.9 36.6 %copy-start.17 = (f32[1,128,2]{1,2,0:T(2,128)S(1)}, f32[1,128,2]{1,2,0:T(2,128)}, u32[]{:S(2)}) copy-start(f32[1,128,2]{1,2,0:T(2,128)} %param.16) | copy-start | bytes 3076
  6.9 36.7 %copy-start.15 = (f32[1,128,16]{1,2,0:T(8,128)S(1)}, f32[1,128,16]{1,2,0:T(8,128)}, u32[]{:S(2)}) copy-start(f32[1,128,16]{1,2,0:T(8,128)} %param.21) | copy-start | bytes 24580
  6.9 36.8 %copy-start.16 = (f32[1,128,16]{1,2,0:T(8,128)S(1)}, f32[1,128,16]{1,2,0:T(8,128)}, u32[]{:S(2)}) copy-start(f32[1,128,16]{1,2,0:T(8,128)} %param.22) | copy-start | bytes 24580
  6.9 38.6 %copy-start.5 = (f32[16,2048]{1,0:T(8,128)S(1)}, f32[16,2048]{1,0:T(8,128)}, u32[]{:S(2)}) copy-start(f32[16,2048]{1,0:T(8,128)} %rate_ref.3) | copy-start | bytes 393220
  35.9 35.4 %collective-permute-start.3 = (bf16[384,2048]{1,0:T(8,128)(2,1)S(1)}, bf16[384,2048]{1,0:T(8,128)(2,1)}, u32[]{:S(2)}, u32[]{:S(2)}) collective-permute-start(bf16[384,2048]{1,0:T(8,128)(2,1)S(1)} %sort_messages.2.refs_0_), channel_id=1, source_target_pairs={{0,96},{32,0},{64,32},{96,64},{1,97},{33,1},{65,33},{97,65},{2,98}... | collective-permute-start | bytes 4718600 | tf_op jit(solution)/shard_map/ppermute | solution.py:444
  39.7 34.8 %collective-permute-start.2 = (bf16[384,2048]{1,0:T(8,128)(2,1)S(1)}, bf16[384,2048]{1,0:T(8,128)(2,1)}, u32[]{:S(2)}, u32[]{:S(2)}) collective-permute-start(bf16[384,2048]{1,0:T(8,128)(2,1)S(1)} %sort_messages.2.refs_0_), channel_id=1, source_target_pairs={{0,32},{32,64},{64,96},{96,0},{1,33},{33,65},{65,97},{97,1},{2,34}... | collective-permute-start | bytes 4718600 | tf_op jit(solution)/shard_map/ppermute | solution.py:444
  39.7 18.5 %all-to-all-start = ((bf16[16,16,2048]{2,1,0:T(8,128)(2,1)}), bf16[16,16,2048]{2,1,0:T(8,128)(2,1)S(1)}, u32[]{:S(2)}, u32[]{:S(2)}) async-start(bf16[16,16,2048]{2,1,0:T(8,128)(2,1)} %bitcast.38), calls=%async_computation | async-start | bytes 2097152 | tf_op jit(solution)/shard_map/all_to_all | solution.py:451
  44.3 0.6 copy-start.9
  44.9 0.6 copy-start.10
  45.6 1.2 copy-start.4
  46.8 14.0 %copy-start.11 = (bf16[128,128]{1,0:T(8,128)(2,1)S(1)}, bf16[128,128]{1,0:T(8,128)(2,1)}, u32[]{:S(2)}) copy-start(bf16[128,128]{1,0:T(8,128)(2,1)} %constant.21.clone.table_ref) | copy-start | bytes 98308
  52.6 25.8 %copy-start.12 = (f32[1,2048]{1,0:T(1,128)}, f32[1,2048]{1,0:T(1,128)S(1)}, u32[]{:S(2)}) copy-start(f32[1,2048]{1,0:T(1,128)S(1)} %get-tuple-element.133.refs_7_) | copy-start | bytes 24580
  58.2 21.7 %copy-start = (bf16[1,896,2048]{2,1,0:T(8,128)(2,1)S(1)}, bf16[1,896,2048]{2,1,0:T(8,128)(2,1)}, u32[]{:S(2)}) copy-start(bf16[1,896,2048]{2,1,0:T(8,128)(2,1)} %param.17) | copy-start | bytes 11010052
  58.2 21.7 %copy-start.1 = (bf16[1,896,2048]{2,1,0:T(8,128)(2,1)S(1)}, bf16[1,896,2048]{2,1,0:T(8,128)(2,1)}, u32[]{:S(2)}) copy-start(bf16[1,896,2048]{2,1,0:T(8,128)(2,1)} %param.18) | copy-start | bytes 11010052
  74.5 39.7 %collective-permute-start.7 = (bf16[256,2048]{1,0:T(8,128)(2,1)S(1)}, bf16[256,2048]{1,0:T(8,128)(2,1)S(1)}, u32[]{:S(2)}, u32[]{:S(2)}) collective-permute-start(bf16[256,2048]{1,0:T(8,128)(2,1)S(1)} %sort_messages.3.refs_2_), channel_id=1, source_target_pairs={{0,96},{32,0},{64,32},{96,64},{1,97},{33,1},{65,33},{97,65},{2,98}... | collective-permute-start | bytes 3145736 | tf_op jit(solution)/shard_map/ppermute | solution.py:444
  74.8 39.4 %collective-permute-start.6 = (bf16[256,2048]{1,0:T(8,128)(2,1)S(1)}, bf16[256,2048]{1,0:T(8,128)(2,1)S(1)}, u32[]{:S(2)}, u32[]{:S(2)}) collective-permute-start(bf16[256,2048]{1,0:T(8,128)(2,1)S(1)} %sort_messages.3.refs_2_), channel_id=1, source_target_pairs={{0,32},{32,64},{64,96},{96,0},{1,33},{33,65},{65,97},{97,1},{2,34}... | collective-permute-start | bytes 3145736 | tf_op jit(solution)/shard_map/ppermute | solution.py:444
  78.4 34.3 %collective-permute-start.5 = (bf16[192,2048]{1,0:T(8,128)(2,1)S(1)}, bf16[192,2048]{1,0:T(8,128)(2,1)S(1)}, u32[]{:S(2)}, u32[]{:S(2)}) collective-permute-start(bf16[192,2048]{1,0:T(8,128)(2,1)S(1)} %slice.13), channel_id=1, source_target_pairs={{0,96},{32,0},{64,32},{96,64},{1,97},{33,1},{65,33},{97,65},{2,98}... | collective-permute-start | bytes 2359304 | tf_op jit(solution)/shard_map/ppermute | solution.py:444
  79.9 34.2 %collective-permute-start.4 = (bf16[192,2048]{1,0:T(8,128)(2,1)S(1)}, bf16[192,2048]{1,0:T(8,128)(2,1)S(1)}, u32[]{:S(2)}, u32[]{:S(2)}) collective-permute-start(bf16[192,2048]{1,0:T(8,128)(2,1)S(1)} %slice.12), channel_id=1, source_target_pairs={{0,32},{32,64},{64,96},{96,0},{1,33},{33,65},{65,97},{97,1},{2,34}... | collective-permute-start | bytes 2359304 | tf_op jit(solution)/shard_map/ppermute | solution.py:444
  114.3 28.0 %collective-permute-start.9 = (bf16[128,2048]{1,0:T(8,128)(2,1)S(1)}, bf16[128,2048]{1,0:T(8,128)(2,1)S(1)}, u32[]{:S(2)}, u32[]{:S(2)}) collective-permute-start(bf16[128,2048]{1,0:T(8,128)(2,1)S(1)} %slice.15), channel_id=1, source_target_pairs={{0,96},{32,0},{64,32},{96,64},{1,97},{33,1},{65,33},{97,65},{2,98}... | collective-permute-start | bytes 1572872 | tf_op jit(solution)/shard_map/ppermute | solution.py:444
  114.8 27.5 %collective-permute-start.8 = (bf16[128,2048]{1,0:T(8,128)(2,1)S(1)}, bf16[128,2048]{1,0:T(8,128)(2,1)S(1)}, u32[]{:S(2)}, u32[]{:S(2)}) collective-permute-start(bf16[128,2048]{1,0:T(8,128)(2,1)S(1)} %slice.14), channel_id=1, source_target_pairs={{0,32},{32,64},{64,96},{96,0},{1,33},{33,65},{65,97},{97,1},{2,34}... | collective-permute-start | bytes 1572872 | tf_op jit(solution)/shard_map/ppermute | solution.py:444
  128.4 13.6 %collective-permute-start.10 = (bf16[96,2048]{1,0:T(8,128)(2,1)S(1)}, bf16[96,2048]{1,0:T(8,128)(2,1)S(1)}, u32[]{:S(2)}, u32[]{:S(2)}) collective-permute-start(bf16[96,2048]{1,0:T(8,128)(2,1)S(1)} %get-tuple-element.112), channel_id=1, source_target_pairs={{0,32},{32,64},{64,96},{96,0},{1,33},{33,65},{65,97},{97,1},{2,34}... | collective-permute-start | bytes 1179656 | tf_op jit(solution)/shard_map/ppermute | solution.py:444
  128.5 13.6 %collective-permute-start.11 = (bf16[96,2048]{1,0:T(8,128)(2,1)S(1)}, bf16[96,2048]{1,0:T(8,128)(2,1)S(1)}, u32[]{:S(2)}, u32[]{:S(2)}) collective-permute-start(bf16[96,2048]{1,0:T(8,128)(2,1)S(1)} %get-tuple-element.113), channel_id=1, source_target_pairs={{0,96},{32,0},{64,32},{96,64},{1,97},{33,1},{65,33},{97,65},{2,98}... | collective-permute-start | bytes 1179656 | tf_op jit(solution)/shard_map/ppermute | solution.py:444
  142.3 15.8 %copy-start.7 = (bf16[256,192]{1,0:T(8,128)(2,1)S(1)}, bf16[256,192]{1,0:T(8,128)(2,1)}, u32[]{:S(2)}) copy-start(bf16[256,192]{1,0:T(8,128)(2,1)} %constant.22.clone.refs_0_) | copy-start | bytes 294916
  142.3 15.8 %collective-permute-start.12 = (bf16[192,2048]{1,0:T(8,128)(2,1)S(1)}, bf16[192,2048]{1,0:T(8,128)(2,1)S(1)}, u32[]{:S(2)}, u32[]{:S(2)}) collective-permute-start(bf16[192,2048]{1,0:T(8,128)(2,1)S(1)} %get-tuple-element.116), channel_id=1, source_target_pairs={{0,32},{32,64},{64,96},{96,0},{1,33},{33,65},{65,97},{97,1},{2,34}... | collective-permute-start | bytes 2359304 | tf_op jit(solution)/shard_map/ppermute | solution.py:444
  142.4 15.7 %collective-permute-start.13 = (bf16[192,2048]{1,0:T(8,128)(2,1)S(1)}, bf16[192,2048]{1,0:T(8,128)(2,1)S(1)}, u32[]{:S(2)}, u32[]{:S(2)}) collective-permute-start(bf16[192,2048]{1,0:T(8,128)(2,1)S(1)} %get-tuple-element.117), channel_id=1, source_target_pairs={{0,96},{32,0},{64,32},{96,64},{1,97},{33,1},{65,33},{97,65},{2,98}... | collective-permute-start | bytes 2359304 | tf_op jit(solution)/shard_map/ppermute | solution.py:444
  155.4 9.7 %collective-permute-start.14 = (bf16[64,2048]{1,0:T(8,128)(2,1)S(1)}, bf16[64,2048]{1,0:T(8,128)(2,1)S(1)}, u32[]{:S(2)}, u32[]{:S(2)}) collective-permute-start(bf16[64,2048]{1,0:T(8,128)(2,1)S(1)} %get-tuple-element.120), channel_id=1, source_target_pairs={{0,32},{32,64},{64,96},{96,0},{1,33},{33,65},{65,97},{97,1},{2,34}... | collective-permute-start | bytes 786440 | tf_op jit(solution)/shard_map/ppermute | solution.py:444
  155.5 9.6 %collective-permute-start.15 = (bf16[64,2048]{1,0:T(8,128)(2,1)S(1)}, bf16[64,2048]{1,0:T(8,128)(2,1)S(1)}, u32[]{:S(2)}, u32[]{:S(2)}) collective-permute-start(bf16[64,2048]{1,0:T(8,128)(2,1)S(1)} %get-tuple-element.121), channel_id=1, source_target_pairs={{0,96},{32,0},{64,32},{96,64},{1,97},{33,1},{65,33},{97,65},{2,98}... | collective-permute-start | bytes 786440 | tf_op jit(solution)/shard_map/ppermute | solution.py:444
  165.1 17.0 %all-to-all-start.2 = ((bf16[16,16,2048]{2,1,0:T(8,128)(2,1)}), bf16[16,16,2048]{2,1,0:T(8,128)(2,1)S(1)}, u32[]{:S(2)}, u32[]{:S(2)}) async-start(bf16[16,16,2048]{2,1,0:T(8,128)(2,1)} %bitcast.14), calls=%async_computation.2 | async-start | bytes 2097152 | tf_op jit(solution)/shard_map/all_to_all | solution.py:451
  170.1 10.3 %collective-permute-start.16 = (bf16[128,2048]{1,0:T(8,128)(2,1)S(1)}, bf16[128,2048]{1,0:T(8,128)(2,1)S(1)}, u32[]{:S(2)}, u32[]{:S(2)}) collective-permute-start(bf16[128,2048]{1,0:T(8,128)(2,1)S(1)} %get-tuple-element.131), channel_id=1, source_target_pairs={{0,32},{32,64},{64,96},{96,0},{1,33},{33,65},{65,97},{97,1},{2,34}... | collective-permute-start | bytes 1572872 | tf_op jit(solution)/shard_map/ppermute | solution.py:444
  170.2 10.2 %collective-permute-start.17 = (bf16[128,2048]{1,0:T(8,128)(2,1)S(1)}, bf16[128,2048]{1,0:T(8,128)(2,1)S(1)}, u32[]{:S(2)}, u32[]{:S(2)}) collective-permute-start(bf16[128,2048]{1,0:T(8,128)(2,1)S(1)} %get-tuple-element.132), channel_id=1, source_target_pairs={{0,96},{32,0},{64,32},{96,64},{1,97},{33,1},{65,33},{97,65},{2,98}... | collective-permute-start | bytes 1572872 | tf_op jit(solution)/shard_map/ppermute | solution.py:444
  182.1 14.7 %copy-start.13 = (bf16[16,16,2048]{2,1,0:T(8,128)(2,1)}, bf16[16,16,2048]{2,1,0:T(8,128)(2,1)S(1)}, u32[]{:S(2)}) copy-start(bf16[16,16,2048]{2,1,0:T(8,128)(2,1)S(1)} %all-to-all-done.2) | copy-start | bytes 3145732
  182.1 14.7 %all-to-all-start.3 = ((bf16[16,8,2048]{2,1,0:T(8,128)(2,1)}), bf16[16,8,2048]{2,1,0:T(8,128)(2,1)S(1)}, u32[]{:S(2)}, u32[]{:S(2)}) async-start(bf16[16,8,2048]{2,1,0:T(8,128)(2,1)} %bitcast.16), calls=%async_computation.3 | async-start | bytes 1048576 | tf_op jit(solution)/shard_map/all_to_all | solution.py:451
  196.8 0.8 copy-start.14

commit v7 on v6

--- a/solution.py
+++ b/solution.py
@@ -15,6 +15,7 @@
 OUT_COLS = 512
 SCAN_COLS = 1024
 BF = jnp.bfloat16
+LOG2_E = 1.4426950408889634
 F32 = jnp.float32
 
 
@@ -291,7 +292,7 @@
     mid = (dout_ref[...].astype(F32) + routed).astype(BF)
     mid_ref[...] = mid
     grad[...] = mid.astype(F32)
-    negative = -rate_ref[...]
+    negative = rate_ref[...] * -LOG2_E
     tokens, cols = grad.shape
     states = negative.shape[0]
     repeat = cols // mix_ref.shape[2]
@@ -306,7 +307,7 @@
             mix = jnp.concatenate([mix_ref[low_t + r]] * repeat, axis=1)
             state = drive * jnp.broadcast_to(grads[r : r + 1], (states, cols)) + flow
             rows.append(jnp.sum(mix * state, axis=0, keepdims=True))
-            decay = jnp.exp(jnp.broadcast_to(deltas[r : r + 1], (states, cols)) * negative)
+            decay = jnp.exp2(jnp.broadcast_to(deltas[r : r + 1], (states, cols)) * negative)
             flow = decay * state
         local_ref[pl.ds(low_t, 8)] = jnp.concatenate(rows[::-1], axis=0)
         return flow
@@ -463,9 +464,12 @@
     def ring(own):
         return shift(own, 1), shift(own, -1)
 
-    def far(prev, next_):
+    def halves(prev, next_):
         half = prev.shape[0] // 2
-        return shift(prev[:half], 1), shift(next_[half:], -1)
+        return prev[:half], next_[half:]
+
+    def far(low_half, high_half):
+        return shift(low_half, 1), shift(high_half, -1)
 
     def some(part, count):
         return (sizes[part] * experts // 2,) * count
@@ -480,14 +484,14 @@
         got_high, reach, total, tables, mix, drive
     )
     high = sort_messages(got_high, experts, sizes[1])
-    low_near, high = tie(low_near, high)
-    low_far = far(*low_near)
+    low_near, low_halves, high = tie(low_near, halves(*low_near), high)
+    low_far = far(*low_halves)
     high_near = ring(high)
     first = expert_rows((low, *low_near), some(0, 3), both)
-    low_far, high_near, first = tie(low_far, high_near, first)
-    high_far = far(*high_near)
+    low_far, first = tie(low_far, first)
     second = expert_rows((*low_far, high), some(0, 2) + some(1, 1), both)
     high_near, second = tie(high_near, second)
+    high_far = far(*halves(*high_near))
     third = expert_rows(high_near, some(1, 2), both)
     low_sums = hop_sums(*first[4:6], *first[2:4], shift(second[0], 1), shift(second[1], -1))
     high_far, third, low_sums = tie(high_far, third, low_sums)

time: 236 us -> 242 us (1.025)
  starting transfers between devices: 35.7 us -> 39.9 us
    ppermute x16, starting transfers between devices: 19.6 us -> 23.3 us  [shift(): return lax.ppermute(value, 'z', ring)]
  transfers between devices with their start and end apart: 21 -> 21, of which waited for: 9 -> 8; matrix products, arithmetic and copies ran while one was open for 3% -> 2% of each run, Pallas kernels for 27% -> 27%
where the time goes in v7:
time: 242 us; the launch traced here: 241 us
  Pallas kernels  81.1 us (34%)
  waiting for transfers between devices  57.4 us (24%)
  blocking collectives  50 us (21%)
  starting transfers between devices  39.9 us (16%)
  local copies, waits for them, and re-layouts  11.7 us (5%)
    pallas_call x4, Pallas kernels, expert_rows(): pl.pallas_call(functools.partial(expert_body, sizes), in_specs=[vmem] * (...  53.1 us
    ppermute x16, waiting for transfers between devices, shift(): return lax.ppermute(value, 'z', ring)  42.3 us
    all_to_all x1, blocking collectives, exchange(): got = lax.all_to_all(parts, 'exp', split_axis=0, concat_axis=0, tiled=True)  28.3 us
    ppermute x16, starting transfers between devices, shift(): return lax.ppermute(value, 'z', ring)  23.3 us
    all_gather x1, blocking collectives, on_device(): starts = lax.all_gather(start, ('z', 'core'))  21.6 us
    all_to_all x3, waiting for transfers between devices, exchange(): got = lax.all_to_all(parts, 'exp', split_axis=0, concat_axis=0, tiled=True)  15.1 us
    all_to_all x3, starting transfers between devices, exchange(): got = lax.all_to_all(parts, 'exp', split_axis=0, concat_axis=0, tiled=True)  15 us
    pallas_call x1, Pallas kernels, combine_and_scan(): pl.pallas_call(scan_body, grid=(dim // cols,), in_specs=[whole(*t.shape)...  10.6 us
  transfers between devices with their start and end apart: 21, of which 8 were waited for; matrix products, arithmetic and copies ran while one was open for 2% of the time, Pallas kernels for 27%

profile of v7, /device:TPU:1, one launch (start us, length us, event | category | flops | bytes accessed | tf_op | source)
XLA Modules:
  0.0 241.0 jit_solution(6098032150740505371)
XLA Ops:
  0.6 1.5 collective-permute-start
  2.2 0.8 copy.15
  3.1 1.1 copy-done.2
  4.2 1.0 copy-done.6
  5.2 1.7 gather_rows.1
  6.9 28.3 %all_to_all.20 = bf16[16,24,2048]{2,1,0:T(8,128)(2,1)S(1)} all-to-all(bf16[16,24,2048]{2,1,0:T(8,128)(2,1)S(1)} %bitcast.37), channel_id=1, replica_groups=mesh['z'=4,'core'=2,'exp'=16] {'exp'}, dimensions={0} | all-to-all | bytes 3145728 | tf_op jit(solution)/shard_map/all_to_all | solution.py:452
  35.3 0.6 sort_messages.2.refs_0_
  35.9 1.7 collective-permute-start.2
  37.6 2.2 collective-permute-start.3
  39.8 3.8 %all-to-all-start = ((bf16[16,16,2048]{2,1,0:T(8,128)(2,1)}), bf16[16,16,2048]{2,1,0:T(8,128)(2,1)S(1)}, u32[]{:S(2)}, u32[]{:S(2)}) async-start(bf16[16,16,2048]{2,1,0:T(8,128)(2,1)} %bitcast.38), calls=%async_computation | async-start | bytes 2097152 | tf_op jit(solution)/shard_map/all_to_all | solution.py:452
  43.9 0.4 weigh_tables.1
  44.4 0.6 copy-done.9
  45.0 0.6 copy-done.10
  45.7 1.2 copy-done.4
  46.9 5.8 %reach_table.1 = (bf16[16,128,2048]{2,1,0:T(8,128)(2,1)}, f32[1,2048]{1,0:T(1,128)S(1)}) custom-call(f32[128,2048]{1,0:T(8,128)S(1)} %bitcast.40, f32[16,2048]{1,0:T(8,128)S(1)} %copy-done.5, f32[128,16]{1,0:T(8,128)S(1)} %bitcast.44), custom_call_target="tpu_custom_call" | custom-call | flops 33554432 | bytes 8388608 | tf_op jit(solution)/shard_map/reach_table/pallas_call | solution.py:377
  52.7 5.6 %all-to-all-done = bf16[16,16,2048]{2,1,0:T(8,128)(2,1)S(1)} async-done(((bf16[16,16,2048]{2,1,0:T(8,128)(2,1)}), bf16[16,16,2048]{2,1,0:T(8,128)(2,1)S(1)}, u32[]{:S(2)}, u32[]{:S(2)}) %all-to-all-start) | async-done | bytes 1048608 | tf_op jit(solution)/shard_map/all_to_all | solution.py:452
  58.3 1.3 broadcast_in_dim.18.refs_8_
  59.6 1.3 broadcast_in_dim.20.refs_9_
  60.9 0.4 sort_messages.3.refs_2_
  61.3 11.1 %collective-permute-done.2.refs_1_ = bf16[384,2048]{1,0:T(8,128)(2,1)} collective-permute-done((bf16[384,2048]{1,0:T(8,128)(2,1)S(1)}, bf16[384,2048]{1,0:T(8,128)(2,1)}, u32[]{:S(2)}, u32[]{:S(2)}) %collective-permute-start.2) | collective-permute-done | bytes 1572896 | tf_op jit(solution)/shard_map/ppermute | solution.py:445
  72.4 1.2 slice.16
  73.6 1.2 slice.17
  74.9 2.7 %collective-permute-start.7 = (bf16[256,2048]{1,0:T(8,128)(2,1)S(1)}, bf16[256,2048]{1,0:T(8,128)(2,1)S(1)}, u32[]{:S(2)}, u32[]{:S(2)}) collective-permute-start(bf16[256,2048]{1,0:T(8,128)(2,1)S(1)} %sort_messages.3.refs_2_), channel_id=1, source_target_pairs={{0,96},{32,0},{64,32},{96,64},{1,97},{33,1},{65,33},{97,65},{2,98}... | collective-permute-start | bytes 3145736 | tf_op jit(solution)/shard_map/ppermute | solution.py:445
  77.6 2.7 %collective-permute-start.5 = (bf16[192,2048]{1,0:T(8,128)(2,1)S(1)}, bf16[192,2048]{1,0:T(8,128)(2,1)S(1)}, u32[]{:S(2)}, u32[]{:S(2)}) collective-permute-start(bf16[192,2048]{1,0:T(8,128)(2,1)S(1)} %slice.17), channel_id=1, source_target_pairs={{0,96},{32,0},{64,32},{96,64},{1,97},{33,1},{65,33},{97,65},{2,98}... | collective-permute-start | bytes 2359304 | tf_op jit(solution)/shard_map/ppermute | solution.py:445
  80.3 19.5 %expert_rows.4 = (bf16[96,2048]{1,0:T(8,128)(2,1)S(1)}, bf16[96,2048]{1,0:T(8,128)(2,1)S(1)}, bf16[96,2048]{1,0:T(8,128)(2,1)S(1)}, bf16[96,2048]{1,0:T(8,128)(2...) custom-call(bf16[384,2048]{1,0:T(8,128)(2,1)S(1)} %sort_messages.2.refs_0_, ...), custom_call_target="tpu_custom_call" | custom-call | flops 1585446912 | bytes 1179648 | tf_op jit(solution)/shard_map/expert_rows/pallas_call | solution.py:219
  99.7 15.1 %collective-permute-done.4.refs_0_ = bf16[192,2048]{1,0:T(8,128)(2,1)S(1)} collective-permute-done((bf16[192,2048]{1,0:T(8,128)(2,1)S(1)}, bf16[192,2048]{1,0:T(8,128)(2,1)S(1)}, u32[]{:S(2)}, u32[]{:S(2)}) %collective-permute-start.4) | collective-permute-done | bytes 786464 | tf_op jit(solution)/shard_map/ppermute | solution.py:445
  114.9 12.4 %expert_rows.5 = (bf16[96,2048]{1,0:T(8,128)(2,1)S(1)}, bf16[96,2048]{1,0:T(8,128)(2,1)S(1)}, bf16[64,2048]{1,0:T(8,128)(2,1)S(1)}, bf16[64,2048]{1,0:T(8,128)(2,1)S(1)}) custom-call(bf16[192,2048]{1,0:T(8,128)(2,1)S(1)} %collective-permute-done.4.refs_0_, bf16[192,2048]{1,0:T(8,128)(2,1)S(1)} %collective-permute-done.5.refs_1_, ...), custom_call_target="tpu_custom_call" | custom-call | flops 880803840 | bytes 655360 | tf_op jit(solution)/shard_map/expert_rows/pallas_call | solution.py:219
  127.5 2.7 %collective-permute-start.9 = (bf16[128,2048]{1,0:T(8,128)(2,1)S(1)}, bf16[128,2048]{1,0:T(8,128)(2,1)S(1)}, u32[]{:S(2)}, u32[]{:S(2)}) collective-permute-start(bf16[128,2048]{1,0:T(8,128)(2,1)S(1)} %slice.15), channel_id=1, source_target_pairs={{0,96},{32,0},{64,32},{96,64},{1,97},{33,1},{65,33},{97,65},{2,98}... | collective-permute-start | bytes 1572872 | tf_op jit(solution)/shard_map/ppermute | solution.py:445
  130.2 2.7 %collective-permute-start.11 = (bf16[96,2048]{1,0:T(8,128)(2,1)S(1)}, bf16[96,2048]{1,0:T(8,128)(2,1)S(1)}, u32[]{:S(2)}, u32[]{:S(2)}) collective-permute-start(bf16[96,2048]{1,0:T(8,128)(2,1)S(1)} %get-tuple-element.113), channel_id=1, source_target_pairs={{0,96},{32,0},{64,32},{96,64},{1,97},{33,1},{65,33},{97,65},{2,98}... | collective-permute-start | bytes 1179656 | tf_op jit(solution)/shard_map/ppermute | solution.py:445
  132.9 10.9 %expert_rows.6 = (bf16[64,2048]{1,0:T(8,128)(2,1)S(1)}, bf16[64,2048]{1,0:T(8,128)(2,1)S(1)}, bf16[64,2048]{1,0:T(8,128)(2,1)S(1)}, bf16[64,2048]{1,0:T(8,128)(2,1)S(1)}) custom-call(bf16[256,2048]{1,0:T(8,128)(2,1)S(1)} %collective-permute-done.6.refs_0_, bf16[256,2048]{1,0:T(8,128)(2,1)S(1)} %collective-permute-done.7.refs_1_, ...), custom_call_target="tpu_custom_call" | custom-call | flops 704643072 | bytes 524288 | tf_op jit(solution)/shard_map/expert_rows/pallas_call | solution.py:219
  143.8 3.0 %collective-permute-done.10.got_a = bf16[96,2048]{1,0:T(8,128)(2,1)S(1)} collective-permute-done((bf16[96,2048]{1,0:T(8,128)(2,1)S(1)}, bf16[96,2048]{1,0:T(8,128)(2,1)S(1)}, u32[]{:S(2)}, u32[]{:S(2)}) %collective-permute-start.10) | collective-permute-done | bytes 393248 | tf_op jit(solution)/shard_map/ppermute | solution.py:445
  147.0 0.5 collective-permute-start.12
  147.5 2.4 collective-permute-start.13
  149.9 10.3 %expert_rows.7 = (bf16[64,2048]{1,0:T(8,128)(2,1)S(1)}, bf16[64,2048]{1,0:T(8,128)(2,1)S(1)}) custom-call(bf16[128,2048]{1,0:T(8,128)(2,1)S(1)} %collective-permute-done.8.refs_0_, bf16[128,2048]{1,0:T(8,128)(2,1)S(1)} %collective-permute-done.9.refs_1_, bf16[896,2048]{1,0:T(8,128)(2,1)S(1)} %bitcast.27, ...), custom_call_target="tpu_custom_call" | custom-call | flops 352321536 | bytes 262144 | tf_op jit(solution)/shard_map/expert_rows/pallas_call | solution.py:219
  160.3 2.7 %collective-permute-start.15 = (bf16[64,2048]{1,0:T(8,128)(2,1)S(1)}, bf16[64,2048]{1,0:T(8,128)(2,1)S(1)}, u32[]{:S(2)}, u32[]{:S(2)}) collective-permute-start(bf16[64,2048]{1,0:T(8,128)(2,1)S(1)} %get-tuple-element.121), channel_id=1, source_target_pairs={{0,96},{32,0},{64,32},{96,64},{1,97},{33,1},{65,33},{97,65},{2,98}... | collective-permute-start | bytes 786440 | tf_op jit(solution)/shard_map/ppermute | solution.py:445
  163.0 1.5 pack_returns.2
  164.5 5.4 %collective-permute-done.14.got_a = bf16[64,2048]{1,0:T(8,128)(2,1)S(1)} collective-permute-done((bf16[64,2048]{1,0:T(8,128)(2,1)S(1)}, bf16[64,2048]{1,0:T(8,128)(2,1)S(1)}, u32[]{:S(2)}, u32[]{:S(2)}) %collective-permute-start.14) | collective-permute-done | bytes 262176 | tf_op jit(solution)/shard_map/ppermute | solution.py:445
  169.9 5.4 %all-to-all-start.2 = ((bf16[16,16,2048]{2,1,0:T(8,128)(2,1)}), bf16[16,16,2048]{2,1,0:T(8,128)(2,1)S(1)}, u32[]{:S(2)}, u32[]{:S(2)}) async-start(bf16[16,16,2048]{2,1,0:T(8,128)(2,1)} %bitcast.14), calls=%async_computation.2 | async-start | bytes 2097152 | tf_op jit(solution)/shard_map/all_to_all | solution.py:452
  175.6 2.7 %collective-permute-start.17 = (bf16[128,2048]{1,0:T(8,128)(2,1)S(1)}, bf16[128,2048]{1,0:T(8,128)(2,1)S(1)}, u32[]{:S(2)}, u32[]{:S(2)}) collective-permute-start(bf16[128,2048]{1,0:T(8,128)(2,1)S(1)} %get-tuple-element.132), channel_id=1, source_target_pairs={{0,96},{32,0},{64,32},{96,64},{1,97},{33,1},{65,33},{97,65},{2,98}... | collective-permute-start | bytes 1572872 | tf_op jit(solution)/shard_map/ppermute | solution.py:445
  178.3 7.6 %collective-permute-done.16.refs_2_ = bf16[128,2048]{1,0:T(8,128)(2,1)S(1)} collective-permute-done((bf16[128,2048]{1,0:T(8,128)(2,1)S(1)}, bf16[128,2048]{1,0:T(8,128)(2,1)S(1)}, u32[]{:S(2)}, u32[]{:S(2)}) %collective-permute-start.16) | collective-permute-done | bytes 524320 | tf_op jit(solution)/shard_map/ppermute | solution.py:445
  185.9 1.0 pack_returns.3
  186.9 0.6 all-to-all-done.2
  187.5 5.8 %all-to-all-start.3 = ((bf16[16,8,2048]{2,1,0:T(8,128)(2,1)}), bf16[16,8,2048]{2,1,0:T(8,128)(2,1)S(1)}, u32[]{:S(2)}, u32[]{:S(2)}) async-start(bf16[16,8,2048]{2,1,0:T(8,128)(2,1)} %bitcast.16), calls=%async_computation.3 | async-start | bytes 1048576 | tf_op jit(solution)/shard_map/all_to_all | solution.py:452
  193.3 8.9 %all-to-all-done.3 = bf16[16,8,2048]{2,1,0:T(8,128)(2,1)S(1)} async-done(((bf16[16,8,2048]{2,1,0:T(8,128)(2,1)}), bf16[16,8,2048]{2,1,0:T(8,128)(2,1)S(1)}, u32[]{:S(2)}, u32[]{:S(2)}) %all-to-all-start.3) | async-done | bytes 524320 | tf_op jit(solution)/shard_map/all_to_all | solution.py:452
  202.2 0.8 copy-done.14
  203.0 10.6 %combine_and_scan.1 = (bf16[128,2048]{1,0:T(8,128)(2,1)}, f32[128,2048]{1,0:T(8,128)}, bf16[24,2048]{1,0:T(8,128)(2,1)}) custom-call(bf16[128,384]{1,0:T(8,128)(2,1)} %copy-done.9, bf16[128,384]{1,0:T(8,128)(2,1)} %copy-done.10, bf16[256,2048]{1,0:T(8,128)(2,1)} %bitcast.47, bf16[128,2048]{1,0:T(8,128)(2,1)} %bitcast.49, bf16[128,2048]{1,0:T(8,128)(2,1)} %bitcast.35, ...), custom_call_target="tpu_custom_call" | custom-call | tf_op jit(solution)/shard_map/combine_and_scan/pallas_call | solution.py:331
  213.6 21.6 %all-gather = bf16[192,2048]{1,0:T(8,128)(2,1)} all-gather(bf16[24,2048]{1,0:T(8,128)(2,1)} %get-tuple-element.137), channel_id=2, replica_groups=mesh['z'=4,'core'=2,'exp'=16] {'z','core'}, dimensions={0}, use_global_device_ids=true | all-gather | bytes 884736 | tf_op jit(solution)/shard_map/all_gather | solution.py:514
  235.3 5.8 %add_carry.1 = bf16[128,2048]{1,0:T(8,128)(2,1)} custom-call(s32[1]{0:T(128)} %bitcast.19.place_ref, bf16[8,24,2048]{2,1,0:T(8,128)(2,1)} %bitcast.48, f32[16,2048]{1,0:T(8,128)} %rate_ref.3, f32[128,2048]{1,0:T(8,128)} %get-tuple-element.138.local_ref, bf16[16,128,2048]{2,1,0:T(8,128)(2,1)} %get-tuple-element.139.reach_ref), custom_call_target="tpu_custom_call" | custom-call | tf_op jit(solution)/shard_map/add_carry/pallas_call | solution.py:421
  (58 shorter events, 1.3 us)
Async XLA Ops:
  0.6 34.7 %copy-start.8 = (bf16[192,192]{1,0:T(8,128)(2,1)S(1)}, bf16[192,192]{1,0:T(8,128)(2,1)}, u32[]{:S(2)}) copy-start(bf16[192,192]{1,0:T(8,128)(2,1)} %constant.20.clone.table_ref) | copy-start | bytes 221188
  0.6 34.6 %collective-permute-start = (bf16[896,2048]{1,0:T(8,128)(2,1)}, bf16[896,2048]{1,0:T(8,128)(2,1)}, u32[]{:S(2)}, u32[]{:S(2)}) collective-permute-start(bf16[896,2048]{1,0:T(8,128)(2,1)} %bitcast.23), channel_id=1, source_target_pairs={{0,16},{16,0},{1,17},{17,1},{2,18},{18,2},{3,19},{19,3},{4,20},{20... | collective-permute-start | bytes 11010056 | tf_op jit(solution)/shard_map/ppermute | solution.py:448
  2.1 33.1 %collective-permute-start.1 = (bf16[896,2048]{1,0:T(8,128)(2,1)}, bf16[896,2048]{1,0:T(8,128)(2,1)}, u32[]{:S(2)}, u32[]{:S(2)}) collective-permute-start(bf16[896,2048]{1,0:T(8,128)(2,1)} %bitcast.28), channel_id=1, source_target_pairs={{0,16},{16,0},{1,17},{17,1},{2,18},{18,2},{3,19},{19,3},{4,20},{20... | collective-permute-start | bytes 11010056 | tf_op jit(solution)/shard_map/ppermute | solution.py:448
  3.1 1.1 copy-start.2
  4.1 1.0 copy-start.6
  6.9 28.4 %copy-start.3 = (bf16[256,2048]{1,0:T(8,128)(2,1)}, bf16[256,2048]{1,0:T(8,128)(2,1)S(1)}, u32[]{:S(2)}) copy-start(bf16[256,2048]{1,0:T(8,128)(2,1)S(1)} %get-tuple-element.71) | copy-start | bytes 3145732
  6.9 36.7 %copy-start.15 = (f32[1,128,16]{1,2,0:T(8,128)S(1)}, f32[1,128,16]{1,2,0:T(8,128)}, u32[]{:S(2)}) copy-start(f32[1,128,16]{1,2,0:T(8,128)} %param.21) | copy-start | bytes 24580
  6.9 36.8 %copy-start.17 = (f32[1,128,2]{1,2,0:T(2,128)S(1)}, f32[1,128,2]{1,2,0:T(2,128)}, u32[]{:S(2)}) copy-start(f32[1,128,2]{1,2,0:T(2,128)} %param.16) | copy-start | bytes 3076
  6.9 36.9 %copy-start.16 = (f32[1,128,16]{1,2,0:T(8,128)S(1)}, f32[1,128,16]{1,2,0:T(8,128)}, u32[]{:S(2)}) copy-start(f32[1,128,16]{1,2,0:T(8,128)} %param.22) | copy-start | bytes 24580
  6.9 38.7 %copy-start.5 = (f32[16,2048]{1,0:T(8,128)S(1)}, f32[16,2048]{1,0:T(8,128)}, u32[]{:S(2)}) copy-start(f32[16,2048]{1,0:T(8,128)} %rate_ref.3) | copy-start | bytes 393220
  35.9 36.5 %collective-permute-start.2 = (bf16[384,2048]{1,0:T(8,128)(2,1)S(1)}, bf16[384,2048]{1,0:T(8,128)(2,1)}, u32[]{:S(2)}, u32[]{:S(2)}) collective-permute-start(bf16[384,2048]{1,0:T(8,128)(2,1)S(1)} %sort_messages.2.refs_0_), channel_id=1, source_target_pairs={{0,32},{32,64},{64,96},{96,0},{1,33},{33,65},{65,97},{97,1},{2,34}... | collective-permute-start | bytes 4718600 | tf_op jit(solution)/shard_map/ppermute | solution.py:445
  37.6 36.0 %collective-permute-start.3 = (bf16[384,2048]{1,0:T(8,128)(2,1)S(1)}, bf16[384,2048]{1,0:T(8,128)(2,1)}, u32[]{:S(2)}, u32[]{:S(2)}) collective-permute-start(bf16[384,2048]{1,0:T(8,128)(2,1)S(1)} %sort_messages.2.refs_0_), channel_id=1, source_target_pairs={{0,96},{32,0},{64,32},{96,64},{1,97},{33,1},{65,33},{97,65},{2,98}... | collective-permute-start | bytes 4718600 | tf_op jit(solution)/shard_map/ppermute | solution.py:445
  39.8 18.5 %all-to-all-start = ((bf16[16,16,2048]{2,1,0:T(8,128)(2,1)}), bf16[16,16,2048]{2,1,0:T(8,128)(2,1)S(1)}, u32[]{:S(2)}, u32[]{:S(2)}) async-start(bf16[16,16,2048]{2,1,0:T(8,128)(2,1)} %bitcast.38), calls=%async_computation | async-start | bytes 2097152 | tf_op jit(solution)/shard_map/all_to_all | solution.py:452
  44.4 0.6 copy-start.9
  45.0 0.6 copy-start.10
  45.7 1.2 copy-start.4
  46.9 14.0 %copy-start.11 = (bf16[128,128]{1,0:T(8,128)(2,1)S(1)}, bf16[128,128]{1,0:T(8,128)(2,1)}, u32[]{:S(2)}) copy-start(bf16[128,128]{1,0:T(8,128)(2,1)} %constant.21.clone.table_ref) | copy-start | bytes 98308
  52.7 22.1 %copy-start.12 = (f32[1,2048]{1,0:T(1,128)}, f32[1,2048]{1,0:T(1,128)S(1)}, u32[]{:S(2)}) copy-start(f32[1,2048]{1,0:T(1,128)S(1)} %get-tuple-element.133.refs_7_) | copy-start | bytes 24580
  58.3 22.0 %copy-start = (bf16[1,896,2048]{2,1,0:T(8,128)(2,1)S(1)}, bf16[1,896,2048]{2,1,0:T(8,128)(2,1)}, u32[]{:S(2)}) copy-start(bf16[1,896,2048]{2,1,0:T(8,128)(2,1)} %param.17) | copy-start | bytes 11010052
  58.3 22.0 %copy-start.1 = (bf16[1,896,2048]{2,1,0:T(8,128)(2,1)S(1)}, bf16[1,896,2048]{2,1,0:T(8,128)(2,1)}, u32[]{:S(2)}) copy-start(bf16[1,896,2048]{2,1,0:T(8,128)(2,1)} %param.18) | copy-start | bytes 11010052
  74.8 52.5 %collective-permute-start.6 = (bf16[256,2048]{1,0:T(8,128)(2,1)S(1)}, bf16[256,2048]{1,0:T(8,128)(2,1)S(1)}, u32[]{:S(2)}, u32[]{:S(2)}) collective-permute-start(bf16[256,2048]{1,0:T(8,128)(2,1)S(1)} %sort_messages.3.refs_2_), channel_id=1, source_target_pairs={{0,32},{32,64},{64,96},{96,0},{1,33},{33,65},{65,97},{97,1},{2,34}... | collective-permute-start | bytes 3145736 | tf_op jit(solution)/shard_map/ppermute | solution.py:445
  74.9 52.4 %collective-permute-start.7 = (bf16[256,2048]{1,0:T(8,128)(2,1)S(1)}, bf16[256,2048]{1,0:T(8,128)(2,1)S(1)}, u32[]{:S(2)}, u32[]{:S(2)}) collective-permute-start(bf16[256,2048]{1,0:T(8,128)(2,1)S(1)} %sort_messages.3.refs_2_), channel_id=1, source_target_pairs={{0,96},{32,0},{64,32},{96,64},{1,97},{33,1},{65,33},{97,65},{2,98}... | collective-permute-start | bytes 3145736 | tf_op jit(solution)/shard_map/ppermute | solution.py:445
  77.6 37.3 %collective-permute-start.4 = (bf16[192,2048]{1,0:T(8,128)(2,1)S(1)}, bf16[192,2048]{1,0:T(8,128)(2,1)S(1)}, u32[]{:S(2)}, u32[]{:S(2)}) collective-permute-start(bf16[192,2048]{1,0:T(8,128)(2,1)S(1)} %slice.16), channel_id=1, source_target_pairs={{0,32},{32,64},{64,96},{96,0},{1,33},{33,65},{65,97},{97,1},{2,34}... | collective-permute-start | bytes 2359304 | tf_op jit(solution)/shard_map/ppermute | solution.py:445
  77.6 37.3 %collective-permute-start.5 = (bf16[192,2048]{1,0:T(8,128)(2,1)S(1)}, bf16[192,2048]{1,0:T(8,128)(2,1)S(1)}, u32[]{:S(2)}, u32[]{:S(2)}) collective-permute-start(bf16[192,2048]{1,0:T(8,128)(2,1)S(1)} %slice.17), channel_id=1, source_target_pairs={{0,96},{32,0},{64,32},{96,64},{1,97},{33,1},{65,33},{97,65},{2,98}... | collective-permute-start | bytes 2359304 | tf_op jit(solution)/shard_map/ppermute | solution.py:445
  127.3 19.7 %collective-permute-start.8 = (bf16[128,2048]{1,0:T(8,128)(2,1)S(1)}, bf16[128,2048]{1,0:T(8,128)(2,1)S(1)}, u32[]{:S(2)}, u32[]{:S(2)}) collective-permute-start(bf16[128,2048]{1,0:T(8,128)(2,1)S(1)} %slice.14), channel_id=1, source_target_pairs={{0,32},{32,64},{64,96},{96,0},{1,33},{33,65},{65,97},{97,1},{2,34}... | collective-permute-start | bytes 1572872 | tf_op jit(solution)/shard_map/ppermute | solution.py:445
  127.5 19.5 %collective-permute-start.9 = (bf16[128,2048]{1,0:T(8,128)(2,1)S(1)}, bf16[128,2048]{1,0:T(8,128)(2,1)S(1)}, u32[]{:S(2)}, u32[]{:S(2)}) collective-permute-start(bf16[128,2048]{1,0:T(8,128)(2,1)S(1)} %slice.15), channel_id=1, source_target_pairs={{0,96},{32,0},{64,32},{96,64},{1,97},{33,1},{65,33},{97,65},{2,98}... | collective-permute-start | bytes 1572872 | tf_op jit(solution)/shard_map/ppermute | solution.py:445
  130.2 16.6 %collective-permute-start.10 = (bf16[96,2048]{1,0:T(8,128)(2,1)S(1)}, bf16[96,2048]{1,0:T(8,128)(2,1)S(1)}, u32[]{:S(2)}, u32[]{:S(2)}) collective-permute-start(bf16[96,2048]{1,0:T(8,128)(2,1)S(1)} %get-tuple-element.112), channel_id=1, source_target_pairs={{0,32},{32,64},{64,96},{96,0},{1,33},{33,65},{65,97},{97,1},{2,34}... | collective-permute-start | bytes 1179656 | tf_op jit(solution)/shard_map/ppermute | solution.py:445
  130.2 16.6 %collective-permute-start.11 = (bf16[96,2048]{1,0:T(8,128)(2,1)S(1)}, bf16[96,2048]{1,0:T(8,128)(2,1)S(1)}, u32[]{:S(2)}, u32[]{:S(2)}) collective-permute-start(bf16[96,2048]{1,0:T(8,128)(2,1)S(1)} %get-tuple-element.113), channel_id=1, source_target_pairs={{0,96},{32,0},{64,32},{96,64},{1,97},{33,1},{65,33},{97,65},{2,98}... | collective-permute-start | bytes 1179656 | tf_op jit(solution)/shard_map/ppermute | solution.py:445
  147.0 16.0 %copy-start.7 = (bf16[256,192]{1,0:T(8,128)(2,1)S(1)}, bf16[256,192]{1,0:T(8,128)(2,1)}, u32[]{:S(2)}) copy-start(bf16[256,192]{1,0:T(8,128)(2,1)} %constant.22.clone.refs_0_) | copy-start | bytes 294916
  147.0 16.0 %collective-permute-start.12 = (bf16[192,2048]{1,0:T(8,128)(2,1)S(1)}, bf16[192,2048]{1,0:T(8,128)(2,1)S(1)}, u32[]{:S(2)}, u32[]{:S(2)}) collective-permute-start(bf16[192,2048]{1,0:T(8,128)(2,1)S(1)} %get-tuple-element.116), channel_id=1, source_target_pairs={{0,32},{32,64},{64,96},{96,0},{1,33},{33,65},{65,97},{97,1},{2,34}... | collective-permute-start | bytes 2359304 | tf_op jit(solution)/shard_map/ppermute | solution.py:445
  147.5 15.5 %collective-permute-start.13 = (bf16[192,2048]{1,0:T(8,128)(2,1)S(1)}, bf16[192,2048]{1,0:T(8,128)(2,1)S(1)}, u32[]{:S(2)}, u32[]{:S(2)}) collective-permute-start(bf16[192,2048]{1,0:T(8,128)(2,1)S(1)} %get-tuple-element.117), channel_id=1, source_target_pairs={{0,96},{32,0},{64,32},{96,64},{1,97},{33,1},{65,33},{97,65},{2,98}... | collective-permute-start | bytes 2359304 | tf_op jit(solution)/shard_map/ppermute | solution.py:445
  160.2 9.7 %collective-permute-start.14 = (bf16[64,2048]{1,0:T(8,128)(2,1)S(1)}, bf16[64,2048]{1,0:T(8,128)(2,1)S(1)}, u32[]{:S(2)}, u32[]{:S(2)}) collective-permute-start(bf16[64,2048]{1,0:T(8,128)(2,1)S(1)} %get-tuple-element.120), channel_id=1, source_target_pairs={{0,32},{32,64},{64,96},{96,0},{1,33},{33,65},{65,97},{97,1},{2,34}... | collective-permute-start | bytes 786440 | tf_op jit(solution)/shard_map/ppermute | solution.py:445
  160.3 9.6 %collective-permute-start.15 = (bf16[64,2048]{1,0:T(8,128)(2,1)S(1)}, bf16[64,2048]{1,0:T(8,128)(2,1)S(1)}, u32[]{:S(2)}, u32[]{:S(2)}) collective-permute-start(bf16[64,2048]{1,0:T(8,128)(2,1)S(1)} %get-tuple-element.121), channel_id=1, source_target_pairs={{0,96},{32,0},{64,32},{96,64},{1,97},{33,1},{65,33},{97,65},{2,98}... | collective-permute-start | bytes 786440 | tf_op jit(solution)/shard_map/ppermute | solution.py:445
  169.9 17.6 %all-to-all-start.2 = ((bf16[16,16,2048]{2,1,0:T(8,128)(2,1)}), bf16[16,16,2048]{2,1,0:T(8,128)(2,1)S(1)}, u32[]{:S(2)}, u32[]{:S(2)}) async-start(bf16[16,16,2048]{2,1,0:T(8,128)(2,1)} %bitcast.14), calls=%async_computation.2 | async-start | bytes 2097152 | tf_op jit(solution)/shard_map/all_to_all | solution.py:452
  175.5 10.4 %collective-permute-start.16 = (bf16[128,2048]{1,0:T(8,128)(2,1)S(1)}, bf16[128,2048]{1,0:T(8,128)(2,1)S(1)}, u32[]{:S(2)}, u32[]{:S(2)}) collective-permute-start(bf16[128,2048]{1,0:T(8,128)(2,1)S(1)} %get-tuple-element.131), channel_id=1, source_target_pairs={{0,32},{32,64},{64,96},{96,0},{1,33},{33,65},{65,97},{97,1},{2,34}... | collective-permute-start | bytes 1572872 | tf_op jit(solution)/shard_map/ppermute | solution.py:445
  175.6 10.4 %collective-permute-start.17 = (bf16[128,2048]{1,0:T(8,128)(2,1)S(1)}, bf16[128,2048]{1,0:T(8,128)(2,1)S(1)}, u32[]{:S(2)}, u32[]{:S(2)}) collective-permute-start(bf16[128,2048]{1,0:T(8,128)(2,1)S(1)} %get-tuple-element.132), channel_id=1, source_target_pairs={{0,96},{32,0},{64,32},{96,64},{1,97},{33,1},{65,33},{97,65},{2,98}... | collective-permute-start | bytes 1572872 | tf_op jit(solution)/shard_map/ppermute | solution.py:445
  187.5 14.8 %copy-start.13 = (bf16[16,16,2048]{2,1,0:T(8,128)(2,1)}, bf16[16,16,2048]{2,1,0:T(8,128)(2,1)S(1)}, u32[]{:S(2)}) copy-start(bf16[16,16,2048]{2,1,0:T(8,128)(2,1)S(1)} %all-to-all-done.2) | copy-start | bytes 3145732
  187.5 14.8 %all-to-all-start.3 = ((bf16[16,8,2048]{2,1,0:T(8,128)(2,1)}), bf16[16,8,2048]{2,1,0:T(8,128)(2,1)S(1)}, u32[]{:S(2)}, u32[]{:S(2)}) async-start(bf16[16,8,2048]{2,1,0:T(8,128)(2,1)} %bitcast.16), calls=%async_computation.3 | async-start | bytes 1048576 | tf_op jit(solution)/shard_map/all_to_all | solution.py:452
  202.2 0.8 copy-start.14

commit v8 on v6

--- a/solution.py
+++ b/solution.py
@@ -140,7 +140,7 @@
     return pl.pallas_call(
         functools.partial(pack_body, spread),
         out_shape=jax.ShapeDtypeStruct((rows // size * wide, dim), BF),
-        compiler_params=params(38),
+        compiler_params=params(16),
         name="pack_returns",
     )(*head, own_a, own_b, *in_vmem((from_prev, from_next)))
 
@@ -158,7 +158,7 @@
     return pl.pallas_call(
         hop_body,
         out_shape=[jax.ShapeDtypeStruct((2 * half, dim), BF)] * 2,
-        compiler_params=params(38),
+        compiler_params=params(16),
         name="hop_sums",
     )(*parts[:4], *in_vmem(parts[4:]))
 
@@ -225,7 +225,7 @@
             pltpu.VMEM((rows, dim), BF),
             pltpu.VMEM((2, hidden // HIDDEN_STEP, rows, HIDDEN_STEP), BF),
         ],
-        compiler_params=params(30),
+        compiler_params=params(24),
         cost_estimate=pl.CostEstimate(
             flops=6 * rows * 2 * hidden * dim // 8,
             bytes_accessed=rows * dim,
@@ -483,10 +483,10 @@
     low_near, high = tie(low_near, high)
     low_far = far(*low_near)
     high_near = ring(high)
-    first = expert_rows((low, *low_near), some(0, 3), both)
+    first = expert_rows((low, *low_near, high), some(0, 3) + some(1, 1), both)
     low_far, high_near, first = tie(low_far, high_near, first)
     high_far = far(*high_near)
-    second = expert_rows((*low_far, high), some(0, 2) + some(1, 1), both)
+    second = expert_rows(low_far, some(0, 2), both)
     high_near, second = tie(high_near, second)
     third = expert_rows(high_near, some(1, 2), both)
     low_sums = hop_sums(*first[4:6], *first[2:4], shift(second[0], 1), shift(second[1], -1))
@@ -502,7 +502,7 @@
     low_home, high_got = tie(low_home, high_got)
     low_back = exchange(low_home)
     high_sums = hop_sums(*third[2:4], *third[:2], *high_got)
-    backs = (low_back, exchange(home(second[2:4], high_sums, sizes[1])))
+    backs = (low_back, exchange(home(first[6:8], high_sums, sizes[1])))
 
     mid, local, start = combine_and_scan(
         tables, backs, dy, steps, rate, total, mix, drive

time: 236 us -> 234 us (level)
  waiting for transfers between devices: 56.1 us -> 48.5 us
  starting transfers between devices: 35.7 us -> 39.5 us
    ppermute x16, waiting for transfers between devices: 41 us -> 33.4 us  [shift(): return lax.ppermute(value, 'z', ring)]
    ppermute x16, starting transfers between devices: 19.6 us -> 23.4 us  [shift(): return lax.ppermute(value, 'z', ring)]
  transfers between devices with their start and end apart: 21 -> 21, of which waited for: 9 -> 7; matrix products, arithmetic and copies ran while one was open for 3% -> 3% of each run, Pallas kernels for 27% -> 28%
where the time goes in v8:
time: 234 us
  Pallas kernels  82.9 us (35%)
  blocking collectives  50.1 us (21%)
  waiting for transfers between devices  48.5 us (21%)
  starting transfers between devices  39.5 us (17%)
  local copies, waits for them, and re-layouts  11.7 us (5%)
    pallas_call x4, Pallas kernels, expert_rows(): pl.pallas_call(functools.partial(expert_body, sizes), in_specs=[vmem] * (...  54.8 us
    ppermute x16, waiting for transfers between devices, shift(): return lax.ppermute(value, 'z', ring)  33.4 us
    all_to_all x1, blocking collectives, exchange(): got = lax.all_to_all(parts, 'exp', split_axis=0, concat_axis=0, tiled=True)  28.3 us
    ppermute x16, starting transfers between devices, shift(): return lax.ppermute(value, 'z', ring)  23.4 us
    all_gather x1, blocking collectives, on_device(): starts = lax.all_gather(start, ('z', 'core'))  21.8 us
    all_to_all x3, waiting for transfers between devices, exchange(): got = lax.all_to_all(parts, 'exp', split_axis=0, concat_axis=0, tiled=True)  15.2 us
    all_to_all x3, starting transfers between devices, exchange(): got = lax.all_to_all(parts, 'exp', split_axis=0, concat_axis=0, tiled=True)  14.5 us
    pallas_call x1, Pallas kernels, combine_and_scan(): pl.pallas_call(scan_body, grid=(dim // cols,), in_specs=[whole(*t.shape)...  10.6 us
  transfers between devices with their start and end apart: 21, of which 7 were waited for; matrix products, arithmetic and copies ran while one was open for 3% of the time, Pallas kernels for 28%

profile of v8, /device:TPU:1, one launch (start us, length us, event | category | flops | bytes accessed | tf_op | source)
XLA Modules:
  0.0 233.7 jit_solution(17241459647118085925)
XLA Ops:
  0.6 1.5 collective-permute-start
  2.2 0.8 copy.15
  3.1 1.1 copy-done.2
  4.2 1.0 copy-done.6
  5.2 1.7 gather_rows.1
  6.9 28.3 %all_to_all.20 = bf16[16,24,2048]{2,1,0:T(8,128)(2,1)S(1)} all-to-all(bf16[16,24,2048]{2,1,0:T(8,128)(2,1)S(1)} %bitcast.37), channel_id=1, replica_groups=mesh['z'=4,'core'=2,'exp'=16] {'exp'}, dimensions={0} | all-to-all | bytes 3145728 | tf_op jit(solution)/shard_map/all_to_all | solution.py:451
  35.3 0.6 sort_messages.2.refs_0_
  35.9 1.7 collective-permute-start.2
  37.6 2.2 collective-permute-start.3
  39.8 3.8 %all-to-all-start = ((bf16[16,16,2048]{2,1,0:T(8,128)(2,1)}), bf16[16,16,2048]{2,1,0:T(8,128)(2,1)S(1)}, u32[]{:S(2)}, u32[]{:S(2)}) async-start(bf16[16,16,2048]{2,1,0:T(8,128)(2,1)} %bitcast.38), calls=%async_computation | async-start | bytes 2097152 | tf_op jit(solution)/shard_map/all_to_all | solution.py:451
  43.9 0.4 weigh_tables.1
  44.4 0.6 copy-done.9
  45.0 0.6 copy-done.10
  45.7 1.2 copy-done.4
  46.9 5.8 %reach_table.1 = (bf16[16,128,2048]{2,1,0:T(8,128)(2,1)}, f32[1,2048]{1,0:T(1,128)S(1)}) custom-call(f32[128,2048]{1,0:T(8,128)S(1)} %bitcast.40, f32[16,2048]{1,0:T(8,128)S(1)} %copy-done.5, f32[128,16]{1,0:T(8,128)S(1)} %bitcast.44), custom_call_target="tpu_custom_call" | custom-call | flops 33554432 | bytes 8388608 | tf_op jit(solution)/shard_map/reach_table/pallas_call | solution.py:376
  52.7 5.6 %all-to-all-done = bf16[16,16,2048]{2,1,0:T(8,128)(2,1)S(1)} async-done(((bf16[16,16,2048]{2,1,0:T(8,128)(2,1)}), bf16[16,16,2048]{2,1,0:T(8,128)(2,1)S(1)}, u32[]{:S(2)}, u32[]{:S(2)}) %all-to-all-start) | async-done | bytes 1048608 | tf_op jit(solution)/shard_map/all_to_all | solution.py:451
  58.3 1.3 broadcast_in_dim.18.refs_8_
  59.6 1.3 broadcast_in_dim.20.refs_9_
  60.9 0.4 sort_messages.3.refs_3_
  61.3 11.1 %collective-permute-done.2.refs_1_ = bf16[384,2048]{1,0:T(8,128)(2,1)} collective-permute-done((bf16[384,2048]{1,0:T(8,128)(2,1)S(1)}, bf16[384,2048]{1,0:T(8,128)(2,1)}, u32[]{:S(2)}, u32[]{:S(2)}) %collective-permute-start.2) | collective-permute-done | bytes 1572896 | tf_op jit(solution)/shard_map/ppermute | solution.py:444
  72.4 0.4 collective-permute-start.6
  72.8 2.2 collective-permute-start.7
  75.1 1.2 slice.12
  76.4 1.2 slice.13
  77.6 2.9 %collective-permute-start.5 = (bf16[192,2048]{1,0:T(8,128)(2,1)S(1)}, bf16[192,2048]{1,0:T(8,128)(2,1)S(1)}, u32[]{:S(2)}, u32[]{:S(2)}) collective-permute-start(bf16[192,2048]{1,0:T(8,128)(2,1)S(1)} %slice.13), channel_id=1, source_target_pairs={{0,96},{32,0},{64,32},{96,64},{1,97},{33,1},{65,33},{97,65},{2,98}... | collective-permute-start | bytes 2359304 | tf_op jit(solution)/shard_map/ppermute | solution.py:444
  80.5 22.5 %expert_rows.4 = (bf16[96,2048]{1,0:T(8,128)(2,1)S(1)}, bf16[96,2048]{1,0:T(8,128)(2,1)S(1)}, bf16[96,2048]{1,0:T(8,128)(2,1)S(1)}, bf16[96,2048]{1,0:T(8,128)(2...) custom-call(bf16[384,2048]{1,0:T(8,128)(2,1)S(1)} %sort_messages.2.r, ...), custom_call_target="tpu_custom_call" | custom-call | flops 1937768448 | bytes 1441792 | tf_op jit(solution)/shard_map/expert_rows/pallas_call | solution.py:218
  103.0 9.3 %collective-permute-done.4.refs_0_ = bf16[192,2048]{1,0:T(8,128)(2,1)S(1)} collective-permute-done((bf16[192,2048]{1,0:T(8,128)(2,1)S(1)}, bf16[192,2048]{1,0:T(8,128)(2,1)S(1)}, u32[]{:S(2)}, u32[]{:S(2)}) %collective-permute-start.4) | collective-permute-done | bytes 786464 | tf_op jit(solution)/shard_map/ppermute | solution.py:444
  112.6 2.7 %collective-permute-start.9 = (bf16[128,2048]{1,0:T(8,128)(2,1)S(1)}, bf16[128,2048]{1,0:T(8,128)(2,1)S(1)}, u32[]{:S(2)}, u32[]{:S(2)}) collective-permute-start(bf16[128,2048]{1,0:T(8,128)(2,1)S(1)} %slice.15), channel_id=1, source_target_pairs={{0,96},{32,0},{64,32},{96,64},{1,97},{33,1},{65,33},{97,65},{2,98}... | collective-permute-start | bytes 1572872 | tf_op jit(solution)/shard_map/ppermute | solution.py:444
  115.3 11.1 %expert_rows.5 = (bf16[96,2048]{1,0:T(8,128)(2,1)S(1)}, bf16[96,2048]{1,0:T(8,128)(2,1)S(1)}) custom-call(bf16[192,2048]{1,0:T(8,128)(2,1)S(1)} %collective-permute-done.4.refs_0_, bf16[192,2048]{1,0:T(8,128)(2,1)S(1)} %collective-permute-done.5.refs_1_, bf16[896,2048]{1,0:T(8,128)(2,1)S(1)} %bitcast.25, ...), custom_call_target="tpu_custom_call" | custom-call | flops 528482304 | bytes 393216 | tf_op jit(solution)/shard_map/expert_rows/pallas_call | solution.py:218
  126.5 2.7 %collective-permute-start.11 = (bf16[96,2048]{1,0:T(8,128)(2,1)S(1)}, bf16[96,2048]{1,0:T(8,128)(2,1)S(1)}, u32[]{:S(2)}, u32[]{:S(2)}) collective-permute-start(bf16[96,2048]{1,0:T(8,128)(2,1)S(1)} %get-tuple-element.113), channel_id=1, source_target_pairs={{0,96},{32,0},{64,32},{96,64},{1,97},{33,1},{65,33},{97,65},{2,98}... | collective-permute-start | bytes 1179656 | tf_op jit(solution)/shard_map/ppermute | solution.py:444
  129.2 10.9 %expert_rows.6 = (bf16[64,2048]{1,0:T(8,128)(2,1)S(1)}, bf16[64,2048]{1,0:T(8,128)(2,1)S(1)}, bf16[64,2048]{1,0:T(8,128)(2,1)S(1)}, bf16[64,2048]{1,0:T(8,128)(2,1)S(1)}) custom-call(bf16[256,2048]{1,0:T(8,128)(2,1)S(1)} %collective-permute-done.6.refs_0_, bf16[256,2048]{1,0:T(8,128)(2,1)S(1)} %collective-permute-done.7.refs_1_, ...), custom_call_target="tpu_custom_call" | custom-call | flops 704643072 | bytes 524288 | tf_op jit(solution)/shard_map/expert_rows/pallas_call | solution.py:218
  140.1 0.2 hop_sums.2
  140.4 2.7 %collective-permute-start.13 = (bf16[192,2048]{1,0:T(8,128)(2,1)S(1)}, bf16[192,2048]{1,0:T(8,128)(2,1)S(1)}, u32[]{:S(2)}, u32[]{:S(2)}) collective-permute-start(bf16[192,2048]{1,0:T(8,128)(2,1)S(1)} %get-tuple-element.117), channel_id=1, source_target_pairs={{0,96},{32,0},{64,32},{96,64},{1,97},{33,1},{65,33},{97,65},{2,98}... | collective-permute-start | bytes 2359304 | tf_op jit(solution)/shard_map/ppermute | solution.py:444
  143.1 10.3 %expert_rows.7 = (bf16[64,2048]{1,0:T(8,128)(2,1)S(1)}, bf16[64,2048]{1,0:T(8,128)(2,1)S(1)}) custom-call(bf16[128,2048]{1,0:T(8,128)(2,1)S(1)} %collective-permute-done.8.refs_0_, bf16[128,2048]{1,0:T(8,128)(2,1)S(1)} %collective-permute-done.9.refs_1_, bf16[896,2048]{1,0:T(8,128)(2,1)S(1)} %bitcast.27, ...), custom_call_target="tpu_custom_call" | custom-call | flops 352321536 | bytes 262144 | tf_op jit(solution)/shard_map/expert_rows/pallas_call | solution.py:218
  153.5 2.7 %collective-permute-start.15 = (bf16[64,2048]{1,0:T(8,128)(2,1)S(1)}, bf16[64,2048]{1,0:T(8,128)(2,1)S(1)}, u32[]{:S(2)}, u32[]{:S(2)}) collective-permute-start(bf16[64,2048]{1,0:T(8,128)(2,1)S(1)} %get-tuple-element.121), channel_id=1, source_target_pairs={{0,96},{32,0},{64,32},{96,64},{1,97},{33,1},{65,33},{97,65},{2,98}... | collective-permute-start | bytes 786440 | tf_op jit(solution)/shard_map/ppermute | solution.py:444
  156.2 1.5 pack_returns.2
  157.6 5.4 %collective-permute-done.14.got_a = bf16[64,2048]{1,0:T(8,128)(2,1)S(1)} collective-permute-done((bf16[64,2048]{1,0:T(8,128)(2,1)S(1)}, bf16[64,2048]{1,0:T(8,128)(2,1)S(1)}, u32[]{:S(2)}, u32[]{:S(2)}) %collective-permute-start.14) | collective-permute-done | bytes 262176 | tf_op jit(solution)/shard_map/ppermute | solution.py:444
  163.1 4.9 %all-to-all-start.2 = ((bf16[16,16,2048]{2,1,0:T(8,128)(2,1)}), bf16[16,16,2048]{2,1,0:T(8,128)(2,1)S(1)}, u32[]{:S(2)}, u32[]{:S(2)}) async-start(bf16[16,16,2048]{2,1,0:T(8,128)(2,1)} %bitcast.14), calls=%async_computation.2 | async-start | bytes 2097152 | tf_op jit(solution)/shard_map/all_to_all | solution.py:451
  168.2 2.7 %collective-permute-start.17 = (bf16[128,2048]{1,0:T(8,128)(2,1)S(1)}, bf16[128,2048]{1,0:T(8,128)(2,1)S(1)}, u32[]{:S(2)}, u32[]{:S(2)}) collective-permute-start(bf16[128,2048]{1,0:T(8,128)(2,1)S(1)} %get-tuple-element.132), channel_id=1, source_target_pairs={{0,96},{32,0},{64,32},{96,64},{1,97},{33,1},{65,33},{97,65},{2,98}... | collective-permute-start | bytes 1572872 | tf_op jit(solution)/shard_map/ppermute | solution.py:444
  170.9 7.5 %collective-permute-done.16.refs_2_ = bf16[128,2048]{1,0:T(8,128)(2,1)S(1)} collective-permute-done((bf16[128,2048]{1,0:T(8,128)(2,1)S(1)}, bf16[128,2048]{1,0:T(8,128)(2,1)S(1)}, u32[]{:S(2)}, u32[]{:S(2)}) %collective-permute-start.16) | collective-permute-done | bytes 524320 | tf_op jit(solution)/shard_map/ppermute | solution.py:444
  178.4 1.0 pack_returns.3
  179.4 0.6 all-to-all-done.2
  180.0 5.7 %all-to-all-start.3 = ((bf16[16,8,2048]{2,1,0:T(8,128)(2,1)}), bf16[16,8,2048]{2,1,0:T(8,128)(2,1)S(1)}, u32[]{:S(2)}, u32[]{:S(2)}) async-start(bf16[16,8,2048]{2,1,0:T(8,128)(2,1)} %bitcast.16), calls=%async_computation.3 | async-start | bytes 1048576 | tf_op jit(solution)/shard_map/all_to_all | solution.py:451
  185.8 8.9 %all-to-all-done.3 = bf16[16,8,2048]{2,1,0:T(8,128)(2,1)S(1)} async-done(((bf16[16,8,2048]{2,1,0:T(8,128)(2,1)}), bf16[16,8,2048]{2,1,0:T(8,128)(2,1)S(1)}, u32[]{:S(2)}, u32[]{:S(2)}) %all-to-all-start.3) | async-done | bytes 524320 | tf_op jit(solution)/shard_map/all_to_all | solution.py:451
  194.7 0.8 copy-done.14
  195.5 10.6 %combine_and_scan.1 = (bf16[128,2048]{1,0:T(8,128)(2,1)}, f32[128,2048]{1,0:T(8,128)}, bf16[24,2048]{1,0:T(8,128)(2,1)}) custom-call(bf16[128,384]{1,0:T(8,128)(2,1)} %copy-done.9, bf16[128,384]{1,0:T(8,128)(2,1)} %copy-done.10, bf16[256,2048]{1,0:T(8,128)(2,1)} %bitcast.47, bf16[128,2048]{1,0:T(8,128)(2,1)} %bitcast.49, bf16[128,2048]{1,0:T(8,128)(2,1)} %bitcast.35, ...), custom_call_target="tpu_custom_call" | custom-call | tf_op jit(solution)/shard_map/combine_and_scan/pallas_call | solution.py:330
  206.1 21.8 %all-gather = bf16[192,2048]{1,0:T(8,128)(2,1)} all-gather(bf16[24,2048]{1,0:T(8,128)(2,1)} %get-tuple-element.137), channel_id=2, replica_groups=mesh['z'=4,'core'=2,'exp'=16] {'z','core'}, dimensions={0}, use_global_device_ids=true | all-gather | bytes 884736 | tf_op jit(solution)/shard_map/all_gather | solution.py:510
  227.9 5.8 %add_carry.1 = bf16[128,2048]{1,0:T(8,128)(2,1)} custom-call(s32[1]{0:T(128)} %bitcast.19.place_ref, bf16[8,24,2048]{2,1,0:T(8,128)(2,1)} %bitcast.48, f32[16,2048]{1,0:T(8,128)} %rate_ref.3, f32[128,2048]{1,0:T(8,128)} %get-tuple-element.138.local_ref, bf16[16,128,2048]{2,1,0:T(8,128)(2,1)} %get-tuple-element.139.reach_ref), custom_call_target="tpu_custom_call" | custom-call | tf_op jit(solution)/shard_map/add_carry/pallas_call | solution.py:420
  (58 shorter events, 1.2 us)
Async XLA Ops:
  0.6 34.7 %copy-start.8 = (bf16[192,192]{1,0:T(8,128)(2,1)S(1)}, bf16[192,192]{1,0:T(8,128)(2,1)}, u32[]{:S(2)}) copy-start(bf16[192,192]{1,0:T(8,128)(2,1)} %constant.20.clone.table_ref) | copy-start | bytes 221188
  0.6 34.6 %collective-permute-start = (bf16[896,2048]{1,0:T(8,128)(2,1)}, bf16[896,2048]{1,0:T(8,128)(2,1)}, u32[]{:S(2)}, u32[]{:S(2)}) collective-permute-start(bf16[896,2048]{1,0:T(8,128)(2,1)} %bitcast.23), channel_id=1, source_target_pairs={{0,16},{16,0},{1,17},{17,1},{2,18},{18,2},{3,19},{19,3},{4,20},{20... | collective-permute-start | bytes 11010056 | tf_op jit(solution)/shard_map/ppermute | solution.py:447
  2.1 33.1 %collective-permute-start.1 = (bf16[896,2048]{1,0:T(8,128)(2,1)}, bf16[896,2048]{1,0:T(8,128)(2,1)}, u32[]{:S(2)}, u32[]{:S(2)}) collective-permute-start(bf16[896,2048]{1,0:T(8,128)(2,1)} %bitcast.28), channel_id=1, source_target_pairs={{0,16},{16,0},{1,17},{17,1},{2,18},{18,2},{3,19},{19,3},{4,20},{20... | collective-permute-start | bytes 11010056 | tf_op jit(solution)/shard_map/ppermute | solution.py:447
  3.1 1.1 copy-start.2
  4.1 1.0 copy-start.6
  6.9 28.4 %copy-start.3 = (bf16[256,2048]{1,0:T(8,128)(2,1)}, bf16[256,2048]{1,0:T(8,128)(2,1)S(1)}, u32[]{:S(2)}) copy-start(bf16[256,2048]{1,0:T(8,128)(2,1)S(1)} %get-tuple-element.71) | copy-start | bytes 3145732
  6.9 36.7 %copy-start.15 = (f32[1,128,16]{1,2,0:T(8,128)S(1)}, f32[1,128,16]{1,2,0:T(8,128)}, u32[]{:S(2)}) copy-start(f32[1,128,16]{1,2,0:T(8,128)} %param.21) | copy-start | bytes 24580
  6.9 36.8 %copy-start.17 = (f32[1,128,2]{1,2,0:T(2,128)S(1)}, f32[1,128,2]{1,2,0:T(2,128)}, u32[]{:S(2)}) copy-start(f32[1,128,2]{1,2,0:T(2,128)} %param.16) | copy-start | bytes 3076
  6.9 36.9 %copy-start.16 = (f32[1,128,16]{1,2,0:T(8,128)S(1)}, f32[1,128,16]{1,2,0:T(8,128)}, u32[]{:S(2)}) copy-start(f32[1,128,16]{1,2,0:T(8,128)} %param.22) | copy-start | bytes 24580
  6.9 38.7 %copy-start.5 = (f32[16,2048]{1,0:T(8,128)S(1)}, f32[16,2048]{1,0:T(8,128)}, u32[]{:S(2)}) copy-start(f32[16,2048]{1,0:T(8,128)} %rate_ref.3) | copy-start | bytes 393220
  35.9 36.5 %collective-permute-start.2 = (bf16[384,2048]{1,0:T(8,128)(2,1)S(1)}, bf16[384,2048]{1,0:T(8,128)(2,1)}, u32[]{:S(2)}, u32[]{:S(2)}) collective-permute-start(bf16[384,2048]{1,0:T(8,128)(2,1)S(1)} %sort_messages.2.refs_0_), channel_id=1, source_target_pairs={{0,32},{32,64},{64,96},{96,0},{1,33},{33,65},{65,97},{97,1},{2,34}... | collective-permute-start | bytes 4718600 | tf_op jit(solution)/shard_map/ppermute | solution.py:444
  37.6 34.8 %collective-permute-start.3 = (bf16[384,2048]{1,0:T(8,128)(2,1)S(1)}, bf16[384,2048]{1,0:T(8,128)(2,1)}, u32[]{:S(2)}, u32[]{:S(2)}) collective-permute-start(bf16[384,2048]{1,0:T(8,128)(2,1)S(1)} %sort_messages.2.refs_0_), channel_id=1, source_target_pairs={{0,96},{32,0},{64,32},{96,64},{1,97},{33,1},{65,33},{97,65},{2,98}... | collective-permute-start | bytes 4718600 | tf_op jit(solution)/shard_map/ppermute | solution.py:444
  39.8 18.5 %all-to-all-start = ((bf16[16,16,2048]{2,1,0:T(8,128)(2,1)}), bf16[16,16,2048]{2,1,0:T(8,128)(2,1)S(1)}, u32[]{:S(2)}, u32[]{:S(2)}) async-start(bf16[16,16,2048]{2,1,0:T(8,128)(2,1)} %bitcast.38), calls=%async_computation | async-start | bytes 2097152 | tf_op jit(solution)/shard_map/all_to_all | solution.py:451
  44.4 0.6 copy-start.9
  45.0 0.6 copy-start.10
  45.7 1.2 copy-start.4
  46.9 14.0 %copy-start.11 = (bf16[128,128]{1,0:T(8,128)(2,1)S(1)}, bf16[128,128]{1,0:T(8,128)(2,1)}, u32[]{:S(2)}) copy-start(bf16[128,128]{1,0:T(8,128)(2,1)} %constant.21.clone.table_ref) | copy-start | bytes 98308
  52.7 24.9 %copy-start.12 = (f32[1,2048]{1,0:T(1,128)}, f32[1,2048]{1,0:T(1,128)S(1)}, u32[]{:S(2)}) copy-start(f32[1,2048]{1,0:T(1,128)S(1)} %get-tuple-element.133.refs_7_) | copy-start | bytes 24580
  58.3 22.2 %copy-start = (bf16[1,896,2048]{2,1,0:T(8,128)(2,1)S(1)}, bf16[1,896,2048]{2,1,0:T(8,128)(2,1)}, u32[]{:S(2)}) copy-start(bf16[1,896,2048]{2,1,0:T(8,128)(2,1)} %param.17) | copy-start | bytes 11010052
  58.3 22.2 %copy-start.1 = (bf16[1,896,2048]{2,1,0:T(8,128)(2,1)S(1)}, bf16[1,896,2048]{2,1,0:T(8,128)(2,1)}, u32[]{:S(2)}) copy-start(bf16[1,896,2048]{2,1,0:T(8,128)(2,1)} %param.18) | copy-start | bytes 11010052
  72.4 40.0 %collective-permute-start.6 = (bf16[256,2048]{1,0:T(8,128)(2,1)S(1)}, bf16[256,2048]{1,0:T(8,128)(2,1)S(1)}, u32[]{:S(2)}, u32[]{:S(2)}) collective-permute-start(bf16[256,2048]{1,0:T(8,128)(2,1)S(1)} %sort_messages.3.refs_3_), channel_id=1, source_target_pairs={{0,32},{32,64},{64,96},{96,0},{1,33},{33,65},{65,97},{97,1},{2,34}... | collective-permute-start | bytes 3145736 | tf_op jit(solution)/shard_map/ppermute | solution.py:444
  72.8 39.5 %collective-permute-start.7 = (bf16[256,2048]{1,0:T(8,128)(2,1)S(1)}, bf16[256,2048]{1,0:T(8,128)(2,1)S(1)}, u32[]{:S(2)}, u32[]{:S(2)}) collective-permute-start(bf16[256,2048]{1,0:T(8,128)(2,1)S(1)} %sort_messages.3.refs_3_), channel_id=1, source_target_pairs={{0,96},{32,0},{64,32},{96,64},{1,97},{33,1},{65,33},{97,65},{2,98}... | collective-permute-start | bytes 3145736 | tf_op jit(solution)/shard_map/ppermute | solution.py:444
  76.3 36.1 %collective-permute-start.4 = (bf16[192,2048]{1,0:T(8,128)(2,1)S(1)}, bf16[192,2048]{1,0:T(8,128)(2,1)S(1)}, u32[]{:S(2)}, u32[]{:S(2)}) collective-permute-start(bf16[192,2048]{1,0:T(8,128)(2,1)S(1)} %slice.12), channel_id=1, source_target_pairs={{0,32},{32,64},{64,96},{96,0},{1,33},{33,65},{65,97},{97,1},{2,34}... | collective-permute-start | bytes 2359304 | tf_op jit(solution)/shard_map/ppermute | solution.py:444
  77.6 34.8 %collective-permute-start.5 = (bf16[192,2048]{1,0:T(8,128)(2,1)S(1)}, bf16[192,2048]{1,0:T(8,128)(2,1)S(1)}, u32[]{:S(2)}, u32[]{:S(2)}) collective-permute-start(bf16[192,2048]{1,0:T(8,128)(2,1)S(1)} %slice.13), channel_id=1, source_target_pairs={{0,96},{32,0},{64,32},{96,64},{1,97},{33,1},{65,33},{97,65},{2,98}... | collective-permute-start | bytes 2359304 | tf_op jit(solution)/shard_map/ppermute | solution.py:444
  112.4 27.9 %collective-permute-start.8 = (bf16[128,2048]{1,0:T(8,128)(2,1)S(1)}, bf16[128,2048]{1,0:T(8,128)(2,1)S(1)}, u32[]{:S(2)}, u32[]{:S(2)}) collective-permute-start(bf16[128,2048]{1,0:T(8,128)(2,1)S(1)} %slice.14), channel_id=1, source_target_pairs={{0,32},{32,64},{64,96},{96,0},{1,33},{33,65},{65,97},{97,1},{2,34}... | collective-permute-start | bytes 1572872 | tf_op jit(solution)/shard_map/ppermute | solution.py:444
  112.6 27.7 %collective-permute-start.9 = (bf16[128,2048]{1,0:T(8,128)(2,1)S(1)}, bf16[128,2048]{1,0:T(8,128)(2,1)S(1)}, u32[]{:S(2)}, u32[]{:S(2)}) collective-permute-start(bf16[128,2048]{1,0:T(8,128)(2,1)S(1)} %slice.15), channel_id=1, source_target_pairs={{0,96},{32,0},{64,32},{96,64},{1,97},{33,1},{65,33},{97,65},{2,98}... | collective-permute-start | bytes 1572872 | tf_op jit(solution)/shard_map/ppermute | solution.py:444
  126.4 13.6 %collective-permute-start.10 = (bf16[96,2048]{1,0:T(8,128)(2,1)S(1)}, bf16[96,2048]{1,0:T(8,128)(2,1)S(1)}, u32[]{:S(2)}, u32[]{:S(2)}) collective-permute-start(bf16[96,2048]{1,0:T(8,128)(2,1)S(1)} %get-tuple-element.112), channel_id=1, source_target_pairs={{0,32},{32,64},{64,96},{96,0},{1,33},{33,65},{65,97},{97,1},{2,34}... | collective-permute-start | bytes 1179656 | tf_op jit(solution)/shard_map/ppermute | solution.py:444
  126.5 13.6 %collective-permute-start.11 = (bf16[96,2048]{1,0:T(8,128)(2,1)S(1)}, bf16[96,2048]{1,0:T(8,128)(2,1)S(1)}, u32[]{:S(2)}, u32[]{:S(2)}) collective-permute-start(bf16[96,2048]{1,0:T(8,128)(2,1)S(1)} %get-tuple-element.113), channel_id=1, source_target_pairs={{0,96},{32,0},{64,32},{96,64},{1,97},{33,1},{65,33},{97,65},{2,98}... | collective-permute-start | bytes 1179656 | tf_op jit(solution)/shard_map/ppermute | solution.py:444
  140.3 15.8 %copy-start.7 = (bf16[256,192]{1,0:T(8,128)(2,1)S(1)}, bf16[256,192]{1,0:T(8,128)(2,1)}, u32[]{:S(2)}) copy-start(bf16[256,192]{1,0:T(8,128)(2,1)} %constant.22.clone.refs_0_) | copy-start | bytes 294916
  140.3 15.8 %collective-permute-start.12 = (bf16[192,2048]{1,0:T(8,128)(2,1)S(1)}, bf16[192,2048]{1,0:T(8,128)(2,1)S(1)}, u32[]{:S(2)}, u32[]{:S(2)}) collective-permute-start(bf16[192,2048]{1,0:T(8,128)(2,1)S(1)} %get-tuple-element.116), channel_id=1, source_target_pairs={{0,32},{32,64},{64,96},{96,0},{1,33},{33,65},{65,97},{97,1},{2,34}... | collective-permute-start | bytes 2359304 | tf_op jit(solution)/shard_map/ppermute | solution.py:444
  140.4 15.7 %collective-permute-start.13 = (bf16[192,2048]{1,0:T(8,128)(2,1)S(1)}, bf16[192,2048]{1,0:T(8,128)(2,1)S(1)}, u32[]{:S(2)}, u32[]{:S(2)}) collective-permute-start(bf16[192,2048]{1,0:T(8,128)(2,1)S(1)} %get-tuple-element.117), channel_id=1, source_target_pairs={{0,96},{32,0},{64,32},{96,64},{1,97},{33,1},{65,33},{97,65},{2,98}... | collective-permute-start | bytes 2359304 | tf_op jit(solution)/shard_map/ppermute | solution.py:444
  153.4 9.7 %collective-permute-start.14 = (bf16[64,2048]{1,0:T(8,128)(2,1)S(1)}, bf16[64,2048]{1,0:T(8,128)(2,1)S(1)}, u32[]{:S(2)}, u32[]{:S(2)}) collective-permute-start(bf16[64,2048]{1,0:T(8,128)(2,1)S(1)} %get-tuple-element.120), channel_id=1, source_target_pairs={{0,32},{32,64},{64,96},{96,0},{1,33},{33,65},{65,97},{97,1},{2,34}... | collective-permute-start | bytes 786440 | tf_op jit(solution)/shard_map/ppermute | solution.py:444
  153.5 9.6 %collective-permute-start.15 = (bf16[64,2048]{1,0:T(8,128)(2,1)S(1)}, bf16[64,2048]{1,0:T(8,128)(2,1)S(1)}, u32[]{:S(2)}, u32[]{:S(2)}) collective-permute-start(bf16[64,2048]{1,0:T(8,128)(2,1)S(1)} %get-tuple-element.121), channel_id=1, source_target_pairs={{0,96},{32,0},{64,32},{96,64},{1,97},{33,1},{65,33},{97,65},{2,98}... | collective-permute-start | bytes 786440 | tf_op jit(solution)/shard_map/ppermute | solution.py:444
  163.1 17.0 %all-to-all-start.2 = ((bf16[16,16,2048]{2,1,0:T(8,128)(2,1)}), bf16[16,16,2048]{2,1,0:T(8,128)(2,1)S(1)}, u32[]{:S(2)}, u32[]{:S(2)}) async-start(bf16[16,16,2048]{2,1,0:T(8,128)(2,1)} %bitcast.14), calls=%async_computation.2 | async-start | bytes 2097152 | tf_op jit(solution)/shard_map/all_to_all | solution.py:451
  168.1 10.3 %collective-permute-start.16 = (bf16[128,2048]{1,0:T(8,128)(2,1)S(1)}, bf16[128,2048]{1,0:T(8,128)(2,1)S(1)}, u32[]{:S(2)}, u32[]{:S(2)}) collective-permute-start(bf16[128,2048]{1,0:T(8,128)(2,1)S(1)} %get-tuple-element.131), channel_id=1, source_target_pairs={{0,32},{32,64},{64,96},{96,0},{1,33},{33,65},{65,97},{97,1},{2,34}... | collective-permute-start | bytes 1572872 | tf_op jit(solution)/shard_map/ppermute | solution.py:444
  168.2 10.2 %collective-permute-start.17 = (bf16[128,2048]{1,0:T(8,128)(2,1)S(1)}, bf16[128,2048]{1,0:T(8,128)(2,1)S(1)}, u32[]{:S(2)}, u32[]{:S(2)}) collective-permute-start(bf16[128,2048]{1,0:T(8,128)(2,1)S(1)} %get-tuple-element.132), channel_id=1, source_target_pairs={{0,96},{32,0},{64,32},{96,64},{1,97},{33,1},{65,33},{97,65},{2,98}... | collective-permute-start | bytes 1572872 | tf_op jit(solution)/shard_map/ppermute | solution.py:444
  180.0 14.7 %copy-start.13 = (bf16[16,16,2048]{2,1,0:T(8,128)(2,1)}, bf16[16,16,2048]{2,1,0:T(8,128)(2,1)S(1)}, u32[]{:S(2)}) copy-start(bf16[16,16,2048]{2,1,0:T(8,128)(2,1)S(1)} %all-to-all-done.2) | copy-start | bytes 3145732
  180.0 14.7 %all-to-all-start.3 = ((bf16[16,8,2048]{2,1,0:T(8,128)(2,1)}), bf16[16,8,2048]{2,1,0:T(8,128)(2,1)S(1)}, u32[]{:S(2)}, u32[]{:S(2)}) async-start(bf16[16,8,2048]{2,1,0:T(8,128)(2,1)} %bitcast.16), calls=%async_computation.3 | async-start | bytes 1048576 | tf_op jit(solution)/shard_map/all_to_all | solution.py:451
  194.7 0.8 copy-start.14

commit v9 on v8

--- a/solution.py
+++ b/solution.py
@@ -280,6 +280,22 @@
     )(ids, weights)
 
 
+def fold_rows(parts):
+    rows = lax.broadcasted_iota(jnp.int32, parts[0].shape, 0)
+    for gap in (4, 2, 1):
+        first = (rows & gap) == 0
+        folded = []
+        for a, b in zip(parts[:gap], parts[gap:]):
+            kept, moved = jnp.where(first, a, b), jnp.where(first, b, a)
+            if gap == 4:
+                moved = pltpu.roll(moved, 4, 0)
+            else:
+                moved = jnp.where(first, pltpu.roll(moved, 8 - gap, 0), pltpu.roll(moved, gap, 0))
+            folded.append(kept + moved)
+        parts = folded
+    return parts[0]
+
+
 def scan_body(*refs):
     high_ref, low_ref = refs[:2]
     backs = refs[2:4]
@@ -305,13 +321,14 @@
             drive = jnp.concatenate([drive_ref[low_t + r]] * repeat, axis=1)
             mix = jnp.concatenate([mix_ref[low_t + r]] * repeat, axis=1)
             state = drive * jnp.broadcast_to(grads[r : r + 1], (states, cols)) + flow
-            rows.append(jnp.sum(mix * state, axis=0, keepdims=True))
+            product = mix * state
+            rows.append(product[:8] + product[8:])
             decay = jnp.exp(jnp.broadcast_to(deltas[r : r + 1], (states, cols)) * negative)
             flow = decay * state
-        local_ref[pl.ds(low_t, 8)] = jnp.concatenate(rows[::-1], axis=0)
+        local_ref[pl.ds(low_t, 8)] = fold_rows(rows[::-1])
         return flow
 
-    flow = lax.fori_loop(0, tokens // 8, block, jnp.zeros((states, cols), F32))
+    flow = lax.fori_loop(0, tokens // 8, block, jnp.zeros((states, cols), F32), unroll=2)
     total = jnp.broadcast_to(total_ref[...], (8, cols))
     whole_part = total.astype(BF).astype(F32)
     row = lax.broadcasted_iota(jnp.int32, (8, cols), 0)

time: 234 us -> 234 us (level)
  no operation moved by 1% of the time
where the time goes in v9:
time: 234 us; the launch traced here: 233 us
  Pallas kernels  82.3 us (35%)
  blocking collectives  50.1 us (21%)
  waiting for transfers between devices  48.5 us (21%)
  starting transfers between devices  39.5 us (17%)
  local copies, waits for them, and re-layouts  11.7 us (5%)
    pallas_call x4, Pallas kernels, expert_rows(): pl.pallas_call(functools.partial(expert_body, sizes), in_specs=[vmem] * (...  54.8 us
    ppermute x16, waiting for transfers between devices, shift(): return lax.ppermute(value, 'z', ring)  33.4 us
    all_to_all x1, blocking collectives, exchange(): got = lax.all_to_all(parts, 'exp', split_axis=0, concat_axis=0, tiled=True)  28.3 us
    ppermute x16, starting transfers between devices, shift(): return lax.ppermute(value, 'z', ring)  23.4 us
    all_gather x1, blocking collectives, on_device(): starts = lax.all_gather(start, ('z', 'core'))  21.8 us
    all_to_all x3, waiting for transfers between devices, exchange(): got = lax.all_to_all(parts, 'exp', split_axis=0, concat_axis=0, tiled=True)  15.2 us
    all_to_all x3, starting transfers between devices, exchange(): got = lax.all_to_all(parts, 'exp', split_axis=0, concat_axis=0, tiled=True)  14.5 us
    pallas_call x1, Pallas kernels, combine_and_scan(): pl.pallas_call(scan_body, grid=(dim // cols,), in_specs=[whole(*t.shape)...  9.96 us
  transfers between devices with their start and end apart: 21, of which 7 were waited for; matrix products, arithmetic and copies ran while one was open for 3% of the time, Pallas kernels for 28%

profile of v9, /device:TPU:1, one launch (start us, length us, event | category | flops | bytes accessed | tf_op | source)
XLA Modules:
  0.0 233.1 jit_solution(6876417307223424672)
XLA Ops:
  0.6 1.5 collective-permute-start
  2.2 0.8 copy.15
  3.1 1.1 copy-done.2
  4.2 1.0 copy-done.6
  5.2 1.7 gather_rows.1
  6.9 28.3 %all_to_all.20 = bf16[16,24,2048]{2,1,0:T(8,128)(2,1)S(1)} all-to-all(bf16[16,24,2048]{2,1,0:T(8,128)(2,1)S(1)} %bitcast.37), channel_id=1, replica_groups=mesh['z'=4,'core'=2,'exp'=16] {'exp'}, dimensions={0} | all-to-all | bytes 3145728 | tf_op jit(solution)/shard_map/all_to_all | solution.py:468
  35.3 0.6 sort_messages.2.refs_0_
  35.9 1.7 collective-permute-start.2
  37.6 2.2 collective-permute-start.3
  39.8 3.8 %all-to-all-start = ((bf16[16,16,2048]{2,1,0:T(8,128)(2,1)}), bf16[16,16,2048]{2,1,0:T(8,128)(2,1)S(1)}, u32[]{:S(2)}, u32[]{:S(2)}) async-start(bf16[16,16,2048]{2,1,0:T(8,128)(2,1)} %bitcast.38), calls=%async_computation | async-start | bytes 2097152 | tf_op jit(solution)/shard_map/all_to_all | solution.py:468
  43.9 0.4 weigh_tables.1
  44.4 0.6 copy-done.9
  45.0 0.6 copy-done.10
  45.7 1.2 copy-done.4
  46.9 5.8 %reach_table.1 = (bf16[16,128,2048]{2,1,0:T(8,128)(2,1)}, f32[1,2048]{1,0:T(1,128)S(1)}) custom-call(f32[128,2048]{1,0:T(8,128)S(1)} %bitcast.40, f32[16,2048]{1,0:T(8,128)S(1)} %copy-done.5, f32[128,16]{1,0:T(8,128)S(1)} %bitcast.44), custom_call_target="tpu_custom_call" | custom-call | flops 33554432 | bytes 8388608 | tf_op jit(solution)/shard_map/reach_table/pallas_call | solution.py:393
  52.7 5.6 %all-to-all-done = bf16[16,16,2048]{2,1,0:T(8,128)(2,1)S(1)} async-done(((bf16[16,16,2048]{2,1,0:T(8,128)(2,1)}), bf16[16,16,2048]{2,1,0:T(8,128)(2,1)S(1)}, u32[]{:S(2)}, u32[]{:S(2)}) %all-to-all-start) | async-done | bytes 1048608 | tf_op jit(solution)/shard_map/all_to_all | solution.py:468
  58.3 1.3 broadcast_in_dim.18.refs_8_
  59.6 1.3 broadcast_in_dim.20.refs_9_
  60.9 0.4 sort_messages.3.refs_3_
  61.3 11.1 %collective-permute-done.2.refs_1_ = bf16[384,2048]{1,0:T(8,128)(2,1)} collective-permute-done((bf16[384,2048]{1,0:T(8,128)(2,1)S(1)}, bf16[384,2048]{1,0:T(8,128)(2,1)}, u32[]{:S(2)}, u32[]{:S(2)}) %collective-permute-start.2) | collective-permute-done | bytes 1572896 | tf_op jit(solution)/shard_map/ppermute | solution.py:461
  72.4 0.4 collective-permute-start.6
  72.8 2.2 collective-permute-start.7
  75.1 1.2 slice.12
  76.4 1.2 slice.13
  77.6 2.9 %collective-permute-start.5 = (bf16[192,2048]{1,0:T(8,128)(2,1)S(1)}, bf16[192,2048]{1,0:T(8,128)(2,1)S(1)}, u32[]{:S(2)}, u32[]{:S(2)}) collective-permute-start(bf16[192,2048]{1,0:T(8,128)(2,1)S(1)} %slice.13), channel_id=1, source_target_pairs={{0,96},{32,0},{64,32},{96,64},{1,97},{33,1},{65,33},{97,65},{2,98}... | collective-permute-start | bytes 2359304 | tf_op jit(solution)/shard_map/ppermute | solution.py:461
  80.5 22.5 %expert_rows.4 = (bf16[96,2048]{1,0:T(8,128)(2,1)S(1)}, bf16[96,2048]{1,0:T(8,128)(2,1)S(1)}, bf16[96,2048]{1,0:T(8,128)(2,1)S(1)}, bf16[96,2048]{1,0:T(8,128)(2...) custom-call(bf16[384,2048]{1,0:T(8,128)(2,1)S(1)} %sort_messages.2.r, ...), custom_call_target="tpu_custom_call" | custom-call | flops 1937768448 | bytes 1441792 | tf_op jit(solution)/shard_map/expert_rows/pallas_call | solution.py:218
  103.0 9.3 %collective-permute-done.4.refs_0_ = bf16[192,2048]{1,0:T(8,128)(2,1)S(1)} collective-permute-done((bf16[192,2048]{1,0:T(8,128)(2,1)S(1)}, bf16[192,2048]{1,0:T(8,128)(2,1)S(1)}, u32[]{:S(2)}, u32[]{:S(2)}) %collective-permute-start.4) | collective-permute-done | bytes 786464 | tf_op jit(solution)/shard_map/ppermute | solution.py:461
  112.6 2.7 %collective-permute-start.9 = (bf16[128,2048]{1,0:T(8,128)(2,1)S(1)}, bf16[128,2048]{1,0:T(8,128)(2,1)S(1)}, u32[]{:S(2)}, u32[]{:S(2)}) collective-permute-start(bf16[128,2048]{1,0:T(8,128)(2,1)S(1)} %slice.15), channel_id=1, source_target_pairs={{0,96},{32,0},{64,32},{96,64},{1,97},{33,1},{65,33},{97,65},{2,98}... | collective-permute-start | bytes 1572872 | tf_op jit(solution)/shard_map/ppermute | solution.py:461
  115.3 11.1 %expert_rows.5 = (bf16[96,2048]{1,0:T(8,128)(2,1)S(1)}, bf16[96,2048]{1,0:T(8,128)(2,1)S(1)}) custom-call(bf16[192,2048]{1,0:T(8,128)(2,1)S(1)} %collective-permute-done.4.refs_0_, bf16[192,2048]{1,0:T(8,128)(2,1)S(1)} %collective-permute-done.5.refs_1_, bf16[896,2048]{1,0:T(8,128)(2,1)S(1)} %bitcast.25, ...), custom_call_target="tpu_custom_call" | custom-call | flops 528482304 | bytes 393216 | tf_op jit(solution)/shard_map/expert_rows/pallas_call | solution.py:218
  126.5 2.7 %collective-permute-start.11 = (bf16[96,2048]{1,0:T(8,128)(2,1)S(1)}, bf16[96,2048]{1,0:T(8,128)(2,1)S(1)}, u32[]{:S(2)}, u32[]{:S(2)}) collective-permute-start(bf16[96,2048]{1,0:T(8,128)(2,1)S(1)} %get-tuple-element.113), channel_id=1, source_target_pairs={{0,96},{32,0},{64,32},{96,64},{1,97},{33,1},{65,33},{97,65},{2,98}... | collective-permute-start | bytes 1179656 | tf_op jit(solution)/shard_map/ppermute | solution.py:461
  129.2 10.9 %expert_rows.6 = (bf16[64,2048]{1,0:T(8,128)(2,1)S(1)}, bf16[64,2048]{1,0:T(8,128)(2,1)S(1)}, bf16[64,2048]{1,0:T(8,128)(2,1)S(1)}, bf16[64,2048]{1,0:T(8,128)(2,1)S(1)}) custom-call(bf16[256,2048]{1,0:T(8,128)(2,1)S(1)} %collective-permute-done.6.refs_0_, bf16[256,2048]{1,0:T(8,128)(2,1)S(1)} %collective-permute-done.7.refs_1_, ...), custom_call_target="tpu_custom_call" | custom-call | flops 704643072 | bytes 524288 | tf_op jit(solution)/shard_map/expert_rows/pallas_call | solution.py:218
  140.1 0.2 hop_sums.2
  140.4 2.7 %collective-permute-start.13 = (bf16[192,2048]{1,0:T(8,128)(2,1)S(1)}, bf16[192,2048]{1,0:T(8,128)(2,1)S(1)}, u32[]{:S(2)}, u32[]{:S(2)}) collective-permute-start(bf16[192,2048]{1,0:T(8,128)(2,1)S(1)} %get-tuple-element.117), channel_id=1, source_target_pairs={{0,96},{32,0},{64,32},{96,64},{1,97},{33,1},{65,33},{97,65},{2,98}... | collective-permute-start | bytes 2359304 | tf_op jit(solution)/shard_map/ppermute | solution.py:461
  143.1 10.3 %expert_rows.7 = (bf16[64,2048]{1,0:T(8,128)(2,1)S(1)}, bf16[64,2048]{1,0:T(8,128)(2,1)S(1)}) custom-call(bf16[128,2048]{1,0:T(8,128)(2,1)S(1)} %collective-permute-done.8.refs_0_, bf16[128,2048]{1,0:T(8,128)(2,1)S(1)} %collective-permute-done.9.refs_1_, bf16[896,2048]{1,0:T(8,128)(2,1)S(1)} %bitcast.27, ...), custom_call_target="tpu_custom_call" | custom-call | flops 352321536 | bytes 262144 | tf_op jit(solution)/shard_map/expert_rows/pallas_call | solution.py:218
  153.5 2.7 %collective-permute-start.15 = (bf16[64,2048]{1,0:T(8,128)(2,1)S(1)}, bf16[64,2048]{1,0:T(8,128)(2,1)S(1)}, u32[]{:S(2)}, u32[]{:S(2)}) collective-permute-start(bf16[64,2048]{1,0:T(8,128)(2,1)S(1)} %get-tuple-element.121), channel_id=1, source_target_pairs={{0,96},{32,0},{64,32},{96,64},{1,97},{33,1},{65,33},{97,65},{2,98}... | collective-permute-start | bytes 786440 | tf_op jit(solution)/shard_map/ppermute | solution.py:461
  156.2 1.5 pack_returns.2
  157.6 5.4 %collective-permute-done.14.got_a = bf16[64,2048]{1,0:T(8,128)(2,1)S(1)} collective-permute-done((bf16[64,2048]{1,0:T(8,128)(2,1)S(1)}, bf16[64,2048]{1,0:T(8,128)(2,1)S(1)}, u32[]{:S(2)}, u32[]{:S(2)}) %collective-permute-start.14) | collective-permute-done | bytes 262176 | tf_op jit(solution)/shard_map/ppermute | solution.py:461
  163.1 4.9 %all-to-all-start.2 = ((bf16[16,16,2048]{2,1,0:T(8,128)(2,1)}), bf16[16,16,2048]{2,1,0:T(8,128)(2,1)S(1)}, u32[]{:S(2)}, u32[]{:S(2)}) async-start(bf16[16,16,2048]{2,1,0:T(8,128)(2,1)} %bitcast.14), calls=%async_computation.2 | async-start | bytes 2097152 | tf_op jit(solution)/shard_map/all_to_all | solution.py:468
  168.2 2.7 %collective-permute-start.17 = (bf16[128,2048]{1,0:T(8,128)(2,1)S(1)}, bf16[128,2048]{1,0:T(8,128)(2,1)S(1)}, u32[]{:S(2)}, u32[]{:S(2)}) collective-permute-start(bf16[128,2048]{1,0:T(8,128)(2,1)S(1)} %get-tuple-element.132), channel_id=1, source_target_pairs={{0,96},{32,0},{64,32},{96,64},{1,97},{33,1},{65,33},{97,65},{2,98}... | collective-permute-start | bytes 1572872 | tf_op jit(solution)/shard_map/ppermute | solution.py:461
  170.9 7.5 %collective-permute-done.16.refs_2_ = bf16[128,2048]{1,0:T(8,128)(2,1)S(1)} collective-permute-done((bf16[128,2048]{1,0:T(8,128)(2,1)S(1)}, bf16[128,2048]{1,0:T(8,128)(2,1)S(1)}, u32[]{:S(2)}, u32[]{:S(2)}) %collective-permute-start.16) | collective-permute-done | bytes 524320 | tf_op jit(solution)/shard_map/ppermute | solution.py:461
  178.4 1.0 pack_returns.3
  179.4 0.6 all-to-all-done.2
  180.0 5.7 %all-to-all-start.3 = ((bf16[16,8,2048]{2,1,0:T(8,128)(2,1)}), bf16[16,8,2048]{2,1,0:T(8,128)(2,1)S(1)}, u32[]{:S(2)}, u32[]{:S(2)}) async-start(bf16[16,8,2048]{2,1,0:T(8,128)(2,1)} %bitcast.16), calls=%async_computation.3 | async-start | bytes 1048576 | tf_op jit(solution)/shard_map/all_to_all | solution.py:468
  185.8 8.9 %all-to-all-done.3 = bf16[16,8,2048]{2,1,0:T(8,128)(2,1)S(1)} async-done(((bf16[16,8,2048]{2,1,0:T(8,128)(2,1)}), bf16[16,8,2048]{2,1,0:T(8,128)(2,1)S(1)}, u32[]{:S(2)}, u32[]{:S(2)}) %all-to-all-start.3) | async-done | bytes 524320 | tf_op jit(solution)/shard_map/all_to_all | solution.py:468
  194.7 0.8 copy-done.14
  195.5 10.0 %combine_and_scan.1 = (bf16[128,2048]{1,0:T(8,128)(2,1)}, f32[128,2048]{1,0:T(8,128)}, bf16[24,2048]{1,0:T(8,128)(2,1)}) custom-call(bf16[128,384]{1,0:T(8,128)(2,1)} %copy-done.9, bf16[128,384]{1,0:T(8,128)(2,1)} %copy-done.10, bf16[256,2048]{1,0:T(8,128)(2,1)} %bitcast.47, bf16[128,2048]{1,0:T(8,128)(2,1)} %bitcast.49, bf16[128,2048]{1,0:T(8,128)(2,1)} %bitcast.35, ...), custom_call_target="tpu_custom_call" | custom-call | tf_op jit(solution)/shard_map/combine_and_scan/pallas_call | solution.py:347
  205.5 21.8 %all-gather = bf16[192,2048]{1,0:T(8,128)(2,1)} all-gather(bf16[24,2048]{1,0:T(8,128)(2,1)} %get-tuple-element.137), channel_id=2, replica_groups=mesh['z'=4,'core'=2,'exp'=16] {'z','core'}, dimensions={0}, use_global_device_ids=true | all-gather | bytes 884736 | tf_op jit(solution)/shard_map/all_gather | solution.py:527
  227.3 5.8 %add_carry.1 = bf16[128,2048]{1,0:T(8,128)(2,1)} custom-call(s32[1]{0:T(128)} %bitcast.19.place_ref, bf16[8,24,2048]{2,1,0:T(8,128)(2,1)} %bitcast.48, f32[16,2048]{1,0:T(8,128)} %rate_ref.3, f32[128,2048]{1,0:T(8,128)} %get-tuple-element.138.local_ref, bf16[16,128,2048]{2,1,0:T(8,128)(2,1)} %get-tuple-element.139.reach_ref), custom_call_target="tpu_custom_call" | custom-call | tf_op jit(solution)/shard_map/add_carry/pallas_call | solution.py:437
  (58 shorter events, 1.2 us)
Async XLA Ops:
  0.6 34.7 %copy-start.8 = (bf16[192,192]{1,0:T(8,128)(2,1)S(1)}, bf16[192,192]{1,0:T(8,128)(2,1)}, u32[]{:S(2)}) copy-start(bf16[192,192]{1,0:T(8,128)(2,1)} %constant.20.clone.table_ref) | copy-start | bytes 221188
  0.6 34.6 %collective-permute-start = (bf16[896,2048]{1,0:T(8,128)(2,1)}, bf16[896,2048]{1,0:T(8,128)(2,1)}, u32[]{:S(2)}, u32[]{:S(2)}) collective-permute-start(bf16[896,2048]{1,0:T(8,128)(2,1)} %bitcast.23), channel_id=1, source_target_pairs={{0,16},{16,0},{1,17},{17,1},{2,18},{18,2},{3,19},{19,3},{4,20},{20... | collective-permute-start | bytes 11010056 | tf_op jit(solution)/shard_map/ppermute | solution.py:464
  2.1 33.1 %collective-permute-start.1 = (bf16[896,2048]{1,0:T(8,128)(2,1)}, bf16[896,2048]{1,0:T(8,128)(2,1)}, u32[]{:S(2)}, u32[]{:S(2)}) collective-permute-start(bf16[896,2048]{1,0:T(8,128)(2,1)} %bitcast.28), channel_id=1, source_target_pairs={{0,16},{16,0},{1,17},{17,1},{2,18},{18,2},{3,19},{19,3},{4,20},{20... | collective-permute-start | bytes 11010056 | tf_op jit(solution)/shard_map/ppermute | solution.py:464
  3.1 1.1 copy-start.2
  4.1 1.0 copy-start.6
  6.9 28.4 %copy-start.3 = (bf16[256,2048]{1,0:T(8,128)(2,1)}, bf16[256,2048]{1,0:T(8,128)(2,1)S(1)}, u32[]{:S(2)}) copy-start(bf16[256,2048]{1,0:T(8,128)(2,1)S(1)} %get-tuple-element.71) | copy-start | bytes 3145732
  6.9 36.7 %copy-start.15 = (f32[1,128,16]{1,2,0:T(8,128)S(1)}, f32[1,128,16]{1,2,0:T(8,128)}, u32[]{:S(2)}) copy-start(f32[1,128,16]{1,2,0:T(8,128)} %param.21) | copy-start | bytes 24580
  6.9 36.8 %copy-start.17 = (f32[1,128,2]{1,2,0:T(2,128)S(1)}, f32[1,128,2]{1,2,0:T(2,128)}, u32[]{:S(2)}) copy-start(f32[1,128,2]{1,2,0:T(2,128)} %param.16) | copy-start | bytes 3076
  6.9 36.9 %copy-start.16 = (f32[1,128,16]{1,2,0:T(8,128)S(1)}, f32[1,128,16]{1,2,0:T(8,128)}, u32[]{:S(2)}) copy-start(f32[1,128,16]{1,2,0:T(8,128)} %param.22) | copy-start | bytes 24580
  6.9 38.7 %copy-start.5 = (f32[16,2048]{1,0:T(8,128)S(1)}, f32[16,2048]{1,0:T(8,128)}, u32[]{:S(2)}) copy-start(f32[16,2048]{1,0:T(8,128)} %rate_ref.3) | copy-start | bytes 393220
  35.9 36.5 %collective-permute-start.2 = (bf16[384,2048]{1,0:T(8,128)(2,1)S(1)}, bf16[384,2048]{1,0:T(8,128)(2,1)}, u32[]{:S(2)}, u32[]{:S(2)}) collective-permute-start(bf16[384,2048]{1,0:T(8,128)(2,1)S(1)} %sort_messages.2.refs_0_), channel_id=1, source_target_pairs={{0,32},{32,64},{64,96},{96,0},{1,33},{33,65},{65,97},{97,1},{2,34}... | collective-permute-start | bytes 4718600 | tf_op jit(solution)/shard_map/ppermute | solution.py:461
  37.6 34.8 %collective-permute-start.3 = (bf16[384,2048]{1,0:T(8,128)(2,1)S(1)}, bf16[384,2048]{1,0:T(8,128)(2,1)}, u32[]{:S(2)}, u32[]{:S(2)}) collective-permute-start(bf16[384,2048]{1,0:T(8,128)(2,1)S(1)} %sort_messages.2.refs_0_), channel_id=1, source_target_pairs={{0,96},{32,0},{64,32},{96,64},{1,97},{33,1},{65,33},{97,65},{2,98}... | collective-permute-start | bytes 4718600 | tf_op jit(solution)/shard_map/ppermute | solution.py:461
  39.8 18.5 %all-to-all-start = ((bf16[16,16,2048]{2,1,0:T(8,128)(2,1)}), bf16[16,16,2048]{2,1,0:T(8,128)(2,1)S(1)}, u32[]{:S(2)}, u32[]{:S(2)}) async-start(bf16[16,16,2048]{2,1,0:T(8,128)(2,1)} %bitcast.38), calls=%async_computation | async-start | bytes 2097152 | tf_op jit(solution)/shard_map/all_to_all | solution.py:468
  44.4 0.6 copy-start.9
  45.0 0.6 copy-start.10
  45.7 1.2 copy-start.4
  46.9 14.0 %copy-start.11 = (bf16[128,128]{1,0:T(8,128)(2,1)S(1)}, bf16[128,128]{1,0:T(8,128)(2,1)}, u32[]{:S(2)}) copy-start(bf16[128,128]{1,0:T(8,128)(2,1)} %constant.21.clone.table_ref) | copy-start | bytes 98308
  52.7 24.9 %copy-start.12 = (f32[1,2048]{1,0:T(1,128)}, f32[1,2048]{1,0:T(1,128)S(1)}, u32[]{:S(2)}) copy-start(f32[1,2048]{1,0:T(1,128)S(1)} %get-tuple-element.133.refs_7_) | copy-start | bytes 24580
  58.3 22.2 %copy-start = (bf16[1,896,2048]{2,1,0:T(8,128)(2,1)S(1)}, bf16[1,896,2048]{2,1,0:T(8,128)(2,1)}, u32[]{:S(2)}) copy-start(bf16[1,896,2048]{2,1,0:T(8,128)(2,1)} %param.17) | copy-start | bytes 11010052
  58.3 22.2 %copy-start.1 = (bf16[1,896,2048]{2,1,0:T(8,128)(2,1)S(1)}, bf16[1,896,2048]{2,1,0:T(8,128)(2,1)}, u32[]{:S(2)}) copy-start(bf16[1,896,2048]{2,1,0:T(8,128)(2,1)} %param.18) | copy-start | bytes 11010052
  72.4 40.0 %collective-permute-start.6 = (bf16[256,2048]{1,0:T(8,128)(2,1)S(1)}, bf16[256,2048]{1,0:T(8,128)(2,1)S(1)}, u32[]{:S(2)}, u32[]{:S(2)}) collective-permute-start(bf16[256,2048]{1,0:T(8,128)(2,1)S(1)} %sort_messages.3.refs_3_), channel_id=1, source_target_pairs={{0,32},{32,64},{64,96},{96,0},{1,33},{33,65},{65,97},{97,1},{2,34}... | collective-permute-start | bytes 3145736 | tf_op jit(solution)/shard_map/ppermute | solution.py:461
  72.8 39.5 %collective-permute-start.7 = (bf16[256,2048]{1,0:T(8,128)(2,1)S(1)}, bf16[256,2048]{1,0:T(8,128)(2,1)S(1)}, u32[]{:S(2)}, u32[]{:S(2)}) collective-permute-start(bf16[256,2048]{1,0:T(8,128)(2,1)S(1)} %sort_messages.3.refs_3_), channel_id=1, source_target_pairs={{0,96},{32,0},{64,32},{96,64},{1,97},{33,1},{65,33},{97,65},{2,98}... | collective-permute-start | bytes 3145736 | tf_op jit(solution)/shard_map/ppermute | solution.py:461
  76.3 36.1 %collective-permute-start.4 = (bf16[192,2048]{1,0:T(8,128)(2,1)S(1)}, bf16[192,2048]{1,0:T(8,128)(2,1)S(1)}, u32[]{:S(2)}, u32[]{:S(2)}) collective-permute-start(bf16[192,2048]{1,0:T(8,128)(2,1)S(1)} %slice.12), channel_id=1, source_target_pairs={{0,32},{32,64},{64,96},{96,0},{1,33},{33,65},{65,97},{97,1},{2,34}... | collective-permute-start | bytes 2359304 | tf_op jit(solution)/shard_map/ppermute | solution.py:461
  77.6 34.8 %collective-permute-start.5 = (bf16[192,2048]{1,0:T(8,128)(2,1)S(1)}, bf16[192,2048]{1,0:T(8,128)(2,1)S(1)}, u32[]{:S(2)}, u32[]{:S(2)}) collective-permute-start(bf16[192,2048]{1,0:T(8,128)(2,1)S(1)} %slice.13), channel_id=1, source_target_pairs={{0,96},{32,0},{64,32},{96,64},{1,97},{33,1},{65,33},{97,65},{2,98}... | collective-permute-start | bytes 2359304 | tf_op jit(solution)/shard_map/ppermute | solution.py:461
  112.4 27.9 %collective-permute-start.8 = (bf16[128,2048]{1,0:T(8,128)(2,1)S(1)}, bf16[128,2048]{1,0:T(8,128)(2,1)S(1)}, u32[]{:S(2)}, u32[]{:S(2)}) collective-permute-start(bf16[128,2048]{1,0:T(8,128)(2,1)S(1)} %slice.14), channel_id=1, source_target_pairs={{0,32},{32,64},{64,96},{96,0},{1,33},{33,65},{65,97},{97,1},{2,34}... | collective-permute-start | bytes 1572872 | tf_op jit(solution)/shard_map/ppermute | solution.py:461
  112.6 27.7 %collective-permute-start.9 = (bf16[128,2048]{1,0:T(8,128)(2,1)S(1)}, bf16[128,2048]{1,0:T(8,128)(2,1)S(1)}, u32[]{:S(2)}, u32[]{:S(2)}) collective-permute-start(bf16[128,2048]{1,0:T(8,128)(2,1)S(1)} %slice.15), channel_id=1, source_target_pairs={{0,96},{32,0},{64,32},{96,64},{1,97},{33,1},{65,33},{97,65},{2,98}... | collective-permute-start | bytes 1572872 | tf_op jit(solution)/shard_map/ppermute | solution.py:461
  126.4 13.6 %collective-permute-start.10 = (bf16[96,2048]{1,0:T(8,128)(2,1)S(1)}, bf16[96,2048]{1,0:T(8,128)(2,1)S(1)}, u32[]{:S(2)}, u32[]{:S(2)}) collective-permute-start(bf16[96,2048]{1,0:T(8,128)(2,1)S(1)} %get-tuple-element.112), channel_id=1, source_target_pairs={{0,32},{32,64},{64,96},{96,0},{1,33},{33,65},{65,97},{97,1},{2,34}... | collective-permute-start | bytes 1179656 | tf_op jit(solution)/shard_map/ppermute | solution.py:461
  126.5 13.6 %collective-permute-start.11 = (bf16[96,2048]{1,0:T(8,128)(2,1)S(1)}, bf16[96,2048]{1,0:T(8,128)(2,1)S(1)}, u32[]{:S(2)}, u32[]{:S(2)}) collective-permute-start(bf16[96,2048]{1,0:T(8,128)(2,1)S(1)} %get-tuple-element.113), channel_id=1, source_target_pairs={{0,96},{32,0},{64,32},{96,64},{1,97},{33,1},{65,33},{97,65},{2,98}... | collective-permute-start | bytes 1179656 | tf_op jit(solution)/shard_map/ppermute | solution.py:461
  140.3 15.8 %copy-start.7 = (bf16[256,192]{1,0:T(8,128)(2,1)S(1)}, bf16[256,192]{1,0:T(8,128)(2,1)}, u32[]{:S(2)}) copy-start(bf16[256,192]{1,0:T(8,128)(2,1)} %constant.22.clone.refs_0_) | copy-start | bytes 294916
  140.3 15.8 %collective-permute-start.12 = (bf16[192,2048]{1,0:T(8,128)(2,1)S(1)}, bf16[192,2048]{1,0:T(8,128)(2,1)S(1)}, u32[]{:S(2)}, u32[]{:S(2)}) collective-permute-start(bf16[192,2048]{1,0:T(8,128)(2,1)S(1)} %get-tuple-element.116), channel_id=1, source_target_pairs={{0,32},{32,64},{64,96},{96,0},{1,33},{33,65},{65,97},{97,1},{2,34}... | collective-permute-start | bytes 2359304 | tf_op jit(solution)/shard_map/ppermute | solution.py:461
  140.4 15.7 %collective-permute-start.13 = (bf16[192,2048]{1,0:T(8,128)(2,1)S(1)}, bf16[192,2048]{1,0:T(8,128)(2,1)S(1)}, u32[]{:S(2)}, u32[]{:S(2)}) collective-permute-start(bf16[192,2048]{1,0:T(8,128)(2,1)S(1)} %get-tuple-element.117), channel_id=1, source_target_pairs={{0,96},{32,0},{64,32},{96,64},{1,97},{33,1},{65,33},{97,65},{2,98}... | collective-permute-start | bytes 2359304 | tf_op jit(solution)/shard_map/ppermute | solution.py:461
  153.4 9.7 %collective-permute-start.14 = (bf16[64,2048]{1,0:T(8,128)(2,1)S(1)}, bf16[64,2048]{1,0:T(8,128)(2,1)S(1)}, u32[]{:S(2)}, u32[]{:S(2)}) collective-permute-start(bf16[64,2048]{1,0:T(8,128)(2,1)S(1)} %get-tuple-element.120), channel_id=1, source_target_pairs={{0,32},{32,64},{64,96},{96,0},{1,33},{33,65},{65,97},{97,1},{2,34}... | collective-permute-start | bytes 786440 | tf_op jit(solution)/shard_map/ppermute | solution.py:461
  153.5 9.6 %collective-permute-start.15 = (bf16[64,2048]{1,0:T(8,128)(2,1)S(1)}, bf16[64,2048]{1,0:T(8,128)(2,1)S(1)}, u32[]{:S(2)}, u32[]{:S(2)}) collective-permute-start(bf16[64,2048]{1,0:T(8,128)(2,1)S(1)} %get-tuple-element.121), channel_id=1, source_target_pairs={{0,96},{32,0},{64,32},{96,64},{1,97},{33,1},{65,33},{97,65},{2,98}... | collective-permute-start | bytes 786440 | tf_op jit(solution)/shard_map/ppermute | solution.py:461
  163.1 17.0 %all-to-all-start.2 = ((bf16[16,16,2048]{2,1,0:T(8,128)(2,1)}), bf16[16,16,2048]{2,1,0:T(8,128)(2,1)S(1)}, u32[]{:S(2)}, u32[]{:S(2)}) async-start(bf16[16,16,2048]{2,1,0:T(8,128)(2,1)} %bitcast.14), calls=%async_computation.2 | async-start | bytes 2097152 | tf_op jit(solution)/shard_map/all_to_all | solution.py:468
  168.1 10.3 %collective-permute-start.16 = (bf16[128,2048]{1,0:T(8,128)(2,1)S(1)}, bf16[128,2048]{1,0:T(8,128)(2,1)S(1)}, u32[]{:S(2)}, u32[]{:S(2)}) collective-permute-start(bf16[128,2048]{1,0:T(8,128)(2,1)S(1)} %get-tuple-element.131), channel_id=1, source_target_pairs={{0,32},{32,64},{64,96},{96,0},{1,33},{33,65},{65,97},{97,1},{2,34}... | collective-permute-start | bytes 1572872 | tf_op jit(solution)/shard_map/ppermute | solution.py:461
  168.2 10.2 %collective-permute-start.17 = (bf16[128,2048]{1,0:T(8,128)(2,1)S(1)}, bf16[128,2048]{1,0:T(8,128)(2,1)S(1)}, u32[]{:S(2)}, u32[]{:S(2)}) collective-permute-start(bf16[128,2048]{1,0:T(8,128)(2,1)S(1)} %get-tuple-element.132), channel_id=1, source_target_pairs={{0,96},{32,0},{64,32},{96,64},{1,97},{33,1},{65,33},{97,65},{2,98}... | collective-permute-start | bytes 1572872 | tf_op jit(solution)/shard_map/ppermute | solution.py:461
  180.0 14.7 %copy-start.13 = (bf16[16,16,2048]{2,1,0:T(8,128)(2,1)}, bf16[16,16,2048]{2,1,0:T(8,128)(2,1)S(1)}, u32[]{:S(2)}) copy-start(bf16[16,16,2048]{2,1,0:T(8,128)(2,1)S(1)} %all-to-all-done.2) | copy-start | bytes 3145732
  180.0 14.7 %all-to-all-start.3 = ((bf16[16,8,2048]{2,1,0:T(8,128)(2,1)}), bf16[16,8,2048]{2,1,0:T(8,128)(2,1)S(1)}, u32[]{:S(2)}, u32[]{:S(2)}) async-start(bf16[16,8,2048]{2,1,0:T(8,128)(2,1)} %bitcast.16), calls=%async_computation.3 | async-start | bytes 1048576 | tf_op jit(solution)/shard_map/all_to_all | solution.py:468
  194.7 0.8 copy-start.14
